TPU v7x, 128 devices: a whole 4x4x4 slice. The times are simulated.
128 devices in a mesh: replica: 8 (over y, core), tensor: 16 (over z, x).
Axes of the slice: x: 4, y: 4, z: 4, core: 2. Of those that a mesh axis runs over, the one named last changes fastest.
Arguments:
- gradient: bfloat16 [8, 6144, 6144], P('replica', None, 'tensor'), may hold values from -40 to 40
- feedback: bfloat16 [8, 6144, 6144], P('replica', None, 'tensor'), may hold values from -6 to 6
- momentum: bfloat16 [6144, 6144], P('replica', 'tensor'), may hold values from -4 to 4
- right_init: float32 [6144, 8], P('tensor'), may hold values from -6 to 6
Outputs:
- feedback_out: bfloat16 [8, 6144, 6144], P('replica', None, 'tensor')
- momentum_out: bfloat16 [6144, 6144], P('replica', 'tensor')
- right_factor: float32 [6144, 8], P('tensor')
All inputs are finite; a program needn't handle non-finite values.
Results may differ from a plain program's by a relative error of at most 0.012.
Values sent between devices are 32-bit elements; how exact they have to be, the bound alone decides.
No kernel may reach another device: no remote copies, remote signals or barrier semaphores. Data moves between devices by JAX's collectives and lax.ppermute only.
A program may use at most 64 MiB of HBM per device.

v0:
```python
import jax
import jax.numpy as jnp
from jax import lax
from jax.sharding import PartitionSpec as P


def orthonormal(left_factor, gram_matrix):
    factor_low = jnp.linalg.cholesky(gram_matrix)
    return lax.linalg.triangular_solve(
        factor_low, left_factor, left_side=False, lower=True, transpose_a=True
    )


def shards(gradient, feedback, momentum, right_init):
    merged = (gradient[0].astype(jnp.float32) + feedback[0].astype(jnp.float32)).astype(
        jnp.bfloat16
    )
    right_bf = right_init.astype(jnp.bfloat16)
    local_term = jnp.dot(merged, right_bf, preferred_element_type=jnp.float32)
    left_factor = lax.psum(local_term, ("replica", "tensor"))
    gram_matrix = jnp.dot(left_factor.T, left_factor, precision=lax.Precision.HIGHEST)
    basis_full = orthonormal(left_factor, gram_matrix)
    basis_bf = basis_full.astype(jnp.bfloat16)
    right_term = jnp.einsum("dc,dr->cr", merged, basis_bf, preferred_element_type=jnp.float32)
    right_factor = lax.psum(right_term, "replica") / lax.axis_size("replica")
    approx = jnp.dot(basis_full, right_factor.T, precision=lax.Precision.HIGHEST)
    feedback_out = (merged.astype(jnp.float32) - approx).astype(jnp.bfloat16)[None]
    mom_rows = momentum.shape[0]
    mom_start = lax.axis_index("replica") * mom_rows
    basis_slice = lax.dynamic_slice_in_dim(basis_full, mom_start, mom_rows, 0)
    approx_rows = jnp.dot(basis_slice, right_factor.T, precision=lax.Precision.HIGHEST)
    momentum_out = (0.9 * momentum.astype(jnp.float32) + approx_rows).astype(jnp.bfloat16)
    return (feedback_out, momentum_out, right_factor)


def solution(mesh):
    placed = (
        P("replica", None, "tensor"),
        P("replica", None, "tensor"),
        P("replica", "tensor"),
        P("tensor", None),
    )
    return jax.shard_map(
        shards,
        mesh=mesh,
        in_specs=placed,
        out_specs=(P("replica", None, "tensor"), P("replica", "tensor"), P("tensor", None)),
        check_vma=False,
    )
```

profile of v0, /device:TPU:1, one launch (start us, length us, event | category | flops | bytes accessed | tf_op | source)
XLA Modules:
  0.0 212.8 jit_solution(8825223028857268261)
XLA Ops:
  7.2 0.0 all-reduce.2.cloned.1.call-start
  7.2 5.8 %fusion.6 = f32[6144,8]{0,1:T(8,128)} fusion(f32[384,8]{0,1:T(8,128)} %param.7, bf16[1,6144,384]{2,1,0:T(8,128)(2,1)} %param.5, bf16[1,6144,384]{2,1,0:T(8,128)(2,1)} %param.4), kind=kOutput, calls=%fused_computation.10 | convolution fusion | flops 47188992 | bytes 9646080 | tf_op jit(solution)/shard_map/dot_general | solution.py:19
  13.0 0.0 all-reduce.2.cloned.1.call-update
  13.0 146.0 %all-reduce.2.cloned.1.call-done = f32[6144,8]{0,1:T(8,128)} async-done(((f32[6144,8]{0,1:T(8,128)}), f32[6144,8]{0,1:T(8,128)}) %all-reduce.2.cloned.1.call-update) | async-done | bytes 196624 | tf_op jit(solution)/shard_map/psum | solution.py:20
  159.0 1.6 fusion.15
  160.6 0.1 copy.7
  160.7 0.7 cholesky.16
  161.4 0.1 select_reduce_fusion
  161.4 0.6 compare_reduce_fusion
  162.1 0.6 fusion.8
  162.7 0.6 custom-call.6
  163.3 1.3 fusion.9
  164.6 5.0 %fusion.3 = f32[384,8]{0,1:T(8,128)S(1)} fusion(f32[6144,8]{0,1:T(8,128)S(1)} %fusion.9, bf16[1,6144,384]{2,1,0:T(8,128)(2,1)} %param.5, bf16[1,6144,384]{2,1,0:T(8,128)(2,1)} %param.4), kind=kOutput, calls=%fused_computation.6 | convolution fusion | flops 47235072 | bytes 9646080 | tf_op jit(solution)/shard_map/dc,dr->cr/dot_general | solution.py:24
  169.6 22.2 %psum.15 = f32[384,8]{0,1:T(8,128)S(1)} all-reduce(f32[384,8]{0,1:T(8,128)S(1)} %fusion.3), channel_id=1, replica_groups=mesh['replica'=8,'tensor'=16] {'replica'}, use_global_device_ids=true, to_apply=%region_3.4 | all-reduce | flops 3072 | bytes 24576 | tf_op jit(solution)/shard_map/psum | solution.py:25
  191.8 0.0 copy-start.1
  191.8 0.0 copy-start
  191.8 12.2 %fusion = bf16[1,6144,384]{2,1,0:T(8,128)(2,1)} fusion(f32[6144,8]{0,1:T(8,128)S(1)} %fusion.9, f32[384,8]{0,1:T(8,128)S(1)} %broadcast_multiply_fusion, bf16[1,6144,384]{2,1,0:T(8,128)(2,1)} %param.5, bf16[1,6144,384]{2,1,0:T(8,128)(2,1)} %param.4), kind=kOutput, calls=%fused_computation.2 | convolution fusion | flops 243007488 | bytes 14364672 | tf_op jit(solution)/shard_map/dot_general | solution.py:26
  203.9 0.0 copy-done.1
  203.9 0.0 copy-done
  203.9 2.0 fusion.2
  (2 shorter events, 0.0 us)
Async XLA Ops:
  7.2 151.8 %all-reduce.2.cloned.1.call-start = ((), (), s32[]{:S(2)}) async-start(), calls=%async_computation | async-start | bytes 393216 | tf_op jit(solution)/shard_map/psum | solution.py:20
  191.8 12.2 %copy-start.1 = (f32[384,8]{0,1:T(8,128)}, f32[384,8]{0,1:T(8,128)S(1)}, u32[]{:S(2)}) copy-start(f32[384,8]{0,1:T(8,128)S(1)} %broadcast_multiply_fusion) | copy-start | bytes 36868
  191.8 12.2 %copy-start = (bf16[768,384]{1,0:T(8,128)(2,1)S(1)}, bf16[768,384]{1,0:T(8,128)(2,1)}, u32[]{:S(2)}) copy-start(bf16[768,384]{1,0:T(8,128)(2,1)} %param.6) | copy-start | bytes 1769476
Sparse Core Ops, SparseCore 0:
  13.3 145.7 all-reduce.1
where the time goes:
time: 215 us; the launch traced here: 213 us
  waiting for transfers between devices  146 us (68%)
  matrix products  27.8 us (13%)
  blocking collectives  22.2 us (10%)
  between operations  14.1 us (7%)
  other arithmetic  2.7 us (1%)
    psum x1, waiting for transfers between devices, shards(): left_factor = lax.psum(local_term, ('replica', 'tensor'))  146 us
    psum x1, blocking collectives, shards(): right_factor = lax.psum(right_term, 'replica') / lax.axis_size('replica')  22.2 us
    dot_general x1, matrix products, shards(): jnp.dot(basis_full, right_factor.T, precision=lax.Precision.HIGHEST)  12.2 us
    dot_general x1, matrix products, shards(): local_term = jnp.dot(merged, right_bf, preferred_element_type=jnp.float32)  5.79 us
    dot_general x1, matrix products, shards(): jnp.einsum('dc,dr->cr', merged, basis_bf, preferred_element_type=jnp.floa...  4.96 us
  transfers between devices with their start and end apart: 1, of which 1 were waited for; matrix products, arithmetic and copies ran while one was open for 0% of the time, Pallas kernels for 0%

commit v1 on v0

v1 whole, which is shorter than its diff:
```python
import jax
import jax.numpy as jnp
from jax import lax
from jax.experimental import pallas as pl
from jax.experimental.pallas import tpu as pltpu
from jax.sharding import PartitionSpec as P

F32, BF16 = jnp.float32, jnp.bfloat16
ROWS, COLS, RANK = 6144, 384, 8
HALF = ROWS // 2
BLOCK = 512
STEPS = ROWS // BLOCK
MIB = 1 << 20


def core_index():
    return lax.rem(lax.axis_index("replica"), 2)


def split(x):
    high = x.astype(BF16)
    return high, (x - high.astype(F32)).astype(BF16)


def merge_kernel(g_ref, f_ref, q_ref, merged_ref, keep_ref, send_ref):
    step = pl.program_id(0)
    merged = (g_ref[0].astype(F32) + f_ref[0].astype(F32)).astype(BF16)
    merged_ref[pl.ds(pl.multiple_of(step * BLOCK, BLOCK), BLOCK), :] = merged
    term = lax.dot_general(
        q_ref[...].astype(BF16), merged, (((1,), (1,)), ((), ())), preferred_element_type=F32
    )
    per_half = STEPS // 2
    where = pl.ds(pl.multiple_of(lax.rem(step, per_half) * BLOCK, BLOCK), BLOCK)
    mine = (step // per_half) == core_index()

    @pl.when(mine)
    def _():
        keep_ref[:, where] = term

    @pl.when(jnp.logical_not(mine))
    def _():
        send_ref[:, where] = term


def whole():
    return pl.BlockSpec(memory_space=pltpu.VMEM)


def merge(gradient, feedback, right_t):
    block = pl.BlockSpec((1, BLOCK, COLS), lambda i: (0, i, 0))
    return pl.pallas_call(
        merge_kernel,
        grid=(STEPS,),
        in_specs=[block, block, whole()],
        out_specs=[whole(), whole(), whole()],
        out_shape=[
            pltpu.VMEM((ROWS, COLS), BF16),
            pltpu.VMEM((RANK, HALF), F32),
            pltpu.VMEM((RANK, HALF), F32),
        ],
        compiler_params=pltpu.CompilerParams(vmem_limit_bytes=16 * MIB),
        cost_estimate=pl.CostEstimate(flops=2 * ROWS * COLS * RANK, bytes_accessed=4 * ROWS * COLS, transcendentals=0),
        name="merge",
    )(gradient, feedback, right_t)


def right_kernel(merged_ref, own_ref, other_ref, out_ref):
    core = core_index()
    total = jnp.zeros((2 * RANK, COLS), F32)
    for ref, half in ((own_ref, core), (other_ref, 1 - core)):
        rows = pl.ds(pl.multiple_of(half * HALF, HALF), HALF)
        pair = jnp.concatenate(split(ref[...]), axis=0)
        total += jnp.dot(pair, merged_ref[rows, :], preferred_element_type=F32)
    out_ref[...] = total[:RANK] + total[RANK:]


def right_term(merged, own, other):
    return pl.pallas_call(
        right_kernel,
        in_specs=[whole(), whole(), whole()],
        out_specs=whole(),
        out_shape=pltpu.VMEM((RANK, COLS), F32),
        compiler_params=pltpu.CompilerParams(vmem_limit_bytes=16 * MIB),
        cost_estimate=pl.CostEstimate(flops=4 * ROWS * COLS * RANK, bytes_accessed=2 * ROWS * COLS, transcendentals=0),
        name="right_term",
    )(merged, own, other)


def basis_kernel(own_ref, other_ref, inverse_ref, basis_ref):
    own, other = own_ref[...], other_ref[...]
    gram = jnp.zeros((RANK, RANK), F32)
    for part in (own, other):
        gram += lax.dot_general(
            part, part, (((1,), (1,)), ((), ())), precision=lax.Precision.HIGHEST, preferred_element_type=F32
        )
    row = lax.broadcasted_iota(jnp.int32, (RANK, RANK), 0)
    column = lax.broadcasted_iota(jnp.int32, (RANK, RANK), 1)
    eye = jnp.where(row == column, 1.0, 0.0)
    inverse = eye
    for k in range(RANK):
        factor = jnp.where(row[:, :1] > k, gram[:, k : k + 1] / gram[k : k + 1, k : k + 1], 0.0)
        inverse -= factor * inverse[k : k + 1, :]
        gram -= factor * gram[k : k + 1, :]
    pivots = jnp.sum(gram * eye, axis=1, keepdims=True)
    inverse = inverse / jnp.sqrt(pivots)
    inverse_ref[...] = inverse
    core = core_index()
    for part, half in ((own, core), (other, 1 - core)):
        basis = jnp.zeros((RANK, HALF), F32)
        for k in range(RANK):
            basis += inverse[:, k : k + 1] * part[k : k + 1, :]
        high, low = split(basis)
        packed = jnp.concatenate([high, high, low, low], axis=0)
        basis_ref[pl.ds(pl.multiple_of(half * HALF, HALF), HALF), :] = packed.T


def make_basis(own, other):
    return pl.pallas_call(
        basis_kernel,
        in_specs=[whole(), whole()],
        out_specs=[whole(), whole()],
        out_shape=[pltpu.VMEM((RANK, RANK), F32), pltpu.VMEM((ROWS, 4 * RANK), BF16)],
        compiler_params=pltpu.CompilerParams(vmem_limit_bytes=16 * MIB),
        cost_estimate=pl.CostEstimate(flops=4 * ROWS * RANK * RANK, bytes_accessed=4 * MIB, transcendentals=0),
        name="basis",
    )(own, other)


def final_kernel(replicas, merged_ref, basis_ref, inverse_ref, sum_ref, mom_ref, fb_ref, mom_out_ref, right_ref, pack_ref):
    step = pl.program_id(0)

    @pl.when(step == 0)
    def _():
        right = jnp.zeros((RANK, COLS), F32)
        for k in range(RANK):
            right += inverse_ref[:, k : k + 1] * sum_ref[k : k + 1, :]
        right = right * (1.0 / replicas)
        right_ref[...] = right
        high, low = split(right)
        pack_ref[...] = jnp.concatenate([high, low, high, low], axis=0)

    pack = pack_ref[...]
    rows = pl.ds(pl.multiple_of(step * BLOCK, BLOCK), BLOCK)
    approx = jnp.dot(basis_ref[rows, :], pack, preferred_element_type=F32)
    fb_ref[0] = (merged_ref[rows, :].astype(F32) - approx).astype(BF16)
    count = mom_ref.shape[0]
    start = lax.axis_index("replica") * (count * STEPS) + step * count
    mom_rows = pl.ds(pl.multiple_of(start, count), count)
    mom_approx = jnp.dot(basis_ref[mom_rows, :], pack, preferred_element_type=F32)
    mom_out_ref[...] = (0.9 * mom_ref[...].astype(F32) + mom_approx).astype(BF16)


def finish(replicas, merged, basis, inverse, right_sum, momentum):
    mom_rows = momentum.shape[0]
    mom_block = pl.BlockSpec((mom_rows // STEPS, COLS), lambda i: (i, 0))

    def body(*refs):
        final_kernel(replicas, *refs)

    return pl.pallas_call(
        body,
        grid=(STEPS,),
        in_specs=[whole(), whole(), whole(), whole(), mom_block],
        out_specs=[pl.BlockSpec((1, BLOCK, COLS), lambda i: (0, i, 0)), mom_block, whole()],
        out_shape=[
            jax.ShapeDtypeStruct((1, ROWS, COLS), BF16),
            jax.ShapeDtypeStruct((mom_rows, COLS), BF16),
            jax.ShapeDtypeStruct((RANK, COLS), F32),
        ],
        scratch_shapes=[pltpu.VMEM((4 * RANK, COLS), BF16)],
        compiler_params=pltpu.CompilerParams(vmem_limit_bytes=16 * MIB),
        cost_estimate=pl.CostEstimate(flops=2 * ROWS * COLS * 32, bytes_accessed=4 * ROWS * COLS, transcendentals=0),
        name="finish",
    )(merged, basis, inverse, right_sum, momentum)


def swap(x, axis, bit):
    return lax.ppermute(x, axis, [(i, i ^ bit) for i in range(lax.axis_size(axis))])


def shards(gradient, feedback, momentum, right_init):
    gradient = pltpu.with_memory_space_constraint(gradient, pltpu.HBM)
    feedback = pltpu.with_memory_space_constraint(feedback, pltpu.HBM)
    merged, keep, send = merge(gradient, feedback, right_init.T)
    own = keep + swap(send, "replica", 1)
    for axis, bit in (("replica", 2), ("replica", 4), ("tensor", 1), ("tensor", 2), ("tensor", 4), ("tensor", 8)):
        own = own + swap(own, axis, bit)
    other = swap(own, "replica", 1)
    right_sum = right_term(merged, own, other)
    inverse, basis = make_basis(own, other)
    for bit in (1, 2, 4):
        right_sum = right_sum + swap(right_sum, "replica", bit)
    feedback_out, momentum_out, right_t = finish(lax.axis_size("replica"), merged, basis, inverse, right_sum, momentum)
    return feedback_out, momentum_out, right_t.T


def solution(mesh):
    placed = (
        P("replica", None, "tensor"),
        P("replica", None, "tensor"),
        P("replica", "tensor"),
        P("tensor", None),
    )
    return jax.shard_map(
        shards,
        mesh=mesh,
        in_specs=placed,
        out_specs=(P("replica", None, "tensor"), P("replica", "tensor"), P("tensor", None)),
        check_vma=False,
    )
```

time: 215 us -> 65 us (0.30)
  the two profiles are of different devices: /device:TPU:1 before, /device:TPU:6 now
where the time goes in v1:
time: 65 us; the launch traced here: 64.7 us
  waiting for transfers between devices  29.4 us (45%)
  Pallas kernels  17.3 us (27%)
  starting transfers between devices  16.5 us (25%)
  local copies, waits for them, and re-layouts  0.7 us (1%)
  between operations  0.7 us (1%)
    ppermute x11, waiting for transfers between devices, swap(): lax.ppermute(x, axis, [(i, i ^ bit) for i in range(lax.axis_size(axis))])  29.4 us
    ppermute x11, starting transfers between devices, swap(): lax.ppermute(x, axis, [(i, i ^ bit) for i in range(lax.axis_size(axis))])  16.5 us
    pallas_call x1, Pallas kernels, merge(): pl.pallas_call(merge_kernel, grid=(STEPS,), in_specs=[block, block, whole...  8.56 us
    pallas_call x1, Pallas kernels, finish(): pl.pallas_call(body, grid=(STEPS,), in_specs=[whole(), whole(), whole(),...  6.35 us
    pallas_call x1, Pallas kernels, make_basis(): pl.pallas_call(basis_kernel, in_specs=[whole(), whole()], out_specs=[whol...  1.66 us
  transfers between devices with their start and end apart: 11, of which 11 were waited for; matrix products, arithmetic and copies ran while one was open for 0% of the time, Pallas kernels for 3%

profile of v1, /device:TPU:6, one launch (start us, length us, event | category | flops | bytes accessed | tf_op | source)
XLA Modules:
  0.0 64.7 jit_solution(12800982219051903659)
XLA Ops:
  0.6 0.7 %copy-done.1 = f32[384,8]{0,1:T(8,128)S(1)} copy-done((f32[384,8]{0,1:T(8,128)S(1)}, f32[384,8]{0,1:T(8,128)}, u32[]{:S(2)}) %copy-start.1) | copy-done | bytes 12312
  1.3 8.6 %merge.1 = (bf16[6144,384]{1,0:T(8,128)(2,1)S(1)}, f32[8,3072]{1,0:T(8,128)S(1)}, f32[8,3072]{1,0:T(8,128)S(1)}) custom-call(bf16[1,6144,384]{2,1,0:T(8,128)(2,1)} %g_ref.1, bf16[1,6144,384]{2,1,0:T(8,128)(2,1)} %f_ref.1, f32[8,384]{1,0:T(8,128)S(1)} %bitcast.2), custom_call_target="tpu_custom_call" | custom-call | flops 37748736 | bytes 9437184 | tf_op jit(solution)/shard_map/merge/pallas_call | solution.py:51
  10.0 1.3 %collective-permute-done = f32[8,3072]{1,0:T(8,128)S(1)} collective-permute-done((f32[8,3072]{1,0:T(8,128)S(1)}, f32[8,3072]{1,0:T(8,128)S(1)}, u32[]{:S(2)}, u32[]{:S(2)}) %collective-permute-start) | collective-permute-done | bytes 98336 | tf_op jit(solution)/shard_map/ppermute | solution.py:178
  11.3 1.7 %collective-permute-start.1 = (f32[8,3072]{1,0:T(8,128)S(1)}, f32[8,3072]{1,0:T(8,128)S(1)}, u32[]{:S(2)}, u32[]{:S(2)}) collective-permute-start(f32[8,3072]{1,0:T(8,128)S(1)} %add.30), channel_id=1, source_target_pairs={{0,32},{16,48},{32,0},{48,16},{64,96},{80,112},{96,64},{112,80},{1... | collective-permute-start | bytes 294920 | tf_op jit(solution)/shard_map/ppermute | solution.py:178
  12.9 3.3 %collective-permute-done.1 = f32[8,3072]{1,0:T(8,128)S(1)} collective-permute-done((f32[8,3072]{1,0:T(8,128)S(1)}, f32[8,3072]{1,0:T(8,128)S(1)}, u32[]{:S(2)}, u32[]{:S(2)}) %collective-permute-start.1) | collective-permute-done | bytes 98336 | tf_op jit(solution)/shard_map/ppermute | solution.py:178
  16.2 3.3 %collective-permute-start.2 = (f32[8,3072]{1,0:T(8,128)S(1)}, f32[8,3072]{1,0:T(8,128)S(1)}, u32[]{:S(2)}, u32[]{:S(2)}) collective-permute-start(f32[8,3072]{1,0:T(8,128)S(1)} %add.31), channel_id=1, source_target_pairs={{0,64},{16,80},{32,96},{48,112},{64,0},{80,16},{96,32},{112,48},{1... | collective-permute-start | bytes 294920 | tf_op jit(solution)/shard_map/ppermute | solution.py:178
  19.5 2.9 %collective-permute-done.2 = f32[8,3072]{1,0:T(8,128)S(1)} collective-permute-done((f32[8,3072]{1,0:T(8,128)S(1)}, f32[8,3072]{1,0:T(8,128)S(1)}, u32[]{:S(2)}, u32[]{:S(2)}) %collective-permute-start.2) | collective-permute-done | bytes 98336 | tf_op jit(solution)/shard_map/ppermute | solution.py:178
  22.4 0.9 %collective-permute-start.3 = (f32[8,3072]{1,0:T(8,128)S(1)}, f32[8,3072]{1,0:T(8,128)S(1)}, u32[]{:S(2)}, u32[]{:S(2)}) collective-permute-start(f32[8,3072]{1,0:T(8,128)S(1)} %add.32), channel_id=1, source_target_pairs={{0,1},{1,0},{2,3},{3,2},{4,5},{5,4},{6,7},{7,6},{8,9},{9,8},{10,11... | collective-permute-start | bytes 294920 | tf_op jit(solution)/shard_map/ppermute | solution.py:178
  23.3 4.8 %collective-permute-done.3 = f32[8,3072]{1,0:T(8,128)S(1)} collective-permute-done((f32[8,3072]{1,0:T(8,128)S(1)}, f32[8,3072]{1,0:T(8,128)S(1)}, u32[]{:S(2)}, u32[]{:S(2)}) %collective-permute-start.3) | collective-permute-done | bytes 98336 | tf_op jit(solution)/shard_map/ppermute | solution.py:178
  28.2 0.5 collective-permute-start.4
  28.6 5.7 %collective-permute-done.4 = f32[8,3072]{1,0:T(8,128)S(1)} collective-permute-done((f32[8,3072]{1,0:T(8,128)S(1)}, f32[8,3072]{1,0:T(8,128)S(1)}, u32[]{:S(2)}, u32[]{:S(2)}) %collective-permute-start.4) | collective-permute-done | bytes 98336 | tf_op jit(solution)/shard_map/ppermute | solution.py:178
  34.4 1.9 %collective-permute-start.5 = (f32[8,3072]{1,0:T(8,128)S(1)}, f32[8,3072]{1,0:T(8,128)S(1)}, u32[]{:S(2)}, u32[]{:S(2)}) collective-permute-start(f32[8,3072]{1,0:T(8,128)S(1)} %add.34), channel_id=1, source_target_pairs={{0,4},{1,5},{2,6},{3,7},{4,0},{5,1},{6,2},{7,3},{8,12},{9,13},{10,... | collective-permute-start | bytes 294920 | tf_op jit(solution)/shard_map/ppermute | solution.py:178
  36.3 3.5 %collective-permute-done.5 = f32[8,3072]{1,0:T(8,128)S(1)} collective-permute-done((f32[8,3072]{1,0:T(8,128)S(1)}, f32[8,3072]{1,0:T(8,128)S(1)}, u32[]{:S(2)}, u32[]{:S(2)}) %collective-permute-start.5) | collective-permute-done | bytes 98336 | tf_op jit(solution)/shard_map/ppermute | solution.py:178
  39.8 3.2 %collective-permute-start.6 = (f32[8,3072]{1,0:T(8,128)S(1)}, f32[8,3072]{1,0:T(8,128)S(1)}, u32[]{:S(2)}, u32[]{:S(2)}) collective-permute-start(f32[8,3072]{1,0:T(8,128)S(1)} %add.35), channel_id=1, source_target_pairs={{0,8},{1,9},{2,10},{3,11},{4,12},{5,13},{6,14},{7,15},{8,0},{9,1},... | collective-permute-start | bytes 294920 | tf_op jit(solution)/shard_map/ppermute | solution.py:178
  43.0 3.0 %collective-permute-done.6 = f32[8,3072]{1,0:T(8,128)S(1)} collective-permute-done((f32[8,3072]{1,0:T(8,128)S(1)}, f32[8,3072]{1,0:T(8,128)S(1)}, u32[]{:S(2)}, u32[]{:S(2)}) %collective-permute-start.6) | collective-permute-done | bytes 98336 | tf_op jit(solution)/shard_map/ppermute | solution.py:178
  46.1 1.3 %collective-permute-done.7.other_ref = f32[8,3072]{1,0:T(8,128)S(1)} collective-permute-done((f32[8,3072]{1,0:T(8,128)S(1)}, f32[8,3072]{1,0:T(8,128)S(1)}, u32[]{:S(2)}, u32[]{:S(2)}) %collective-permute-start.7) | collective-permute-done | bytes 98336 | tf_op jit(solution)/shard_map/ppermute | solution.py:178
  47.4 0.7 %right_term.1 = f32[8,384]{1,0:T(8,128)S(1)} custom-call(bf16[6144,384]{1,0:T(8,128)(2,1)S(1)} %get-tuple-element.11.merged_ref.refs_0_, f32[8,3072]{1,0:T(8,128)S(1)} %add.36.own_ref, f32[8,3072]{1,0:T(8,128)S(1)} %collective-permute-done.7.other_ref), custom_call_target="tpu_custom_call" | custom-call | flops 75497472 | bytes 4718592 | tf_op jit(solution)/shard_map/right_term/pallas_call | solution.py:78
  48.4 1.0 %collective-permute-done.8 = f32[8,384]{1,0:T(8,128)S(1)} collective-permute-done((f32[8,384]{1,0:T(8,128)S(1)}, f32[8,384]{1,0:T(8,128)S(1)}, u32[]{:S(2)}, u32[]{:S(2)}) %collective-permute-start.8) | collective-permute-done | bytes 12320 | tf_op jit(solution)/shard_map/ppermute | solution.py:178
  49.4 1.6 %collective-permute-start.9 = (f32[8,384]{1,0:T(8,128)S(1)}, f32[8,384]{1,0:T(8,128)S(1)}, u32[]{:S(2)}, u32[]{:S(2)}) collective-permute-start(f32[8,384]{1,0:T(8,128)S(1)} %add.37), channel_id=1, source_target_pairs={{0,32},{16,48},{32,0},{48,16},{64,96},{80,112},{96,64},{112,80},{1... | collective-permute-start | bytes 36872 | tf_op jit(solution)/shard_map/ppermute | solution.py:178
  51.0 2.1 %collective-permute-done.9 = f32[8,384]{1,0:T(8,128)S(1)} collective-permute-done((f32[8,384]{1,0:T(8,128)S(1)}, f32[8,384]{1,0:T(8,128)S(1)}, u32[]{:S(2)}, u32[]{:S(2)}) %collective-permute-start.9) | collective-permute-done | bytes 12320 | tf_op jit(solution)/shard_map/ppermute | solution.py:178
  53.1 3.2 %collective-permute-start.10 = (f32[8,384]{1,0:T(8,128)S(1)}, f32[8,384]{1,0:T(8,128)S(1)}, u32[]{:S(2)}, u32[]{:S(2)}) collective-permute-start(f32[8,384]{1,0:T(8,128)S(1)} %add.38), channel_id=1, source_target_pairs={{0,64},{16,80},{32,96},{48,112},{64,0},{80,16},{96,32},{112,48},{1... | collective-permute-start | bytes 36872 | tf_op jit(solution)/shard_map/ppermute | solution.py:178
  56.3 1.7 %basis.1 = (f32[8,8]{1,0:T(8,128)S(1)}, bf16[6144,32]{1,0:T(8,128)(2,1)S(1)}) custom-call(f32[8,3072]{1,0:T(8,128)S(1)} %add.36.own_ref, f32[8,3072]{1,0:T(8,128)S(1)} %collective-permute-done.7.other_ref), custom_call_target="tpu_custom_call" | custom-call | flops 1572864 | bytes 4194304 | tf_op jit(solution)/shard_map/basis/pallas_call | solution.py:118
  58.0 0.4 collective-permute-done.10
  58.3 6.4 %finish.1 = (bf16[1,6144,384]{2,1,0:T(8,128)(2,1)}, bf16[768,384]{1,0:T(8,128)(2,1)}, f32[8,384]{1,0:T(8,128)}) custom-call(bf16[6144,384]{1,0:T(8,128)(2,1)S(1)} %get-tuple-element.11.merged_ref.refs_0_, bf16[6144,32]{1,0:T(8,128)(2,1)S(1)} %get-tuple-element.14.refs_1_, f32[8,8]{1,0:T(8,128)S(1)} %get-tuple-element.15.refs_2_, f32[8,384]{1,0:T(8,128)S(1)} %add.39.refs_3_, ...), custom_call_target="tpu_custom_call" | custom-call | flops 150994944 | bytes 9437184 | tf_op jit(solution)/shard_map/finish/pallas_call | solution.py:160
  (16 shorter events, 0.5 us)
Async XLA Ops:
  0.6 0.7 %copy-start.1 = (f32[384,8]{0,1:T(8,128)S(1)}, f32[384,8]{0,1:T(8,128)}, u32[]{:S(2)}) copy-start(f32[384,8]{0,1:T(8,128)} %param.7) | copy-start | bytes 36868
  9.9 48.4 %copy-start = (bf16[768,384]{1,0:T(8,128)(2,1)S(1)}, bf16[768,384]{1,0:T(8,128)(2,1)}, u32[]{:S(2)}) copy-start(bf16[768,384]{1,0:T(8,128)(2,1)} %refs_4_.1) | copy-start | bytes 1769476
  9.9 1.3 %collective-permute-start = (f32[8,3072]{1,0:T(8,128)S(1)}, f32[8,3072]{1,0:T(8,128)S(1)}, u32[]{:S(2)}, u32[]{:S(2)}) collective-permute-start(f32[8,3072]{1,0:T(8,128)S(1)} %get-tuple-element.13), channel_id=1, source_target_pairs={{0,16},{16,0},{32,48},{48,32},{64,80},{80,64},{96,112},{112,96},{1... | collective-permute-start | bytes 294920 | tf_op jit(solution)/shard_map/ppermute | solution.py:178
  11.3 4.9 %collective-permute-start.1 = (f32[8,3072]{1,0:T(8,128)S(1)}, f32[8,3072]{1,0:T(8,128)S(1)}, u32[]{:S(2)}, u32[]{:S(2)}) collective-permute-start(f32[8,3072]{1,0:T(8,128)S(1)} %add.30), channel_id=1, source_target_pairs={{0,32},{16,48},{32,0},{48,16},{64,96},{80,112},{96,64},{112,80},{1... | collective-permute-start | bytes 294920 | tf_op jit(solution)/shard_map/ppermute | solution.py:178
  16.2 6.2 %collective-permute-start.2 = (f32[8,3072]{1,0:T(8,128)S(1)}, f32[8,3072]{1,0:T(8,128)S(1)}, u32[]{:S(2)}, u32[]{:S(2)}) collective-permute-start(f32[8,3072]{1,0:T(8,128)S(1)} %add.31), channel_id=1, source_target_pairs={{0,64},{16,80},{32,96},{48,112},{64,0},{80,16},{96,32},{112,48},{1... | collective-permute-start | bytes 294920 | tf_op jit(solution)/shard_map/ppermute | solution.py:178
  22.4 5.7 %collective-permute-start.3 = (f32[8,3072]{1,0:T(8,128)S(1)}, f32[8,3072]{1,0:T(8,128)S(1)}, u32[]{:S(2)}, u32[]{:S(2)}) collective-permute-start(f32[8,3072]{1,0:T(8,128)S(1)} %add.32), channel_id=1, source_target_pairs={{0,1},{1,0},{2,3},{3,2},{4,5},{5,4},{6,7},{7,6},{8,9},{9,8},{10,11... | collective-permute-start | bytes 294920 | tf_op jit(solution)/shard_map/ppermute | solution.py:178
  28.2 6.2 %collective-permute-start.4 = (f32[8,3072]{1,0:T(8,128)S(1)}, f32[8,3072]{1,0:T(8,128)S(1)}, u32[]{:S(2)}, u32[]{:S(2)}) collective-permute-start(f32[8,3072]{1,0:T(8,128)S(1)} %add.33), channel_id=1, source_target_pairs={{0,2},{1,3},{2,0},{3,1},{4,6},{5,7},{6,4},{7,5},{8,10},{9,11},{10,... | collective-permute-start | bytes 294920 | tf_op jit(solution)/shard_map/ppermute | solution.py:178
  34.4 5.4 %collective-permute-start.5 = (f32[8,3072]{1,0:T(8,128)S(1)}, f32[8,3072]{1,0:T(8,128)S(1)}, u32[]{:S(2)}, u32[]{:S(2)}) collective-permute-start(f32[8,3072]{1,0:T(8,128)S(1)} %add.34), channel_id=1, source_target_pairs={{0,4},{1,5},{2,6},{3,7},{4,0},{5,1},{6,2},{7,3},{8,12},{9,13},{10,... | collective-permute-start | bytes 294920 | tf_op jit(solution)/shard_map/ppermute | solution.py:178
  39.8 6.2 %collective-permute-start.6 = (f32[8,3072]{1,0:T(8,128)S(1)}, f32[8,3072]{1,0:T(8,128)S(1)}, u32[]{:S(2)}, u32[]{:S(2)}) collective-permute-start(f32[8,3072]{1,0:T(8,128)S(1)} %add.35), channel_id=1, source_target_pairs={{0,8},{1,9},{2,10},{3,11},{4,12},{5,13},{6,14},{7,15},{8,0},{9,1},... | collective-permute-start | bytes 294920 | tf_op jit(solution)/shard_map/ppermute | solution.py:178
  46.1 1.4 %collective-permute-start.7 = (f32[8,3072]{1,0:T(8,128)S(1)}, f32[8,3072]{1,0:T(8,128)S(1)}, u32[]{:S(2)}, u32[]{:S(2)}) collective-permute-start(f32[8,3072]{1,0:T(8,128)S(1)} %add.36.own_ref), channel_id=1, source_target_pairs={{0,16},{16,0},{32,48},{48,32},{64,80},{80,64},{96,112},{112,96},{1... | collective-permute-start | bytes 294920 | tf_op jit(solution)/shard_map/ppermute | solution.py:178
  48.2 1.3 %collective-permute-start.8 = (f32[8,384]{1,0:T(8,128)S(1)}, f32[8,384]{1,0:T(8,128)S(1)}, u32[]{:S(2)}, u32[]{:S(2)}) collective-permute-start(f32[8,384]{1,0:T(8,128)S(1)} %right_term.1), channel_id=1, source_target_pairs={{0,16},{16,0},{32,48},{48,32},{64,80},{80,64},{96,112},{112,96},{1... | collective-permute-start | bytes 36872 | tf_op jit(solution)/shard_map/ppermute | solution.py:178
  49.4 3.7 %collective-permute-start.9 = (f32[8,384]{1,0:T(8,128)S(1)}, f32[8,384]{1,0:T(8,128)S(1)}, u32[]{:S(2)}, u32[]{:S(2)}) collective-permute-start(f32[8,384]{1,0:T(8,128)S(1)} %add.37), channel_id=1, source_target_pairs={{0,32},{16,48},{32,0},{48,16},{64,96},{80,112},{96,64},{112,80},{1... | collective-permute-start | bytes 36872 | tf_op jit(solution)/shard_map/ppermute | solution.py:178
  53.1 5.2 %collective-permute-start.10 = (f32[8,384]{1,0:T(8,128)S(1)}, f32[8,384]{1,0:T(8,128)S(1)}, u32[]{:S(2)}, u32[]{:S(2)}) collective-permute-start(f32[8,384]{1,0:T(8,128)S(1)} %add.38), channel_id=1, source_target_pairs={{0,64},{16,80},{32,96},{48,112},{64,0},{80,16},{96,32},{112,48},{1... | collective-permute-start | bytes 36872 | tf_op jit(solution)/shard_map/ppermute | solution.py:178

commit v2 on v1

v2 whole, which is shorter than its diff:
```python
import itertools

import jax
import jax.numpy as jnp
from jax import lax
from jax.experimental import pallas as pl
from jax.experimental.pallas import tpu as pltpu
from jax.sharding import PartitionSpec as P

F32, BF16 = jnp.float32, jnp.bfloat16
ROWS, COLS, RANK = 6144, 384, 8
HALF = ROWS // 2
CHUNKS = 6
CHUNK = ROWS // CHUNKS
MIB = 1 << 20


def own_half():
    replica, tensor = lax.axis_index("replica"), lax.axis_index("tensor")
    return lax.rem(replica + replica // 2 + tensor + tensor // 4, 2)


def split(x):
    high = x.astype(BF16)
    return high, (x - high.astype(F32)).astype(BF16)


def merge_kernel(g_ref, f_ref, q_ref, merged_ref, keep_ref, send_ref, g_buf, f_buf, q_buf, g_sem, f_sem, q_sem):
    q_copy = pltpu.make_async_copy(q_ref, q_buf, q_sem.at[0])
    q_copy.start()
    copies = []
    for i in range(CHUNKS):
        rows = pl.ds(i * CHUNK, CHUNK)
        pair = (
            pltpu.make_async_copy(g_ref.at[0, rows, :], g_buf.at[rows, :], g_sem.at[i]),
            pltpu.make_async_copy(f_ref.at[0, rows, :], f_buf.at[rows, :], f_sem.at[i]),
        )
        for copy in pair:
            copy.start()
        copies.append(pair)
    q_copy.wait()
    right = q_buf[...].astype(BF16)
    keep_first = own_half() == 0
    for i in range(CHUNKS):
        for copy in copies[i]:
            copy.wait()
        rows = pl.ds(i * CHUNK, CHUNK)
        merged = (g_buf[rows, :].astype(F32) + f_buf[rows, :].astype(F32)).astype(BF16)
        merged_ref[rows, :] = merged
        term = lax.dot_general(right, merged, (((1,), (1,)), ((), ())), preferred_element_type=F32)
        where = pl.ds(i % (CHUNKS // 2) * CHUNK, CHUNK)
        keep = keep_first if i < CHUNKS // 2 else jnp.logical_not(keep_first)

        @pl.when(keep)
        def _():
            keep_ref[:, where] = term

        @pl.when(jnp.logical_not(keep))
        def _():
            send_ref[:, where] = term


def whole():
    return pl.BlockSpec(memory_space=pltpu.VMEM)


def in_hbm(count):
    return [pl.BlockSpec(memory_space=pltpu.HBM)] * count


def merge(gradient, feedback, right_t):
    return pl.pallas_call(
        merge_kernel,
        in_specs=in_hbm(3),
        out_specs=[whole(), whole(), whole()],
        out_shape=[
            pltpu.VMEM((ROWS, COLS), BF16),
            pltpu.VMEM((RANK, HALF), F32),
            pltpu.VMEM((RANK, HALF), F32),
        ],
        scratch_shapes=[
            pltpu.VMEM((ROWS, COLS), BF16),
            pltpu.VMEM((ROWS, COLS), BF16),
            pltpu.VMEM((RANK, COLS), F32),
            pltpu.SemaphoreType.DMA((CHUNKS,)),
            pltpu.SemaphoreType.DMA((CHUNKS,)),
            pltpu.SemaphoreType.DMA((1,)),
        ],
        compiler_params=pltpu.CompilerParams(vmem_limit_bytes=20 * MIB),
        cost_estimate=pl.CostEstimate(flops=2 * ROWS * COLS * RANK, bytes_accessed=4 * ROWS * COLS, transcendentals=0),
        name="merge",
    )(gradient, feedback, right_t)


def right_kernel(merged_ref, own_ref, other_ref, out_ref):
    mine = own_half()
    total = jnp.zeros((2 * RANK, COLS), F32)
    for ref, half in ((own_ref, mine), (other_ref, 1 - mine)):
        rows = pl.ds(pl.multiple_of(half * HALF, HALF), HALF)
        pair = jnp.concatenate(split(ref[...]), axis=0)
        total += jnp.dot(pair, merged_ref[rows, :], preferred_element_type=F32)
    out_ref[...] = total[:RANK] + total[RANK:]


def right_term(merged, own, other):
    return pl.pallas_call(
        right_kernel,
        in_specs=[whole(), whole(), whole()],
        out_specs=whole(),
        out_shape=pltpu.VMEM((RANK, COLS), F32),
        compiler_params=pltpu.CompilerParams(vmem_limit_bytes=16 * MIB),
        cost_estimate=pl.CostEstimate(flops=4 * ROWS * COLS * RANK, bytes_accessed=2 * ROWS * COLS, transcendentals=0),
        name="right_term",
    )(merged, own, other)


def basis_kernel(own_ref, other_ref, inverse_ref, basis_ref):
    own, other = own_ref[...], other_ref[...]
    gram = jnp.zeros((RANK, RANK), F32)
    for part in (own, other):
        gram += lax.dot_general(
            part, part, (((1,), (1,)), ((), ())), precision=lax.Precision.HIGHEST, preferred_element_type=F32
        )
    row = lax.broadcasted_iota(jnp.int32, (RANK, RANK), 0)
    column = lax.broadcasted_iota(jnp.int32, (RANK, RANK), 1)
    eye = jnp.where(row == column, 1.0, 0.0)
    inverse = eye
    for k in range(RANK):
        factor = jnp.where(row[:, :1] > k, gram[:, k : k + 1] / gram[k : k + 1, k : k + 1], 0.0)
        inverse -= factor * inverse[k : k + 1, :]
        gram -= factor * gram[k : k + 1, :]
    pivots = jnp.sum(gram * eye, axis=1, keepdims=True)
    inverse = inverse / jnp.sqrt(pivots)
    inverse_ref[...] = inverse
    mine = own_half()
    for part, half in ((own, mine), (other, 1 - mine)):
        basis = jnp.zeros((RANK, HALF), F32)
        for k in range(RANK):
            basis += inverse[:, k : k + 1] * part[k : k + 1, :]
        high, low = split(basis)
        packed = jnp.concatenate([high, high, low, low], axis=0)
        basis_ref[pl.ds(pl.multiple_of(half * HALF, HALF), HALF), :] = packed.T


def make_basis(own, other):
    return pl.pallas_call(
        basis_kernel,
        in_specs=[whole(), whole()],
        out_specs=[whole(), whole()],
        out_shape=[pltpu.VMEM((RANK, RANK), F32), pltpu.VMEM((ROWS, 4 * RANK), BF16)],
        compiler_params=pltpu.CompilerParams(vmem_limit_bytes=16 * MIB),
        cost_estimate=pl.CostEstimate(flops=4 * ROWS * RANK * RANK, bytes_accessed=4 * MIB, transcendentals=0),
        name="basis",
    )(own, other)


def final_kernel(
    replicas,
    merged_ref, basis_ref, inverse_ref, sum_ref, last_ref, mom_ref,
    fb_ref, mom_out_ref, right_ref,
    fb_buf, mom_buf, right_buf, fb_sem, mom_sem, right_sem,
):
    total = sum_ref[...] + last_ref[...]
    right = jnp.zeros((RANK, COLS), F32)
    for k in range(RANK):
        right += inverse_ref[:, k : k + 1] * total[k : k + 1, :]
    right = right * (1.0 / replicas)
    right_buf[...] = right
    copies = [pltpu.make_async_copy(right_buf, right_ref, right_sem.at[0])]
    copies[0].start()
    high, low = split(right)
    pack = jnp.concatenate([high, low, high, low], axis=0)
    for i in range(CHUNKS):
        rows = pl.ds(i * CHUNK, CHUNK)
        approx = jnp.dot(basis_ref[rows, :], pack, preferred_element_type=F32)
        fb_buf[rows, :] = (merged_ref[rows, :].astype(F32) - approx).astype(BF16)
        copies.append(pltpu.make_async_copy(fb_buf.at[rows, :], fb_ref.at[0, rows, :], fb_sem.at[i]))
        copies[-1].start()
        if i == 0:
            count = mom_ref.shape[0]
            mom_rows = pl.ds(pl.multiple_of(lax.axis_index("replica") * count, count), count)
            approx = jnp.dot(basis_ref[mom_rows, :], pack, preferred_element_type=F32)
            mom_buf[...] = (0.9 * mom_ref[...].astype(F32) + approx).astype(BF16)
            copies.append(pltpu.make_async_copy(mom_buf, mom_out_ref, mom_sem.at[0]))
            copies[-1].start()
    for copy in copies:
        copy.wait()


def finish(replicas, merged, basis, inverse, right_sum, right_last, momentum):
    mom_rows = momentum.shape[0]

    def body(*refs):
        final_kernel(replicas, *refs)

    return pl.pallas_call(
        body,
        in_specs=[whole()] * 6,
        out_specs=in_hbm(3),
        out_shape=[
            jax.ShapeDtypeStruct((1, ROWS, COLS), BF16),
            jax.ShapeDtypeStruct((mom_rows, COLS), BF16),
            jax.ShapeDtypeStruct((RANK, COLS), F32),
        ],
        scratch_shapes=[
            pltpu.VMEM((ROWS, COLS), BF16),
            pltpu.VMEM((mom_rows, COLS), BF16),
            pltpu.VMEM((RANK, COLS), F32),
            pltpu.SemaphoreType.DMA((CHUNKS,)),
            pltpu.SemaphoreType.DMA((1,)),
            pltpu.SemaphoreType.DMA((1,)),
        ],
        compiler_params=pltpu.CompilerParams(vmem_limit_bytes=20 * MIB),
        cost_estimate=pl.CostEstimate(flops=2 * ROWS * COLS * 32, bytes_accessed=4 * ROWS * COLS, transcendentals=0),
        name="finish",
    )(merged, basis, inverse, right_sum, right_last, momentum)


NEAR = {0: 1, 1: 0, 2: 3, 3: 2}
WRAP = {0: 3, 3: 0, 1: 2, 2: 1}


def step_pairs(axes, partner):
    pairs = []
    for y, core, z, x in itertools.product(range(4), range(2), range(4), range(4)):
        here = {"y": y, "z": z, "x": x}
        axis = axes[(core + y + z + x) % 2]
        there = {**here, axis: partner[here[axis]]}
        place = lambda at, c: (2 * at["y"] + c) * 16 + 4 * at["z"] + at["x"]
        pairs.append((place(here, core), place(there, 1 - core)))
    return pairs


def step(x, axes, partner):
    return lax.ppermute(x, ("replica", "tensor"), step_pairs(axes, partner))


def sibling(x):
    return lax.ppermute(x, "replica", [(i, i ^ 1) for i in range(lax.axis_size("replica"))])


def shards(gradient, feedback, momentum, right_init):
    gradient = pltpu.with_memory_space_constraint(gradient, pltpu.HBM)
    feedback = pltpu.with_memory_space_constraint(feedback, pltpu.HBM)
    right_t = pltpu.with_memory_space_constraint(right_init.T, pltpu.HBM)
    momentum = pltpu.with_memory_space_constraint(momentum, pltpu.VMEM)
    merged, keep, send = merge(gradient, feedback, right_t)
    own = keep + sibling(send)
    for axes in ("yx", "xz", "zy"):
        for partner in (NEAR, WRAP):
            own = own + step(own, axes, partner)
    other = sibling(own)
    term = right_term(merged, own, other)
    inverse, basis = make_basis(own, other)
    term = term + sibling(term)
    term = term + step(term, "yy", NEAR)
    last = step(term, "yy", WRAP)
    feedback_out, momentum_out, right_t = finish(lax.axis_size("replica"), merged, basis, inverse, term, last, momentum)
    return feedback_out, momentum_out, right_t.T


def solution(mesh):
    placed = (
        P("replica", None, "tensor"),
        P("replica", None, "tensor"),
        P("replica", "tensor"),
        P("tensor", None),
    )
    return jax.shard_map(
        shards,
        mesh=mesh,
        in_specs=placed,
        out_specs=(P("replica", None, "tensor"), P("replica", "tensor"), P("tensor", None)),
        check_vma=False,
    )
```

time: 65 us -> 52.1 us (0.80)
  the two profiles are of different devices: /device:TPU:6 before, /device:TPU:1 now
where the time goes in v2:
time: 52.1 us; the launch traced here: 52 us
  waiting for transfers between devices  20.6 us (40%)
  starting transfers between devices  19.8 us (38%)
  Pallas kernels  10.7 us (21%)
  between operations  0.7 us (1%)
    ppermute x8, starting transfers between devices, step(): return lax.ppermute(x, ('replica', 'tensor'), step_pairs(axes, partner))  17.8 us
    ppermute x8, waiting for transfers between devices, step(): return lax.ppermute(x, ('replica', 'tensor'), step_pairs(axes, partner))  17.6 us
    pallas_call x1, Pallas kernels, merge(): pl.pallas_call(merge_kernel, in_specs=in_hbm(3), out_specs=[whole(), whol...  5.3 us
    ppermute x3, waiting for transfers between devices, sibling(): lax.ppermute(x, 'replica', [(i, i ^ 1) for i in range(lax.axis_size('repl...  3.07 us
    pallas_call x1, Pallas kernels, finish(): pl.pallas_call(body, in_specs=[whole()] * 6, out_specs=in_hbm(3), out_sha...  3 us
    ppermute x3, starting transfers between devices, sibling(): lax.ppermute(x, 'replica', [(i, i ^ 1) for i in range(lax.axis_size('repl...  2.01 us
    pallas_call x1, Pallas kernels, make_basis(): pl.pallas_call(basis_kernel, in_specs=[whole(), whole()], out_specs=[whol...  1.66 us
  transfers between devices with their start and end apart: 11, of which 10 were waited for; matrix products, arithmetic and copies ran while one was open for 0% of the time, Pallas kernels for 3%

profile of v2, /device:TPU:1, one launch (start us, length us, event | category | flops | bytes accessed | tf_op | source)
XLA Modules:
  0.0 52.0 jit_solution(3284957643448199979)
XLA Ops:
  0.6 5.3 %merge.1 = (bf16[6144,384]{1,0:T(8,128)(2,1)S(1)}, f32[8,3072]{1,0:T(8,128)S(1)}, f32[8,3072]{1,0:T(8,128)S(1)}) custom-call(bf16[1,6144,384]{2,1,0:T(8,128)(2,1)} %g_ref.1, bf16[1,6144,384]{2,1,0:T(8,128)(2,1)} %f_ref.1, f32[8,384]{1,0:T(8,128)} %bitcast.2), custom_call_target="tpu_custom_call" | custom-call | flops 37748736 | bytes 9437184 | tf_op jit(solution)/shard_map/merge/pallas_call | solution.py:72
  5.9 1.5 %collective-permute-start = (f32[8,3072]{1,0:T(8,128)S(1)}, f32[8,3072]{1,0:T(8,128)S(1)}, u32[]{:S(2)}, u32[]{:S(2)}) collective-permute-start(f32[8,3072]{1,0:T(8,128)S(1)} %get-tuple-element.13), channel_id=1, source_target_pairs={{0,16},{16,0},{32,48},{48,32},{64,80},{80,64},{96,112},{112,96},{1... | collective-permute-start | bytes 294920 | tf_op jit(solution)/shard_map/ppermute | solution.py:239
  7.4 0.9 %collective-permute-done = f32[8,3072]{1,0:T(8,128)S(1)} collective-permute-done((f32[8,3072]{1,0:T(8,128)S(1)}, f32[8,3072]{1,0:T(8,128)S(1)}, u32[]{:S(2)}, u32[]{:S(2)}) %collective-permute-start) | collective-permute-done | bytes 98336 | tf_op jit(solution)/shard_map/ppermute | solution.py:239
  8.4 1.6 %collective-permute-start.1 = (f32[8,3072]{1,0:T(8,128)S(1)}, f32[8,3072]{1,0:T(8,128)S(1)}, u32[]{:S(2)}, u32[]{:S(2)}) collective-permute-start(f32[8,3072]{1,0:T(8,128)S(1)} %add.27), channel_id=1, source_target_pairs={{0,48},{1,16},{2,50},{3,18},{4,21},{5,53},{6,23},{7,55},{8,56},{9,... | collective-permute-start | bytes 294920 | tf_op jit(solution)/shard_map/ppermute | solution.py:235
  10.0 2.5 %collective-permute-done.1 = f32[8,3072]{1,0:T(8,128)S(1)} collective-permute-done((f32[8,3072]{1,0:T(8,128)S(1)}, f32[8,3072]{1,0:T(8,128)S(1)}, u32[]{:S(2)}, u32[]{:S(2)}) %collective-permute-start.1) | collective-permute-done | bytes 98336 | tf_op jit(solution)/shard_map/ppermute | solution.py:235
  12.5 2.9 %collective-permute-start.2 = (f32[8,3072]{1,0:T(8,128)S(1)}, f32[8,3072]{1,0:T(8,128)S(1)}, u32[]{:S(2)}, u32[]{:S(2)}) collective-permute-start(f32[8,3072]{1,0:T(8,128)S(1)} %add.28), channel_id=1, source_target_pairs={{0,112},{1,18},{2,114},{3,16},{4,23},{5,117},{6,21},{7,119},{8,120... | collective-permute-start | bytes 294920 | tf_op jit(solution)/shard_map/ppermute | solution.py:235
  15.4 2.4 %collective-permute-done.2 = f32[8,3072]{1,0:T(8,128)S(1)} collective-permute-done((f32[8,3072]{1,0:T(8,128)S(1)}, f32[8,3072]{1,0:T(8,128)S(1)}, u32[]{:S(2)}, u32[]{:S(2)}) %collective-permute-start.2) | collective-permute-done | bytes 98336 | tf_op jit(solution)/shard_map/ppermute | solution.py:235
  17.9 2.0 %collective-permute-start.3 = (f32[8,3072]{1,0:T(8,128)S(1)}, f32[8,3072]{1,0:T(8,128)S(1)}, u32[]{:S(2)}, u32[]{:S(2)}) collective-permute-start(f32[8,3072]{1,0:T(8,128)S(1)} %add.29), channel_id=1, source_target_pairs={{0,17},{1,21},{2,19},{3,23},{4,16},{5,20},{6,18},{7,22},{8,25},{9,... | collective-permute-start | bytes 294920 | tf_op jit(solution)/shard_map/ppermute | solution.py:235
  19.9 2.3 %collective-permute-done.3 = f32[8,3072]{1,0:T(8,128)S(1)} collective-permute-done((f32[8,3072]{1,0:T(8,128)S(1)}, f32[8,3072]{1,0:T(8,128)S(1)}, u32[]{:S(2)}, u32[]{:S(2)}) %collective-permute-start.3) | collective-permute-done | bytes 98336 | tf_op jit(solution)/shard_map/ppermute | solution.py:235
  22.3 3.9 %collective-permute-start.4 = (f32[8,3072]{1,0:T(8,128)S(1)}, f32[8,3072]{1,0:T(8,128)S(1)}, u32[]{:S(2)}, u32[]{:S(2)}) collective-permute-start(f32[8,3072]{1,0:T(8,128)S(1)} %add.30), channel_id=1, source_target_pairs={{0,19},{1,29},{2,17},{3,31},{4,24},{5,22},{6,26},{7,20},{8,27},{9,... | collective-permute-start | bytes 294920 | tf_op jit(solution)/shard_map/ppermute | solution.py:235
  26.2 2.3 %collective-permute-done.4 = f32[8,3072]{1,0:T(8,128)S(1)} collective-permute-done((f32[8,3072]{1,0:T(8,128)S(1)}, f32[8,3072]{1,0:T(8,128)S(1)}, u32[]{:S(2)}, u32[]{:S(2)}) %collective-permute-start.4) | collective-permute-done | bytes 98336 | tf_op jit(solution)/shard_map/ppermute | solution.py:235
  28.5 1.4 %collective-permute-start.5 = (f32[8,3072]{1,0:T(8,128)S(1)}, f32[8,3072]{1,0:T(8,128)S(1)}, u32[]{:S(2)}, u32[]{:S(2)}) collective-permute-start(f32[8,3072]{1,0:T(8,128)S(1)} %add.31), channel_id=1, source_target_pairs={{0,20},{1,49},{2,22},{3,51},{4,52},{5,17},{6,54},{7,19},{8,28},{9,... | collective-permute-start | bytes 294920 | tf_op jit(solution)/shard_map/ppermute | solution.py:235
  29.9 2.7 %collective-permute-done.5 = f32[8,3072]{1,0:T(8,128)S(1)} collective-permute-done((f32[8,3072]{1,0:T(8,128)S(1)}, f32[8,3072]{1,0:T(8,128)S(1)}, u32[]{:S(2)}, u32[]{:S(2)}) %collective-permute-start.5) | collective-permute-done | bytes 98336 | tf_op jit(solution)/shard_map/ppermute | solution.py:235
  32.6 2.9 %collective-permute-start.6 = (f32[8,3072]{1,0:T(8,128)S(1)}, f32[8,3072]{1,0:T(8,128)S(1)}, u32[]{:S(2)}, u32[]{:S(2)}) collective-permute-start(f32[8,3072]{1,0:T(8,128)S(1)} %add.32), channel_id=1, source_target_pairs={{0,28},{1,113},{2,30},{3,115},{4,116},{5,25},{6,118},{7,27},{8,20}... | collective-permute-start | bytes 294920 | tf_op jit(solution)/shard_map/ppermute | solution.py:235
  35.5 2.5 %collective-permute-done.6 = f32[8,3072]{1,0:T(8,128)S(1)} collective-permute-done((f32[8,3072]{1,0:T(8,128)S(1)}, f32[8,3072]{1,0:T(8,128)S(1)}, u32[]{:S(2)}, u32[]{:S(2)}) %collective-permute-start.6) | collective-permute-done | bytes 98336 | tf_op jit(solution)/shard_map/ppermute | solution.py:235
  38.0 0.3 collective-permute-start.7
  38.3 1.1 %collective-permute-done.7.other_ref = f32[8,3072]{1,0:T(8,128)S(1)} collective-permute-done((f32[8,3072]{1,0:T(8,128)S(1)}, f32[8,3072]{1,0:T(8,128)S(1)}, u32[]{:S(2)}, u32[]{:S(2)}) %collective-permute-start.7) | collective-permute-done | bytes 98336 | tf_op jit(solution)/shard_map/ppermute | solution.py:239
  39.4 0.7 %right_term.1 = f32[8,384]{1,0:T(8,128)S(1)} custom-call(bf16[6144,384]{1,0:T(8,128)(2,1)S(1)} %get-tuple-element.11.merged_ref.refs_0_, f32[8,3072]{1,0:T(8,128)S(1)} %add.33.own_ref, f32[8,3072]{1,0:T(8,128)S(1)} %collective-permute-done.7.other_ref), custom_call_target="tpu_custom_call" | custom-call | flops 75497472 | bytes 4718592 | tf_op jit(solution)/shard_map/right_term/pallas_call | solution.py:106
  40.4 1.0 %collective-permute-done.8 = f32[8,384]{1,0:T(8,128)S(1)} collective-permute-done((f32[8,384]{1,0:T(8,128)S(1)}, f32[8,384]{1,0:T(8,128)S(1)}, u32[]{:S(2)}, u32[]{:S(2)}) %collective-permute-start.8) | collective-permute-done | bytes 12320 | tf_op jit(solution)/shard_map/ppermute | solution.py:239
  41.4 0.3 collective-permute-start.9
  41.7 2.8 %collective-permute-done.9 = f32[8,384]{1,0:T(8,128)S(1)} collective-permute-done((f32[8,384]{1,0:T(8,128)S(1)}, f32[8,384]{1,0:T(8,128)S(1)}, u32[]{:S(2)}, u32[]{:S(2)}) %collective-permute-start.9) | collective-permute-done | bytes 12320 | tf_op jit(solution)/shard_map/ppermute | solution.py:235
  44.5 2.8 %collective-permute-start.10 = (f32[8,384]{1,0:T(8,128)S(1)}, f32[8,384]{1,0:T(8,128)S(1)}, u32[]{:S(2)}, u32[]{:S(2)}) collective-permute-start(f32[8,384]{1,0:T(8,128)S(1)} %add.35.refs_3_), channel_id=1, source_target_pairs={{0,112},{1,113},{2,114},{3,115},{4,116},{5,117},{6,118},{7,119},{8... | collective-permute-start | bytes 36872 | tf_op jit(solution)/shard_map/ppermute | solution.py:235
  47.3 1.7 %basis.1 = (f32[8,8]{1,0:T(8,128)S(1)}, bf16[6144,32]{1,0:T(8,128)(2,1)S(1)}) custom-call(f32[8,3072]{1,0:T(8,128)S(1)} %add.33.own_ref, f32[8,3072]{1,0:T(8,128)S(1)} %collective-permute-done.7.other_ref), custom_call_target="tpu_custom_call" | custom-call | flops 1572864 | bytes 4194304 | tf_op jit(solution)/shard_map/basis/pallas_call | solution.py:146
  49.0 3.0 %finish.1 = (bf16[1,6144,384]{2,1,0:T(8,128)(2,1)}, bf16[768,384]{1,0:T(8,128)(2,1)}, f32[8,384]{1,0:T(8,128)}) custom-call(bf16[6144,384]{1,0:T(8,128)(2,1)S(1)} %get-tuple-element.11.merged_ref.refs_0_, bf16[6144,32]{1,0:T(8,128)(2,1)S(1)} %get-tuple-element.14.refs_1_, f32[8,8]{1,0:T(8,128)S(1)} %get-tuple-element.15.refs_2_, f32[8,384]{1,0:T(8,128)S(1)} %add.35.refs_3_, ...), custom_call_target="tpu_custom_call" | custom-call | flops 150994944 | bytes 9437184 | tf_op jit(solution)/shard_map/finish/pallas_call | solution.py:196
  (13 shorter events, 0.4 us)
Async XLA Ops:
  5.9 43.0 %copy-start = (bf16[768,384]{1,0:T(8,128)(2,1)S(1)}, bf16[768,384]{1,0:T(8,128)(2,1)}, u32[]{:S(2)}) copy-start(bf16[768,384]{1,0:T(8,128)(2,1)} %refs_5_.1) | copy-start | bytes 1769476
  5.9 2.4 %collective-permute-start = (f32[8,3072]{1,0:T(8,128)S(1)}, f32[8,3072]{1,0:T(8,128)S(1)}, u32[]{:S(2)}, u32[]{:S(2)}) collective-permute-start(f32[8,3072]{1,0:T(8,128)S(1)} %get-tuple-element.13), channel_id=1, source_target_pairs={{0,16},{16,0},{32,48},{48,32},{64,80},{80,64},{96,112},{112,96},{1... | collective-permute-start | bytes 294920 | tf_op jit(solution)/shard_map/ppermute | solution.py:239
  8.4 4.1 %collective-permute-start.1 = (f32[8,3072]{1,0:T(8,128)S(1)}, f32[8,3072]{1,0:T(8,128)S(1)}, u32[]{:S(2)}, u32[]{:S(2)}) collective-permute-start(f32[8,3072]{1,0:T(8,128)S(1)} %add.27), channel_id=1, source_target_pairs={{0,48},{1,16},{2,50},{3,18},{4,21},{5,53},{6,23},{7,55},{8,56},{9,... | collective-permute-start | bytes 294920 | tf_op jit(solution)/shard_map/ppermute | solution.py:235
  12.5 5.3 %collective-permute-start.2 = (f32[8,3072]{1,0:T(8,128)S(1)}, f32[8,3072]{1,0:T(8,128)S(1)}, u32[]{:S(2)}, u32[]{:S(2)}) collective-permute-start(f32[8,3072]{1,0:T(8,128)S(1)} %add.28), channel_id=1, source_target_pairs={{0,112},{1,18},{2,114},{3,16},{4,23},{5,117},{6,21},{7,119},{8,120... | collective-permute-start | bytes 294920 | tf_op jit(solution)/shard_map/ppermute | solution.py:235
  17.9 4.3 %collective-permute-start.3 = (f32[8,3072]{1,0:T(8,128)S(1)}, f32[8,3072]{1,0:T(8,128)S(1)}, u32[]{:S(2)}, u32[]{:S(2)}) collective-permute-start(f32[8,3072]{1,0:T(8,128)S(1)} %add.29), channel_id=1, source_target_pairs={{0,17},{1,21},{2,19},{3,23},{4,16},{5,20},{6,18},{7,22},{8,25},{9,... | collective-permute-start | bytes 294920 | tf_op jit(solution)/shard_map/ppermute | solution.py:235
  22.3 6.2 %collective-permute-start.4 = (f32[8,3072]{1,0:T(8,128)S(1)}, f32[8,3072]{1,0:T(8,128)S(1)}, u32[]{:S(2)}, u32[]{:S(2)}) collective-permute-start(f32[8,3072]{1,0:T(8,128)S(1)} %add.30), channel_id=1, source_target_pairs={{0,19},{1,29},{2,17},{3,31},{4,24},{5,22},{6,26},{7,20},{8,27},{9,... | collective-permute-start | bytes 294920 | tf_op jit(solution)/shard_map/ppermute | solution.py:235
  28.5 4.1 %collective-permute-start.5 = (f32[8,3072]{1,0:T(8,128)S(1)}, f32[8,3072]{1,0:T(8,128)S(1)}, u32[]{:S(2)}, u32[]{:S(2)}) collective-permute-start(f32[8,3072]{1,0:T(8,128)S(1)} %add.31), channel_id=1, source_target_pairs={{0,20},{1,49},{2,22},{3,51},{4,52},{5,17},{6,54},{7,19},{8,28},{9,... | collective-permute-start | bytes 294920 | tf_op jit(solution)/shard_map/ppermute | solution.py:235
  32.6 5.3 %collective-permute-start.6 = (f32[8,3072]{1,0:T(8,128)S(1)}, f32[8,3072]{1,0:T(8,128)S(1)}, u32[]{:S(2)}, u32[]{:S(2)}) collective-permute-start(f32[8,3072]{1,0:T(8,128)S(1)} %add.32), channel_id=1, source_target_pairs={{0,28},{1,113},{2,30},{3,115},{4,116},{5,25},{6,118},{7,27},{8,20}... | collective-permute-start | bytes 294920 | tf_op jit(solution)/shard_map/ppermute | solution.py:235
  38.0 1.4 %collective-permute-start.7 = (f32[8,3072]{1,0:T(8,128)S(1)}, f32[8,3072]{1,0:T(8,128)S(1)}, u32[]{:S(2)}, u32[]{:S(2)}) collective-permute-start(f32[8,3072]{1,0:T(8,128)S(1)} %add.33.own_ref), channel_id=1, source_target_pairs={{0,16},{16,0},{32,48},{48,32},{64,80},{80,64},{96,112},{112,96},{1... | collective-permute-start | bytes 294920 | tf_op jit(solution)/shard_map/ppermute | solution.py:239
  40.1 1.3 %collective-permute-start.8 = (f32[8,384]{1,0:T(8,128)S(1)}, f32[8,384]{1,0:T(8,128)S(1)}, u32[]{:S(2)}, u32[]{:S(2)}) collective-permute-start(f32[8,384]{1,0:T(8,128)S(1)} %right_term.1), channel_id=1, source_target_pairs={{0,16},{16,0},{32,48},{48,32},{64,80},{80,64},{96,112},{112,96},{1... | collective-permute-start | bytes 36872 | tf_op jit(solution)/shard_map/ppermute | solution.py:239
  41.4 3.1 %collective-permute-start.9 = (f32[8,384]{1,0:T(8,128)S(1)}, f32[8,384]{1,0:T(8,128)S(1)}, u32[]{:S(2)}, u32[]{:S(2)}) collective-permute-start(f32[8,384]{1,0:T(8,128)S(1)} %add.34), channel_id=1, source_target_pairs={{0,48},{1,49},{2,50},{3,51},{4,52},{5,53},{6,54},{7,55},{8,56},{9,... | collective-permute-start | bytes 36872 | tf_op jit(solution)/shard_map/ppermute | solution.py:235
  44.5 4.5 %collective-permute-start.10 = (f32[8,384]{1,0:T(8,128)S(1)}, f32[8,384]{1,0:T(8,128)S(1)}, u32[]{:S(2)}, u32[]{:S(2)}) collective-permute-start(f32[8,384]{1,0:T(8,128)S(1)} %add.35.refs_3_), channel_id=1, source_target_pairs={{0,112},{1,113},{2,114},{3,115},{4,116},{5,117},{6,118},{7,119},{8... | collective-permute-start | bytes 36872 | tf_op jit(solution)/shard_map/ppermute | solution.py:235

commit v3 on v2

--- a/solution.py
+++ b/solution.py
@@ -156,11 +156,11 @@
 
 def final_kernel(
     replicas,
-    merged_ref, basis_ref, inverse_ref, sum_ref, last_ref, mom_ref,
+    merged_ref, basis_ref, inverse_ref, sum_ref, near_ref, wrap_ref, far_ref, mom_ref,
     fb_ref, mom_out_ref, right_ref,
     fb_buf, mom_buf, right_buf, fb_sem, mom_sem, right_sem,
 ):
-    total = sum_ref[...] + last_ref[...]
+    total = (sum_ref[...] + near_ref[...]) + (wrap_ref[...] + far_ref[...])
     right = jnp.zeros((RANK, COLS), F32)
     for k in range(RANK):
         right += inverse_ref[:, k : k + 1] * total[k : k + 1, :]
@@ -187,7 +187,7 @@
         copy.wait()
 
 
-def finish(replicas, merged, basis, inverse, right_sum, right_last, momentum):
+def finish(replicas, merged, basis, inverse, parts, momentum):
     mom_rows = momentum.shape[0]
 
     def body(*refs):
@@ -195,7 +195,7 @@
 
     return pl.pallas_call(
         body,
-        in_specs=[whole()] * 6,
+        in_specs=[whole()] * 8,
         out_specs=in_hbm(3),
         out_shape=[
             jax.ShapeDtypeStruct((1, ROWS, COLS), BF16),
@@ -213,26 +213,23 @@
         compiler_params=pltpu.CompilerParams(vmem_limit_bytes=20 * MIB),
         cost_estimate=pl.CostEstimate(flops=2 * ROWS * COLS * 32, bytes_accessed=4 * ROWS * COLS, transcendentals=0),
         name="finish",
-    )(merged, basis, inverse, right_sum, right_last, momentum)
-
-
-NEAR = {0: 1, 1: 0, 2: 3, 3: 2}
-WRAP = {0: 3, 3: 0, 1: 2, 2: 1}
-
-
-def step_pairs(axes, partner):
+    )(merged, basis, inverse, *parts, momentum)
+
+
+def step_pairs(axes, flip, swap_cores):
     pairs = []
     for y, core, z, x in itertools.product(range(4), range(2), range(4), range(4)):
         here = {"y": y, "z": z, "x": x}
         axis = axes[(core + y + z + x) % 2]
-        there = {**here, axis: partner[here[axis]]}
+        there = {**here, axis: here[axis] ^ flip}
         place = lambda at, c: (2 * at["y"] + c) * 16 + 4 * at["z"] + at["x"]
-        pairs.append((place(here, core), place(there, 1 - core)))
+        pairs.append((place(here, core), place(there, core ^ swap_cores)))
     return pairs
 
 
-def step(x, axes, partner):
-    return lax.ppermute(x, ("replica", "tensor"), step_pairs(axes, partner))
+def ring(x, axes, far_swap):
+    steps = ((1, 1), (3, 1), (2, far_swap))
+    return [lax.ppermute(x, ("replica", "tensor"), step_pairs(axes, *s)) for s in steps]
 
 
 def sibling(x):
@@ -247,15 +244,14 @@
     merged, keep, send = merge(gradient, feedback, right_t)
     own = keep + sibling(send)
     for axes in ("yx", "xz", "zy"):
-        for partner in (NEAR, WRAP):
-            own = own + step(own, axes, partner)
+        near, wrap, far = ring(own, axes, 0)
+        own = own + near + wrap + far
     other = sibling(own)
     term = right_term(merged, own, other)
     inverse, basis = make_basis(own, other)
     term = term + sibling(term)
-    term = term + step(term, "yy", NEAR)
-    last = step(term, "yy", WRAP)
-    feedback_out, momentum_out, right_t = finish(lax.axis_size("replica"), merged, basis, inverse, term, last, momentum)
+    parts = [term, *ring(term, "yy", 1)]
+    feedback_out, momentum_out, right_t = finish(lax.axis_size("replica"), merged, basis, inverse, parts, momentum)
     return feedback_out, momentum_out, right_t.T
 
 

time: 52.1 us -> 47 us (0.902)
  waiting for transfers between devices: 20.6 us -> 16.3 us
  starting transfers between devices: 19.8 us -> 19.1 us
    ppermute x8 -> x12, waiting for transfers between devices: 17.6 us -> 13.6 us  [ring(): lax.ppermute(x, ('replica', 'tensor'), step_pairs(axes, *s))]
    ppermute x8 -> x12, starting transfers between devices: 17.8 us -> 16.7 us  [ring(): lax.ppermute(x, ('replica', 'tensor'), step_pairs(axes, *s))]
  transfers between devices with their start and end apart: 11 -> 15, of which waited for: 10 -> 13; matrix products, arithmetic and copies ran while one was open for 0% -> 0% of each run, Pallas kernels for 3% -> 4%
where the time goes in v3:
time: 47 us; the launch traced here: 46.9 us
  starting transfers between devices  19.1 us (41%)
  waiting for transfers between devices  16.3 us (35%)
  Pallas kernels  10.7 us (23%)
  between operations  0.69 us (1%)
    ppermute x12, starting transfers between devices, ring(): lax.ppermute(x, ('replica', 'tensor'), step_pairs(axes, *s))  16.7 us
    ppermute x12, waiting for transfers between devices, ring(): lax.ppermute(x, ('replica', 'tensor'), step_pairs(axes, *s))  13.6 us
    pallas_call x1, Pallas kernels, merge(): pl.pallas_call(merge_kernel, in_specs=in_hbm(3), out_specs=[whole(), whol...  5.3 us
    pallas_call x1, Pallas kernels, finish(): pl.pallas_call(body, in_specs=[whole()] * 8, out_specs=in_hbm(3), out_sha...  2.98 us
    ppermute x3, waiting for transfers between devices, sibling(): lax.ppermute(x, 'replica', [(i, i ^ 1) for i in range(lax.axis_size('repl...  2.72 us
    ppermute x3, starting transfers between devices, sibling(): lax.ppermute(x, 'replica', [(i, i ^ 1) for i in range(lax.axis_size('repl...  2.41 us
    pallas_call x1, Pallas kernels, make_basis(): pl.pallas_call(basis_kernel, in_specs=[whole(), whole()], out_specs=[whol...  1.66 us
  transfers between devices with their start and end apart: 15, of which 13 were waited for; matrix products, arithmetic and copies ran while one was open for 0% of the time, Pallas kernels for 4%

profile of v3, /device:TPU:1, one launch (start us, length us, event | category | flops | bytes accessed | tf_op | source)
XLA Modules:
  0.0 46.9 jit_solution(15244382859956904859)
XLA Ops:
  0.6 5.3 %merge.1 = (bf16[6144,384]{1,0:T(8,128)(2,1)S(1)}, f32[8,3072]{1,0:T(8,128)S(1)}, f32[8,3072]{1,0:T(8,128)S(1)}) custom-call(bf16[1,6144,384]{2,1,0:T(8,128)(2,1)} %g_ref.1, bf16[1,6144,384]{2,1,0:T(8,128)(2,1)} %f_ref.1, f32[8,384]{1,0:T(8,128)} %bitcast.2), custom_call_target="tpu_custom_call" | custom-call | flops 37748736 | bytes 9437184 | tf_op jit(solution)/shard_map/merge/pallas_call | solution.py:72
  5.9 1.5 %collective-permute-start = (f32[8,3072]{1,0:T(8,128)S(1)}, f32[8,3072]{1,0:T(8,128)S(1)}, u32[]{:S(2)}, u32[]{:S(2)}) collective-permute-start(f32[8,3072]{1,0:T(8,128)S(1)} %get-tuple-element.13), channel_id=1, source_target_pairs={{0,16},{16,0},{32,48},{48,32},{64,80},{80,64},{96,112},{112,96},{1... | collective-permute-start | bytes 294920 | tf_op jit(solution)/shard_map/ppermute | solution.py:236
  7.4 0.9 %collective-permute-done = f32[8,3072]{1,0:T(8,128)S(1)} collective-permute-done((f32[8,3072]{1,0:T(8,128)S(1)}, f32[8,3072]{1,0:T(8,128)S(1)}, u32[]{:S(2)}, u32[]{:S(2)}) %collective-permute-start) | collective-permute-done | bytes 98336 | tf_op jit(solution)/shard_map/ppermute | solution.py:236
  8.4 2.9 %collective-permute-start.3 = (f32[8,3072]{1,0:T(8,128)S(1)}, f32[8,3072]{1,0:T(8,128)S(1)}, u32[]{:S(2)}, u32[]{:S(2)}) collective-permute-start(f32[8,3072]{1,0:T(8,128)S(1)} %add.33), channel_id=1, source_target_pairs={{0,64},{1,3},{2,66},{3,1},{4,6},{5,69},{6,4},{7,71},{8,72},{9,11},... | collective-permute-start | bytes 294920 | tf_op jit(solution)/shard_map/ppermute | solution.py:232
  11.3 1.4 %collective-permute-start.2 = (f32[8,3072]{1,0:T(8,128)S(1)}, f32[8,3072]{1,0:T(8,128)S(1)}, u32[]{:S(2)}, u32[]{:S(2)}) collective-permute-start(f32[8,3072]{1,0:T(8,128)S(1)} %add.33), channel_id=1, source_target_pairs={{0,112},{1,18},{2,114},{3,16},{4,23},{5,117},{6,21},{7,119},{8,120... | collective-permute-start | bytes 294920 | tf_op jit(solution)/shard_map/ppermute | solution.py:232
  12.7 1.1 %collective-permute-done.3 = f32[8,3072]{1,0:T(8,128)S(1)} collective-permute-done((f32[8,3072]{1,0:T(8,128)S(1)}, f32[8,3072]{1,0:T(8,128)S(1)}, u32[]{:S(2)}, u32[]{:S(2)}) %collective-permute-start.3) | collective-permute-done | bytes 98336 | tf_op jit(solution)/shard_map/ppermute | solution.py:232
  13.8 3.1 %collective-permute-done.2 = f32[8,3072]{1,0:T(8,128)S(1)} collective-permute-done((f32[8,3072]{1,0:T(8,128)S(1)}, f32[8,3072]{1,0:T(8,128)S(1)}, u32[]{:S(2)}, u32[]{:S(2)}) %collective-permute-start.2) | collective-permute-done | bytes 98336 | tf_op jit(solution)/shard_map/ppermute | solution.py:232
  17.0 3.7 %collective-permute-start.6 = (f32[8,3072]{1,0:T(8,128)S(1)}, f32[8,3072]{1,0:T(8,128)S(1)}, u32[]{:S(2)}, u32[]{:S(2)}) collective-permute-start(f32[8,3072]{1,0:T(8,128)S(1)} %add_add_fusion.2), channel_id=1, source_target_pairs={{0,2},{1,9},{2,0},{3,11},{4,12},{5,7},{6,14},{7,5},{8,10},{9,1},{1... | collective-permute-start | bytes 294920 | tf_op jit(solution)/shard_map/ppermute | solution.py:232
  20.7 0.8 %collective-permute-start.5 = (f32[8,3072]{1,0:T(8,128)S(1)}, f32[8,3072]{1,0:T(8,128)S(1)}, u32[]{:S(2)}, u32[]{:S(2)}) collective-permute-start(f32[8,3072]{1,0:T(8,128)S(1)} %add_add_fusion.2), channel_id=1, source_target_pairs={{0,19},{1,29},{2,17},{3,31},{4,24},{5,22},{6,26},{7,20},{8,27},{9,... | collective-permute-start | bytes 294920 | tf_op jit(solution)/shard_map/ppermute | solution.py:232
  21.8 1.2 %collective-permute-done.6 = f32[8,3072]{1,0:T(8,128)S(1)} collective-permute-done((f32[8,3072]{1,0:T(8,128)S(1)}, f32[8,3072]{1,0:T(8,128)S(1)}, u32[]{:S(2)}, u32[]{:S(2)}) %collective-permute-start.6) | collective-permute-done | bytes 98336 | tf_op jit(solution)/shard_map/ppermute | solution.py:232
  23.0 3.0 %collective-permute-done.5 = f32[8,3072]{1,0:T(8,128)S(1)} collective-permute-done((f32[8,3072]{1,0:T(8,128)S(1)}, f32[8,3072]{1,0:T(8,128)S(1)}, u32[]{:S(2)}, u32[]{:S(2)}) %collective-permute-start.5) | collective-permute-done | bytes 98336 | tf_op jit(solution)/shard_map/ppermute | solution.py:232
  26.0 2.8 %collective-permute-start.9 = (f32[8,3072]{1,0:T(8,128)S(1)}, f32[8,3072]{1,0:T(8,128)S(1)}, u32[]{:S(2)}, u32[]{:S(2)}) collective-permute-start(f32[8,3072]{1,0:T(8,128)S(1)} %add_add_fusion.1), channel_id=1, source_target_pairs={{0,8},{1,65},{2,10},{3,67},{4,68},{5,13},{6,70},{7,15},{8,0},{9,73... | collective-permute-start | bytes 294920 | tf_op jit(solution)/shard_map/ppermute | solution.py:232
  28.7 1.7 %collective-permute-start.8 = (f32[8,3072]{1,0:T(8,128)S(1)}, f32[8,3072]{1,0:T(8,128)S(1)}, u32[]{:S(2)}, u32[]{:S(2)}) collective-permute-start(f32[8,3072]{1,0:T(8,128)S(1)} %add_add_fusion.1), channel_id=1, source_target_pairs={{0,28},{1,113},{2,30},{3,115},{4,116},{5,25},{6,118},{7,27},{8,20}... | collective-permute-start | bytes 294920 | tf_op jit(solution)/shard_map/ppermute | solution.py:232
  30.4 0.9 %collective-permute-done.9 = f32[8,3072]{1,0:T(8,128)S(1)} collective-permute-done((f32[8,3072]{1,0:T(8,128)S(1)}, f32[8,3072]{1,0:T(8,128)S(1)}, u32[]{:S(2)}, u32[]{:S(2)}) %collective-permute-start.9) | collective-permute-done | bytes 98336 | tf_op jit(solution)/shard_map/ppermute | solution.py:232
  31.3 3.0 %collective-permute-done.8 = f32[8,3072]{1,0:T(8,128)S(1)} collective-permute-done((f32[8,3072]{1,0:T(8,128)S(1)}, f32[8,3072]{1,0:T(8,128)S(1)}, u32[]{:S(2)}, u32[]{:S(2)}) %collective-permute-start.8) | collective-permute-done | bytes 98336 | tf_op jit(solution)/shard_map/ppermute | solution.py:232
  34.6 0.5 %collective-permute-start.10 = (f32[8,3072]{1,0:T(8,128)S(1)}, f32[8,3072]{1,0:T(8,128)S(1)}, u32[]{:S(2)}, u32[]{:S(2)}) collective-permute-start(f32[8,3072]{1,0:T(8,128)S(1)} %add_add_fusion.own_ref), channel_id=1, source_target_pairs={{0,16},{16,0},{32,48},{48,32},{64,80},{80,64},{96,112},{112,96},{1... | collective-permute-start | bytes 294920 | tf_op jit(solution)/shard_map/ppermute | solution.py:236
  35.1 0.9 %collective-permute-done.10.other_ref = f32[8,3072]{1,0:T(8,128)S(1)} collective-permute-done((f32[8,3072]{1,0:T(8,128)S(1)}, f32[8,3072]{1,0:T(8,128)S(1)}, u32[]{:S(2)}, u32[]{:S(2)}) %collective-permute-start.10) | collective-permute-done | bytes 98336 | tf_op jit(solution)/shard_map/ppermute | solution.py:236
  36.1 0.7 %right_term.1 = f32[8,384]{1,0:T(8,128)S(1)} custom-call(bf16[6144,384]{1,0:T(8,128)(2,1)S(1)} %get-tuple-element.11.merged_ref.refs_0_, f32[8,3072]{1,0:T(8,128)S(1)} %add_add_fusion.own_ref, f32[8,3072]{1,0:T(8,128)S(1)} %collective-permute-done.10.other_ref), custom_call_target="tpu_custom_call" | custom-call | flops 75497472 | bytes 4718592 | tf_op jit(solution)/shard_map/right_term/pallas_call | solution.py:106
  37.2 0.8 %collective-permute-done.11 = f32[8,384]{1,0:T(8,128)S(1)} collective-permute-done((f32[8,384]{1,0:T(8,128)S(1)}, f32[8,384]{1,0:T(8,128)S(1)}, u32[]{:S(2)}, u32[]{:S(2)}) %collective-permute-start.11) | collective-permute-done | bytes 12320 | tf_op jit(solution)/shard_map/ppermute | solution.py:236
  38.1 1.4 %collective-permute-start.14 = (f32[8,384]{1,0:T(8,128)S(1)}, f32[8,384]{1,0:T(8,128)S(1)}, u32[]{:S(2)}, u32[]{:S(2)}) collective-permute-start(f32[8,384]{1,0:T(8,128)S(1)} %add.43.refs_3_), channel_id=1, source_target_pairs={{0,80},{1,81},{2,82},{3,83},{4,84},{5,85},{6,86},{7,87},{8,88},{9,... | collective-permute-start | bytes 36872 | tf_op jit(solution)/shard_map/ppermute | solution.py:232
  39.5 1.3 %collective-permute-start.13 = (f32[8,384]{1,0:T(8,128)S(1)}, f32[8,384]{1,0:T(8,128)S(1)}, u32[]{:S(2)}, u32[]{:S(2)}) collective-permute-start(f32[8,384]{1,0:T(8,128)S(1)} %add.43.refs_3_), channel_id=1, source_target_pairs={{0,112},{1,113},{2,114},{3,115},{4,116},{5,117},{6,118},{7,119},{8... | collective-permute-start | bytes 36872 | tf_op jit(solution)/shard_map/ppermute | solution.py:232
  41.2 1.7 %basis.1 = (f32[8,8]{1,0:T(8,128)S(1)}, bf16[6144,32]{1,0:T(8,128)(2,1)S(1)}) custom-call(f32[8,3072]{1,0:T(8,128)S(1)} %add_add_fusion.own_ref, f32[8,3072]{1,0:T(8,128)S(1)} %collective-permute-done.10.other_ref), custom_call_target="tpu_custom_call" | custom-call | flops 1572864 | bytes 4194304 | tf_op jit(solution)/shard_map/basis/pallas_call | solution.py:146
  42.9 0.9 %collective-permute-done.13.refs_5_ = f32[8,384]{1,0:T(8,128)S(1)} collective-permute-done((f32[8,384]{1,0:T(8,128)S(1)}, f32[8,384]{1,0:T(8,128)S(1)}, u32[]{:S(2)}, u32[]{:S(2)}) %collective-permute-start.13) | collective-permute-done | bytes 12320 | tf_op jit(solution)/shard_map/ppermute | solution.py:232
  43.9 3.0 %finish.1 = (bf16[1,6144,384]{2,1,0:T(8,128)(2,1)}, bf16[768,384]{1,0:T(8,128)(2,1)}, f32[8,384]{1,0:T(8,128)}) custom-call(bf16[6144,384]{1,0:T(8,128)(2,1)S(1)} %get-tuple-element.11.merged_ref.refs_0_, bf16[6144,32]{1,0:T(8,128)(2,1)S(1)} %get-tuple-element.14.refs_1_, f32[8,8]{1,0:T(8,128)S(1)} %get-tuple-element.15.refs_2_, f32[8,384]{1,0:T(8,128)S(1)} %add.43.refs_3_, ...), custom_call_target="tpu_custom_call" | custom-call | flops 150994944 | bytes 9437184 | tf_op jit(solution)/shard_map/finish/pallas_call | solution.py:196
  (17 shorter events, 1.8 us)
Async XLA Ops:
  5.9 38.0 %copy-start = (bf16[768,384]{1,0:T(8,128)(2,1)S(1)}, bf16[768,384]{1,0:T(8,128)(2,1)}, u32[]{:S(2)}) copy-start(bf16[768,384]{1,0:T(8,128)(2,1)} %refs_7_.1) | copy-start | bytes 1769476
  5.9 2.4 %collective-permute-start = (f32[8,3072]{1,0:T(8,128)S(1)}, f32[8,3072]{1,0:T(8,128)S(1)}, u32[]{:S(2)}, u32[]{:S(2)}) collective-permute-start(f32[8,3072]{1,0:T(8,128)S(1)} %get-tuple-element.13), channel_id=1, source_target_pairs={{0,16},{16,0},{32,48},{48,32},{64,80},{80,64},{96,112},{112,96},{1... | collective-permute-start | bytes 294920 | tf_op jit(solution)/shard_map/ppermute | solution.py:236
  8.4 5.3 %collective-permute-start.3 = (f32[8,3072]{1,0:T(8,128)S(1)}, f32[8,3072]{1,0:T(8,128)S(1)}, u32[]{:S(2)}, u32[]{:S(2)}) collective-permute-start(f32[8,3072]{1,0:T(8,128)S(1)} %add.33), channel_id=1, source_target_pairs={{0,64},{1,3},{2,66},{3,1},{4,6},{5,69},{6,4},{7,71},{8,72},{9,11},... | collective-permute-start | bytes 294920 | tf_op jit(solution)/shard_map/ppermute | solution.py:232
  11.3 5.5 %collective-permute-start.2 = (f32[8,3072]{1,0:T(8,128)S(1)}, f32[8,3072]{1,0:T(8,128)S(1)}, u32[]{:S(2)}, u32[]{:S(2)}) collective-permute-start(f32[8,3072]{1,0:T(8,128)S(1)} %add.33), channel_id=1, source_target_pairs={{0,112},{1,18},{2,114},{3,16},{4,23},{5,117},{6,21},{7,119},{8,120... | collective-permute-start | bytes 294920 | tf_op jit(solution)/shard_map/ppermute | solution.py:232
  12.7 4.3 %collective-permute-start.1 = (f32[8,3072]{1,0:T(8,128)S(1)}, f32[8,3072]{1,0:T(8,128)S(1)}, u32[]{:S(2)}, u32[]{:S(2)}) collective-permute-start(f32[8,3072]{1,0:T(8,128)S(1)} %add.33), channel_id=1, source_target_pairs={{0,48},{1,16},{2,50},{3,18},{4,21},{5,53},{6,23},{7,55},{8,56},{9,... | collective-permute-start | bytes 294920 | tf_op jit(solution)/shard_map/ppermute | solution.py:232
  17.0 6.0 %collective-permute-start.6 = (f32[8,3072]{1,0:T(8,128)S(1)}, f32[8,3072]{1,0:T(8,128)S(1)}, u32[]{:S(2)}, u32[]{:S(2)}) collective-permute-start(f32[8,3072]{1,0:T(8,128)S(1)} %add_add_fusion.2), channel_id=1, source_target_pairs={{0,2},{1,9},{2,0},{3,11},{4,12},{5,7},{6,14},{7,5},{8,10},{9,1},{1... | collective-permute-start | bytes 294920 | tf_op jit(solution)/shard_map/ppermute | solution.py:232
  20.7 5.3 %collective-permute-start.5 = (f32[8,3072]{1,0:T(8,128)S(1)}, f32[8,3072]{1,0:T(8,128)S(1)}, u32[]{:S(2)}, u32[]{:S(2)}) collective-permute-start(f32[8,3072]{1,0:T(8,128)S(1)} %add_add_fusion.2), channel_id=1, source_target_pairs={{0,19},{1,29},{2,17},{3,31},{4,24},{5,22},{6,26},{7,20},{8,27},{9,... | collective-permute-start | bytes 294920 | tf_op jit(solution)/shard_map/ppermute | solution.py:232
  21.5 4.4 %collective-permute-start.4 = (f32[8,3072]{1,0:T(8,128)S(1)}, f32[8,3072]{1,0:T(8,128)S(1)}, u32[]{:S(2)}, u32[]{:S(2)}) collective-permute-start(f32[8,3072]{1,0:T(8,128)S(1)} %add_add_fusion.2), channel_id=1, source_target_pairs={{0,17},{1,21},{2,19},{3,23},{4,16},{5,20},{6,18},{7,22},{8,25},{9,... | collective-permute-start | bytes 294920 | tf_op jit(solution)/shard_map/ppermute | solution.py:232
  26.0 5.3 %collective-permute-start.9 = (f32[8,3072]{1,0:T(8,128)S(1)}, f32[8,3072]{1,0:T(8,128)S(1)}, u32[]{:S(2)}, u32[]{:S(2)}) collective-permute-start(f32[8,3072]{1,0:T(8,128)S(1)} %add_add_fusion.1), channel_id=1, source_target_pairs={{0,8},{1,65},{2,10},{3,67},{4,68},{5,13},{6,70},{7,15},{8,0},{9,73... | collective-permute-start | bytes 294920 | tf_op jit(solution)/shard_map/ppermute | solution.py:232
  28.7 5.5 %collective-permute-start.8 = (f32[8,3072]{1,0:T(8,128)S(1)}, f32[8,3072]{1,0:T(8,128)S(1)}, u32[]{:S(2)}, u32[]{:S(2)}) collective-permute-start(f32[8,3072]{1,0:T(8,128)S(1)} %add_add_fusion.1), channel_id=1, source_target_pairs={{0,28},{1,113},{2,30},{3,115},{4,116},{5,25},{6,118},{7,27},{8,20}... | collective-permute-start | bytes 294920 | tf_op jit(solution)/shard_map/ppermute | solution.py:232
  30.4 4.2 %collective-permute-start.7 = (f32[8,3072]{1,0:T(8,128)S(1)}, f32[8,3072]{1,0:T(8,128)S(1)}, u32[]{:S(2)}, u32[]{:S(2)}) collective-permute-start(f32[8,3072]{1,0:T(8,128)S(1)} %add_add_fusion.1), channel_id=1, source_target_pairs={{0,20},{1,49},{2,22},{3,51},{4,52},{5,17},{6,54},{7,19},{8,28},{9,... | collective-permute-start | bytes 294920 | tf_op jit(solution)/shard_map/ppermute | solution.py:232
  34.6 1.4 %collective-permute-start.10 = (f32[8,3072]{1,0:T(8,128)S(1)}, f32[8,3072]{1,0:T(8,128)S(1)}, u32[]{:S(2)}, u32[]{:S(2)}) collective-permute-start(f32[8,3072]{1,0:T(8,128)S(1)} %add_add_fusion.own_ref), channel_id=1, source_target_pairs={{0,16},{16,0},{32,48},{48,32},{64,80},{80,64},{96,112},{112,96},{1... | collective-permute-start | bytes 294920 | tf_op jit(solution)/shard_map/ppermute | solution.py:236
  36.8 1.3 %collective-permute-start.11 = (f32[8,384]{1,0:T(8,128)S(1)}, f32[8,384]{1,0:T(8,128)S(1)}, u32[]{:S(2)}, u32[]{:S(2)}) collective-permute-start(f32[8,384]{1,0:T(8,128)S(1)} %right_term.1), channel_id=1, source_target_pairs={{0,16},{16,0},{32,48},{48,32},{64,80},{80,64},{96,112},{112,96},{1... | collective-permute-start | bytes 36872 | tf_op jit(solution)/shard_map/ppermute | solution.py:236
  38.1 4.8 %collective-permute-start.14 = (f32[8,384]{1,0:T(8,128)S(1)}, f32[8,384]{1,0:T(8,128)S(1)}, u32[]{:S(2)}, u32[]{:S(2)}) collective-permute-start(f32[8,384]{1,0:T(8,128)S(1)} %add.43.refs_3_), channel_id=1, source_target_pairs={{0,80},{1,81},{2,82},{3,83},{4,84},{5,85},{6,86},{7,87},{8,88},{9,... | collective-permute-start | bytes 36872 | tf_op jit(solution)/shard_map/ppermute | solution.py:232
  39.5 4.3 %collective-permute-start.13 = (f32[8,384]{1,0:T(8,128)S(1)}, f32[8,384]{1,0:T(8,128)S(1)}, u32[]{:S(2)}, u32[]{:S(2)}) collective-permute-start(f32[8,384]{1,0:T(8,128)S(1)} %add.43.refs_3_), channel_id=1, source_target_pairs={{0,112},{1,113},{2,114},{3,115},{4,116},{5,117},{6,118},{7,119},{8... | collective-permute-start | bytes 36872 | tf_op jit(solution)/shard_map/ppermute | solution.py:232
  40.8 3.1 %collective-permute-start.12 = (f32[8,384]{1,0:T(8,128)S(1)}, f32[8,384]{1,0:T(8,128)S(1)}, u32[]{:S(2)}, u32[]{:S(2)}) collective-permute-start(f32[8,384]{1,0:T(8,128)S(1)} %add.43.refs_3_), channel_id=1, source_target_pairs={{0,48},{1,49},{2,50},{3,51},{4,52},{5,53},{6,54},{7,55},{8,56},{9,... | collective-permute-start | bytes 36872 | tf_op jit(solution)/shard_map/ppermute | solution.py:232

commit v4 on v3

v4 whole, which is shorter than its diff:
```python
import itertools

import jax
import jax.numpy as jnp
from jax import lax
from jax.experimental import pallas as pl
from jax.experimental.pallas import tpu as pltpu
from jax.sharding import PartitionSpec as P

F32, BF16 = jnp.float32, jnp.bfloat16
ROWS, COLS, RANK = 6144, 384, 8
HALF = ROWS // 2
CHUNKS = 3
CHUNK = HALF // CHUNKS
MIB = 1 << 20


def own_half():
    replica, tensor = lax.axis_index("replica"), lax.axis_index("tensor")
    return lax.rem(replica + replica // 2 + tensor + tensor // 4, 2)


def split(x):
    high = x.astype(BF16)
    return high, (x - high.astype(F32)).astype(BF16)


def rows_of(half, chunk):
    return pl.ds(pl.multiple_of(half * HALF + chunk * CHUNK, CHUNK), CHUNK)


def merge_kernel(mine, g_ref, f_ref, q_ref, merged_ref, term_ref, g_buf, f_buf, q_buf, g_sem, f_sem, q_sem):
    half = own_half() if mine else 1 - own_half()
    q_copy = pltpu.make_async_copy(q_ref, q_buf, q_sem.at[0])
    q_copy.start()
    copies = []
    for i in range(CHUNKS):
        here = pl.ds(i * CHUNK, CHUNK)
        pair = (
            pltpu.make_async_copy(g_ref.at[0, rows_of(half, i), :], g_buf.at[here, :], g_sem.at[i]),
            pltpu.make_async_copy(f_ref.at[0, rows_of(half, i), :], f_buf.at[here, :], f_sem.at[i]),
        )
        for copy in pair:
            copy.start()
        copies.append(pair)
    q_copy.wait()
    right = q_buf[...].astype(BF16)
    for i in range(CHUNKS):
        for copy in copies[i]:
            copy.wait()
        here = pl.ds(i * CHUNK, CHUNK)
        merged = (g_buf[here, :].astype(F32) + f_buf[here, :].astype(F32)).astype(BF16)
        merged_ref[here, :] = merged
        term_ref[:, here] = lax.dot_general(
            right, merged, (((1,), (1,)), ((), ())), preferred_element_type=F32
        )


def whole():
    return pl.BlockSpec(memory_space=pltpu.VMEM)


def in_hbm(count):
    return [pl.BlockSpec(memory_space=pltpu.HBM)] * count


def merge(mine, gradient, feedback, right_t):
    def body(*refs):
        merge_kernel(mine, *refs)

    return pl.pallas_call(
        body,
        in_specs=in_hbm(3),
        out_specs=[whole(), whole()],
        out_shape=[pltpu.VMEM((HALF, COLS), BF16), pltpu.VMEM((RANK, HALF), F32)],
        scratch_shapes=[
            pltpu.VMEM((HALF, COLS), BF16),
            pltpu.VMEM((HALF, COLS), BF16),
            pltpu.VMEM((RANK, COLS), F32),
            pltpu.SemaphoreType.DMA((CHUNKS,)),
            pltpu.SemaphoreType.DMA((CHUNKS,)),
            pltpu.SemaphoreType.DMA((1,)),
        ],
        compiler_params=pltpu.CompilerParams(vmem_limit_bytes=16 * MIB),
        cost_estimate=pl.CostEstimate(flops=HALF * COLS * RANK * 2, bytes_accessed=4 * HALF * COLS, transcendentals=0),
        name="merge_own" if mine else "merge_other",
    )(gradient, feedback, right_t)


def right_kernel(merged_ref, left_ref, *refs):
    pair = jnp.concatenate(split(left_ref[...]), axis=0)
    total = jnp.dot(pair, merged_ref[...], preferred_element_type=F32)
    total = total[:RANK] + total[RANK:]
    for ref in refs[:-1]:
        total += ref[...]
    refs[-1][...] = total


def right_term(merged, left, *before):
    return pl.pallas_call(
        right_kernel,
        in_specs=[whole()] * (2 + len(before)),
        out_specs=whole(),
        out_shape=pltpu.VMEM((RANK, COLS), F32),
        compiler_params=pltpu.CompilerParams(vmem_limit_bytes=16 * MIB),
        cost_estimate=pl.CostEstimate(flops=4 * HALF * COLS * RANK, bytes_accessed=2 * HALF * COLS, transcendentals=0),
        name="right_other" if before else "right_own",
    )(merged, left, *before)


def basis_kernel(own_ref, other_ref, inverse_ref, basis_ref):
    own, other = own_ref[...], other_ref[...]
    gram = jnp.zeros((RANK, RANK), F32)
    for part in (own, other):
        gram += lax.dot_general(
            part, part, (((1,), (1,)), ((), ())), precision=lax.Precision.HIGHEST, preferred_element_type=F32
        )
    row = lax.broadcasted_iota(jnp.int32, (RANK, RANK), 0)
    column = lax.broadcasted_iota(jnp.int32, (RANK, RANK), 1)
    eye = jnp.where(row == column, 1.0, 0.0)
    inverse = eye
    for k in range(RANK):
        factor = jnp.where(row[:, :1] > k, gram[:, k : k + 1] / gram[k : k + 1, k : k + 1], 0.0)
        inverse -= factor * inverse[k : k + 1, :]
        gram -= factor * gram[k : k + 1, :]
    pivots = jnp.sum(gram * eye, axis=1, keepdims=True)
    inverse = inverse / jnp.sqrt(pivots)
    inverse_ref[...] = inverse
    for part, start in ((own, 0), (other, HALF)):
        basis = jnp.zeros((RANK, HALF), F32)
        for k in range(RANK):
            basis += inverse[:, k : k + 1] * part[k : k + 1, :]
        high, low = split(basis)
        packed = jnp.concatenate([high, high, low, low], axis=0)
        basis_ref[start : start + HALF, :] = packed.T


def make_basis(own, other):
    return pl.pallas_call(
        basis_kernel,
        in_specs=[whole(), whole()],
        out_specs=[whole(), whole()],
        out_shape=[pltpu.VMEM((RANK, RANK), F32), pltpu.VMEM((ROWS, 4 * RANK), BF16)],
        compiler_params=pltpu.CompilerParams(vmem_limit_bytes=16 * MIB),
        cost_estimate=pl.CostEstimate(flops=4 * ROWS * RANK * RANK, bytes_accessed=4 * MIB, transcendentals=0),
        name="basis",
    )(own, other)


def final_kernel(
    replicas,
    own_ref, other_ref, basis_ref, inverse_ref, sum_ref, near_ref, wrap_ref, far_ref, mom_ref,
    fb_ref, mom_out_ref, right_ref,
    fb_buf, mom_buf, right_buf, fb_sem, mom_sem, right_sem,
):
    total = (sum_ref[...] + near_ref[...]) + (wrap_ref[...] + far_ref[...])
    right = jnp.zeros((RANK, COLS), F32)
    for k in range(RANK):
        right += inverse_ref[:, k : k + 1] * total[k : k + 1, :]
    right = right * (1.0 / replicas)
    right_buf[...] = right
    copies = [pltpu.make_async_copy(right_buf, right_ref, right_sem.at[0])]
    copies[0].start()
    high, low = split(right)
    pack = jnp.concatenate([high, low, high, low], axis=0)
    mine = own_half()
    for i in range(2 * CHUNKS):
        rows = pl.ds(i * CHUNK, CHUNK)
        merged_ref, half = (own_ref, mine) if i < CHUNKS else (other_ref, 1 - mine)
        merged = merged_ref[pl.ds(i % CHUNKS * CHUNK, CHUNK), :]
        approx = jnp.dot(basis_ref[rows, :], pack, preferred_element_type=F32)
        fb_buf[rows, :] = (merged.astype(F32) - approx).astype(BF16)
        target = fb_ref.at[0, rows_of(half, i % CHUNKS), :]
        copies.append(pltpu.make_async_copy(fb_buf.at[rows, :], target, fb_sem.at[i]))
        copies[-1].start()
        if i == 0:
            count = mom_ref.shape[0]
            replica, per_half = lax.axis_index("replica"), HALF // count
            start = jnp.where(replica // per_half == mine, 0, HALF) + lax.rem(replica, per_half) * count
            mom_rows = pl.ds(pl.multiple_of(start, count), count)
            approx = jnp.dot(basis_ref[mom_rows, :], pack, preferred_element_type=F32)
            mom_buf[...] = (0.9 * mom_ref[...].astype(F32) + approx).astype(BF16)
            copies.append(pltpu.make_async_copy(mom_buf, mom_out_ref, mom_sem.at[0]))
            copies[-1].start()
    for copy in copies:
        copy.wait()


def finish(replicas, merged_own, merged_other, basis, inverse, parts, momentum):
    mom_rows = momentum.shape[0]

    def body(*refs):
        final_kernel(replicas, *refs)

    return pl.pallas_call(
        body,
        in_specs=[whole()] * 9,
        out_specs=in_hbm(3),
        out_shape=[
            jax.ShapeDtypeStruct((1, ROWS, COLS), BF16),
            jax.ShapeDtypeStruct((mom_rows, COLS), BF16),
            jax.ShapeDtypeStruct((RANK, COLS), F32),
        ],
        scratch_shapes=[
            pltpu.VMEM((ROWS, COLS), BF16),
            pltpu.VMEM((mom_rows, COLS), BF16),
            pltpu.VMEM((RANK, COLS), F32),
            pltpu.SemaphoreType.DMA((2 * CHUNKS,)),
            pltpu.SemaphoreType.DMA((1,)),
            pltpu.SemaphoreType.DMA((1,)),
        ],
        compiler_params=pltpu.CompilerParams(vmem_limit_bytes=20 * MIB),
        cost_estimate=pl.CostEstimate(flops=2 * ROWS * COLS * 32, bytes_accessed=4 * ROWS * COLS, transcendentals=0),
        name="finish",
    )(merged_own, merged_other, basis, inverse, *parts, momentum)


def step_pairs(axes, flip, swap_cores):
    pairs = []
    for y, core, z, x in itertools.product(range(4), range(2), range(4), range(4)):
        here = {"y": y, "z": z, "x": x}
        axis = axes[(core + y + z + x) % 2]
        there = {**here, axis: here[axis] ^ flip}
        place = lambda at, c: (2 * at["y"] + c) * 16 + 4 * at["z"] + at["x"]
        pairs.append((place(here, core), place(there, core ^ swap_cores)))
    return pairs


def ring(x, axes, far_swap):
    steps = ((1, 1), (3, 1), (2, far_swap))
    return [lax.ppermute(x, ("replica", "tensor"), step_pairs(axes, *s)) for s in steps]


def sibling(x):
    return lax.ppermute(x, "replica", [(i, i ^ 1) for i in range(lax.axis_size("replica"))])


def shards(gradient, feedback, momentum, right_init):
    gradient = pltpu.with_memory_space_constraint(gradient, pltpu.HBM)
    feedback = pltpu.with_memory_space_constraint(feedback, pltpu.HBM)
    right_t = pltpu.with_memory_space_constraint(right_init.T, pltpu.HBM)
    momentum = pltpu.with_memory_space_constraint(momentum, pltpu.VMEM)
    merged_other, send = merge(False, gradient, feedback, right_t)
    received = sibling(send)
    merged_own, keep = merge(True, gradient, feedback, right_t)
    own = keep + received
    for axes in ("yx", "xz", "zy"):
        near, wrap, far = ring(own, axes, 0)
        own = own + near + wrap + far
    other = sibling(own)
    term = right_term(merged_other, other, right_term(merged_own, own))
    inverse, basis = make_basis(own, other)
    term = term + sibling(term)
    parts = [term, *ring(term, "yy", 1)]
    feedback_out, momentum_out, right_t = finish(
        lax.axis_size("replica"), merged_own, merged_other, basis, inverse, parts, momentum
    )
    return feedback_out, momentum_out, right_t.T


def solution(mesh):
    placed = (
        P("replica", None, "tensor"),
        P("replica", None, "tensor"),
        P("replica", "tensor"),
        P("tensor", None),
    )
    return jax.shard_map(
        shards,
        mesh=mesh,
        in_specs=placed,
        out_specs=(P("replica", None, "tensor"), P("replica", "tensor"), P("tensor", None)),
        check_vma=False,
    )
```

time: 47 us -> 45.7 us (0.972)
  waiting for transfers between devices: 16.3 us -> 14.9 us
    ppermute x3, waiting for transfers between devices: 2.72 us -> 1.37 us  [sibling(): lax.ppermute(x, 'replica', [(i, i ^ 1) for i in range(lax.axis_size('repl...]
    pallas_call x3 -> x5, Pallas kernels: 9.01 us -> 9.28 us  [the longest x2 5.47 us: merge(): pl.pallas_call(body, in_specs=in_hbm(3), out_specs=[whole(), whole()], ou...]
  transfers between devices with their start and end apart: 15 -> 15, of which waited for: 13 -> 11; matrix products, arithmetic and copies ran while one was open for 0% -> 0% of each run, Pallas kernels for 4% -> 11%
where the time goes in v4:
time: 45.7 us; the launch traced here: 45.5 us
  starting transfers between devices  18.8 us (41%)
  waiting for transfers between devices  14.9 us (33%)
  Pallas kernels  10.9 us (24%)
  between operations  0.71 us (2%)
    ppermute x12, starting transfers between devices, ring(): lax.ppermute(x, ('replica', 'tensor'), step_pairs(axes, *s))  16.4 us
    ppermute x12, waiting for transfers between devices, ring(): lax.ppermute(x, ('replica', 'tensor'), step_pairs(axes, *s))  13.6 us
    pallas_call x2, Pallas kernels, merge(): pl.pallas_call(body, in_specs=in_hbm(3), out_specs=[whole(), whole()], ou...  5.47 us
    pallas_call x1, Pallas kernels, finish(): pl.pallas_call(body, in_specs=[whole()] * 9, out_specs=in_hbm(3), out_sha...  2.99 us
    ppermute x3, starting transfers between devices, sibling(): lax.ppermute(x, 'replica', [(i, i ^ 1) for i in range(lax.axis_size('repl...  2.41 us
    pallas_call x1, Pallas kernels, make_basis(): pl.pallas_call(basis_kernel, in_specs=[whole(), whole()], out_specs=[whol...  1.66 us
    ppermute x3, waiting for transfers between devices, sibling(): lax.ppermute(x, 'replica', [(i, i ^ 1) for i in range(lax.axis_size('repl...  1.37 us
  transfers between devices with their start and end apart: 15, of which 11 were waited for; matrix products, arithmetic and copies ran while one was open for 0% of the time, Pallas kernels for 11%

profile of v4, /device:TPU:1, one launch (start us, length us, event | category | flops | bytes accessed | tf_op | source)
XLA Modules:
  0.0 45.5 jit_solution(15681281274129052203)
XLA Ops:
  0.6 2.7 %merge_other.1 = (bf16[3072,384]{1,0:T(8,128)(2,1)S(1)}, f32[8,3072]{1,0:T(8,128)S(1)}) custom-call(bf16[1,6144,384]{2,1,0:T(8,128)(2,1)} %refs_0_.3, bf16[1,6144,384]{2,1,0:T(8,128)(2,1)} %refs_1_.3, f32[8,384]{1,0:T(8,128)} %bitcast.2), custom_call_target="tpu_custom_call" | custom-call | flops 18874368 | bytes 4718592 | tf_op jit(solution)/shard_map/merge_other/pallas_call | solution.py:71
  3.4 1.5 %collective-permute-start = (f32[8,3072]{1,0:T(8,128)S(1)}, f32[8,3072]{1,0:T(8,128)S(1)}, u32[]{:S(2)}, u32[]{:S(2)}) collective-permute-start(f32[8,3072]{1,0:T(8,128)S(1)} %get-tuple-element.15), channel_id=1, source_target_pairs={{0,16},{16,0},{32,48},{48,32},{64,80},{80,64},{96,112},{112,96},{1... | collective-permute-start | bytes 294920 | tf_op jit(solution)/shard_map/ppermute | solution.py:235
  4.9 2.7 %merge_own.1 = (bf16[3072,384]{1,0:T(8,128)(2,1)S(1)}, f32[8,3072]{1,0:T(8,128)S(1)}) custom-call(bf16[1,6144,384]{2,1,0:T(8,128)(2,1)} %refs_0_.3, bf16[1,6144,384]{2,1,0:T(8,128)(2,1)} %refs_1_.3, f32[8,384]{1,0:T(8,128)} %bitcast.3), custom_call_target="tpu_custom_call" | custom-call | flops 18874368 | bytes 4718592 | tf_op jit(solution)/shard_map/merge_own/pallas_call | solution.py:71
  7.7 2.9 %collective-permute-start.3 = (f32[8,3072]{1,0:T(8,128)S(1)}, f32[8,3072]{1,0:T(8,128)S(1)}, u32[]{:S(2)}, u32[]{:S(2)}) collective-permute-start(f32[8,3072]{1,0:T(8,128)S(1)} %add.33), channel_id=1, source_target_pairs={{0,64},{1,3},{2,66},{3,1},{4,6},{5,69},{6,4},{7,71},{8,72},{9,11},... | collective-permute-start | bytes 294920 | tf_op jit(solution)/shard_map/ppermute | solution.py:231
  10.6 1.1 %collective-permute-start.2 = (f32[8,3072]{1,0:T(8,128)S(1)}, f32[8,3072]{1,0:T(8,128)S(1)}, u32[]{:S(2)}, u32[]{:S(2)}) collective-permute-start(f32[8,3072]{1,0:T(8,128)S(1)} %add.33), channel_id=1, source_target_pairs={{0,112},{1,18},{2,114},{3,16},{4,23},{5,117},{6,21},{7,119},{8,120... | collective-permute-start | bytes 294920 | tf_op jit(solution)/shard_map/ppermute | solution.py:231
  11.6 1.4 %collective-permute-done.3 = f32[8,3072]{1,0:T(8,128)S(1)} collective-permute-done((f32[8,3072]{1,0:T(8,128)S(1)}, f32[8,3072]{1,0:T(8,128)S(1)}, u32[]{:S(2)}, u32[]{:S(2)}) %collective-permute-start.3) | collective-permute-done | bytes 98336 | tf_op jit(solution)/shard_map/ppermute | solution.py:231
  13.0 2.9 %collective-permute-done.2 = f32[8,3072]{1,0:T(8,128)S(1)} collective-permute-done((f32[8,3072]{1,0:T(8,128)S(1)}, f32[8,3072]{1,0:T(8,128)S(1)}, u32[]{:S(2)}, u32[]{:S(2)}) %collective-permute-start.2) | collective-permute-done | bytes 98336 | tf_op jit(solution)/shard_map/ppermute | solution.py:231
  15.9 3.7 %collective-permute-start.6 = (f32[8,3072]{1,0:T(8,128)S(1)}, f32[8,3072]{1,0:T(8,128)S(1)}, u32[]{:S(2)}, u32[]{:S(2)}) collective-permute-start(f32[8,3072]{1,0:T(8,128)S(1)} %add_add_fusion.2), channel_id=1, source_target_pairs={{0,2},{1,9},{2,0},{3,11},{4,12},{5,7},{6,14},{7,5},{8,10},{9,1},{1... | collective-permute-start | bytes 294920 | tf_op jit(solution)/shard_map/ppermute | solution.py:231
  19.6 0.8 %collective-permute-start.5 = (f32[8,3072]{1,0:T(8,128)S(1)}, f32[8,3072]{1,0:T(8,128)S(1)}, u32[]{:S(2)}, u32[]{:S(2)}) collective-permute-start(f32[8,3072]{1,0:T(8,128)S(1)} %add_add_fusion.2), channel_id=1, source_target_pairs={{0,19},{1,29},{2,17},{3,31},{4,24},{5,22},{6,26},{7,20},{8,27},{9,... | collective-permute-start | bytes 294920 | tf_op jit(solution)/shard_map/ppermute | solution.py:231
  20.7 1.2 %collective-permute-done.6 = f32[8,3072]{1,0:T(8,128)S(1)} collective-permute-done((f32[8,3072]{1,0:T(8,128)S(1)}, f32[8,3072]{1,0:T(8,128)S(1)}, u32[]{:S(2)}, u32[]{:S(2)}) %collective-permute-start.6) | collective-permute-done | bytes 98336 | tf_op jit(solution)/shard_map/ppermute | solution.py:231
  21.9 3.0 %collective-permute-done.5 = f32[8,3072]{1,0:T(8,128)S(1)} collective-permute-done((f32[8,3072]{1,0:T(8,128)S(1)}, f32[8,3072]{1,0:T(8,128)S(1)}, u32[]{:S(2)}, u32[]{:S(2)}) %collective-permute-start.5) | collective-permute-done | bytes 98336 | tf_op jit(solution)/shard_map/ppermute | solution.py:231
  24.9 2.9 %collective-permute-start.9 = (f32[8,3072]{1,0:T(8,128)S(1)}, f32[8,3072]{1,0:T(8,128)S(1)}, u32[]{:S(2)}, u32[]{:S(2)}) collective-permute-start(f32[8,3072]{1,0:T(8,128)S(1)} %add_add_fusion.1), channel_id=1, source_target_pairs={{0,8},{1,65},{2,10},{3,67},{4,68},{5,13},{6,70},{7,15},{8,0},{9,73... | collective-permute-start | bytes 294920 | tf_op jit(solution)/shard_map/ppermute | solution.py:231
  27.8 1.5 %collective-permute-start.8 = (f32[8,3072]{1,0:T(8,128)S(1)}, f32[8,3072]{1,0:T(8,128)S(1)}, u32[]{:S(2)}, u32[]{:S(2)}) collective-permute-start(f32[8,3072]{1,0:T(8,128)S(1)} %add_add_fusion.1), channel_id=1, source_target_pairs={{0,28},{1,113},{2,30},{3,115},{4,116},{5,25},{6,118},{7,27},{8,20}... | collective-permute-start | bytes 294920 | tf_op jit(solution)/shard_map/ppermute | solution.py:231
  29.3 0.9 %collective-permute-done.9 = f32[8,3072]{1,0:T(8,128)S(1)} collective-permute-done((f32[8,3072]{1,0:T(8,128)S(1)}, f32[8,3072]{1,0:T(8,128)S(1)}, u32[]{:S(2)}, u32[]{:S(2)}) %collective-permute-start.9) | collective-permute-done | bytes 98336 | tf_op jit(solution)/shard_map/ppermute | solution.py:231
  30.2 3.1 %collective-permute-done.8 = f32[8,3072]{1,0:T(8,128)S(1)} collective-permute-done((f32[8,3072]{1,0:T(8,128)S(1)}, f32[8,3072]{1,0:T(8,128)S(1)}, u32[]{:S(2)}, u32[]{:S(2)}) %collective-permute-start.8) | collective-permute-done | bytes 98336 | tf_op jit(solution)/shard_map/ppermute | solution.py:231
  33.6 0.5 %collective-permute-start.10 = (f32[8,3072]{1,0:T(8,128)S(1)}, f32[8,3072]{1,0:T(8,128)S(1)}, u32[]{:S(2)}, u32[]{:S(2)}) collective-permute-start(f32[8,3072]{1,0:T(8,128)S(1)} %add_add_fusion.own_ref.left_ref), channel_id=1, source_target_pairs={{0,16},{16,0},{32,48},{48,32},{64,80},{80,64},{96,112},{112,96},{1... | collective-permute-start | bytes 294920 | tf_op jit(solution)/shard_map/ppermute | solution.py:235
  34.5 0.5 %collective-permute-done.10.other_ref.left_ref = f32[8,3072]{1,0:T(8,128)S(1)} collective-permute-done((f32[8,3072]{1,0:T(8,128)S(1)}, f32[8,3072]{1,0:T(8,128)S(1)}, u32[]{:S(2)}, u32[]{:S(2)}) %collective-permute-start.10) | collective-permute-done | bytes 98336 | tf_op jit(solution)/shard_map/ppermute | solution.py:235
  35.8 0.8 %collective-permute-done.11 = f32[8,384]{1,0:T(8,128)S(1)} collective-permute-done((f32[8,384]{1,0:T(8,128)S(1)}, f32[8,384]{1,0:T(8,128)S(1)}, u32[]{:S(2)}, u32[]{:S(2)}) %collective-permute-start.11) | collective-permute-done | bytes 12320 | tf_op jit(solution)/shard_map/ppermute | solution.py:235
  36.7 1.4 %collective-permute-start.14 = (f32[8,384]{1,0:T(8,128)S(1)}, f32[8,384]{1,0:T(8,128)S(1)}, u32[]{:S(2)}, u32[]{:S(2)}) collective-permute-start(f32[8,384]{1,0:T(8,128)S(1)} %add.43.refs_4_), channel_id=1, source_target_pairs={{0,80},{1,81},{2,82},{3,83},{4,84},{5,85},{6,86},{7,87},{8,88},{9,... | collective-permute-start | bytes 36872 | tf_op jit(solution)/shard_map/ppermute | solution.py:231
  38.1 1.3 %collective-permute-start.13 = (f32[8,384]{1,0:T(8,128)S(1)}, f32[8,384]{1,0:T(8,128)S(1)}, u32[]{:S(2)}, u32[]{:S(2)}) collective-permute-start(f32[8,384]{1,0:T(8,128)S(1)} %add.43.refs_4_), channel_id=1, source_target_pairs={{0,112},{1,113},{2,114},{3,115},{4,116},{5,117},{6,118},{7,119},{8... | collective-permute-start | bytes 36872 | tf_op jit(solution)/shard_map/ppermute | solution.py:231
  39.4 0.5 %collective-permute-start.12 = (f32[8,384]{1,0:T(8,128)S(1)}, f32[8,384]{1,0:T(8,128)S(1)}, u32[]{:S(2)}, u32[]{:S(2)}) collective-permute-start(f32[8,384]{1,0:T(8,128)S(1)} %add.43.refs_4_), channel_id=1, source_target_pairs={{0,48},{1,49},{2,50},{3,51},{4,52},{5,53},{6,54},{7,55},{8,56},{9,... | collective-permute-start | bytes 36872 | tf_op jit(solution)/shard_map/ppermute | solution.py:231
  39.8 1.7 %basis.1 = (f32[8,8]{1,0:T(8,128)S(1)}, bf16[6144,32]{1,0:T(8,128)(2,1)S(1)}) custom-call(f32[8,3072]{1,0:T(8,128)S(1)} %add_add_fusion.own_ref.left_ref, f32[8,3072]{1,0:T(8,128)S(1)} %collective-permute-done.10.other_ref.left_ref), custom_call_target="tpu_custom_call" | custom-call | flops 1572864 | bytes 4194304 | tf_op jit(solution)/shard_map/basis/pallas_call | solution.py:139
  41.5 0.9 %collective-permute-done.13.refs_6_ = f32[8,384]{1,0:T(8,128)S(1)} collective-permute-done((f32[8,384]{1,0:T(8,128)S(1)}, f32[8,384]{1,0:T(8,128)S(1)}, u32[]{:S(2)}, u32[]{:S(2)}) %collective-permute-start.13) | collective-permute-done | bytes 12320 | tf_op jit(solution)/shard_map/ppermute | solution.py:231
  42.5 3.0 %finish.1 = (bf16[1,6144,384]{2,1,0:T(8,128)(2,1)}, bf16[768,384]{1,0:T(8,128)(2,1)}, f32[8,384]{1,0:T(8,128)}) custom-call(bf16[3072,384]{1,0:T(8,128)(2,1)S(1)} %get-tuple-element.12.merged_ref.refs_0_, bf16[3072,384]{1,0:T(8,128)(2,1)S(1)} %get-tuple-element.13.merged_ref.refs_1_, bf16[6144,32]{1,0:T(8,128)(2,1)S(1)} %get-tuple-element.16.refs_2_, ...), custom_call_target="tpu_custom_call" | custom-call | flops 150994944 | bytes 9437184 | tf_op jit(solution)/shard_map/finish/pallas_call | solution.py:195
  (19 shorter events, 1.9 us)
Async XLA Ops:
  3.4 4.2 %collective-permute-start = (f32[8,3072]{1,0:T(8,128)S(1)}, f32[8,3072]{1,0:T(8,128)S(1)}, u32[]{:S(2)}, u32[]{:S(2)}) collective-permute-start(f32[8,3072]{1,0:T(8,128)S(1)} %get-tuple-element.15), channel_id=1, source_target_pairs={{0,16},{16,0},{32,48},{48,32},{64,80},{80,64},{96,112},{112,96},{1... | collective-permute-start | bytes 294920 | tf_op jit(solution)/shard_map/ppermute | solution.py:235
  7.6 34.9 %copy-start = (bf16[768,384]{1,0:T(8,128)(2,1)S(1)}, bf16[768,384]{1,0:T(8,128)(2,1)}, u32[]{:S(2)}) copy-start(bf16[768,384]{1,0:T(8,128)(2,1)} %refs_8_.1) | copy-start | bytes 1769476
  7.7 5.3 %collective-permute-start.3 = (f32[8,3072]{1,0:T(8,128)S(1)}, f32[8,3072]{1,0:T(8,128)S(1)}, u32[]{:S(2)}, u32[]{:S(2)}) collective-permute-start(f32[8,3072]{1,0:T(8,128)S(1)} %add.33), channel_id=1, source_target_pairs={{0,64},{1,3},{2,66},{3,1},{4,6},{5,69},{6,4},{7,71},{8,72},{9,11},... | collective-permute-start | bytes 294920 | tf_op jit(solution)/shard_map/ppermute | solution.py:231
  10.6 5.3 %collective-permute-start.2 = (f32[8,3072]{1,0:T(8,128)S(1)}, f32[8,3072]{1,0:T(8,128)S(1)}, u32[]{:S(2)}, u32[]{:S(2)}) collective-permute-start(f32[8,3072]{1,0:T(8,128)S(1)} %add.33), channel_id=1, source_target_pairs={{0,112},{1,18},{2,114},{3,16},{4,23},{5,117},{6,21},{7,119},{8,120... | collective-permute-start | bytes 294920 | tf_op jit(solution)/shard_map/ppermute | solution.py:231
  11.6 4.3 %collective-permute-start.1 = (f32[8,3072]{1,0:T(8,128)S(1)}, f32[8,3072]{1,0:T(8,128)S(1)}, u32[]{:S(2)}, u32[]{:S(2)}) collective-permute-start(f32[8,3072]{1,0:T(8,128)S(1)} %add.33), channel_id=1, source_target_pairs={{0,48},{1,16},{2,50},{3,18},{4,21},{5,53},{6,23},{7,55},{8,56},{9,... | collective-permute-start | bytes 294920 | tf_op jit(solution)/shard_map/ppermute | solution.py:231
  15.9 6.0 %collective-permute-start.6 = (f32[8,3072]{1,0:T(8,128)S(1)}, f32[8,3072]{1,0:T(8,128)S(1)}, u32[]{:S(2)}, u32[]{:S(2)}) collective-permute-start(f32[8,3072]{1,0:T(8,128)S(1)} %add_add_fusion.2), channel_id=1, source_target_pairs={{0,2},{1,9},{2,0},{3,11},{4,12},{5,7},{6,14},{7,5},{8,10},{9,1},{1... | collective-permute-start | bytes 294920 | tf_op jit(solution)/shard_map/ppermute | solution.py:231
  19.6 5.3 %collective-permute-start.5 = (f32[8,3072]{1,0:T(8,128)S(1)}, f32[8,3072]{1,0:T(8,128)S(1)}, u32[]{:S(2)}, u32[]{:S(2)}) collective-permute-start(f32[8,3072]{1,0:T(8,128)S(1)} %add_add_fusion.2), channel_id=1, source_target_pairs={{0,19},{1,29},{2,17},{3,31},{4,24},{5,22},{6,26},{7,20},{8,27},{9,... | collective-permute-start | bytes 294920 | tf_op jit(solution)/shard_map/ppermute | solution.py:231
  20.4 4.4 %collective-permute-start.4 = (f32[8,3072]{1,0:T(8,128)S(1)}, f32[8,3072]{1,0:T(8,128)S(1)}, u32[]{:S(2)}, u32[]{:S(2)}) collective-permute-start(f32[8,3072]{1,0:T(8,128)S(1)} %add_add_fusion.2), channel_id=1, source_target_pairs={{0,17},{1,21},{2,19},{3,23},{4,16},{5,20},{6,18},{7,22},{8,25},{9,... | collective-permute-start | bytes 294920 | tf_op jit(solution)/shard_map/ppermute | solution.py:231
  24.9 5.3 %collective-permute-start.9 = (f32[8,3072]{1,0:T(8,128)S(1)}, f32[8,3072]{1,0:T(8,128)S(1)}, u32[]{:S(2)}, u32[]{:S(2)}) collective-permute-start(f32[8,3072]{1,0:T(8,128)S(1)} %add_add_fusion.1), channel_id=1, source_target_pairs={{0,8},{1,65},{2,10},{3,67},{4,68},{5,13},{6,70},{7,15},{8,0},{9,73... | collective-permute-start | bytes 294920 | tf_op jit(solution)/shard_map/ppermute | solution.py:231
  27.8 5.5 %collective-permute-start.8 = (f32[8,3072]{1,0:T(8,128)S(1)}, f32[8,3072]{1,0:T(8,128)S(1)}, u32[]{:S(2)}, u32[]{:S(2)}) collective-permute-start(f32[8,3072]{1,0:T(8,128)S(1)} %add_add_fusion.1), channel_id=1, source_target_pairs={{0,28},{1,113},{2,30},{3,115},{4,116},{5,25},{6,118},{7,27},{8,20}... | collective-permute-start | bytes 294920 | tf_op jit(solution)/shard_map/ppermute | solution.py:231
  29.3 4.2 %collective-permute-start.7 = (f32[8,3072]{1,0:T(8,128)S(1)}, f32[8,3072]{1,0:T(8,128)S(1)}, u32[]{:S(2)}, u32[]{:S(2)}) collective-permute-start(f32[8,3072]{1,0:T(8,128)S(1)} %add_add_fusion.1), channel_id=1, source_target_pairs={{0,20},{1,49},{2,22},{3,51},{4,52},{5,17},{6,54},{7,19},{8,28},{9,... | collective-permute-start | bytes 294920 | tf_op jit(solution)/shard_map/ppermute | solution.py:231
  33.6 1.4 %collective-permute-start.10 = (f32[8,3072]{1,0:T(8,128)S(1)}, f32[8,3072]{1,0:T(8,128)S(1)}, u32[]{:S(2)}, u32[]{:S(2)}) collective-permute-start(f32[8,3072]{1,0:T(8,128)S(1)} %add_add_fusion.own_ref.left_ref), channel_id=1, source_target_pairs={{0,16},{16,0},{32,48},{48,32},{64,80},{80,64},{96,112},{112,96},{1... | collective-permute-start | bytes 294920 | tf_op jit(solution)/shard_map/ppermute | solution.py:235
  35.4 1.3 %collective-permute-start.11 = (f32[8,384]{1,0:T(8,128)S(1)}, f32[8,384]{1,0:T(8,128)S(1)}, u32[]{:S(2)}, u32[]{:S(2)}) collective-permute-start(f32[8,384]{1,0:T(8,128)S(1)} %right_other.1), channel_id=1, source_target_pairs={{0,16},{16,0},{32,48},{48,32},{64,80},{80,64},{96,112},{112,96},{1... | collective-permute-start | bytes 36872 | tf_op jit(solution)/shard_map/ppermute | solution.py:235
  36.7 4.8 %collective-permute-start.14 = (f32[8,384]{1,0:T(8,128)S(1)}, f32[8,384]{1,0:T(8,128)S(1)}, u32[]{:S(2)}, u32[]{:S(2)}) collective-permute-start(f32[8,384]{1,0:T(8,128)S(1)} %add.43.refs_4_), channel_id=1, source_target_pairs={{0,80},{1,81},{2,82},{3,83},{4,84},{5,85},{6,86},{7,87},{8,88},{9,... | collective-permute-start | bytes 36872 | tf_op jit(solution)/shard_map/ppermute | solution.py:231
  38.1 4.3 %collective-permute-start.13 = (f32[8,384]{1,0:T(8,128)S(1)}, f32[8,384]{1,0:T(8,128)S(1)}, u32[]{:S(2)}, u32[]{:S(2)}) collective-permute-start(f32[8,384]{1,0:T(8,128)S(1)} %add.43.refs_4_), channel_id=1, source_target_pairs={{0,112},{1,113},{2,114},{3,115},{4,116},{5,117},{6,118},{7,119},{8... | collective-permute-start | bytes 36872 | tf_op jit(solution)/shard_map/ppermute | solution.py:231
  39.4 3.1 %collective-permute-start.12 = (f32[8,384]{1,0:T(8,128)S(1)}, f32[8,384]{1,0:T(8,128)S(1)}, u32[]{:S(2)}, u32[]{:S(2)}) collective-permute-start(f32[8,384]{1,0:T(8,128)S(1)} %add.43.refs_4_), channel_id=1, source_target_pairs={{0,48},{1,49},{2,50},{3,51},{4,52},{5,53},{6,54},{7,55},{8,56},{9,... | collective-permute-start | bytes 36872 | tf_op jit(solution)/shard_map/ppermute | solution.py:231

commit v5 on v4

--- a/solution.py
+++ b/solution.py
@@ -29,31 +29,41 @@
     return pl.ds(pl.multiple_of(half * HALF + chunk * CHUNK, CHUNK), CHUNK)
 
 
-def merge_kernel(mine, g_ref, f_ref, q_ref, merged_ref, term_ref, g_buf, f_buf, q_buf, g_sem, f_sem, q_sem):
-    half = own_half() if mine else 1 - own_half()
-    q_copy = pltpu.make_async_copy(q_ref, q_buf, q_sem.at[0])
+def merge_chunk(g_ref, f_ref, right, merged_ref, term_ref, i):
+    here = pl.ds(i * CHUNK, CHUNK)
+    merged = (g_ref[here, :].astype(F32) + f_ref[here, :].astype(F32)).astype(BF16)
+    merged_ref[here, :] = merged
+    term_ref[:, here] = lax.dot_general(right, merged, (((1,), (1,)), ((), ())), preferred_element_type=F32)
+
+
+def load_kernel(g_ref, f_ref, q_ref, merged_ref, term_ref, g_own, f_own, q_own, g_buf, f_buf, g_sem, f_sem, q_sem):
+    mine = own_half()
+    q_copy = pltpu.make_async_copy(q_ref, q_own, q_sem.at[0])
     q_copy.start()
     copies = []
-    for i in range(CHUNKS):
-        here = pl.ds(i * CHUNK, CHUNK)
-        pair = (
-            pltpu.make_async_copy(g_ref.at[0, rows_of(half, i), :], g_buf.at[here, :], g_sem.at[i]),
-            pltpu.make_async_copy(f_ref.at[0, rows_of(half, i), :], f_buf.at[here, :], f_sem.at[i]),
-        )
-        for copy in pair:
-            copy.start()
-        copies.append(pair)
+    for half, g_to, f_to in ((1 - mine, g_buf, f_buf), (mine, g_own, f_own)):
+        for i in range(CHUNKS):
+            here, n = pl.ds(i * CHUNK, CHUNK), len(copies)
+            pair = (
+                pltpu.make_async_copy(g_ref.at[0, rows_of(half, i), :], g_to.at[here, :], g_sem.at[n]),
+                pltpu.make_async_copy(f_ref.at[0, rows_of(half, i), :], f_to.at[here, :], f_sem.at[n]),
+            )
+            for copy in pair:
+                copy.start()
+            copies.append(pair)
     q_copy.wait()
-    right = q_buf[...].astype(BF16)
-    for i in range(CHUNKS):
+    right = q_own[...].astype(BF16)
+    for i in range(2 * CHUNKS):
         for copy in copies[i]:
             copy.wait()
-        here = pl.ds(i * CHUNK, CHUNK)
-        merged = (g_buf[here, :].astype(F32) + f_buf[here, :].astype(F32)).astype(BF16)
-        merged_ref[here, :] = merged
-        term_ref[:, here] = lax.dot_general(
-            right, merged, (((1,), (1,)), ((), ())), preferred_element_type=F32
-        )
+        if i < CHUNKS:
+            merge_chunk(g_buf, f_buf, right, merged_ref, term_ref, i)
+
+
+def merge_kernel(g_ref, f_ref, q_ref, merged_ref, term_ref):
+    right = q_ref[...].astype(BF16)
+    for i in range(CHUNKS):
+        merge_chunk(g_ref, f_ref, right, merged_ref, term_ref, i)
 
 
 def whole():
@@ -64,26 +74,35 @@
     return [pl.BlockSpec(memory_space=pltpu.HBM)] * count
 
 
-def merge(mine, gradient, feedback, right_t):
-    def body(*refs):
-        merge_kernel(mine, *refs)
-
-    return pl.pallas_call(
-        body,
+def merge_other(gradient, feedback, right_t):
+    half_rows = pltpu.VMEM((HALF, COLS), BF16)
+    return pl.pallas_call(
+        load_kernel,
         in_specs=in_hbm(3),
-        out_specs=[whole(), whole()],
-        out_shape=[pltpu.VMEM((HALF, COLS), BF16), pltpu.VMEM((RANK, HALF), F32)],
+        out_specs=[whole()] * 5,
+        out_shape=[half_rows, pltpu.VMEM((RANK, HALF), F32), half_rows, half_rows, pltpu.VMEM((RANK, COLS), F32)],
         scratch_shapes=[
-            pltpu.VMEM((HALF, COLS), BF16),
-            pltpu.VMEM((HALF, COLS), BF16),
-            pltpu.VMEM((RANK, COLS), F32),
-            pltpu.SemaphoreType.DMA((CHUNKS,)),
-            pltpu.SemaphoreType.DMA((CHUNKS,)),
+            half_rows,
+            half_rows,
+            pltpu.SemaphoreType.DMA((2 * CHUNKS,)),
+            pltpu.SemaphoreType.DMA((2 * CHUNKS,)),
             pltpu.SemaphoreType.DMA((1,)),
         ],
         compiler_params=pltpu.CompilerParams(vmem_limit_bytes=16 * MIB),
+        cost_estimate=pl.CostEstimate(flops=HALF * COLS * RANK * 2, bytes_accessed=8 * HALF * COLS, transcendentals=0),
+        name="merge_other",
+    )(gradient, feedback, right_t)
+
+
+def merge_own(gradient, feedback, right_t):
+    return pl.pallas_call(
+        merge_kernel,
+        in_specs=[whole()] * 3,
+        out_specs=[whole(), whole()],
+        out_shape=[pltpu.VMEM((HALF, COLS), BF16), pltpu.VMEM((RANK, HALF), F32)],
+        compiler_params=pltpu.CompilerParams(vmem_limit_bytes=16 * MIB),
         cost_estimate=pl.CostEstimate(flops=HALF * COLS * RANK * 2, bytes_accessed=4 * HALF * COLS, transcendentals=0),
-        name="merge_own" if mine else "merge_other",
+        name="merge_own",
     )(gradient, feedback, right_t)
 
 
@@ -215,20 +234,29 @@
     )(merged_own, merged_other, basis, inverse, *parts, momentum)
 
 
-def step_pairs(axes, flip, swap_cores):
+FLIP = {"n": 1, "w": 3, "f": 2}
+
+
+def move_pairs(moves, swap):
     pairs = []
     for y, core, z, x in itertools.product(range(4), range(2), range(4), range(4)):
-        here = {"y": y, "z": z, "x": x}
-        axis = axes[(core + y + z + x) % 2]
-        there = {**here, axis: here[axis] ^ flip}
-        place = lambda at, c: (2 * at["y"] + c) * 16 + 4 * at["z"] + at["x"]
-        pairs.append((place(here, core), place(there, core ^ swap_cores)))
+        there = {"y": y, "z": z, "x": x}
+        for kind, axis in moves[(core + y + z + x) % 2]:
+            there[axis] ^= FLIP[kind]
+        to = 2 * there["y"] + (core ^ swap)
+        pairs.append((16 * (2 * y + core) + 4 * z + x, 16 * to + 4 * there["z"] + there["x"]))
     return pairs
 
 
-def ring(x, axes, far_swap):
-    steps = ((1, 1), (3, 1), (2, far_swap))
-    return [lax.ppermute(x, ("replica", "tensor"), step_pairs(axes, *s)) for s in steps]
+def move(x, moves, swap):
+    return lax.ppermute(x, ("replica", "tensor"), move_pairs(moves, swap))
+
+
+def group_sum(x, first, second):
+    both = [[a, b] for a, b in zip(first, second)]
+    near = move(x, [[a] for a in first], 1)
+    wrap = move(x, [[b] for b in second], 1)
+    return x + near + wrap + move(x, both, 0)
 
 
 def sibling(x):
@@ -240,18 +268,18 @@
     feedback = pltpu.with_memory_space_constraint(feedback, pltpu.HBM)
     right_t = pltpu.with_memory_space_constraint(right_init.T, pltpu.HBM)
     momentum = pltpu.with_memory_space_constraint(momentum, pltpu.VMEM)
-    merged_other, send = merge(False, gradient, feedback, right_t)
+    merged_other, send, *loaded = merge_other(gradient, feedback, right_t)
     received = sibling(send)
-    merged_own, keep = merge(True, gradient, feedback, right_t)
+    merged_own, keep = merge_own(*loaded)
     own = keep + received
-    for axes in ("yx", "xz", "zy"):
-        near, wrap, far = ring(own, axes, 0)
-        own = own + near + wrap + far
+    own = group_sum(own, ("ny", "nx"), ("wx", "wy"))
+    own = group_sum(own, ("nz", "ny"), ("wy", "wz"))
+    own = group_sum(own, ("nx", "nz"), ("wz", "wx"))
     other = sibling(own)
     term = right_term(merged_other, other, right_term(merged_own, own))
     inverse, basis = make_basis(own, other)
     term = term + sibling(term)
-    parts = [term, *ring(term, "yy", 1)]
+    parts = [term, *(move(term, [[kind]] * 2, 1) for kind in ("ny", "wy", "fy"))]
     feedback_out, momentum_out, right_t = finish(
         lax.axis_size("replica"), merged_own, merged_other, basis, inverse, parts, momentum
     )

time: 45.7 us -> 46.8 us (1.024)
  starting transfers between devices: 18.8 us -> 22.1 us
  waiting for transfers between devices: 14.9 us -> 13.6 us
  Pallas kernels: 10.9 us -> 10.1 us
    ppermute x12, starting transfers between devices: 16.4 us -> 19.1 us  [move(): return lax.ppermute(x, ('replica', 'tensor'), move_pairs(moves, swap))]
    ppermute x12, waiting for transfers between devices: 13.6 us -> 12.1 us  [move(): return lax.ppermute(x, ('replica', 'tensor'), move_pairs(moves, swap))]
    pallas_call x2, Pallas kernels: 5.47 us -> 4.62 us  [the longest x1 3.84 us: merge_other(): pl.pallas_call(load_kernel, in_specs=in_hbm(3), out_specs=[whole()] * 5,...]
    ppermute x3, starting transfers between devices: 2.41 us -> 3.04 us  [sibling(): lax.ppermute(x, 'replica', [(i, i ^ 1) for i in range(lax.axis_size('repl...]
  transfers between devices with their start and end apart: 15 -> 15, of which waited for: 11 -> 11; matrix products, arithmetic and copies ran while one was open for 0% -> 0% of each run, Pallas kernels for 11% -> 6%
where the time goes in v5:
time: 46.8 us; the launch traced here: 46.6 us
  starting transfers between devices  22.1 us (47%)
  waiting for transfers between devices  13.6 us (29%)
  Pallas kernels  10.1 us (22%)
  between operations  0.69 us (1%)
    ppermute x12, starting transfers between devices, move(): return lax.ppermute(x, ('replica', 'tensor'), move_pairs(moves, swap))  19.1 us
    ppermute x12, waiting for transfers between devices, move(): return lax.ppermute(x, ('replica', 'tensor'), move_pairs(moves, swap))  12.1 us
    pallas_call x1, Pallas kernels, merge_other(): pl.pallas_call(load_kernel, in_specs=in_hbm(3), out_specs=[whole()] * 5,...  3.84 us
    ppermute x3, starting transfers between devices, sibling(): lax.ppermute(x, 'replica', [(i, i ^ 1) for i in range(lax.axis_size('repl...  3.04 us
    pallas_call x1, Pallas kernels, finish(): pl.pallas_call(body, in_specs=[whole()] * 9, out_specs=in_hbm(3), out_sha...  2.99 us
    pallas_call x1, Pallas kernels, make_basis(): pl.pallas_call(basis_kernel, in_specs=[whole(), whole()], out_specs=[whol...  1.66 us
    ppermute x3, waiting for transfers between devices, sibling(): lax.ppermute(x, 'replica', [(i, i ^ 1) for i in range(lax.axis_size('repl...  1.53 us
  transfers between devices with their start and end apart: 15, of which 11 were waited for; matrix products, arithmetic and copies ran while one was open for 0% of the time, Pallas kernels for 6%

profile of v5, /device:TPU:1, one launch (start us, length us, event | category | flops | bytes accessed | tf_op | source)
XLA Modules:
  0.0 46.6 jit_solution(1879052117202228078)
XLA Ops:
  0.6 3.8 %merge_other.1 = (bf16[3072,384]{1,0:T(8,128)(2,1)S(1)}, f32[8,3072]{1,0:T(8,128)S(1)}, bf16[3072,384]{1,0:T(8,128)(2,1)S(1)}, bf16[3072,384]{1,0:T(8,128)(2,1)S(1)}, f32[8,384]{1,0:T(8,128)S(1)}) custom-call(bf16[1,6144,384]{2,1,0:T(8,128)(2,1)} %g_ref.1, bf16[1,6144,384]{2,1,0:T(8,128)(2,1)} %f_ref.1, f32[8,384]{1,0:T(8,128)} %bitcast.2), custom_call_target="tpu_custom_call" | custom-call | flops 18874368 | bytes 9437184 | tf_op jit(solution)/shard_map/merge_other/pallas_call | solution.py:79
  4.5 1.5 %collective-permute-start = (f32[8,3072]{1,0:T(8,128)S(1)}, f32[8,3072]{1,0:T(8,128)S(1)}, u32[]{:S(2)}, u32[]{:S(2)}) collective-permute-start(f32[8,3072]{1,0:T(8,128)S(1)} %get-tuple-element.21), channel_id=1, source_target_pairs={{0,16},{16,0},{32,48},{48,32},{64,80},{80,64},{96,112},{112,96},{1... | collective-permute-start | bytes 294920 | tf_op jit(solution)/shard_map/ppermute | solution.py:263
  6.0 0.8 %merge_own.1 = (bf16[3072,384]{1,0:T(8,128)(2,1)S(1)}, f32[8,3072]{1,0:T(8,128)S(1)}) custom-call(bf16[3072,384]{1,0:T(8,128)(2,1)S(1)} %get-tuple-element.15.g_ref, bf16[3072,384]{1,0:T(8,128)(2,1)S(1)} %get-tuple-element.16.f_ref, f32[8,384]{1,0:T(8,128)S(1)} %get-tuple-element.17.q_ref), custom_call_target="tpu_custom_call" | custom-call | flops 18874368 | bytes 4718592 | tf_op jit(solution)/shard_map/merge_own/pallas_call | solution.py:98
  6.9 3.8 %collective-permute-start.3 = (f32[8,3072]{1,0:T(8,128)S(1)}, f32[8,3072]{1,0:T(8,128)S(1)}, u32[]{:S(2)}, u32[]{:S(2)}) collective-permute-start(f32[8,3072]{1,0:T(8,128)S(1)} %add.33), channel_id=1, source_target_pairs={{0,35},{1,96},{2,33},{3,98},{4,101},{5,38},{6,103},{7,36},{8,43},{... | collective-permute-start | bytes 294920 | tf_op jit(solution)/shard_map/ppermute | solution.py:252
  10.8 0.5 collective-permute-start.2
  11.5 1.5 %collective-permute-done.3 = f32[8,3072]{1,0:T(8,128)S(1)} collective-permute-done((f32[8,3072]{1,0:T(8,128)S(1)}, f32[8,3072]{1,0:T(8,128)S(1)}, u32[]{:S(2)}, u32[]{:S(2)}) %collective-permute-start.3) | collective-permute-done | bytes 98336 | tf_op jit(solution)/shard_map/ppermute | solution.py:252
  13.1 3.0 %collective-permute-done.2 = f32[8,3072]{1,0:T(8,128)S(1)} collective-permute-done((f32[8,3072]{1,0:T(8,128)S(1)}, f32[8,3072]{1,0:T(8,128)S(1)}, u32[]{:S(2)}, u32[]{:S(2)}) %collective-permute-start.2) | collective-permute-done | bytes 98336 | tf_op jit(solution)/shard_map/ppermute | solution.py:252
  16.1 3.1 %collective-permute-start.6 = (f32[8,3072]{1,0:T(8,128)S(1)}, f32[8,3072]{1,0:T(8,128)S(1)}, u32[]{:S(2)}, u32[]{:S(2)}) collective-permute-start(f32[8,3072]{1,0:T(8,128)S(1)} %add_add_fusion.2), channel_id=1, source_target_pairs={{0,100},{1,45},{2,102},{3,47},{4,40},{5,97},{6,42},{7,99},{8,108},... | collective-permute-start | bytes 294920 | tf_op jit(solution)/shard_map/ppermute | solution.py:252
  19.2 1.3 %collective-permute-start.5 = (f32[8,3072]{1,0:T(8,128)S(1)}, f32[8,3072]{1,0:T(8,128)S(1)}, u32[]{:S(2)}, u32[]{:S(2)}) collective-permute-start(f32[8,3072]{1,0:T(8,128)S(1)} %add_add_fusion.2), channel_id=1, source_target_pairs={{0,112},{1,29},{2,114},{3,31},{4,24},{5,117},{6,26},{7,119},{8,120... | collective-permute-start | bytes 294920 | tf_op jit(solution)/shard_map/ppermute | solution.py:252
  20.5 1.4 %collective-permute-start.4 = (f32[8,3072]{1,0:T(8,128)S(1)}, f32[8,3072]{1,0:T(8,128)S(1)}, u32[]{:S(2)}, u32[]{:S(2)}) collective-permute-start(f32[8,3072]{1,0:T(8,128)S(1)} %add_add_fusion.2), channel_id=1, source_target_pairs={{0,20},{1,49},{2,22},{3,51},{4,52},{5,17},{6,54},{7,19},{8,28},{9,... | collective-permute-start | bytes 294920 | tf_op jit(solution)/shard_map/ppermute | solution.py:252
  22.1 2.7 %collective-permute-done.5 = f32[8,3072]{1,0:T(8,128)S(1)} collective-permute-done((f32[8,3072]{1,0:T(8,128)S(1)}, f32[8,3072]{1,0:T(8,128)S(1)}, u32[]{:S(2)}, u32[]{:S(2)}) %collective-permute-start.5) | collective-permute-done | bytes 98336 | tf_op jit(solution)/shard_map/ppermute | solution.py:252
  25.2 1.4 %collective-permute-start.9 = (f32[8,3072]{1,0:T(8,128)S(1)}, f32[8,3072]{1,0:T(8,128)S(1)}, u32[]{:S(2)}, u32[]{:S(2)}) collective-permute-start(f32[8,3072]{1,0:T(8,128)S(1)} %add_add_fusion.1), channel_id=1, source_target_pairs={{0,13},{1,6},{2,15},{3,4},{4,3},{5,8},{6,1},{7,10},{8,5},{9,14},{1... | collective-permute-start | bytes 294920 | tf_op jit(solution)/shard_map/ppermute | solution.py:252
  26.7 0.4 collective-permute-start.8
  27.1 2.3 %collective-permute-start.7 = (f32[8,3072]{1,0:T(8,128)S(1)}, f32[8,3072]{1,0:T(8,128)S(1)}, u32[]{:S(2)}, u32[]{:S(2)}) collective-permute-start(f32[8,3072]{1,0:T(8,128)S(1)} %add_add_fusion.1), channel_id=1, source_target_pairs={{0,17},{1,21},{2,19},{3,23},{4,16},{5,20},{6,18},{7,22},{8,25},{9,... | collective-permute-start | bytes 294920 | tf_op jit(solution)/shard_map/ppermute | solution.py:252
  29.5 1.7 %collective-permute-done.9 = f32[8,3072]{1,0:T(8,128)S(1)} collective-permute-done((f32[8,3072]{1,0:T(8,128)S(1)}, f32[8,3072]{1,0:T(8,128)S(1)}, u32[]{:S(2)}, u32[]{:S(2)}) %collective-permute-start.9) | collective-permute-done | bytes 98336 | tf_op jit(solution)/shard_map/ppermute | solution.py:252
  31.2 1.0 %collective-permute-done.8 = f32[8,3072]{1,0:T(8,128)S(1)} collective-permute-done((f32[8,3072]{1,0:T(8,128)S(1)}, f32[8,3072]{1,0:T(8,128)S(1)}, u32[]{:S(2)}, u32[]{:S(2)}) %collective-permute-start.8) | collective-permute-done | bytes 98336 | tf_op jit(solution)/shard_map/ppermute | solution.py:252
  32.3 1.1 %collective-permute-start.10 = (f32[8,3072]{1,0:T(8,128)S(1)}, f32[8,3072]{1,0:T(8,128)S(1)}, u32[]{:S(2)}, u32[]{:S(2)}) collective-permute-start(f32[8,3072]{1,0:T(8,128)S(1)} %add_add_fusion.own_ref.left_ref), channel_id=1, source_target_pairs={{0,16},{16,0},{32,48},{48,32},{64,80},{80,64},{96,112},{112,96},{1... | collective-permute-start | bytes 294920 | tf_op jit(solution)/shard_map/ppermute | solution.py:263
  33.8 0.5 %collective-permute-done.10.other_ref.left_ref = f32[8,3072]{1,0:T(8,128)S(1)} collective-permute-done((f32[8,3072]{1,0:T(8,128)S(1)}, f32[8,3072]{1,0:T(8,128)S(1)}, u32[]{:S(2)}, u32[]{:S(2)}) %collective-permute-start.10) | collective-permute-done | bytes 98336 | tf_op jit(solution)/shard_map/ppermute | solution.py:263
  35.2 0.8 %collective-permute-done.11 = f32[8,384]{1,0:T(8,128)S(1)} collective-permute-done((f32[8,384]{1,0:T(8,128)S(1)}, f32[8,384]{1,0:T(8,128)S(1)}, u32[]{:S(2)}, u32[]{:S(2)}) %collective-permute-start.11) | collective-permute-done | bytes 12320 | tf_op jit(solution)/shard_map/ppermute | solution.py:263
  36.0 1.9 %collective-permute-start.14 = (f32[8,384]{1,0:T(8,128)S(1)}, f32[8,384]{1,0:T(8,128)S(1)}, u32[]{:S(2)}, u32[]{:S(2)}) collective-permute-start(f32[8,384]{1,0:T(8,128)S(1)} %add.43.refs_4_), channel_id=1, source_target_pairs={{0,80},{1,81},{2,82},{3,83},{4,84},{5,85},{6,86},{7,87},{8,88},{9,... | collective-permute-start | bytes 36872 | tf_op jit(solution)/shard_map/ppermute | solution.py:252
  37.9 2.6 %collective-permute-start.13 = (f32[8,384]{1,0:T(8,128)S(1)}, f32[8,384]{1,0:T(8,128)S(1)}, u32[]{:S(2)}, u32[]{:S(2)}) collective-permute-start(f32[8,384]{1,0:T(8,128)S(1)} %add.43.refs_4_), channel_id=1, source_target_pairs={{0,112},{1,113},{2,114},{3,115},{4,116},{5,117},{6,118},{7,119},{8... | collective-permute-start | bytes 36872 | tf_op jit(solution)/shard_map/ppermute | solution.py:252
  40.5 1.7 %basis.1 = (f32[8,8]{1,0:T(8,128)S(1)}, bf16[6144,32]{1,0:T(8,128)(2,1)S(1)}) custom-call(f32[8,3072]{1,0:T(8,128)S(1)} %add_add_fusion.own_ref.left_ref, f32[8,3072]{1,0:T(8,128)S(1)} %collective-permute-done.10.other_ref.left_ref), custom_call_target="tpu_custom_call" | custom-call | flops 1572864 | bytes 4194304 | tf_op jit(solution)/shard_map/basis/pallas_call | solution.py:158
  42.2 1.4 %collective-permute-done.12.refs_5_ = f32[8,384]{1,0:T(8,128)S(1)} collective-permute-done((f32[8,384]{1,0:T(8,128)S(1)}, f32[8,384]{1,0:T(8,128)S(1)}, u32[]{:S(2)}, u32[]{:S(2)}) %collective-permute-start.12) | collective-permute-done | bytes 12320 | tf_op jit(solution)/shard_map/ppermute | solution.py:252
  43.7 3.0 %finish.1 = (bf16[1,6144,384]{2,1,0:T(8,128)(2,1)}, bf16[768,384]{1,0:T(8,128)(2,1)}, f32[8,384]{1,0:T(8,128)}) custom-call(bf16[3072,384]{1,0:T(8,128)(2,1)S(1)} %get-tuple-element.18.merged_ref.refs_0_, bf16[3072,384]{1,0:T(8,128)(2,1)S(1)} %get-tuple-element.19.merged_ref.refs_1_, bf16[6144,32]{1,0:T(8,128)(2,1)S(1)} %get-tuple-element.22.refs_2_, ...), custom_call_target="tpu_custom_call" | custom-call | flops 150994944 | bytes 9437184 | tf_op jit(solution)/shard_map/finish/pallas_call | solution.py:214
  (19 shorter events, 2.5 us)
Async XLA Ops:
  4.5 2.4 %collective-permute-start = (f32[8,3072]{1,0:T(8,128)S(1)}, f32[8,3072]{1,0:T(8,128)S(1)}, u32[]{:S(2)}, u32[]{:S(2)}) collective-permute-start(f32[8,3072]{1,0:T(8,128)S(1)} %get-tuple-element.21), channel_id=1, source_target_pairs={{0,16},{16,0},{32,48},{48,32},{64,80},{80,64},{96,112},{112,96},{1... | collective-permute-start | bytes 294920 | tf_op jit(solution)/shard_map/ppermute | solution.py:263
  6.9 6.1 %collective-permute-start.3 = (f32[8,3072]{1,0:T(8,128)S(1)}, f32[8,3072]{1,0:T(8,128)S(1)}, u32[]{:S(2)}, u32[]{:S(2)}) collective-permute-start(f32[8,3072]{1,0:T(8,128)S(1)} %add.33), channel_id=1, source_target_pairs={{0,35},{1,96},{2,33},{3,98},{4,101},{5,38},{6,103},{7,36},{8,43},{... | collective-permute-start | bytes 294920 | tf_op jit(solution)/shard_map/ppermute | solution.py:252
  10.8 5.3 %collective-permute-start.2 = (f32[8,3072]{1,0:T(8,128)S(1)}, f32[8,3072]{1,0:T(8,128)S(1)}, u32[]{:S(2)}, u32[]{:S(2)}) collective-permute-start(f32[8,3072]{1,0:T(8,128)S(1)} %add.33), channel_id=1, source_target_pairs={{0,19},{1,113},{2,17},{3,115},{4,116},{5,22},{6,118},{7,20},{8,27}... | collective-permute-start | bytes 294920 | tf_op jit(solution)/shard_map/ppermute | solution.py:252
  11.2 4.9 %collective-permute-start.1 = (f32[8,3072]{1,0:T(8,128)S(1)}, f32[8,3072]{1,0:T(8,128)S(1)}, u32[]{:S(2)}, u32[]{:S(2)}) collective-permute-start(f32[8,3072]{1,0:T(8,128)S(1)} %add.33), channel_id=1, source_target_pairs={{0,48},{1,16},{2,50},{3,18},{4,21},{5,53},{6,23},{7,55},{8,56},{9,... | collective-permute-start | bytes 294920 | tf_op jit(solution)/shard_map/ppermute | solution.py:252
  16.1 6.0 %collective-permute-start.6 = (f32[8,3072]{1,0:T(8,128)S(1)}, f32[8,3072]{1,0:T(8,128)S(1)}, u32[]{:S(2)}, u32[]{:S(2)}) collective-permute-start(f32[8,3072]{1,0:T(8,128)S(1)} %add_add_fusion.2), channel_id=1, source_target_pairs={{0,100},{1,45},{2,102},{3,47},{4,40},{5,97},{6,42},{7,99},{8,108},... | collective-permute-start | bytes 294920 | tf_op jit(solution)/shard_map/ppermute | solution.py:252
  19.2 5.5 %collective-permute-start.5 = (f32[8,3072]{1,0:T(8,128)S(1)}, f32[8,3072]{1,0:T(8,128)S(1)}, u32[]{:S(2)}, u32[]{:S(2)}) collective-permute-start(f32[8,3072]{1,0:T(8,128)S(1)} %add_add_fusion.2), channel_id=1, source_target_pairs={{0,112},{1,29},{2,114},{3,31},{4,24},{5,117},{6,26},{7,119},{8,120... | collective-permute-start | bytes 294920 | tf_op jit(solution)/shard_map/ppermute | solution.py:252
  20.5 4.7 %collective-permute-start.4 = (f32[8,3072]{1,0:T(8,128)S(1)}, f32[8,3072]{1,0:T(8,128)S(1)}, u32[]{:S(2)}, u32[]{:S(2)}) collective-permute-start(f32[8,3072]{1,0:T(8,128)S(1)} %add_add_fusion.2), channel_id=1, source_target_pairs={{0,20},{1,49},{2,22},{3,51},{4,52},{5,17},{6,54},{7,19},{8,28},{9,... | collective-permute-start | bytes 294920 | tf_op jit(solution)/shard_map/ppermute | solution.py:252
  25.2 6.0 %collective-permute-start.9 = (f32[8,3072]{1,0:T(8,128)S(1)}, f32[8,3072]{1,0:T(8,128)S(1)}, u32[]{:S(2)}, u32[]{:S(2)}) collective-permute-start(f32[8,3072]{1,0:T(8,128)S(1)} %add_add_fusion.1), channel_id=1, source_target_pairs={{0,13},{1,6},{2,15},{3,4},{4,3},{5,8},{6,1},{7,10},{8,5},{9,14},{1... | collective-permute-start | bytes 294920 | tf_op jit(solution)/shard_map/ppermute | solution.py:252
  26.7 5.5 %collective-permute-start.8 = (f32[8,3072]{1,0:T(8,128)S(1)}, f32[8,3072]{1,0:T(8,128)S(1)}, u32[]{:S(2)}, u32[]{:S(2)}) collective-permute-start(f32[8,3072]{1,0:T(8,128)S(1)} %add_add_fusion.1), channel_id=1, source_target_pairs={{0,28},{1,18},{2,30},{3,16},{4,23},{5,25},{6,21},{7,27},{8,20},{9,... | collective-permute-start | bytes 294920 | tf_op jit(solution)/shard_map/ppermute | solution.py:252
  27.1 5.1 %collective-permute-start.7 = (f32[8,3072]{1,0:T(8,128)S(1)}, f32[8,3072]{1,0:T(8,128)S(1)}, u32[]{:S(2)}, u32[]{:S(2)}) collective-permute-start(f32[8,3072]{1,0:T(8,128)S(1)} %add_add_fusion.1), channel_id=1, source_target_pairs={{0,17},{1,21},{2,19},{3,23},{4,16},{5,20},{6,18},{7,22},{8,25},{9,... | collective-permute-start | bytes 294920 | tf_op jit(solution)/shard_map/ppermute | solution.py:252
  32.3 2.0 %collective-permute-start.10 = (f32[8,3072]{1,0:T(8,128)S(1)}, f32[8,3072]{1,0:T(8,128)S(1)}, u32[]{:S(2)}, u32[]{:S(2)}) collective-permute-start(f32[8,3072]{1,0:T(8,128)S(1)} %add_add_fusion.own_ref.left_ref), channel_id=1, source_target_pairs={{0,16},{16,0},{32,48},{48,32},{64,80},{80,64},{96,112},{112,96},{1... | collective-permute-start | bytes 294920 | tf_op jit(solution)/shard_map/ppermute | solution.py:263
  33.4 10.3 %copy-start = (bf16[768,384]{1,0:T(8,128)(2,1)S(1)}, bf16[768,384]{1,0:T(8,128)(2,1)}, u32[]{:S(2)}) copy-start(bf16[768,384]{1,0:T(8,128)(2,1)} %refs_8_.1) | copy-start | bytes 1769476
  34.7 1.3 %collective-permute-start.11 = (f32[8,384]{1,0:T(8,128)S(1)}, f32[8,384]{1,0:T(8,128)S(1)}, u32[]{:S(2)}, u32[]{:S(2)}) collective-permute-start(f32[8,384]{1,0:T(8,128)S(1)} %right_other.1), channel_id=1, source_target_pairs={{0,16},{16,0},{32,48},{48,32},{64,80},{80,64},{96,112},{112,96},{1... | collective-permute-start | bytes 36872 | tf_op jit(solution)/shard_map/ppermute | solution.py:263
  36.0 6.2 %collective-permute-start.14 = (f32[8,384]{1,0:T(8,128)S(1)}, f32[8,384]{1,0:T(8,128)S(1)}, u32[]{:S(2)}, u32[]{:S(2)}) collective-permute-start(f32[8,384]{1,0:T(8,128)S(1)} %add.43.refs_4_), channel_id=1, source_target_pairs={{0,80},{1,81},{2,82},{3,83},{4,84},{5,85},{6,86},{7,87},{8,88},{9,... | collective-permute-start | bytes 36872 | tf_op jit(solution)/shard_map/ppermute | solution.py:252
  37.9 4.3 %collective-permute-start.13 = (f32[8,384]{1,0:T(8,128)S(1)}, f32[8,384]{1,0:T(8,128)S(1)}, u32[]{:S(2)}, u32[]{:S(2)}) collective-permute-start(f32[8,384]{1,0:T(8,128)S(1)} %add.43.refs_4_), channel_id=1, source_target_pairs={{0,112},{1,113},{2,114},{3,115},{4,116},{5,117},{6,118},{7,119},{8... | collective-permute-start | bytes 36872 | tf_op jit(solution)/shard_map/ppermute | solution.py:252
  40.5 3.1 %collective-permute-start.12 = (f32[8,384]{1,0:T(8,128)S(1)}, f32[8,384]{1,0:T(8,128)S(1)}, u32[]{:S(2)}, u32[]{:S(2)}) collective-permute-start(f32[8,384]{1,0:T(8,128)S(1)} %add.43.refs_4_), channel_id=1, source_target_pairs={{0,48},{1,49},{2,50},{3,51},{4,52},{5,53},{6,54},{7,55},{8,56},{9,... | collective-permute-start | bytes 36872 | tf_op jit(solution)/shard_map/ppermute | solution.py:252

commit v6 on v5

--- a/solution.py
+++ b/solution.py
@@ -36,34 +36,44 @@
     term_ref[:, here] = lax.dot_general(right, merged, (((1,), (1,)), ((), ())), preferred_element_type=F32)
 
 
+def load_pair(g_ref, f_ref, half, i, g_to, f_to, g_sem, f_sem):
+    here = pl.ds(i * CHUNK, CHUNK)
+    pair = (
+        pltpu.make_async_copy(g_ref.at[0, rows_of(half, i), :], g_to.at[here, :], g_sem),
+        pltpu.make_async_copy(f_ref.at[0, rows_of(half, i), :], f_to.at[here, :], f_sem),
+    )
+    for copy in pair:
+        copy.start()
+    return pair
+
+
 def load_kernel(g_ref, f_ref, q_ref, merged_ref, term_ref, g_own, f_own, q_own, g_buf, f_buf, g_sem, f_sem, q_sem):
     mine = own_half()
     q_copy = pltpu.make_async_copy(q_ref, q_own, q_sem.at[0])
     q_copy.start()
     copies = []
-    for half, g_to, f_to in ((1 - mine, g_buf, f_buf), (mine, g_own, f_own)):
-        for i in range(CHUNKS):
-            here, n = pl.ds(i * CHUNK, CHUNK), len(copies)
-            pair = (
-                pltpu.make_async_copy(g_ref.at[0, rows_of(half, i), :], g_to.at[here, :], g_sem.at[n]),
-                pltpu.make_async_copy(f_ref.at[0, rows_of(half, i), :], f_to.at[here, :], f_sem.at[n]),
-            )
-            for copy in pair:
-                copy.start()
-            copies.append(pair)
+    for half, g_to, f_to, count in ((1 - mine, g_buf, f_buf, CHUNKS), (mine, g_own, f_own, CHUNKS - 1)):
+        for i in range(count):
+            n = len(copies)
+            copies.append(load_pair(g_ref, f_ref, half, i, g_to, f_to, g_sem.at[n], f_sem.at[n]))
     q_copy.wait()
     right = q_own[...].astype(BF16)
-    for i in range(2 * CHUNKS):
-        for copy in copies[i]:
+    for i, pair in enumerate(copies):
+        for copy in pair:
             copy.wait()
         if i < CHUNKS:
             merge_chunk(g_buf, f_buf, right, merged_ref, term_ref, i)
 
 
-def merge_kernel(g_ref, f_ref, q_ref, merged_ref, term_ref):
+def merge_kernel(g_ref, f_ref, g_own, f_own, q_ref, merged_ref, term_ref, g_buf, f_buf, g_sem, f_sem):
+    last = CHUNKS - 1
+    pair = load_pair(g_ref, f_ref, own_half(), last, g_buf, f_buf, g_sem.at[0], f_sem.at[0])
     right = q_ref[...].astype(BF16)
-    for i in range(CHUNKS):
-        merge_chunk(g_ref, f_ref, right, merged_ref, term_ref, i)
+    for i in range(last):
+        merge_chunk(g_own, f_own, right, merged_ref, term_ref, i)
+    for copy in pair:
+        copy.wait()
+    merge_chunk(g_buf, f_buf, right, merged_ref, term_ref, last)
 
 
 def whole():
@@ -75,17 +85,23 @@
 
 
 def merge_other(gradient, feedback, right_t):
-    half_rows = pltpu.VMEM((HALF, COLS), BF16)
+    half_rows, loaded_rows = pltpu.VMEM((HALF, COLS), BF16), pltpu.VMEM((HALF - CHUNK, COLS), BF16)
     return pl.pallas_call(
         load_kernel,
         in_specs=in_hbm(3),
         out_specs=[whole()] * 5,
-        out_shape=[half_rows, pltpu.VMEM((RANK, HALF), F32), half_rows, half_rows, pltpu.VMEM((RANK, COLS), F32)],
+        out_shape=[
+            half_rows,
+            pltpu.VMEM((RANK, HALF), F32),
+            loaded_rows,
+            loaded_rows,
+            pltpu.VMEM((RANK, COLS), F32),
+        ],
         scratch_shapes=[
             half_rows,
             half_rows,
-            pltpu.SemaphoreType.DMA((2 * CHUNKS,)),
-            pltpu.SemaphoreType.DMA((2 * CHUNKS,)),
+            pltpu.SemaphoreType.DMA((2 * CHUNKS - 1,)),
+            pltpu.SemaphoreType.DMA((2 * CHUNKS - 1,)),
             pltpu.SemaphoreType.DMA((1,)),
         ],
         compiler_params=pltpu.CompilerParams(vmem_limit_bytes=16 * MIB),
@@ -94,16 +110,22 @@
     )(gradient, feedback, right_t)
 
 
-def merge_own(gradient, feedback, right_t):
+def merge_own(gradient, feedback, *loaded):
     return pl.pallas_call(
         merge_kernel,
-        in_specs=[whole()] * 3,
+        in_specs=in_hbm(2) + [whole()] * 3,
         out_specs=[whole(), whole()],
         out_shape=[pltpu.VMEM((HALF, COLS), BF16), pltpu.VMEM((RANK, HALF), F32)],
+        scratch_shapes=[
+            pltpu.VMEM((HALF, COLS), BF16),
+            pltpu.VMEM((HALF, COLS), BF16),
+            pltpu.SemaphoreType.DMA((1,)),
+            pltpu.SemaphoreType.DMA((1,)),
+        ],
         compiler_params=pltpu.CompilerParams(vmem_limit_bytes=16 * MIB),
         cost_estimate=pl.CostEstimate(flops=HALF * COLS * RANK * 2, bytes_accessed=4 * HALF * COLS, transcendentals=0),
         name="merge_own",
-    )(gradient, feedback, right_t)
+    )(gradient, feedback, *loaded)
 
 
 def right_kernel(merged_ref, left_ref, *refs):
@@ -252,11 +274,10 @@
     return lax.ppermute(x, ("replica", "tensor"), move_pairs(moves, swap))
 
 
-def group_sum(x, first, second):
-    both = [[a, b] for a, b in zip(first, second)]
-    near = move(x, [[a] for a in first], 1)
-    wrap = move(x, [[b] for b in second], 1)
-    return x + near + wrap + move(x, both, 0)
+def ring_sum(x, axes):
+    near = move(x, [["n" + a] for a in axes], 1)
+    wrap = move(x, [["w" + a] for a in axes], 1)
+    return x + near + wrap + move(x, [["f" + a] for a in axes], 0)
 
 
 def sibling(x):
@@ -270,11 +291,10 @@
     momentum = pltpu.with_memory_space_constraint(momentum, pltpu.VMEM)
     merged_other, send, *loaded = merge_other(gradient, feedback, right_t)
     received = sibling(send)
-    merged_own, keep = merge_own(*loaded)
+    merged_own, keep = merge_own(gradient, feedback, *loaded)
     own = keep + received
-    own = group_sum(own, ("ny", "nx"), ("wx", "wy"))
-    own = group_sum(own, ("nz", "ny"), ("wy", "wz"))
-    own = group_sum(own, ("nx", "nz"), ("wz", "wx"))
+    for axes in ("yx", "xz", "zy"):
+        own = ring_sum(own, axes)
     other = sibling(own)
     term = right_term(merged_other, other, right_term(merged_own, own))
     inverse, basis = make_basis(own, other)

time: 46.8 us -> 45.8 us (0.979)
  starting transfers between devices: 22.1 us -> 19 us
  waiting for transfers between devices: 13.6 us -> 14.8 us
  Pallas kernels: 10.1 us -> 11.1 us
    ppermute x12, starting transfers between devices: 19.1 us -> 16.6 us  [move(): return lax.ppermute(x, ('replica', 'tensor'), move_pairs(moves, swap))]
    pallas_call x1, Pallas kernels: 0.78 us -> 2.16 us  [merge_own(): pl.pallas_call(merge_kernel, in_specs=in_hbm(2) + [whole()] * 3, out_spec...]
    ppermute x12, waiting for transfers between devices: 12.1 us -> 13.4 us  [move(): return lax.ppermute(x, ('replica', 'tensor'), move_pairs(moves, swap))]
    ppermute x3, starting transfers between devices: 3.04 us -> 2.32 us  [sibling(): lax.ppermute(x, 'replica', [(i, i ^ 1) for i in range(lax.axis_size('repl...]
  transfers between devices with their start and end apart: 15 -> 15, of which waited for: 11 -> 11; matrix products, arithmetic and copies ran while one was open for 0% -> 0% of each run, Pallas kernels for 6% -> 9%
where the time goes in v6:
time: 45.8 us; the launch traced here: 45.6 us
  starting transfers between devices  19 us (41%)
  waiting for transfers between devices  14.8 us (32%)
  Pallas kernels  11.1 us (24%)
  between operations  0.71 us (2%)
    ppermute x12, starting transfers between devices, move(): return lax.ppermute(x, ('replica', 'tensor'), move_pairs(moves, swap))  16.6 us
    ppermute x12, waiting for transfers between devices, move(): return lax.ppermute(x, ('replica', 'tensor'), move_pairs(moves, swap))  13.4 us
    pallas_call x1, Pallas kernels, merge_other(): pl.pallas_call(load_kernel, in_specs=in_hbm(3), out_specs=[whole()] * 5,...  3.47 us
    pallas_call x1, Pallas kernels, finish(): pl.pallas_call(body, in_specs=[whole()] * 9, out_specs=in_hbm(3), out_sha...  2.98 us
    ppermute x3, starting transfers between devices, sibling(): lax.ppermute(x, 'replica', [(i, i ^ 1) for i in range(lax.axis_size('repl...  2.32 us
    pallas_call x1, Pallas kernels, merge_own(): pl.pallas_call(merge_kernel, in_specs=in_hbm(2) + [whole()] * 3, out_spec...  2.16 us
    pallas_call x1, Pallas kernels, make_basis(): pl.pallas_call(basis_kernel, in_specs=[whole(), whole()], out_specs=[whol...  1.66 us
    ppermute x3, waiting for transfers between devices, sibling(): lax.ppermute(x, 'replica', [(i, i ^ 1) for i in range(lax.axis_size('repl...  1.37 us
  transfers between devices with their start and end apart: 15, of which 11 were waited for; matrix products, arithmetic and copies ran while one was open for 0% of the time, Pallas kernels for 9%

profile of v6, /device:TPU:1, one launch (start us, length us, event | category | flops | bytes accessed | tf_op | source)
XLA Modules:
  0.0 45.6 jit_solution(14708372458460159236)
XLA Ops:
  0.6 3.5 %merge_other.1 = (bf16[3072,384]{1,0:T(8,128)(2,1)S(1)}, f32[8,3072]{1,0:T(8,128)S(1)}, bf16[2048,384]{1,0:T(8,128)(2,1)S(1)}, bf16[2048,384]{1,0:T(8,128)(2,1)S(1)}, f32[8,384]{1,0:T(8,128)S(1)}) custom-call(bf16[1,6144,384]{2,1,0:T(8,128)(2,1)} %g_ref.3, bf16[1,6144,384]{2,1,0:T(8,128)(2,1)} %f_ref.3, f32[8,384]{1,0:T(8,128)} %bitcast.2), custom_call_target="tpu_custom_call" | custom-call | flops 18874368 | bytes 9437184 | tf_op jit(solution)/shard_map/merge_other/pallas_call | solution.py:89
  4.1 1.4 %collective-permute-start = (f32[8,3072]{1,0:T(8,128)S(1)}, f32[8,3072]{1,0:T(8,128)S(1)}, u32[]{:S(2)}, u32[]{:S(2)}) collective-permute-start(f32[8,3072]{1,0:T(8,128)S(1)} %get-tuple-element.21), channel_id=1, source_target_pairs={{0,16},{16,0},{32,48},{48,32},{64,80},{80,64},{96,112},{112,96},{1... | collective-permute-start | bytes 294920 | tf_op jit(solution)/shard_map/ppermute | solution.py:284
  5.5 2.2 %merge_own.1 = (bf16[3072,384]{1,0:T(8,128)(2,1)S(1)}, f32[8,3072]{1,0:T(8,128)S(1)}) custom-call(bf16[1,6144,384]{2,1,0:T(8,128)(2,1)} %g_ref.3, bf16[1,6144,384]{2,1,0:T(8,128)(2,1)} %f_ref.3, bf16[2048,384]{1,0:T(8,128)(2,1)S(1)} %get-tuple-element.15.g_own, bf16[2048,384]{1,0:T(8,128)(2,1)S(1)} %get-tuple-element.16.f_own, ...), custom_call_target="tpu_custom_call" | custom-call | flops 18874368 | bytes 4718592 | tf_op jit(solution)/shard_map/merge_own/pallas_call | solution.py:114
  7.7 2.9 %collective-permute-start.3 = (f32[8,3072]{1,0:T(8,128)S(1)}, f32[8,3072]{1,0:T(8,128)S(1)}, u32[]{:S(2)}, u32[]{:S(2)}) collective-permute-start(f32[8,3072]{1,0:T(8,128)S(1)} %add.33), channel_id=1, source_target_pairs={{0,64},{1,3},{2,66},{3,1},{4,6},{5,69},{6,4},{7,71},{8,72},{9,11},... | collective-permute-start | bytes 294920 | tf_op jit(solution)/shard_map/ppermute | solution.py:274
  10.6 1.1 %collective-permute-start.2 = (f32[8,3072]{1,0:T(8,128)S(1)}, f32[8,3072]{1,0:T(8,128)S(1)}, u32[]{:S(2)}, u32[]{:S(2)}) collective-permute-start(f32[8,3072]{1,0:T(8,128)S(1)} %add.33), channel_id=1, source_target_pairs={{0,112},{1,18},{2,114},{3,16},{4,23},{5,117},{6,21},{7,119},{8,120... | collective-permute-start | bytes 294920 | tf_op jit(solution)/shard_map/ppermute | solution.py:274
  11.8 1.3 %collective-permute-done.3 = f32[8,3072]{1,0:T(8,128)S(1)} collective-permute-done((f32[8,3072]{1,0:T(8,128)S(1)}, f32[8,3072]{1,0:T(8,128)S(1)}, u32[]{:S(2)}, u32[]{:S(2)}) %collective-permute-start.3) | collective-permute-done | bytes 98336 | tf_op jit(solution)/shard_map/ppermute | solution.py:274
  13.1 2.9 %collective-permute-done.2 = f32[8,3072]{1,0:T(8,128)S(1)} collective-permute-done((f32[8,3072]{1,0:T(8,128)S(1)}, f32[8,3072]{1,0:T(8,128)S(1)}, u32[]{:S(2)}, u32[]{:S(2)}) %collective-permute-start.2) | collective-permute-done | bytes 98336 | tf_op jit(solution)/shard_map/ppermute | solution.py:274
  16.0 3.7 %collective-permute-start.6 = (f32[8,3072]{1,0:T(8,128)S(1)}, f32[8,3072]{1,0:T(8,128)S(1)}, u32[]{:S(2)}, u32[]{:S(2)}) collective-permute-start(f32[8,3072]{1,0:T(8,128)S(1)} %add_add_fusion.2), channel_id=1, source_target_pairs={{0,2},{1,9},{2,0},{3,11},{4,12},{5,7},{6,14},{7,5},{8,10},{9,1},{1... | collective-permute-start | bytes 294920 | tf_op jit(solution)/shard_map/ppermute | solution.py:274
  19.7 0.9 %collective-permute-start.5 = (f32[8,3072]{1,0:T(8,128)S(1)}, f32[8,3072]{1,0:T(8,128)S(1)}, u32[]{:S(2)}, u32[]{:S(2)}) collective-permute-start(f32[8,3072]{1,0:T(8,128)S(1)} %add_add_fusion.2), channel_id=1, source_target_pairs={{0,19},{1,29},{2,17},{3,31},{4,24},{5,22},{6,26},{7,20},{8,27},{9,... | collective-permute-start | bytes 294920 | tf_op jit(solution)/shard_map/ppermute | solution.py:274
  20.9 1.1 %collective-permute-done.6 = f32[8,3072]{1,0:T(8,128)S(1)} collective-permute-done((f32[8,3072]{1,0:T(8,128)S(1)}, f32[8,3072]{1,0:T(8,128)S(1)}, u32[]{:S(2)}, u32[]{:S(2)}) %collective-permute-start.6) | collective-permute-done | bytes 98336 | tf_op jit(solution)/shard_map/ppermute | solution.py:274
  22.0 3.0 %collective-permute-done.5 = f32[8,3072]{1,0:T(8,128)S(1)} collective-permute-done((f32[8,3072]{1,0:T(8,128)S(1)}, f32[8,3072]{1,0:T(8,128)S(1)}, u32[]{:S(2)}, u32[]{:S(2)}) %collective-permute-start.5) | collective-permute-done | bytes 98336 | tf_op jit(solution)/shard_map/ppermute | solution.py:274
  24.9 2.9 %collective-permute-start.9 = (f32[8,3072]{1,0:T(8,128)S(1)}, f32[8,3072]{1,0:T(8,128)S(1)}, u32[]{:S(2)}, u32[]{:S(2)}) collective-permute-start(f32[8,3072]{1,0:T(8,128)S(1)} %add_add_fusion.1), channel_id=1, source_target_pairs={{0,8},{1,65},{2,10},{3,67},{4,68},{5,13},{6,70},{7,15},{8,0},{9,73... | collective-permute-start | bytes 294920 | tf_op jit(solution)/shard_map/ppermute | solution.py:274
  27.9 1.6 %collective-permute-start.8 = (f32[8,3072]{1,0:T(8,128)S(1)}, f32[8,3072]{1,0:T(8,128)S(1)}, u32[]{:S(2)}, u32[]{:S(2)}) collective-permute-start(f32[8,3072]{1,0:T(8,128)S(1)} %add_add_fusion.1), channel_id=1, source_target_pairs={{0,28},{1,113},{2,30},{3,115},{4,116},{5,25},{6,118},{7,27},{8,20}... | collective-permute-start | bytes 294920 | tf_op jit(solution)/shard_map/ppermute | solution.py:274
  29.5 0.8 %collective-permute-done.9 = f32[8,3072]{1,0:T(8,128)S(1)} collective-permute-done((f32[8,3072]{1,0:T(8,128)S(1)}, f32[8,3072]{1,0:T(8,128)S(1)}, u32[]{:S(2)}, u32[]{:S(2)}) %collective-permute-start.9) | collective-permute-done | bytes 98336 | tf_op jit(solution)/shard_map/ppermute | solution.py:274
  30.3 3.1 %collective-permute-done.8 = f32[8,3072]{1,0:T(8,128)S(1)} collective-permute-done((f32[8,3072]{1,0:T(8,128)S(1)}, f32[8,3072]{1,0:T(8,128)S(1)}, u32[]{:S(2)}, u32[]{:S(2)}) %collective-permute-start.8) | collective-permute-done | bytes 98336 | tf_op jit(solution)/shard_map/ppermute | solution.py:274
  33.6 0.5 %collective-permute-start.10 = (f32[8,3072]{1,0:T(8,128)S(1)}, f32[8,3072]{1,0:T(8,128)S(1)}, u32[]{:S(2)}, u32[]{:S(2)}) collective-permute-start(f32[8,3072]{1,0:T(8,128)S(1)} %add_add_fusion.own_ref.left_ref), channel_id=1, source_target_pairs={{0,16},{16,0},{32,48},{48,32},{64,80},{80,64},{96,112},{112,96},{1... | collective-permute-start | bytes 294920 | tf_op jit(solution)/shard_map/ppermute | solution.py:284
  34.5 0.5 %collective-permute-done.10.other_ref.left_ref = f32[8,3072]{1,0:T(8,128)S(1)} collective-permute-done((f32[8,3072]{1,0:T(8,128)S(1)}, f32[8,3072]{1,0:T(8,128)S(1)}, u32[]{:S(2)}, u32[]{:S(2)}) %collective-permute-start.10) | collective-permute-done | bytes 98336 | tf_op jit(solution)/shard_map/ppermute | solution.py:284
  35.4 0.4 collective-permute-start.11
  35.9 0.8 %collective-permute-done.11 = f32[8,384]{1,0:T(8,128)S(1)} collective-permute-done((f32[8,384]{1,0:T(8,128)S(1)}, f32[8,384]{1,0:T(8,128)S(1)}, u32[]{:S(2)}, u32[]{:S(2)}) %collective-permute-start.11) | collective-permute-done | bytes 12320 | tf_op jit(solution)/shard_map/ppermute | solution.py:284
  36.7 1.4 %collective-permute-start.14 = (f32[8,384]{1,0:T(8,128)S(1)}, f32[8,384]{1,0:T(8,128)S(1)}, u32[]{:S(2)}, u32[]{:S(2)}) collective-permute-start(f32[8,384]{1,0:T(8,128)S(1)} %add.43.refs_4_), channel_id=1, source_target_pairs={{0,80},{1,81},{2,82},{3,83},{4,84},{5,85},{6,86},{7,87},{8,88},{9,... | collective-permute-start | bytes 36872 | tf_op jit(solution)/shard_map/ppermute | solution.py:274
  38.1 1.4 %collective-permute-start.13 = (f32[8,384]{1,0:T(8,128)S(1)}, f32[8,384]{1,0:T(8,128)S(1)}, u32[]{:S(2)}, u32[]{:S(2)}) collective-permute-start(f32[8,384]{1,0:T(8,128)S(1)} %add.43.refs_4_), channel_id=1, source_target_pairs={{0,112},{1,113},{2,114},{3,115},{4,116},{5,117},{6,118},{7,119},{8... | collective-permute-start | bytes 36872 | tf_op jit(solution)/shard_map/ppermute | solution.py:274
  39.9 1.7 %basis.1 = (f32[8,8]{1,0:T(8,128)S(1)}, bf16[6144,32]{1,0:T(8,128)(2,1)S(1)}) custom-call(f32[8,3072]{1,0:T(8,128)S(1)} %add_add_fusion.own_ref.left_ref, f32[8,3072]{1,0:T(8,128)S(1)} %collective-permute-done.10.other_ref.left_ref), custom_call_target="tpu_custom_call" | custom-call | flops 1572864 | bytes 4194304 | tf_op jit(solution)/shard_map/basis/pallas_call | solution.py:180
  41.6 0.9 %collective-permute-done.13.refs_6_ = f32[8,384]{1,0:T(8,128)S(1)} collective-permute-done((f32[8,384]{1,0:T(8,128)S(1)}, f32[8,384]{1,0:T(8,128)S(1)}, u32[]{:S(2)}, u32[]{:S(2)}) %collective-permute-start.13) | collective-permute-done | bytes 12320 | tf_op jit(solution)/shard_map/ppermute | solution.py:274
  42.6 3.0 %finish.1 = (bf16[1,6144,384]{2,1,0:T(8,128)(2,1)}, bf16[768,384]{1,0:T(8,128)(2,1)}, f32[8,384]{1,0:T(8,128)}) custom-call(bf16[3072,384]{1,0:T(8,128)(2,1)S(1)} %get-tuple-element.18.merged_ref.refs_0_, bf16[3072,384]{1,0:T(8,128)(2,1)S(1)} %get-tuple-element.19.merged_ref.refs_1_, bf16[6144,32]{1,0:T(8,128)(2,1)S(1)} %get-tuple-element.22.refs_2_, ...), custom_call_target="tpu_custom_call" | custom-call | flops 150994944 | bytes 9437184 | tf_op jit(solution)/shard_map/finish/pallas_call | solution.py:236
  (19 shorter events, 1.9 us)
Async XLA Ops:
  4.1 3.6 %collective-permute-start = (f32[8,3072]{1,0:T(8,128)S(1)}, f32[8,3072]{1,0:T(8,128)S(1)}, u32[]{:S(2)}, u32[]{:S(2)}) collective-permute-start(f32[8,3072]{1,0:T(8,128)S(1)} %get-tuple-element.21), channel_id=1, source_target_pairs={{0,16},{16,0},{32,48},{48,32},{64,80},{80,64},{96,112},{112,96},{1... | collective-permute-start | bytes 294920 | tf_op jit(solution)/shard_map/ppermute | solution.py:284
  7.7 5.3 %collective-permute-start.3 = (f32[8,3072]{1,0:T(8,128)S(1)}, f32[8,3072]{1,0:T(8,128)S(1)}, u32[]{:S(2)}, u32[]{:S(2)}) collective-permute-start(f32[8,3072]{1,0:T(8,128)S(1)} %add.33), channel_id=1, source_target_pairs={{0,64},{1,3},{2,66},{3,1},{4,6},{5,69},{6,4},{7,71},{8,72},{9,11},... | collective-permute-start | bytes 294920 | tf_op jit(solution)/shard_map/ppermute | solution.py:274
  10.6 5.3 %collective-permute-start.2 = (f32[8,3072]{1,0:T(8,128)S(1)}, f32[8,3072]{1,0:T(8,128)S(1)}, u32[]{:S(2)}, u32[]{:S(2)}) collective-permute-start(f32[8,3072]{1,0:T(8,128)S(1)} %add.33), channel_id=1, source_target_pairs={{0,112},{1,18},{2,114},{3,16},{4,23},{5,117},{6,21},{7,119},{8,120... | collective-permute-start | bytes 294920 | tf_op jit(solution)/shard_map/ppermute | solution.py:274
  11.8 4.2 %collective-permute-start.1 = (f32[8,3072]{1,0:T(8,128)S(1)}, f32[8,3072]{1,0:T(8,128)S(1)}, u32[]{:S(2)}, u32[]{:S(2)}) collective-permute-start(f32[8,3072]{1,0:T(8,128)S(1)} %add.33), channel_id=1, source_target_pairs={{0,48},{1,16},{2,50},{3,18},{4,21},{5,53},{6,23},{7,55},{8,56},{9,... | collective-permute-start | bytes 294920 | tf_op jit(solution)/shard_map/ppermute | solution.py:274
  16.0 6.0 %collective-permute-start.6 = (f32[8,3072]{1,0:T(8,128)S(1)}, f32[8,3072]{1,0:T(8,128)S(1)}, u32[]{:S(2)}, u32[]{:S(2)}) collective-permute-start(f32[8,3072]{1,0:T(8,128)S(1)} %add_add_fusion.2), channel_id=1, source_target_pairs={{0,2},{1,9},{2,0},{3,11},{4,12},{5,7},{6,14},{7,5},{8,10},{9,1},{1... | collective-permute-start | bytes 294920 | tf_op jit(solution)/shard_map/ppermute | solution.py:274
  19.7 5.3 %collective-permute-start.5 = (f32[8,3072]{1,0:T(8,128)S(1)}, f32[8,3072]{1,0:T(8,128)S(1)}, u32[]{:S(2)}, u32[]{:S(2)}) collective-permute-start(f32[8,3072]{1,0:T(8,128)S(1)} %add_add_fusion.2), channel_id=1, source_target_pairs={{0,19},{1,29},{2,17},{3,31},{4,24},{5,22},{6,26},{7,20},{8,27},{9,... | collective-permute-start | bytes 294920 | tf_op jit(solution)/shard_map/ppermute | solution.py:274
  20.6 4.3 %collective-permute-start.4 = (f32[8,3072]{1,0:T(8,128)S(1)}, f32[8,3072]{1,0:T(8,128)S(1)}, u32[]{:S(2)}, u32[]{:S(2)}) collective-permute-start(f32[8,3072]{1,0:T(8,128)S(1)} %add_add_fusion.2), channel_id=1, source_target_pairs={{0,17},{1,21},{2,19},{3,23},{4,16},{5,20},{6,18},{7,22},{8,25},{9,... | collective-permute-start | bytes 294920 | tf_op jit(solution)/shard_map/ppermute | solution.py:274
  24.9 5.3 %collective-permute-start.9 = (f32[8,3072]{1,0:T(8,128)S(1)}, f32[8,3072]{1,0:T(8,128)S(1)}, u32[]{:S(2)}, u32[]{:S(2)}) collective-permute-start(f32[8,3072]{1,0:T(8,128)S(1)} %add_add_fusion.1), channel_id=1, source_target_pairs={{0,8},{1,65},{2,10},{3,67},{4,68},{5,13},{6,70},{7,15},{8,0},{9,73... | collective-permute-start | bytes 294920 | tf_op jit(solution)/shard_map/ppermute | solution.py:274
  27.9 5.5 %collective-permute-start.8 = (f32[8,3072]{1,0:T(8,128)S(1)}, f32[8,3072]{1,0:T(8,128)S(1)}, u32[]{:S(2)}, u32[]{:S(2)}) collective-permute-start(f32[8,3072]{1,0:T(8,128)S(1)} %add_add_fusion.1), channel_id=1, source_target_pairs={{0,28},{1,113},{2,30},{3,115},{4,116},{5,25},{6,118},{7,27},{8,20}... | collective-permute-start | bytes 294920 | tf_op jit(solution)/shard_map/ppermute | solution.py:274
  29.5 4.1 %collective-permute-start.7 = (f32[8,3072]{1,0:T(8,128)S(1)}, f32[8,3072]{1,0:T(8,128)S(1)}, u32[]{:S(2)}, u32[]{:S(2)}) collective-permute-start(f32[8,3072]{1,0:T(8,128)S(1)} %add_add_fusion.1), channel_id=1, source_target_pairs={{0,20},{1,49},{2,22},{3,51},{4,52},{5,17},{6,54},{7,19},{8,28},{9,... | collective-permute-start | bytes 294920 | tf_op jit(solution)/shard_map/ppermute | solution.py:274
  33.6 1.4 %collective-permute-start.10 = (f32[8,3072]{1,0:T(8,128)S(1)}, f32[8,3072]{1,0:T(8,128)S(1)}, u32[]{:S(2)}, u32[]{:S(2)}) collective-permute-start(f32[8,3072]{1,0:T(8,128)S(1)} %add_add_fusion.own_ref.left_ref), channel_id=1, source_target_pairs={{0,16},{16,0},{32,48},{48,32},{64,80},{80,64},{96,112},{112,96},{1... | collective-permute-start | bytes 294920 | tf_op jit(solution)/shard_map/ppermute | solution.py:284
  34.1 8.6 %copy-start = (bf16[768,384]{1,0:T(8,128)(2,1)S(1)}, bf16[768,384]{1,0:T(8,128)(2,1)}, u32[]{:S(2)}) copy-start(bf16[768,384]{1,0:T(8,128)(2,1)} %refs_8_.1) | copy-start | bytes 1769476
  35.4 1.3 %collective-permute-start.11 = (f32[8,384]{1,0:T(8,128)S(1)}, f32[8,384]{1,0:T(8,128)S(1)}, u32[]{:S(2)}, u32[]{:S(2)}) collective-permute-start(f32[8,384]{1,0:T(8,128)S(1)} %right_other.1), channel_id=1, source_target_pairs={{0,16},{16,0},{32,48},{48,32},{64,80},{80,64},{96,112},{112,96},{1... | collective-permute-start | bytes 36872 | tf_op jit(solution)/shard_map/ppermute | solution.py:284
  36.7 4.8 %collective-permute-start.14 = (f32[8,384]{1,0:T(8,128)S(1)}, f32[8,384]{1,0:T(8,128)S(1)}, u32[]{:S(2)}, u32[]{:S(2)}) collective-permute-start(f32[8,384]{1,0:T(8,128)S(1)} %add.43.refs_4_), channel_id=1, source_target_pairs={{0,80},{1,81},{2,82},{3,83},{4,84},{5,85},{6,86},{7,87},{8,88},{9,... | collective-permute-start | bytes 36872 | tf_op jit(solution)/shard_map/ppermute | solution.py:274
  38.1 4.3 %collective-permute-start.13 = (f32[8,384]{1,0:T(8,128)S(1)}, f32[8,384]{1,0:T(8,128)S(1)}, u32[]{:S(2)}, u32[]{:S(2)}) collective-permute-start(f32[8,384]{1,0:T(8,128)S(1)} %add.43.refs_4_), channel_id=1, source_target_pairs={{0,112},{1,113},{2,114},{3,115},{4,116},{5,117},{6,118},{7,119},{8... | collective-permute-start | bytes 36872 | tf_op jit(solution)/shard_map/ppermute | solution.py:274
  39.5 3.1 %collective-permute-start.12 = (f32[8,384]{1,0:T(8,128)S(1)}, f32[8,384]{1,0:T(8,128)S(1)}, u32[]{:S(2)}, u32[]{:S(2)}) collective-permute-start(f32[8,384]{1,0:T(8,128)S(1)} %add.43.refs_4_), channel_id=1, source_target_pairs={{0,48},{1,49},{2,50},{3,51},{4,52},{5,53},{6,54},{7,55},{8,56},{9,... | collective-permute-start | bytes 36872 | tf_op jit(solution)/shard_map/ppermute | solution.py:274

commit v7 on v6

--- a/solution.py
+++ b/solution.py
@@ -12,6 +12,7 @@
 HALF = ROWS // 2
 CHUNKS = 3
 CHUNK = HALF // CHUNKS
+WRITES = ((0, 256), (256, 768), *((i * CHUNK, CHUNK) for i in range(1, 2 * CHUNKS)))
 MIB = 1 << 20
 
 
@@ -20,9 +21,12 @@
     return lax.rem(replica + replica // 2 + tensor + tensor // 4, 2)
 
 
-def split(x):
-    high = x.astype(BF16)
-    return high, (x - high.astype(F32)).astype(BF16)
+def split(x, count):
+    terms = []
+    for _ in range(count):
+        terms.append(x.astype(BF16))
+        x = x - terms[-1].astype(F32)
+    return terms
 
 
 def rows_of(half, chunk):
@@ -52,8 +56,8 @@
     q_copy = pltpu.make_async_copy(q_ref, q_own, q_sem.at[0])
     q_copy.start()
     copies = []
-    for half, g_to, f_to, count in ((1 - mine, g_buf, f_buf, CHUNKS), (mine, g_own, f_own, CHUNKS - 1)):
-        for i in range(count):
+    for half, g_to, f_to in ((1 - mine, g_buf, f_buf), (mine, g_own, f_own)):
+        for i in range(CHUNKS):
             n = len(copies)
             copies.append(load_pair(g_ref, f_ref, half, i, g_to, f_to, g_sem.at[n], f_sem.at[n]))
     q_copy.wait()
@@ -65,15 +69,10 @@
             merge_chunk(g_buf, f_buf, right, merged_ref, term_ref, i)
 
 
-def merge_kernel(g_ref, f_ref, g_own, f_own, q_ref, merged_ref, term_ref, g_buf, f_buf, g_sem, f_sem):
-    last = CHUNKS - 1
-    pair = load_pair(g_ref, f_ref, own_half(), last, g_buf, f_buf, g_sem.at[0], f_sem.at[0])
+def merge_kernel(g_ref, f_ref, q_ref, merged_ref, term_ref):
     right = q_ref[...].astype(BF16)
-    for i in range(last):
-        merge_chunk(g_own, f_own, right, merged_ref, term_ref, i)
-    for copy in pair:
-        copy.wait()
-    merge_chunk(g_buf, f_buf, right, merged_ref, term_ref, last)
+    for i in range(CHUNKS):
+        merge_chunk(g_ref, f_ref, right, merged_ref, term_ref, i)
 
 
 def whole():
@@ -85,7 +84,7 @@
 
 
 def merge_other(gradient, feedback, right_t):
-    half_rows, loaded_rows = pltpu.VMEM((HALF, COLS), BF16), pltpu.VMEM((HALF - CHUNK, COLS), BF16)
+    half_rows = pltpu.VMEM((HALF, COLS), BF16)
     return pl.pallas_call(
         load_kernel,
         in_specs=in_hbm(3),
@@ -93,15 +92,15 @@
         out_shape=[
             half_rows,
             pltpu.VMEM((RANK, HALF), F32),
-            loaded_rows,
-            loaded_rows,
+            half_rows,
+            half_rows,
             pltpu.VMEM((RANK, COLS), F32),
         ],
         scratch_shapes=[
             half_rows,
             half_rows,
-            pltpu.SemaphoreType.DMA((2 * CHUNKS - 1,)),
-            pltpu.SemaphoreType.DMA((2 * CHUNKS - 1,)),
+            pltpu.SemaphoreType.DMA((2 * CHUNKS,)),
+            pltpu.SemaphoreType.DMA((2 * CHUNKS,)),
             pltpu.SemaphoreType.DMA((1,)),
         ],
         compiler_params=pltpu.CompilerParams(vmem_limit_bytes=16 * MIB),
@@ -110,28 +109,22 @@
     )(gradient, feedback, right_t)
 
 
-def merge_own(gradient, feedback, *loaded):
+def merge_own(gradient, feedback, right_t):
     return pl.pallas_call(
         merge_kernel,
-        in_specs=in_hbm(2) + [whole()] * 3,
+        in_specs=[whole()] * 3,
         out_specs=[whole(), whole()],
         out_shape=[pltpu.VMEM((HALF, COLS), BF16), pltpu.VMEM((RANK, HALF), F32)],
-        scratch_shapes=[
-            pltpu.VMEM((HALF, COLS), BF16),
-            pltpu.VMEM((HALF, COLS), BF16),
-            pltpu.SemaphoreType.DMA((1,)),
-            pltpu.SemaphoreType.DMA((1,)),
-        ],
         compiler_params=pltpu.CompilerParams(vmem_limit_bytes=16 * MIB),
         cost_estimate=pl.CostEstimate(flops=HALF * COLS * RANK * 2, bytes_accessed=4 * HALF * COLS, transcendentals=0),
         name="merge_own",
-    )(gradient, feedback, *loaded)
+    )(gradient, feedback, right_t)
 
 
 def right_kernel(merged_ref, left_ref, *refs):
-    pair = jnp.concatenate(split(left_ref[...]), axis=0)
-    total = jnp.dot(pair, merged_ref[...], preferred_element_type=F32)
-    total = total[:RANK] + total[RANK:]
+    terms = jnp.concatenate(split(left_ref[...], 3), axis=0)
+    total = jnp.dot(terms, merged_ref[...], preferred_element_type=F32)
+    total = total[2 * RANK :] + total[RANK : 2 * RANK] + total[:RANK]
     for ref in refs[:-1]:
         total += ref[...]
     refs[-1][...] = total
@@ -171,7 +164,7 @@
         basis = jnp.zeros((RANK, HALF), F32)
         for k in range(RANK):
             basis += inverse[:, k : k + 1] * part[k : k + 1, :]
-        high, low = split(basis)
+        high, low = split(basis, 2)
         packed = jnp.concatenate([high, high, low, low], axis=0)
         basis_ref[start : start + HALF, :] = packed.T
 
@@ -202,19 +195,19 @@
     right_buf[...] = right
     copies = [pltpu.make_async_copy(right_buf, right_ref, right_sem.at[0])]
     copies[0].start()
-    high, low = split(right)
+    high, low = split(right, 2)
     pack = jnp.concatenate([high, low, high, low], axis=0)
     mine = own_half()
-    for i in range(2 * CHUNKS):
-        rows = pl.ds(i * CHUNK, CHUNK)
-        merged_ref, half = (own_ref, mine) if i < CHUNKS else (other_ref, 1 - mine)
-        merged = merged_ref[pl.ds(i % CHUNKS * CHUNK, CHUNK), :]
+    for i, (start, count) in enumerate(WRITES):
+        rows = pl.ds(start, count)
+        merged_ref, half, low_row = (own_ref, mine, start) if start < HALF else (other_ref, 1 - mine, start - HALF)
+        merged = merged_ref[pl.ds(low_row, count), :]
         approx = jnp.dot(basis_ref[rows, :], pack, preferred_element_type=F32)
         fb_buf[rows, :] = (merged.astype(F32) - approx).astype(BF16)
-        target = fb_ref.at[0, rows_of(half, i % CHUNKS), :]
+        target = fb_ref.at[0, pl.ds(pl.multiple_of(half * HALF + low_row, WRITES[0][1]), count), :]
         copies.append(pltpu.make_async_copy(fb_buf.at[rows, :], target, fb_sem.at[i]))
         copies[-1].start()
-        if i == 0:
+        if i == 1:
             count = mom_ref.shape[0]
             replica, per_half = lax.axis_index("replica"), HALF // count
             start = jnp.where(replica // per_half == mine, 0, HALF) + lax.rem(replica, per_half) * count
@@ -246,7 +239,7 @@
             pltpu.VMEM((ROWS, COLS), BF16),
             pltpu.VMEM((mom_rows, COLS), BF16),
             pltpu.VMEM((RANK, COLS), F32),
-            pltpu.SemaphoreType.DMA((2 * CHUNKS,)),
+            pltpu.SemaphoreType.DMA((len(WRITES),)),
             pltpu.SemaphoreType.DMA((1,)),
             pltpu.SemaphoreType.DMA((1,)),
         ],
@@ -291,7 +284,7 @@
     momentum = pltpu.with_memory_space_constraint(momentum, pltpu.VMEM)
     merged_other, send, *loaded = merge_other(gradient, feedback, right_t)
     received = sibling(send)
-    merged_own, keep = merge_own(gradient, feedback, *loaded)
+    merged_own, keep = merge_own(*loaded)
     own = keep + received
     for axes in ("yx", "xz", "zy"):
         own = ring_sum(own, axes)

time: 45.8 us -> 45.3 us (0.989)
  Pallas kernels: 11.1 us -> 10.2 us
    pallas_call x1, Pallas kernels: 2.16 us -> 0.78 us  [merge_own(): pl.pallas_call(merge_kernel, in_specs=[whole()] * 3, out_specs=[whole(),...]
  transfers between devices with their start and end apart: 15 -> 15, of which waited for: 11 -> 13; matrix products, arithmetic and copies ran while one was open for 0% -> 0% of each run, Pallas kernels for 9% -> 6%
where the time goes in v7:
time: 45.3 us; the launch traced here: 45.1 us
  starting transfers between devices  19.1 us (42%)
  waiting for transfers between devices  15.1 us (33%)
  Pallas kernels  10.2 us (23%)
  between operations  0.7 us (2%)
    ppermute x12, starting transfers between devices, move(): return lax.ppermute(x, ('replica', 'tensor'), move_pairs(moves, swap))  16.7 us
    ppermute x12, waiting for transfers between devices, move(): return lax.ppermute(x, ('replica', 'tensor'), move_pairs(moves, swap))  13.6 us
    pallas_call x1, Pallas kernels, merge_other(): pl.pallas_call(load_kernel, in_specs=in_hbm(3), out_specs=[whole()] * 5,...  3.84 us
    pallas_call x1, Pallas kernels, finish(): pl.pallas_call(body, in_specs=[whole()] * 9, out_specs=in_hbm(3), out_sha...  3 us
    ppermute x3, starting transfers between devices, sibling(): lax.ppermute(x, 'replica', [(i, i ^ 1) for i in range(lax.axis_size('repl...  2.42 us
    pallas_call x1, Pallas kernels, make_basis(): pl.pallas_call(basis_kernel, in_specs=[whole(), whole()], out_specs=[whol...  1.66 us
    ppermute x3, waiting for transfers between devices, sibling(): lax.ppermute(x, 'replica', [(i, i ^ 1) for i in range(lax.axis_size('repl...  1.48 us
  transfers between devices with their start and end apart: 15, of which 13 were waited for; matrix products, arithmetic and copies ran while one was open for 0% of the time, Pallas kernels for 6%

profile of v7, /device:TPU:1, one launch (start us, length us, event | category | flops | bytes accessed | tf_op | source)
XLA Modules:
  0.0 45.1 jit_solution(3001322407648001333)
XLA Ops:
  0.6 3.8 %merge_other.1 = (bf16[3072,384]{1,0:T(8,128)(2,1)S(1)}, f32[8,3072]{1,0:T(8,128)S(1)}, bf16[3072,384]{1,0:T(8,128)(2,1)S(1)}, bf16[3072,384]{1,0:T(8,128)(2,1)S(1)}, f32[8,384]{1,0:T(8,128)S(1)}) custom-call(bf16[1,6144,384]{2,1,0:T(8,128)(2,1)} %g_ref.1, bf16[1,6144,384]{2,1,0:T(8,128)(2,1)} %f_ref.1, f32[8,384]{1,0:T(8,128)} %bitcast.2), custom_call_target="tpu_custom_call" | custom-call | flops 18874368 | bytes 9437184 | tf_op jit(solution)/shard_map/merge_other/pallas_call | solution.py:88
  4.5 1.5 %collective-permute-start = (f32[8,3072]{1,0:T(8,128)S(1)}, f32[8,3072]{1,0:T(8,128)S(1)}, u32[]{:S(2)}, u32[]{:S(2)}) collective-permute-start(f32[8,3072]{1,0:T(8,128)S(1)} %get-tuple-element.21), channel_id=1, source_target_pairs={{0,16},{16,0},{32,48},{48,32},{64,80},{80,64},{96,112},{112,96},{1... | collective-permute-start | bytes 294920 | tf_op jit(solution)/shard_map/ppermute | solution.py:277
  6.0 0.8 %merge_own.1 = (bf16[3072,384]{1,0:T(8,128)(2,1)S(1)}, f32[8,3072]{1,0:T(8,128)S(1)}) custom-call(bf16[3072,384]{1,0:T(8,128)(2,1)S(1)} %get-tuple-element.15.g_ref, bf16[3072,384]{1,0:T(8,128)(2,1)S(1)} %get-tuple-element.16.f_ref, f32[8,384]{1,0:T(8,128)S(1)} %get-tuple-element.17.q_ref), custom_call_target="tpu_custom_call" | custom-call | flops 18874368 | bytes 4718592 | tf_op jit(solution)/shard_map/merge_own/pallas_call | solution.py:113
  6.9 2.9 %collective-permute-start.3 = (f32[8,3072]{1,0:T(8,128)S(1)}, f32[8,3072]{1,0:T(8,128)S(1)}, u32[]{:S(2)}, u32[]{:S(2)}) collective-permute-start(f32[8,3072]{1,0:T(8,128)S(1)} %add.33), channel_id=1, source_target_pairs={{0,64},{1,3},{2,66},{3,1},{4,6},{5,69},{6,4},{7,71},{8,72},{9,11},... | collective-permute-start | bytes 294920 | tf_op jit(solution)/shard_map/ppermute | solution.py:267
  9.8 1.4 %collective-permute-start.2 = (f32[8,3072]{1,0:T(8,128)S(1)}, f32[8,3072]{1,0:T(8,128)S(1)}, u32[]{:S(2)}, u32[]{:S(2)}) collective-permute-start(f32[8,3072]{1,0:T(8,128)S(1)} %add.33), channel_id=1, source_target_pairs={{0,112},{1,18},{2,114},{3,16},{4,23},{5,117},{6,21},{7,119},{8,120... | collective-permute-start | bytes 294920 | tf_op jit(solution)/shard_map/ppermute | solution.py:267
  11.2 1.1 %collective-permute-done.3 = f32[8,3072]{1,0:T(8,128)S(1)} collective-permute-done((f32[8,3072]{1,0:T(8,128)S(1)}, f32[8,3072]{1,0:T(8,128)S(1)}, u32[]{:S(2)}, u32[]{:S(2)}) %collective-permute-start.3) | collective-permute-done | bytes 98336 | tf_op jit(solution)/shard_map/ppermute | solution.py:267
  12.3 3.1 %collective-permute-done.2 = f32[8,3072]{1,0:T(8,128)S(1)} collective-permute-done((f32[8,3072]{1,0:T(8,128)S(1)}, f32[8,3072]{1,0:T(8,128)S(1)}, u32[]{:S(2)}, u32[]{:S(2)}) %collective-permute-start.2) | collective-permute-done | bytes 98336 | tf_op jit(solution)/shard_map/ppermute | solution.py:267
  15.5 3.7 %collective-permute-start.6 = (f32[8,3072]{1,0:T(8,128)S(1)}, f32[8,3072]{1,0:T(8,128)S(1)}, u32[]{:S(2)}, u32[]{:S(2)}) collective-permute-start(f32[8,3072]{1,0:T(8,128)S(1)} %add_add_fusion.2), channel_id=1, source_target_pairs={{0,2},{1,9},{2,0},{3,11},{4,12},{5,7},{6,14},{7,5},{8,10},{9,1},{1... | collective-permute-start | bytes 294920 | tf_op jit(solution)/shard_map/ppermute | solution.py:267
  19.2 0.8 %collective-permute-start.5 = (f32[8,3072]{1,0:T(8,128)S(1)}, f32[8,3072]{1,0:T(8,128)S(1)}, u32[]{:S(2)}, u32[]{:S(2)}) collective-permute-start(f32[8,3072]{1,0:T(8,128)S(1)} %add_add_fusion.2), channel_id=1, source_target_pairs={{0,19},{1,29},{2,17},{3,31},{4,24},{5,22},{6,26},{7,20},{8,27},{9,... | collective-permute-start | bytes 294920 | tf_op jit(solution)/shard_map/ppermute | solution.py:267
  20.3 1.2 %collective-permute-done.6 = f32[8,3072]{1,0:T(8,128)S(1)} collective-permute-done((f32[8,3072]{1,0:T(8,128)S(1)}, f32[8,3072]{1,0:T(8,128)S(1)}, u32[]{:S(2)}, u32[]{:S(2)}) %collective-permute-start.6) | collective-permute-done | bytes 98336 | tf_op jit(solution)/shard_map/ppermute | solution.py:267
  21.5 3.0 %collective-permute-done.5 = f32[8,3072]{1,0:T(8,128)S(1)} collective-permute-done((f32[8,3072]{1,0:T(8,128)S(1)}, f32[8,3072]{1,0:T(8,128)S(1)}, u32[]{:S(2)}, u32[]{:S(2)}) %collective-permute-start.5) | collective-permute-done | bytes 98336 | tf_op jit(solution)/shard_map/ppermute | solution.py:267
  24.5 2.8 %collective-permute-start.9 = (f32[8,3072]{1,0:T(8,128)S(1)}, f32[8,3072]{1,0:T(8,128)S(1)}, u32[]{:S(2)}, u32[]{:S(2)}) collective-permute-start(f32[8,3072]{1,0:T(8,128)S(1)} %add_add_fusion.1), channel_id=1, source_target_pairs={{0,8},{1,65},{2,10},{3,67},{4,68},{5,13},{6,70},{7,15},{8,0},{9,73... | collective-permute-start | bytes 294920 | tf_op jit(solution)/shard_map/ppermute | solution.py:267
  27.3 1.7 %collective-permute-start.8 = (f32[8,3072]{1,0:T(8,128)S(1)}, f32[8,3072]{1,0:T(8,128)S(1)}, u32[]{:S(2)}, u32[]{:S(2)}) collective-permute-start(f32[8,3072]{1,0:T(8,128)S(1)} %add_add_fusion.1), channel_id=1, source_target_pairs={{0,28},{1,113},{2,30},{3,115},{4,116},{5,25},{6,118},{7,27},{8,20}... | collective-permute-start | bytes 294920 | tf_op jit(solution)/shard_map/ppermute | solution.py:267
  28.9 0.9 %collective-permute-done.9 = f32[8,3072]{1,0:T(8,128)S(1)} collective-permute-done((f32[8,3072]{1,0:T(8,128)S(1)}, f32[8,3072]{1,0:T(8,128)S(1)}, u32[]{:S(2)}, u32[]{:S(2)}) %collective-permute-start.9) | collective-permute-done | bytes 98336 | tf_op jit(solution)/shard_map/ppermute | solution.py:267
  29.8 3.0 %collective-permute-done.8 = f32[8,3072]{1,0:T(8,128)S(1)} collective-permute-done((f32[8,3072]{1,0:T(8,128)S(1)}, f32[8,3072]{1,0:T(8,128)S(1)}, u32[]{:S(2)}, u32[]{:S(2)}) %collective-permute-start.8) | collective-permute-done | bytes 98336 | tf_op jit(solution)/shard_map/ppermute | solution.py:267
  33.2 0.5 %collective-permute-start.10 = (f32[8,3072]{1,0:T(8,128)S(1)}, f32[8,3072]{1,0:T(8,128)S(1)}, u32[]{:S(2)}, u32[]{:S(2)}) collective-permute-start(f32[8,3072]{1,0:T(8,128)S(1)} %add_add_fusion.own_ref.left_ref), channel_id=1, source_target_pairs={{0,16},{16,0},{32,48},{48,32},{64,80},{80,64},{96,112},{112,96},{1... | collective-permute-start | bytes 294920 | tf_op jit(solution)/shard_map/ppermute | solution.py:277
  34.1 0.5 %collective-permute-done.10.other_ref.left_ref = f32[8,3072]{1,0:T(8,128)S(1)} collective-permute-done((f32[8,3072]{1,0:T(8,128)S(1)}, f32[8,3072]{1,0:T(8,128)S(1)}, u32[]{:S(2)}, u32[]{:S(2)}) %collective-permute-start.10) | collective-permute-done | bytes 98336 | tf_op jit(solution)/shard_map/ppermute | solution.py:277
  35.5 0.8 %collective-permute-done.11 = f32[8,384]{1,0:T(8,128)S(1)} collective-permute-done((f32[8,384]{1,0:T(8,128)S(1)}, f32[8,384]{1,0:T(8,128)S(1)}, u32[]{:S(2)}, u32[]{:S(2)}) %collective-permute-start.11) | collective-permute-done | bytes 12320 | tf_op jit(solution)/shard_map/ppermute | solution.py:277
  36.3 1.4 %collective-permute-start.14 = (f32[8,384]{1,0:T(8,128)S(1)}, f32[8,384]{1,0:T(8,128)S(1)}, u32[]{:S(2)}, u32[]{:S(2)}) collective-permute-start(f32[8,384]{1,0:T(8,128)S(1)} %add.43.refs_4_), channel_id=1, source_target_pairs={{0,80},{1,81},{2,82},{3,83},{4,84},{5,85},{6,86},{7,87},{8,88},{9,... | collective-permute-start | bytes 36872 | tf_op jit(solution)/shard_map/ppermute | solution.py:267
  37.7 1.3 %collective-permute-start.13 = (f32[8,384]{1,0:T(8,128)S(1)}, f32[8,384]{1,0:T(8,128)S(1)}, u32[]{:S(2)}, u32[]{:S(2)}) collective-permute-start(f32[8,384]{1,0:T(8,128)S(1)} %add.43.refs_4_), channel_id=1, source_target_pairs={{0,112},{1,113},{2,114},{3,115},{4,116},{5,117},{6,118},{7,119},{8... | collective-permute-start | bytes 36872 | tf_op jit(solution)/shard_map/ppermute | solution.py:267
  39.0 0.5 %collective-permute-start.12 = (f32[8,384]{1,0:T(8,128)S(1)}, f32[8,384]{1,0:T(8,128)S(1)}, u32[]{:S(2)}, u32[]{:S(2)}) collective-permute-start(f32[8,384]{1,0:T(8,128)S(1)} %add.43.refs_4_), channel_id=1, source_target_pairs={{0,48},{1,49},{2,50},{3,51},{4,52},{5,53},{6,54},{7,55},{8,56},{9,... | collective-permute-start | bytes 36872 | tf_op jit(solution)/shard_map/ppermute | solution.py:267
  39.5 1.7 %basis.1 = (f32[8,8]{1,0:T(8,128)S(1)}, bf16[6144,32]{1,0:T(8,128)(2,1)S(1)}) custom-call(f32[8,3072]{1,0:T(8,128)S(1)} %add_add_fusion.own_ref.left_ref, f32[8,3072]{1,0:T(8,128)S(1)} %collective-permute-done.10.other_ref.left_ref), custom_call_target="tpu_custom_call" | custom-call | flops 1572864 | bytes 4194304 | tf_op jit(solution)/shard_map/basis/pallas_call | solution.py:173
  41.2 0.9 %collective-permute-done.13.refs_6_ = f32[8,384]{1,0:T(8,128)S(1)} collective-permute-done((f32[8,384]{1,0:T(8,128)S(1)}, f32[8,384]{1,0:T(8,128)S(1)}, u32[]{:S(2)}, u32[]{:S(2)}) %collective-permute-start.13) | collective-permute-done | bytes 12320 | tf_op jit(solution)/shard_map/ppermute | solution.py:267
  42.2 3.0 %finish.1 = (bf16[1,6144,384]{2,1,0:T(8,128)(2,1)}, bf16[768,384]{1,0:T(8,128)(2,1)}, f32[8,384]{1,0:T(8,128)}) custom-call(bf16[3072,384]{1,0:T(8,128)(2,1)S(1)} %get-tuple-element.18.merged_ref.refs_0_, bf16[3072,384]{1,0:T(8,128)(2,1)S(1)} %get-tuple-element.19.merged_ref.refs_1_, bf16[6144,32]{1,0:T(8,128)(2,1)S(1)} %get-tuple-element.22.refs_2_, ...), custom_call_target="tpu_custom_call" | custom-call | flops 150994944 | bytes 9437184 | tf_op jit(solution)/shard_map/finish/pallas_call | solution.py:229
  (19 shorter events, 2.4 us)
Async XLA Ops:
  4.5 2.4 %collective-permute-start = (f32[8,3072]{1,0:T(8,128)S(1)}, f32[8,3072]{1,0:T(8,128)S(1)}, u32[]{:S(2)}, u32[]{:S(2)}) collective-permute-start(f32[8,3072]{1,0:T(8,128)S(1)} %get-tuple-element.21), channel_id=1, source_target_pairs={{0,16},{16,0},{32,48},{48,32},{64,80},{80,64},{96,112},{112,96},{1... | collective-permute-start | bytes 294920 | tf_op jit(solution)/shard_map/ppermute | solution.py:277
  6.9 5.3 %collective-permute-start.3 = (f32[8,3072]{1,0:T(8,128)S(1)}, f32[8,3072]{1,0:T(8,128)S(1)}, u32[]{:S(2)}, u32[]{:S(2)}) collective-permute-start(f32[8,3072]{1,0:T(8,128)S(1)} %add.33), channel_id=1, source_target_pairs={{0,64},{1,3},{2,66},{3,1},{4,6},{5,69},{6,4},{7,71},{8,72},{9,11},... | collective-permute-start | bytes 294920 | tf_op jit(solution)/shard_map/ppermute | solution.py:267
  9.8 5.5 %collective-permute-start.2 = (f32[8,3072]{1,0:T(8,128)S(1)}, f32[8,3072]{1,0:T(8,128)S(1)}, u32[]{:S(2)}, u32[]{:S(2)}) collective-permute-start(f32[8,3072]{1,0:T(8,128)S(1)} %add.33), channel_id=1, source_target_pairs={{0,112},{1,18},{2,114},{3,16},{4,23},{5,117},{6,21},{7,119},{8,120... | collective-permute-start | bytes 294920 | tf_op jit(solution)/shard_map/ppermute | solution.py:267
  11.2 4.3 %collective-permute-start.1 = (f32[8,3072]{1,0:T(8,128)S(1)}, f32[8,3072]{1,0:T(8,128)S(1)}, u32[]{:S(2)}, u32[]{:S(2)}) collective-permute-start(f32[8,3072]{1,0:T(8,128)S(1)} %add.33), channel_id=1, source_target_pairs={{0,48},{1,16},{2,50},{3,18},{4,21},{5,53},{6,23},{7,55},{8,56},{9,... | collective-permute-start | bytes 294920 | tf_op jit(solution)/shard_map/ppermute | solution.py:267
  15.5 6.0 %collective-permute-start.6 = (f32[8,3072]{1,0:T(8,128)S(1)}, f32[8,3072]{1,0:T(8,128)S(1)}, u32[]{:S(2)}, u32[]{:S(2)}) collective-permute-start(f32[8,3072]{1,0:T(8,128)S(1)} %add_add_fusion.2), channel_id=1, source_target_pairs={{0,2},{1,9},{2,0},{3,11},{4,12},{5,7},{6,14},{7,5},{8,10},{9,1},{1... | collective-permute-start | bytes 294920 | tf_op jit(solution)/shard_map/ppermute | solution.py:267
  19.2 5.3 %collective-permute-start.5 = (f32[8,3072]{1,0:T(8,128)S(1)}, f32[8,3072]{1,0:T(8,128)S(1)}, u32[]{:S(2)}, u32[]{:S(2)}) collective-permute-start(f32[8,3072]{1,0:T(8,128)S(1)} %add_add_fusion.2), channel_id=1, source_target_pairs={{0,19},{1,29},{2,17},{3,31},{4,24},{5,22},{6,26},{7,20},{8,27},{9,... | collective-permute-start | bytes 294920 | tf_op jit(solution)/shard_map/ppermute | solution.py:267
  20.0 4.4 %collective-permute-start.4 = (f32[8,3072]{1,0:T(8,128)S(1)}, f32[8,3072]{1,0:T(8,128)S(1)}, u32[]{:S(2)}, u32[]{:S(2)}) collective-permute-start(f32[8,3072]{1,0:T(8,128)S(1)} %add_add_fusion.2), channel_id=1, source_target_pairs={{0,17},{1,21},{2,19},{3,23},{4,16},{5,20},{6,18},{7,22},{8,25},{9,... | collective-permute-start | bytes 294920 | tf_op jit(solution)/shard_map/ppermute | solution.py:267
  24.5 5.3 %collective-permute-start.9 = (f32[8,3072]{1,0:T(8,128)S(1)}, f32[8,3072]{1,0:T(8,128)S(1)}, u32[]{:S(2)}, u32[]{:S(2)}) collective-permute-start(f32[8,3072]{1,0:T(8,128)S(1)} %add_add_fusion.1), channel_id=1, source_target_pairs={{0,8},{1,65},{2,10},{3,67},{4,68},{5,13},{6,70},{7,15},{8,0},{9,73... | collective-permute-start | bytes 294920 | tf_op jit(solution)/shard_map/ppermute | solution.py:267
  27.3 5.5 %collective-permute-start.8 = (f32[8,3072]{1,0:T(8,128)S(1)}, f32[8,3072]{1,0:T(8,128)S(1)}, u32[]{:S(2)}, u32[]{:S(2)}) collective-permute-start(f32[8,3072]{1,0:T(8,128)S(1)} %add_add_fusion.1), channel_id=1, source_target_pairs={{0,28},{1,113},{2,30},{3,115},{4,116},{5,25},{6,118},{7,27},{8,20}... | collective-permute-start | bytes 294920 | tf_op jit(solution)/shard_map/ppermute | solution.py:267
  28.9 4.2 %collective-permute-start.7 = (f32[8,3072]{1,0:T(8,128)S(1)}, f32[8,3072]{1,0:T(8,128)S(1)}, u32[]{:S(2)}, u32[]{:S(2)}) collective-permute-start(f32[8,3072]{1,0:T(8,128)S(1)} %add_add_fusion.1), channel_id=1, source_target_pairs={{0,20},{1,49},{2,22},{3,51},{4,52},{5,17},{6,54},{7,19},{8,28},{9,... | collective-permute-start | bytes 294920 | tf_op jit(solution)/shard_map/ppermute | solution.py:267
  33.2 1.4 %collective-permute-start.10 = (f32[8,3072]{1,0:T(8,128)S(1)}, f32[8,3072]{1,0:T(8,128)S(1)}, u32[]{:S(2)}, u32[]{:S(2)}) collective-permute-start(f32[8,3072]{1,0:T(8,128)S(1)} %add_add_fusion.own_ref.left_ref), channel_id=1, source_target_pairs={{0,16},{16,0},{32,48},{48,32},{64,80},{80,64},{96,112},{112,96},{1... | collective-permute-start | bytes 294920 | tf_op jit(solution)/shard_map/ppermute | solution.py:277
  33.6 8.5 %copy-start = (bf16[768,384]{1,0:T(8,128)(2,1)S(1)}, bf16[768,384]{1,0:T(8,128)(2,1)}, u32[]{:S(2)}) copy-start(bf16[768,384]{1,0:T(8,128)(2,1)} %refs_8_.1) | copy-start | bytes 1769476
  35.1 1.3 %collective-permute-start.11 = (f32[8,384]{1,0:T(8,128)S(1)}, f32[8,384]{1,0:T(8,128)S(1)}, u32[]{:S(2)}, u32[]{:S(2)}) collective-permute-start(f32[8,384]{1,0:T(8,128)S(1)} %right_other.1), channel_id=1, source_target_pairs={{0,16},{16,0},{32,48},{48,32},{64,80},{80,64},{96,112},{112,96},{1... | collective-permute-start | bytes 36872 | tf_op jit(solution)/shard_map/ppermute | solution.py:277
  36.3 4.8 %collective-permute-start.14 = (f32[8,384]{1,0:T(8,128)S(1)}, f32[8,384]{1,0:T(8,128)S(1)}, u32[]{:S(2)}, u32[]{:S(2)}) collective-permute-start(f32[8,384]{1,0:T(8,128)S(1)} %add.43.refs_4_), channel_id=1, source_target_pairs={{0,80},{1,81},{2,82},{3,83},{4,84},{5,85},{6,86},{7,87},{8,88},{9,... | collective-permute-start | bytes 36872 | tf_op jit(solution)/shard_map/ppermute | solution.py:267
  37.7 4.3 %collective-permute-start.13 = (f32[8,384]{1,0:T(8,128)S(1)}, f32[8,384]{1,0:T(8,128)S(1)}, u32[]{:S(2)}, u32[]{:S(2)}) collective-permute-start(f32[8,384]{1,0:T(8,128)S(1)} %add.43.refs_4_), channel_id=1, source_target_pairs={{0,112},{1,113},{2,114},{3,115},{4,116},{5,117},{6,118},{7,119},{8... | collective-permute-start | bytes 36872 | tf_op jit(solution)/shard_map/ppermute | solution.py:267
  39.0 3.1 %collective-permute-start.12 = (f32[8,384]{1,0:T(8,128)S(1)}, f32[8,384]{1,0:T(8,128)S(1)}, u32[]{:S(2)}, u32[]{:S(2)}) collective-permute-start(f32[8,384]{1,0:T(8,128)S(1)} %add.43.refs_4_), channel_id=1, source_target_pairs={{0,48},{1,49},{2,50},{3,51},{4,52},{5,53},{6,54},{7,55},{8,56},{9,... | collective-permute-start | bytes 36872 | tf_op jit(solution)/shard_map/ppermute | solution.py:267

commit v8 on v7

--- a/solution.py
+++ b/solution.py
@@ -1,5 +1,3 @@
-import itertools
-
 import jax
 import jax.numpy as jnp
 from jax import lax
@@ -12,13 +10,14 @@
 HALF = ROWS // 2
 CHUNKS = 3
 CHUNK = HALF // CHUNKS
-WRITES = ((0, 256), (256, 768), *((i * CHUNK, CHUNK) for i in range(1, 2 * CHUNKS)))
+WRITES = [(i * CHUNK, CHUNK) for i in range(2 * CHUNKS)]
 MIB = 1 << 20
 
 
 def own_half():
     replica, tensor = lax.axis_index("replica"), lax.axis_index("tensor")
-    return lax.rem(replica + replica // 2 + tensor + tensor // 4, 2)
+    bits = replica + replica // 2 + replica // 4 + tensor + tensor // 2 + tensor // 4 + tensor // 8
+    return lax.rem(bits, 2)
 
 
 def split(x, count):
@@ -207,7 +206,7 @@
         target = fb_ref.at[0, pl.ds(pl.multiple_of(half * HALF + low_row, WRITES[0][1]), count), :]
         copies.append(pltpu.make_async_copy(fb_buf.at[rows, :], target, fb_sem.at[i]))
         copies[-1].start()
-        if i == 1:
+        if i == 0:
             count = mom_ref.shape[0]
             replica, per_half = lax.axis_index("replica"), HALF // count
             start = jnp.where(replica // per_half == mine, 0, HALF) + lax.rem(replica, per_half) * count
@@ -249,32 +248,22 @@
     )(merged_own, merged_other, basis, inverse, *parts, momentum)
 
 
-FLIP = {"n": 1, "w": 3, "f": 2}
-
-
-def move_pairs(moves, swap):
-    pairs = []
-    for y, core, z, x in itertools.product(range(4), range(2), range(4), range(4)):
-        there = {"y": y, "z": z, "x": x}
-        for kind, axis in moves[(core + y + z + x) % 2]:
-            there[axis] ^= FLIP[kind]
-        to = 2 * there["y"] + (core ^ swap)
-        pairs.append((16 * (2 * y + core) + 4 * z + x, 16 * to + 4 * there["z"] + there["x"]))
-    return pairs
-
-
-def move(x, moves, swap):
-    return lax.ppermute(x, ("replica", "tensor"), move_pairs(moves, swap))
+CORE, LOW = 16, {"y": 32, "z": 4, "x": 1}
+
+
+def swap(x, masks):
+    pairs = [(i, i ^ masks[i.bit_count() % 2]) for i in range(128)]
+    return lax.ppermute(x, ("replica", "tensor"), pairs)
 
 
 def ring_sum(x, axes):
-    near = move(x, [["n" + a] for a in axes], 1)
-    wrap = move(x, [["w" + a] for a in axes], 1)
-    return x + near + wrap + move(x, [["f" + a] for a in axes], 0)
+    near = swap(x, [LOW[a] | CORE for a in axes])
+    wrap = swap(x, [3 * LOW[a] for a in axes])
+    return x + near + wrap + swap(x, [2 * LOW[a] | CORE for a in axes])
 
 
 def sibling(x):
-    return lax.ppermute(x, "replica", [(i, i ^ 1) for i in range(lax.axis_size("replica"))])
+    return swap(x, [CORE] * 2)
 
 
 def shards(gradient, feedback, momentum, right_init):
@@ -292,7 +281,7 @@
     term = right_term(merged_other, other, right_term(merged_own, own))
     inverse, basis = make_basis(own, other)
     term = term + sibling(term)
-    parts = [term, *(move(term, [[kind]] * 2, 1) for kind in ("ny", "wy", "fy"))]
+    parts = [term, *(swap(term, [steps * LOW["y"] | CORE] * 2) for steps in (1, 3, 2))]
     feedback_out, momentum_out, right_t = finish(
         lax.axis_size("replica"), merged_own, merged_other, basis, inverse, parts, momentum
     )

time: 45.3 us -> 44.9 us (level)
  transfers between devices with their start and end apart: 15 -> 15, of which waited for: 13 -> 12; matrix products, arithmetic and copies ran while one was open for 0% -> 0% of each run, Pallas kernels for 6% -> 6%
where the time goes in v8:
time: 44.9 us; the launch traced here: 44.8 us
  starting transfers between devices  19.1 us (43%)
  waiting for transfers between devices  14.7 us (33%)
  Pallas kernels  10.2 us (23%)
  between operations  0.7 us (2%)
    ppermute x15, starting transfers between devices, swap(): return lax.ppermute(x, ('replica', 'tensor'), pairs)  19.1 us
    ppermute x15, waiting for transfers between devices, swap(): return lax.ppermute(x, ('replica', 'tensor'), pairs)  14.7 us
    pallas_call x1, Pallas kernels, merge_other(): pl.pallas_call(load_kernel, in_specs=in_hbm(3), out_specs=[whole()] * 5,...  3.9 us
    pallas_call x1, Pallas kernels, finish(): pl.pallas_call(body, in_specs=[whole()] * 9, out_specs=in_hbm(3), out_sha...  2.99 us
    pallas_call x1, Pallas kernels, make_basis(): pl.pallas_call(basis_kernel, in_specs=[whole(), whole()], out_specs=[whol...  1.66 us
    pallas_call x2, Pallas kernels, right_term(): pl.pallas_call(right_kernel, in_specs=[whole()] * (2 + len(before)), out_...  0.9 us
  transfers between devices with their start and end apart: 15, of which 12 were waited for; matrix products, arithmetic and copies ran while one was open for 0% of the time, Pallas kernels for 6%

profile of v8, /device:TPU:1, one launch (start us, length us, event | category | flops | bytes accessed | tf_op | source)
XLA Modules:
  0.0 44.8 jit_solution(3199004413348982981)
XLA Ops:
  0.6 3.9 %merge_other.1 = (bf16[3072,384]{1,0:T(8,128)(2,1)S(1)}, f32[8,3072]{1,0:T(8,128)S(1)}, bf16[3072,384]{1,0:T(8,128)(2,1)S(1)}, bf16[3072,384]{1,0:T(8,128)(2,1)S(1)}, f32[8,384]{1,0:T(8,128)S(1)}) custom-call(bf16[1,6144,384]{2,1,0:T(8,128)(2,1)} %g_ref.1, bf16[1,6144,384]{2,1,0:T(8,128)(2,1)} %f_ref.1, f32[8,384]{1,0:T(8,128)} %bitcast.2), custom_call_target="tpu_custom_call" | custom-call | flops 18874368 | bytes 9437184 | tf_op jit(solution)/shard_map/merge_other/pallas_call | solution.py:87
  4.5 1.4 %collective-permute-start = (f32[8,3072]{1,0:T(8,128)S(1)}, f32[8,3072]{1,0:T(8,128)S(1)}, u32[]{:S(2)}, u32[]{:S(2)}) collective-permute-start(f32[8,3072]{1,0:T(8,128)S(1)} %get-tuple-element.21), channel_id=1, source_target_pairs={{0,16},{1,17},{2,18},{3,19},{4,20},{5,21},{6,22},{7,23},{8,24},{9,... | collective-permute-start | bytes 294920 | tf_op jit(solution)/shard_map/ppermute | solution.py:256
  6.0 0.8 %merge_own.1 = (bf16[3072,384]{1,0:T(8,128)(2,1)S(1)}, f32[8,3072]{1,0:T(8,128)S(1)}) custom-call(bf16[3072,384]{1,0:T(8,128)(2,1)S(1)} %get-tuple-element.15.g_ref, bf16[3072,384]{1,0:T(8,128)(2,1)S(1)} %get-tuple-element.16.f_ref, f32[8,384]{1,0:T(8,128)S(1)} %get-tuple-element.17.q_ref), custom_call_target="tpu_custom_call" | custom-call | flops 18874368 | bytes 4718592 | tf_op jit(solution)/shard_map/merge_own/pallas_call | solution.py:112
  6.9 3.2 %collective-permute-start.3 = (f32[8,3072]{1,0:T(8,128)S(1)}, f32[8,3072]{1,0:T(8,128)S(1)}, u32[]{:S(2)}, u32[]{:S(2)}) collective-permute-start(f32[8,3072]{1,0:T(8,128)S(1)} %add.33), channel_id=1, source_target_pairs={{0,80},{1,19},{2,16},{3,83},{4,22},{5,85},{6,86},{7,21},{8,26},{9,... | collective-permute-start | bytes 294920 | tf_op jit(solution)/shard_map/ppermute | solution.py:256
  10.1 0.9 %collective-permute-start.2 = (f32[8,3072]{1,0:T(8,128)S(1)}, f32[8,3072]{1,0:T(8,128)S(1)}, u32[]{:S(2)}, u32[]{:S(2)}) collective-permute-start(f32[8,3072]{1,0:T(8,128)S(1)} %add.33), channel_id=1, source_target_pairs={{0,96},{1,2},{2,1},{3,99},{4,7},{5,101},{6,102},{7,4},{8,11},{9,10... | collective-permute-start | bytes 294920 | tf_op jit(solution)/shard_map/ppermute | solution.py:256
  11.0 1.6 %collective-permute-done.3 = f32[8,3072]{1,0:T(8,128)S(1)} collective-permute-done((f32[8,3072]{1,0:T(8,128)S(1)}, f32[8,3072]{1,0:T(8,128)S(1)}, u32[]{:S(2)}, u32[]{:S(2)}) %collective-permute-start.3) | collective-permute-done | bytes 98336 | tf_op jit(solution)/shard_map/ppermute | solution.py:256
  12.6 2.5 %collective-permute-done.2 = f32[8,3072]{1,0:T(8,128)S(1)} collective-permute-done((f32[8,3072]{1,0:T(8,128)S(1)}, f32[8,3072]{1,0:T(8,128)S(1)}, u32[]{:S(2)}, u32[]{:S(2)}) %collective-permute-start.2) | collective-permute-done | bytes 98336 | tf_op jit(solution)/shard_map/ppermute | solution.py:256
  15.4 4.3 %collective-permute-start.6 = (f32[8,3072]{1,0:T(8,128)S(1)}, f32[8,3072]{1,0:T(8,128)S(1)}, u32[]{:S(2)}, u32[]{:S(2)}) collective-permute-start(f32[8,3072]{1,0:T(8,128)S(1)} %add_add_fusion.2), channel_id=1, source_target_pairs={{0,18},{1,25},{2,26},{3,17},{4,28},{5,23},{6,20},{7,31},{8,16},{9,... | collective-permute-start | bytes 294920 | tf_op jit(solution)/shard_map/ppermute | solution.py:256
  20.1 1.9 %collective-permute-done.6 = f32[8,3072]{1,0:T(8,128)S(1)} collective-permute-done((f32[8,3072]{1,0:T(8,128)S(1)}, f32[8,3072]{1,0:T(8,128)S(1)}, u32[]{:S(2)}, u32[]{:S(2)}) %collective-permute-start.6) | collective-permute-done | bytes 98336 | tf_op jit(solution)/shard_map/ppermute | solution.py:256
  22.0 2.4 %collective-permute-done.5 = f32[8,3072]{1,0:T(8,128)S(1)} collective-permute-done((f32[8,3072]{1,0:T(8,128)S(1)}, f32[8,3072]{1,0:T(8,128)S(1)}, u32[]{:S(2)}, u32[]{:S(2)}) %collective-permute-start.5) | collective-permute-done | bytes 98336 | tf_op jit(solution)/shard_map/ppermute | solution.py:256
  24.4 3.5 %collective-permute-start.9 = (f32[8,3072]{1,0:T(8,128)S(1)}, f32[8,3072]{1,0:T(8,128)S(1)}, u32[]{:S(2)}, u32[]{:S(2)}) collective-permute-start(f32[8,3072]{1,0:T(8,128)S(1)} %add_add_fusion.1), channel_id=1, source_target_pairs={{0,24},{1,81},{2,82},{3,27},{4,84},{5,29},{6,30},{7,87},{8,88},{9,... | collective-permute-start | bytes 294920 | tf_op jit(solution)/shard_map/ppermute | solution.py:256
  27.9 0.8 %collective-permute-start.8 = (f32[8,3072]{1,0:T(8,128)S(1)}, f32[8,3072]{1,0:T(8,128)S(1)}, u32[]{:S(2)}, u32[]{:S(2)}) collective-permute-start(f32[8,3072]{1,0:T(8,128)S(1)} %add_add_fusion.1), channel_id=1, source_target_pairs={{0,12},{1,97},{2,98},{3,15},{4,100},{5,9},{6,10},{7,103},{8,104},{... | collective-permute-start | bytes 294920 | tf_op jit(solution)/shard_map/ppermute | solution.py:256
  28.7 1.5 %collective-permute-done.9 = f32[8,3072]{1,0:T(8,128)S(1)} collective-permute-done((f32[8,3072]{1,0:T(8,128)S(1)}, f32[8,3072]{1,0:T(8,128)S(1)}, u32[]{:S(2)}, u32[]{:S(2)}) %collective-permute-start.9) | collective-permute-done | bytes 98336 | tf_op jit(solution)/shard_map/ppermute | solution.py:256
  30.2 2.7 %collective-permute-done.8 = f32[8,3072]{1,0:T(8,128)S(1)} collective-permute-done((f32[8,3072]{1,0:T(8,128)S(1)}, f32[8,3072]{1,0:T(8,128)S(1)}, u32[]{:S(2)}, u32[]{:S(2)}) %collective-permute-start.8) | collective-permute-done | bytes 98336 | tf_op jit(solution)/shard_map/ppermute | solution.py:256
  33.0 1.0 %collective-permute-start.10 = (f32[8,3072]{1,0:T(8,128)S(1)}, f32[8,3072]{1,0:T(8,128)S(1)}, u32[]{:S(2)}, u32[]{:S(2)}) collective-permute-start(f32[8,3072]{1,0:T(8,128)S(1)} %add_add_fusion.own_ref.left_ref), channel_id=1, source_target_pairs={{0,16},{1,17},{2,18},{3,19},{4,20},{5,21},{6,22},{7,23},{8,24},{9,... | collective-permute-start | bytes 294920 | tf_op jit(solution)/shard_map/ppermute | solution.py:256
  34.0 0.4 right_own.1.refs_0_
  34.4 0.5 %collective-permute-done.10.other_ref.left_ref = f32[8,3072]{1,0:T(8,128)S(1)} collective-permute-done((f32[8,3072]{1,0:T(8,128)S(1)}, f32[8,3072]{1,0:T(8,128)S(1)}, u32[]{:S(2)}, u32[]{:S(2)}) %collective-permute-start.10) | collective-permute-done | bytes 98336 | tf_op jit(solution)/shard_map/ppermute | solution.py:256
  34.9 0.5 %right_other.1 = f32[8,384]{1,0:T(8,128)S(1)} custom-call(bf16[3072,384]{1,0:T(8,128)(2,1)S(1)} %get-tuple-element.19.merged_ref.refs_1_, f32[8,3072]{1,0:T(8,128)S(1)} %collective-permute-done.10.other_ref.left_ref, f32[8,384]{1,0:T(8,128)S(1)} %right_own.1.refs_0_), custom_call_target="tpu_custom_call" | custom-call | flops 37748736 | bytes 2359296 | tf_op jit(solution)/shard_map/right_other/pallas_call | solution.py:133
  35.8 0.8 %collective-permute-done.11 = f32[8,384]{1,0:T(8,128)S(1)} collective-permute-done((f32[8,384]{1,0:T(8,128)S(1)}, f32[8,384]{1,0:T(8,128)S(1)}, u32[]{:S(2)}, u32[]{:S(2)}) %collective-permute-start.11) | collective-permute-done | bytes 12320 | tf_op jit(solution)/shard_map/ppermute | solution.py:256
  36.7 0.8 %collective-permute-start.14 = (f32[8,384]{1,0:T(8,128)S(1)}, f32[8,384]{1,0:T(8,128)S(1)}, u32[]{:S(2)}, u32[]{:S(2)}) collective-permute-start(f32[8,384]{1,0:T(8,128)S(1)} %add.43.refs_4_), channel_id=1, source_target_pairs={{0,80},{1,81},{2,82},{3,83},{4,84},{5,85},{6,86},{7,87},{8,88},{9,... | collective-permute-start | bytes 36872 | tf_op jit(solution)/shard_map/ppermute | solution.py:256
  37.5 1.1 %collective-permute-start.13 = (f32[8,384]{1,0:T(8,128)S(1)}, f32[8,384]{1,0:T(8,128)S(1)}, u32[]{:S(2)}, u32[]{:S(2)}) collective-permute-start(f32[8,384]{1,0:T(8,128)S(1)} %add.43.refs_4_), channel_id=1, source_target_pairs={{0,112},{1,113},{2,114},{3,115},{4,116},{5,117},{6,118},{7,119},{8... | collective-permute-start | bytes 36872 | tf_op jit(solution)/shard_map/ppermute | solution.py:256
  38.6 1.2 %collective-permute-start.12 = (f32[8,384]{1,0:T(8,128)S(1)}, f32[8,384]{1,0:T(8,128)S(1)}, u32[]{:S(2)}, u32[]{:S(2)}) collective-permute-start(f32[8,384]{1,0:T(8,128)S(1)} %add.43.refs_4_), channel_id=1, source_target_pairs={{0,48},{1,49},{2,50},{3,51},{4,52},{5,53},{6,54},{7,55},{8,56},{9,... | collective-permute-start | bytes 36872 | tf_op jit(solution)/shard_map/ppermute | solution.py:256
  39.8 1.7 %basis.1 = (f32[8,8]{1,0:T(8,128)S(1)}, bf16[6144,32]{1,0:T(8,128)(2,1)S(1)}) custom-call(f32[8,3072]{1,0:T(8,128)S(1)} %add_add_fusion.own_ref.left_ref, f32[8,3072]{1,0:T(8,128)S(1)} %collective-permute-done.10.other_ref.left_ref), custom_call_target="tpu_custom_call" | custom-call | flops 1572864 | bytes 4194304 | tf_op jit(solution)/shard_map/basis/pallas_call | solution.py:172
  41.8 3.0 %finish.1 = (bf16[1,6144,384]{2,1,0:T(8,128)(2,1)}, bf16[768,384]{1,0:T(8,128)(2,1)}, f32[8,384]{1,0:T(8,128)}) custom-call(bf16[3072,384]{1,0:T(8,128)(2,1)S(1)} %get-tuple-element.18.merged_ref.refs_0_, bf16[3072,384]{1,0:T(8,128)(2,1)S(1)} %get-tuple-element.19.merged_ref.refs_1_, bf16[6144,32]{1,0:T(8,128)(2,1)S(1)} %get-tuple-element.22.refs_2_, ...), custom_call_target="tpu_custom_call" | custom-call | flops 150994944 | bytes 9437184 | tf_op jit(solution)/shard_map/finish/pallas_call | solution.py:228
  (19 shorter events, 1.8 us)
Async XLA Ops:
  4.5 2.4 %collective-permute-start = (f32[8,3072]{1,0:T(8,128)S(1)}, f32[8,3072]{1,0:T(8,128)S(1)}, u32[]{:S(2)}, u32[]{:S(2)}) collective-permute-start(f32[8,3072]{1,0:T(8,128)S(1)} %get-tuple-element.21), channel_id=1, source_target_pairs={{0,16},{1,17},{2,18},{3,19},{4,20},{5,21},{6,22},{7,23},{8,24},{9,... | collective-permute-start | bytes 294920 | tf_op jit(solution)/shard_map/ppermute | solution.py:256
  6.9 5.6 %collective-permute-start.3 = (f32[8,3072]{1,0:T(8,128)S(1)}, f32[8,3072]{1,0:T(8,128)S(1)}, u32[]{:S(2)}, u32[]{:S(2)}) collective-permute-start(f32[8,3072]{1,0:T(8,128)S(1)} %add.33), channel_id=1, source_target_pairs={{0,80},{1,19},{2,16},{3,83},{4,22},{5,85},{6,86},{7,21},{8,26},{9,... | collective-permute-start | bytes 294920 | tf_op jit(solution)/shard_map/ppermute | solution.py:256
  10.1 5.0 %collective-permute-start.2 = (f32[8,3072]{1,0:T(8,128)S(1)}, f32[8,3072]{1,0:T(8,128)S(1)}, u32[]{:S(2)}, u32[]{:S(2)}) collective-permute-start(f32[8,3072]{1,0:T(8,128)S(1)} %add.33), channel_id=1, source_target_pairs={{0,96},{1,2},{2,1},{3,99},{4,7},{5,101},{6,102},{7,4},{8,11},{9,10... | collective-permute-start | bytes 294920 | tf_op jit(solution)/shard_map/ppermute | solution.py:256
  11.0 4.3 %collective-permute-start.1 = (f32[8,3072]{1,0:T(8,128)S(1)}, f32[8,3072]{1,0:T(8,128)S(1)}, u32[]{:S(2)}, u32[]{:S(2)}) collective-permute-start(f32[8,3072]{1,0:T(8,128)S(1)} %add.33), channel_id=1, source_target_pairs={{0,48},{1,16},{2,19},{3,51},{4,21},{5,53},{6,54},{7,22},{8,25},{9,... | collective-permute-start | bytes 294920 | tf_op jit(solution)/shard_map/ppermute | solution.py:256
  15.4 6.6 %collective-permute-start.6 = (f32[8,3072]{1,0:T(8,128)S(1)}, f32[8,3072]{1,0:T(8,128)S(1)}, u32[]{:S(2)}, u32[]{:S(2)}) collective-permute-start(f32[8,3072]{1,0:T(8,128)S(1)} %add_add_fusion.2), channel_id=1, source_target_pairs={{0,18},{1,25},{2,26},{3,17},{4,28},{5,23},{6,20},{7,31},{8,16},{9,... | collective-permute-start | bytes 294920 | tf_op jit(solution)/shard_map/ppermute | solution.py:256
  19.7 4.7 %collective-permute-start.5 = (f32[8,3072]{1,0:T(8,128)S(1)}, f32[8,3072]{1,0:T(8,128)S(1)}, u32[]{:S(2)}, u32[]{:S(2)}) collective-permute-start(f32[8,3072]{1,0:T(8,128)S(1)} %add_add_fusion.2), channel_id=1, source_target_pairs={{0,3},{1,13},{2,14},{3,0},{4,8},{5,6},{6,5},{7,11},{8,4},{9,10},{1... | collective-permute-start | bytes 294920 | tf_op jit(solution)/shard_map/ppermute | solution.py:256
  20.1 4.2 %collective-permute-start.4 = (f32[8,3072]{1,0:T(8,128)S(1)}, f32[8,3072]{1,0:T(8,128)S(1)}, u32[]{:S(2)}, u32[]{:S(2)}) collective-permute-start(f32[8,3072]{1,0:T(8,128)S(1)} %add_add_fusion.2), channel_id=1, source_target_pairs={{0,17},{1,21},{2,22},{3,18},{4,16},{5,20},{6,23},{7,19},{8,28},{9,... | collective-permute-start | bytes 294920 | tf_op jit(solution)/shard_map/ppermute | solution.py:256
  24.4 5.8 %collective-permute-start.9 = (f32[8,3072]{1,0:T(8,128)S(1)}, f32[8,3072]{1,0:T(8,128)S(1)}, u32[]{:S(2)}, u32[]{:S(2)}) collective-permute-start(f32[8,3072]{1,0:T(8,128)S(1)} %add_add_fusion.1), channel_id=1, source_target_pairs={{0,24},{1,81},{2,82},{3,27},{4,84},{5,29},{6,30},{7,87},{8,88},{9,... | collective-permute-start | bytes 294920 | tf_op jit(solution)/shard_map/ppermute | solution.py:256
  27.9 5.0 %collective-permute-start.8 = (f32[8,3072]{1,0:T(8,128)S(1)}, f32[8,3072]{1,0:T(8,128)S(1)}, u32[]{:S(2)}, u32[]{:S(2)}) collective-permute-start(f32[8,3072]{1,0:T(8,128)S(1)} %add_add_fusion.1), channel_id=1, source_target_pairs={{0,12},{1,97},{2,98},{3,15},{4,100},{5,9},{6,10},{7,103},{8,104},{... | collective-permute-start | bytes 294920 | tf_op jit(solution)/shard_map/ppermute | solution.py:256
  28.7 4.3 %collective-permute-start.7 = (f32[8,3072]{1,0:T(8,128)S(1)}, f32[8,3072]{1,0:T(8,128)S(1)}, u32[]{:S(2)}, u32[]{:S(2)}) collective-permute-start(f32[8,3072]{1,0:T(8,128)S(1)} %add_add_fusion.1), channel_id=1, source_target_pairs={{0,20},{1,49},{2,50},{3,23},{4,52},{5,17},{6,18},{7,55},{8,56},{9,... | collective-permute-start | bytes 294920 | tf_op jit(solution)/shard_map/ppermute | solution.py:256
  33.0 1.9 %collective-permute-start.10 = (f32[8,3072]{1,0:T(8,128)S(1)}, f32[8,3072]{1,0:T(8,128)S(1)}, u32[]{:S(2)}, u32[]{:S(2)}) collective-permute-start(f32[8,3072]{1,0:T(8,128)S(1)} %add_add_fusion.own_ref.left_ref), channel_id=1, source_target_pairs={{0,16},{1,17},{2,18},{3,19},{4,20},{5,21},{6,22},{7,23},{8,24},{9,... | collective-permute-start | bytes 294920 | tf_op jit(solution)/shard_map/ppermute | solution.py:256
  34.0 7.8 %copy-start = (bf16[768,384]{1,0:T(8,128)(2,1)S(1)}, bf16[768,384]{1,0:T(8,128)(2,1)}, u32[]{:S(2)}) copy-start(bf16[768,384]{1,0:T(8,128)(2,1)} %refs_8_.1) | copy-start | bytes 1769476
  35.4 1.3 %collective-permute-start.11 = (f32[8,384]{1,0:T(8,128)S(1)}, f32[8,384]{1,0:T(8,128)S(1)}, u32[]{:S(2)}, u32[]{:S(2)}) collective-permute-start(f32[8,384]{1,0:T(8,128)S(1)} %right_other.1), channel_id=1, source_target_pairs={{0,16},{1,17},{2,18},{3,19},{4,20},{5,21},{6,22},{7,23},{8,24},{9,... | collective-permute-start | bytes 36872 | tf_op jit(solution)/shard_map/ppermute | solution.py:256
  36.7 4.8 %collective-permute-start.14 = (f32[8,384]{1,0:T(8,128)S(1)}, f32[8,384]{1,0:T(8,128)S(1)}, u32[]{:S(2)}, u32[]{:S(2)}) collective-permute-start(f32[8,384]{1,0:T(8,128)S(1)} %add.43.refs_4_), channel_id=1, source_target_pairs={{0,80},{1,81},{2,82},{3,83},{4,84},{5,85},{6,86},{7,87},{8,88},{9,... | collective-permute-start | bytes 36872 | tf_op jit(solution)/shard_map/ppermute | solution.py:256
  37.5 4.3 %collective-permute-start.13 = (f32[8,384]{1,0:T(8,128)S(1)}, f32[8,384]{1,0:T(8,128)S(1)}, u32[]{:S(2)}, u32[]{:S(2)}) collective-permute-start(f32[8,384]{1,0:T(8,128)S(1)} %add.43.refs_4_), channel_id=1, source_target_pairs={{0,112},{1,113},{2,114},{3,115},{4,116},{5,117},{6,118},{7,119},{8... | collective-permute-start | bytes 36872 | tf_op jit(solution)/shard_map/ppermute | solution.py:256
  38.6 3.2 %collective-permute-start.12 = (f32[8,384]{1,0:T(8,128)S(1)}, f32[8,384]{1,0:T(8,128)S(1)}, u32[]{:S(2)}, u32[]{:S(2)}) collective-permute-start(f32[8,384]{1,0:T(8,128)S(1)} %add.43.refs_4_), channel_id=1, source_target_pairs={{0,48},{1,49},{2,50},{3,51},{4,52},{5,53},{6,54},{7,55},{8,56},{9,... | collective-permute-start | bytes 36872 | tf_op jit(solution)/shard_map/ppermute | solution.py:256

commit v9 on v8

--- a/solution.py
+++ b/solution.py
@@ -11,6 +11,7 @@
 CHUNKS = 3
 CHUNK = HALF // CHUNKS
 WRITES = [(i * CHUNK, CHUNK) for i in range(2 * CHUNKS)]
+LANES = 128
 MIB = 1 << 20
 
 
@@ -141,7 +142,7 @@
     )(merged, left, *before)
 
 
-def basis_kernel(own_ref, other_ref, inverse_ref, basis_ref):
+def basis_kernel(replicas, own_ref, other_ref, inverse_ref, basis_ref):
     own, other = own_ref[...], other_ref[...]
     gram = jnp.zeros((RANK, RANK), F32)
     for part in (own, other):
@@ -158,7 +159,9 @@
         gram -= factor * gram[k : k + 1, :]
     pivots = jnp.sum(gram * eye, axis=1, keepdims=True)
     inverse = inverse / jnp.sqrt(pivots)
-    inverse_ref[...] = inverse
+    for k in range(RANK):
+        column = inverse[:, k : k + 1] * (1.0 / replicas)
+        inverse_ref[k * RANK : (k + 1) * RANK, :] = jnp.broadcast_to(column, (RANK, LANES))
     for part, start in ((own, 0), (other, HALF)):
         basis = jnp.zeros((RANK, HALF), F32)
         for k in range(RANK):
@@ -168,12 +171,15 @@
         basis_ref[start : start + HALF, :] = packed.T
 
 
-def make_basis(own, other):
-    return pl.pallas_call(
-        basis_kernel,
+def make_basis(replicas, own, other):
+    def body(*refs):
+        basis_kernel(replicas, *refs)
+
+    return pl.pallas_call(
+        body,
         in_specs=[whole(), whole()],
         out_specs=[whole(), whole()],
-        out_shape=[pltpu.VMEM((RANK, RANK), F32), pltpu.VMEM((ROWS, 4 * RANK), BF16)],
+        out_shape=[pltpu.VMEM((RANK * RANK, LANES), F32), pltpu.VMEM((ROWS, 4 * RANK), BF16)],
         compiler_params=pltpu.CompilerParams(vmem_limit_bytes=16 * MIB),
         cost_estimate=pl.CostEstimate(flops=4 * ROWS * RANK * RANK, bytes_accessed=4 * MIB, transcendentals=0),
         name="basis",
@@ -181,16 +187,18 @@
 
 
 def final_kernel(
-    replicas,
     own_ref, other_ref, basis_ref, inverse_ref, sum_ref, near_ref, wrap_ref, far_ref, mom_ref,
     fb_ref, mom_out_ref, right_ref,
     fb_buf, mom_buf, right_buf, fb_sem, mom_sem, right_sem,
 ):
     total = (sum_ref[...] + near_ref[...]) + (wrap_ref[...] + far_ref[...])
-    right = jnp.zeros((RANK, COLS), F32)
-    for k in range(RANK):
-        right += inverse_ref[:, k : k + 1] * total[k : k + 1, :]
-    right = right * (1.0 / replicas)
+    pieces = []
+    for start in range(0, COLS, LANES):
+        piece = jnp.zeros((RANK, LANES), F32)
+        for k in range(RANK):
+            piece += inverse_ref[k * RANK : (k + 1) * RANK, :] * total[k : k + 1, start : start + LANES]
+        pieces.append(piece)
+    right = jnp.concatenate(pieces, axis=1)
     right_buf[...] = right
     copies = [pltpu.make_async_copy(right_buf, right_ref, right_sem.at[0])]
     copies[0].start()
@@ -219,14 +227,10 @@
         copy.wait()
 
 
-def finish(replicas, merged_own, merged_other, basis, inverse, parts, momentum):
+def finish(merged_own, merged_other, basis, inverse, parts, momentum):
     mom_rows = momentum.shape[0]
-
-    def body(*refs):
-        final_kernel(replicas, *refs)
-
-    return pl.pallas_call(
-        body,
+    return pl.pallas_call(
+        final_kernel,
         in_specs=[whole()] * 9,
         out_specs=in_hbm(3),
         out_shape=[
@@ -279,12 +283,10 @@
         own = ring_sum(own, axes)
     other = sibling(own)
     term = right_term(merged_other, other, right_term(merged_own, own))
-    inverse, basis = make_basis(own, other)
+    inverse, basis = make_basis(lax.axis_size("replica"), own, other)
     term = term + sibling(term)
     parts = [term, *(swap(term, [steps * LOW["y"] | CORE] * 2) for steps in (1, 3, 2))]
-    feedback_out, momentum_out, right_t = finish(
-        lax.axis_size("replica"), merged_own, merged_other, basis, inverse, parts, momentum
-    )
+    feedback_out, momentum_out, right_t = finish(merged_own, merged_other, basis, inverse, parts, momentum)
     return feedback_out, momentum_out, right_t.T
 
 

time: 44.9 us -> 44.8 us (level)
  no operation moved by 1% of the time
where the time goes in v9:
time: 44.8 us; the launch traced here: 44.7 us
  starting transfers between devices  19.1 us (43%)
  waiting for transfers between devices  14.7 us (33%)
  Pallas kernels  10.2 us (23%)
  between operations  0.7 us (2%)
    ppermute x15, starting transfers between devices, swap(): return lax.ppermute(x, ('replica', 'tensor'), pairs)  19.1 us
    ppermute x15, waiting for transfers between devices, swap(): return lax.ppermute(x, ('replica', 'tensor'), pairs)  14.7 us
    pallas_call x1, Pallas kernels, merge_other(): pl.pallas_call(load_kernel, in_specs=in_hbm(3), out_specs=[whole()] * 5,...  3.9 us
    pallas_call x1, Pallas kernels, finish(): pl.pallas_call(final_kernel, in_specs=[whole()] * 9, out_specs=in_hbm(3),...  2.92 us
    pallas_call x1, Pallas kernels, make_basis(): pl.pallas_call(body, in_specs=[whole(), whole()], out_specs=[whole(), who...  1.66 us
    pallas_call x2, Pallas kernels, right_term(): pl.pallas_call(right_kernel, in_specs=[whole()] * (2 + len(before)), out_...  0.9 us
  transfers between devices with their start and end apart: 15, of which 12 were waited for; matrix products, arithmetic and copies ran while one was open for 0% of the time, Pallas kernels for 6%

profile of v9, /device:TPU:1, one launch (start us, length us, event | category | flops | bytes accessed | tf_op | source)
XLA Modules:
  0.0 44.7 jit_solution(7550058602354328323)
XLA Ops:
  0.6 3.9 %merge_other.1 = (bf16[3072,384]{1,0:T(8,128)(2,1)S(1)}, f32[8,3072]{1,0:T(8,128)S(1)}, bf16[3072,384]{1,0:T(8,128)(2,1)S(1)}, bf16[3072,384]{1,0:T(8,128)(2,1)S(1)}, f32[8,384]{1,0:T(8,128)S(1)}) custom-call(bf16[1,6144,384]{2,1,0:T(8,128)(2,1)} %g_ref.1, bf16[1,6144,384]{2,1,0:T(8,128)(2,1)} %f_ref.1, f32[8,384]{1,0:T(8,128)} %bitcast.2), custom_call_target="tpu_custom_call" | custom-call | flops 18874368 | bytes 9437184 | tf_op jit(solution)/shard_map/merge_other/pallas_call | solution.py:88
  4.5 1.4 %collective-permute-start = (f32[8,3072]{1,0:T(8,128)S(1)}, f32[8,3072]{1,0:T(8,128)S(1)}, u32[]{:S(2)}, u32[]{:S(2)}) collective-permute-start(f32[8,3072]{1,0:T(8,128)S(1)} %get-tuple-element.21), channel_id=1, source_target_pairs={{0,16},{1,17},{2,18},{3,19},{4,20},{5,21},{6,22},{7,23},{8,24},{9,... | collective-permute-start | bytes 294920 | tf_op jit(solution)/shard_map/ppermute | solution.py:260
  6.0 0.8 %merge_own.1 = (bf16[3072,384]{1,0:T(8,128)(2,1)S(1)}, f32[8,3072]{1,0:T(8,128)S(1)}) custom-call(bf16[3072,384]{1,0:T(8,128)(2,1)S(1)} %get-tuple-element.15.g_ref, bf16[3072,384]{1,0:T(8,128)(2,1)S(1)} %get-tuple-element.16.f_ref, f32[8,384]{1,0:T(8,128)S(1)} %get-tuple-element.17.q_ref), custom_call_target="tpu_custom_call" | custom-call | flops 18874368 | bytes 4718592 | tf_op jit(solution)/shard_map/merge_own/pallas_call | solution.py:113
  6.9 3.2 %collective-permute-start.3 = (f32[8,3072]{1,0:T(8,128)S(1)}, f32[8,3072]{1,0:T(8,128)S(1)}, u32[]{:S(2)}, u32[]{:S(2)}) collective-permute-start(f32[8,3072]{1,0:T(8,128)S(1)} %add.33), channel_id=1, source_target_pairs={{0,80},{1,19},{2,16},{3,83},{4,22},{5,85},{6,86},{7,21},{8,26},{9,... | collective-permute-start | bytes 294920 | tf_op jit(solution)/shard_map/ppermute | solution.py:260
  10.1 0.9 %collective-permute-start.2 = (f32[8,3072]{1,0:T(8,128)S(1)}, f32[8,3072]{1,0:T(8,128)S(1)}, u32[]{:S(2)}, u32[]{:S(2)}) collective-permute-start(f32[8,3072]{1,0:T(8,128)S(1)} %add.33), channel_id=1, source_target_pairs={{0,96},{1,2},{2,1},{3,99},{4,7},{5,101},{6,102},{7,4},{8,11},{9,10... | collective-permute-start | bytes 294920 | tf_op jit(solution)/shard_map/ppermute | solution.py:260
  11.0 1.6 %collective-permute-done.3 = f32[8,3072]{1,0:T(8,128)S(1)} collective-permute-done((f32[8,3072]{1,0:T(8,128)S(1)}, f32[8,3072]{1,0:T(8,128)S(1)}, u32[]{:S(2)}, u32[]{:S(2)}) %collective-permute-start.3) | collective-permute-done | bytes 98336 | tf_op jit(solution)/shard_map/ppermute | solution.py:260
  12.6 2.5 %collective-permute-done.2 = f32[8,3072]{1,0:T(8,128)S(1)} collective-permute-done((f32[8,3072]{1,0:T(8,128)S(1)}, f32[8,3072]{1,0:T(8,128)S(1)}, u32[]{:S(2)}, u32[]{:S(2)}) %collective-permute-start.2) | collective-permute-done | bytes 98336 | tf_op jit(solution)/shard_map/ppermute | solution.py:260
  15.4 4.3 %collective-permute-start.6 = (f32[8,3072]{1,0:T(8,128)S(1)}, f32[8,3072]{1,0:T(8,128)S(1)}, u32[]{:S(2)}, u32[]{:S(2)}) collective-permute-start(f32[8,3072]{1,0:T(8,128)S(1)} %add_add_fusion.2), channel_id=1, source_target_pairs={{0,18},{1,25},{2,26},{3,17},{4,28},{5,23},{6,20},{7,31},{8,16},{9,... | collective-permute-start | bytes 294920 | tf_op jit(solution)/shard_map/ppermute | solution.py:260
  20.1 1.9 %collective-permute-done.6 = f32[8,3072]{1,0:T(8,128)S(1)} collective-permute-done((f32[8,3072]{1,0:T(8,128)S(1)}, f32[8,3072]{1,0:T(8,128)S(1)}, u32[]{:S(2)}, u32[]{:S(2)}) %collective-permute-start.6) | collective-permute-done | bytes 98336 | tf_op jit(solution)/shard_map/ppermute | solution.py:260
  22.0 2.4 %collective-permute-done.5 = f32[8,3072]{1,0:T(8,128)S(1)} collective-permute-done((f32[8,3072]{1,0:T(8,128)S(1)}, f32[8,3072]{1,0:T(8,128)S(1)}, u32[]{:S(2)}, u32[]{:S(2)}) %collective-permute-start.5) | collective-permute-done | bytes 98336 | tf_op jit(solution)/shard_map/ppermute | solution.py:260
  24.4 3.5 %collective-permute-start.9 = (f32[8,3072]{1,0:T(8,128)S(1)}, f32[8,3072]{1,0:T(8,128)S(1)}, u32[]{:S(2)}, u32[]{:S(2)}) collective-permute-start(f32[8,3072]{1,0:T(8,128)S(1)} %add_add_fusion.1), channel_id=1, source_target_pairs={{0,24},{1,81},{2,82},{3,27},{4,84},{5,29},{6,30},{7,87},{8,88},{9,... | collective-permute-start | bytes 294920 | tf_op jit(solution)/shard_map/ppermute | solution.py:260
  27.9 0.8 %collective-permute-start.8 = (f32[8,3072]{1,0:T(8,128)S(1)}, f32[8,3072]{1,0:T(8,128)S(1)}, u32[]{:S(2)}, u32[]{:S(2)}) collective-permute-start(f32[8,3072]{1,0:T(8,128)S(1)} %add_add_fusion.1), channel_id=1, source_target_pairs={{0,12},{1,97},{2,98},{3,15},{4,100},{5,9},{6,10},{7,103},{8,104},{... | collective-permute-start | bytes 294920 | tf_op jit(solution)/shard_map/ppermute | solution.py:260
  28.7 1.5 %collective-permute-done.9 = f32[8,3072]{1,0:T(8,128)S(1)} collective-permute-done((f32[8,3072]{1,0:T(8,128)S(1)}, f32[8,3072]{1,0:T(8,128)S(1)}, u32[]{:S(2)}, u32[]{:S(2)}) %collective-permute-start.9) | collective-permute-done | bytes 98336 | tf_op jit(solution)/shard_map/ppermute | solution.py:260
  30.2 2.7 %collective-permute-done.8 = f32[8,3072]{1,0:T(8,128)S(1)} collective-permute-done((f32[8,3072]{1,0:T(8,128)S(1)}, f32[8,3072]{1,0:T(8,128)S(1)}, u32[]{:S(2)}, u32[]{:S(2)}) %collective-permute-start.8) | collective-permute-done | bytes 98336 | tf_op jit(solution)/shard_map/ppermute | solution.py:260
  33.0 1.0 %collective-permute-start.10 = (f32[8,3072]{1,0:T(8,128)S(1)}, f32[8,3072]{1,0:T(8,128)S(1)}, u32[]{:S(2)}, u32[]{:S(2)}) collective-permute-start(f32[8,3072]{1,0:T(8,128)S(1)} %add_add_fusion.refs_0_.left_ref), channel_id=1, source_target_pairs={{0,16},{1,17},{2,18},{3,19},{4,20},{5,21},{6,22},{7,23},{8,24},{9,... | collective-permute-start | bytes 294920 | tf_op jit(solution)/shard_map/ppermute | solution.py:260
  34.0 0.4 right_own.1.refs_0_
  34.4 0.5 %collective-permute-done.10.refs_1_.left_ref = f32[8,3072]{1,0:T(8,128)S(1)} collective-permute-done((f32[8,3072]{1,0:T(8,128)S(1)}, f32[8,3072]{1,0:T(8,128)S(1)}, u32[]{:S(2)}, u32[]{:S(2)}) %collective-permute-start.10) | collective-permute-done | bytes 98336 | tf_op jit(solution)/shard_map/ppermute | solution.py:260
  34.9 0.5 %right_other.1 = f32[8,384]{1,0:T(8,128)S(1)} custom-call(bf16[3072,384]{1,0:T(8,128)(2,1)S(1)} %get-tuple-element.19.merged_ref.other_ref, f32[8,3072]{1,0:T(8,128)S(1)} %collective-permute-done.10.refs_1_.left_ref, f32[8,384]{1,0:T(8,128)S(1)} %right_own.1.refs_0_), custom_call_target="tpu_custom_call" | custom-call | flops 37748736 | bytes 2359296 | tf_op jit(solution)/shard_map/right_other/pallas_call | solution.py:134
  35.8 0.8 %collective-permute-done.11 = f32[8,384]{1,0:T(8,128)S(1)} collective-permute-done((f32[8,384]{1,0:T(8,128)S(1)}, f32[8,384]{1,0:T(8,128)S(1)}, u32[]{:S(2)}, u32[]{:S(2)}) %collective-permute-start.11) | collective-permute-done | bytes 12320 | tf_op jit(solution)/shard_map/ppermute | solution.py:260
  36.7 0.8 %collective-permute-start.14 = (f32[8,384]{1,0:T(8,128)S(1)}, f32[8,384]{1,0:T(8,128)S(1)}, u32[]{:S(2)}, u32[]{:S(2)}) collective-permute-start(f32[8,384]{1,0:T(8,128)S(1)} %add.43.sum_ref), channel_id=1, source_target_pairs={{0,80},{1,81},{2,82},{3,83},{4,84},{5,85},{6,86},{7,87},{8,88},{9,... | collective-permute-start | bytes 36872 | tf_op jit(solution)/shard_map/ppermute | solution.py:260
  37.5 1.1 %collective-permute-start.13 = (f32[8,384]{1,0:T(8,128)S(1)}, f32[8,384]{1,0:T(8,128)S(1)}, u32[]{:S(2)}, u32[]{:S(2)}) collective-permute-start(f32[8,384]{1,0:T(8,128)S(1)} %add.43.sum_ref), channel_id=1, source_target_pairs={{0,112},{1,113},{2,114},{3,115},{4,116},{5,117},{6,118},{7,119},{8... | collective-permute-start | bytes 36872 | tf_op jit(solution)/shard_map/ppermute | solution.py:260
  38.6 1.2 %collective-permute-start.12 = (f32[8,384]{1,0:T(8,128)S(1)}, f32[8,384]{1,0:T(8,128)S(1)}, u32[]{:S(2)}, u32[]{:S(2)}) collective-permute-start(f32[8,384]{1,0:T(8,128)S(1)} %add.43.sum_ref), channel_id=1, source_target_pairs={{0,48},{1,49},{2,50},{3,51},{4,52},{5,53},{6,54},{7,55},{8,56},{9,... | collective-permute-start | bytes 36872 | tf_op jit(solution)/shard_map/ppermute | solution.py:260
  39.8 1.7 %basis.1 = (f32[64,128]{1,0:T(8,128)S(1)}, bf16[6144,32]{1,0:T(8,128)(2,1)S(1)}) custom-call(f32[8,3072]{1,0:T(8,128)S(1)} %add_add_fusion.refs_0_.left_ref, f32[8,3072]{1,0:T(8,128)S(1)} %collective-permute-done.10.refs_1_.left_ref), custom_call_target="tpu_custom_call" | custom-call | flops 1572864 | bytes 4194304 | tf_op jit(solution)/shard_map/basis/pallas_call | solution.py:178
  41.8 2.9 %finish.1 = (bf16[1,6144,384]{2,1,0:T(8,128)(2,1)}, bf16[768,384]{1,0:T(8,128)(2,1)}, f32[8,384]{1,0:T(8,128)}) custom-call(bf16[3072,384]{1,0:T(8,128)(2,1)S(1)} %get-tuple-element.18.merged_ref.own_ref, bf16[3072,384]{1,0:T(8,128)(2,1)S(1)} %get-tuple-element.19.merged_ref.other_ref, bf16[6144,32]{1,0:T(8,128)(2,1)S(1)} %get-tuple-element.22.basis_ref, ...), custom_call_target="tpu_custom_call" | custom-call | flops 150994944 | bytes 9437184 | tf_op jit(solution)/shard_map/finish/pallas_call | solution.py:232
  (19 shorter events, 1.8 us)
Async XLA Ops:
  4.5 2.4 %collective-permute-start = (f32[8,3072]{1,0:T(8,128)S(1)}, f32[8,3072]{1,0:T(8,128)S(1)}, u32[]{:S(2)}, u32[]{:S(2)}) collective-permute-start(f32[8,3072]{1,0:T(8,128)S(1)} %get-tuple-element.21), channel_id=1, source_target_pairs={{0,16},{1,17},{2,18},{3,19},{4,20},{5,21},{6,22},{7,23},{8,24},{9,... | collective-permute-start | bytes 294920 | tf_op jit(solution)/shard_map/ppermute | solution.py:260
  6.9 5.6 %collective-permute-start.3 = (f32[8,3072]{1,0:T(8,128)S(1)}, f32[8,3072]{1,0:T(8,128)S(1)}, u32[]{:S(2)}, u32[]{:S(2)}) collective-permute-start(f32[8,3072]{1,0:T(8,128)S(1)} %add.33), channel_id=1, source_target_pairs={{0,80},{1,19},{2,16},{3,83},{4,22},{5,85},{6,86},{7,21},{8,26},{9,... | collective-permute-start | bytes 294920 | tf_op jit(solution)/shard_map/ppermute | solution.py:260
  10.1 5.0 %collective-permute-start.2 = (f32[8,3072]{1,0:T(8,128)S(1)}, f32[8,3072]{1,0:T(8,128)S(1)}, u32[]{:S(2)}, u32[]{:S(2)}) collective-permute-start(f32[8,3072]{1,0:T(8,128)S(1)} %add.33), channel_id=1, source_target_pairs={{0,96},{1,2},{2,1},{3,99},{4,7},{5,101},{6,102},{7,4},{8,11},{9,10... | collective-permute-start | bytes 294920 | tf_op jit(solution)/shard_map/ppermute | solution.py:260
  11.0 4.3 %collective-permute-start.1 = (f32[8,3072]{1,0:T(8,128)S(1)}, f32[8,3072]{1,0:T(8,128)S(1)}, u32[]{:S(2)}, u32[]{:S(2)}) collective-permute-start(f32[8,3072]{1,0:T(8,128)S(1)} %add.33), channel_id=1, source_target_pairs={{0,48},{1,16},{2,19},{3,51},{4,21},{5,53},{6,54},{7,22},{8,25},{9,... | collective-permute-start | bytes 294920 | tf_op jit(solution)/shard_map/ppermute | solution.py:260
  15.4 6.6 %collective-permute-start.6 = (f32[8,3072]{1,0:T(8,128)S(1)}, f32[8,3072]{1,0:T(8,128)S(1)}, u32[]{:S(2)}, u32[]{:S(2)}) collective-permute-start(f32[8,3072]{1,0:T(8,128)S(1)} %add_add_fusion.2), channel_id=1, source_target_pairs={{0,18},{1,25},{2,26},{3,17},{4,28},{5,23},{6,20},{7,31},{8,16},{9,... | collective-permute-start | bytes 294920 | tf_op jit(solution)/shard_map/ppermute | solution.py:260
  19.7 4.7 %collective-permute-start.5 = (f32[8,3072]{1,0:T(8,128)S(1)}, f32[8,3072]{1,0:T(8,128)S(1)}, u32[]{:S(2)}, u32[]{:S(2)}) collective-permute-start(f32[8,3072]{1,0:T(8,128)S(1)} %add_add_fusion.2), channel_id=1, source_target_pairs={{0,3},{1,13},{2,14},{3,0},{4,8},{5,6},{6,5},{7,11},{8,4},{9,10},{1... | collective-permute-start | bytes 294920 | tf_op jit(solution)/shard_map/ppermute | solution.py:260
  20.1 4.2 %collective-permute-start.4 = (f32[8,3072]{1,0:T(8,128)S(1)}, f32[8,3072]{1,0:T(8,128)S(1)}, u32[]{:S(2)}, u32[]{:S(2)}) collective-permute-start(f32[8,3072]{1,0:T(8,128)S(1)} %add_add_fusion.2), channel_id=1, source_target_pairs={{0,17},{1,21},{2,22},{3,18},{4,16},{5,20},{6,23},{7,19},{8,28},{9,... | collective-permute-start | bytes 294920 | tf_op jit(solution)/shard_map/ppermute | solution.py:260
  24.4 5.8 %collective-permute-start.9 = (f32[8,3072]{1,0:T(8,128)S(1)}, f32[8,3072]{1,0:T(8,128)S(1)}, u32[]{:S(2)}, u32[]{:S(2)}) collective-permute-start(f32[8,3072]{1,0:T(8,128)S(1)} %add_add_fusion.1), channel_id=1, source_target_pairs={{0,24},{1,81},{2,82},{3,27},{4,84},{5,29},{6,30},{7,87},{8,88},{9,... | collective-permute-start | bytes 294920 | tf_op jit(solution)/shard_map/ppermute | solution.py:260
  27.9 5.0 %collective-permute-start.8 = (f32[8,3072]{1,0:T(8,128)S(1)}, f32[8,3072]{1,0:T(8,128)S(1)}, u32[]{:S(2)}, u32[]{:S(2)}) collective-permute-start(f32[8,3072]{1,0:T(8,128)S(1)} %add_add_fusion.1), channel_id=1, source_target_pairs={{0,12},{1,97},{2,98},{3,15},{4,100},{5,9},{6,10},{7,103},{8,104},{... | collective-permute-start | bytes 294920 | tf_op jit(solution)/shard_map/ppermute | solution.py:260
  28.7 4.3 %collective-permute-start.7 = (f32[8,3072]{1,0:T(8,128)S(1)}, f32[8,3072]{1,0:T(8,128)S(1)}, u32[]{:S(2)}, u32[]{:S(2)}) collective-permute-start(f32[8,3072]{1,0:T(8,128)S(1)} %add_add_fusion.1), channel_id=1, source_target_pairs={{0,20},{1,49},{2,50},{3,23},{4,52},{5,17},{6,18},{7,55},{8,56},{9,... | collective-permute-start | bytes 294920 | tf_op jit(solution)/shard_map/ppermute | solution.py:260
  33.0 1.9 %collective-permute-start.10 = (f32[8,3072]{1,0:T(8,128)S(1)}, f32[8,3072]{1,0:T(8,128)S(1)}, u32[]{:S(2)}, u32[]{:S(2)}) collective-permute-start(f32[8,3072]{1,0:T(8,128)S(1)} %add_add_fusion.refs_0_.left_ref), channel_id=1, source_target_pairs={{0,16},{1,17},{2,18},{3,19},{4,20},{5,21},{6,22},{7,23},{8,24},{9,... | collective-permute-start | bytes 294920 | tf_op jit(solution)/shard_map/ppermute | solution.py:260
  34.0 7.8 %copy-start = (bf16[768,384]{1,0:T(8,128)(2,1)S(1)}, bf16[768,384]{1,0:T(8,128)(2,1)}, u32[]{:S(2)}) copy-start(bf16[768,384]{1,0:T(8,128)(2,1)} %mom_ref.1) | copy-start | bytes 1769476
  35.4 1.3 %collective-permute-start.11 = (f32[8,384]{1,0:T(8,128)S(1)}, f32[8,384]{1,0:T(8,128)S(1)}, u32[]{:S(2)}, u32[]{:S(2)}) collective-permute-start(f32[8,384]{1,0:T(8,128)S(1)} %right_other.1), channel_id=1, source_target_pairs={{0,16},{1,17},{2,18},{3,19},{4,20},{5,21},{6,22},{7,23},{8,24},{9,... | collective-permute-start | bytes 36872 | tf_op jit(solution)/shard_map/ppermute | solution.py:260
  36.7 4.8 %collective-permute-start.14 = (f32[8,384]{1,0:T(8,128)S(1)}, f32[8,384]{1,0:T(8,128)S(1)}, u32[]{:S(2)}, u32[]{:S(2)}) collective-permute-start(f32[8,384]{1,0:T(8,128)S(1)} %add.43.sum_ref), channel_id=1, source_target_pairs={{0,80},{1,81},{2,82},{3,83},{4,84},{5,85},{6,86},{7,87},{8,88},{9,... | collective-permute-start | bytes 36872 | tf_op jit(solution)/shard_map/ppermute | solution.py:260
  37.5 4.3 %collective-permute-start.13 = (f32[8,384]{1,0:T(8,128)S(1)}, f32[8,384]{1,0:T(8,128)S(1)}, u32[]{:S(2)}, u32[]{:S(2)}) collective-permute-start(f32[8,384]{1,0:T(8,128)S(1)} %add.43.sum_ref), channel_id=1, source_target_pairs={{0,112},{1,113},{2,114},{3,115},{4,116},{5,117},{6,118},{7,119},{8... | collective-permute-start | bytes 36872 | tf_op jit(solution)/shard_map/ppermute | solution.py:260
  38.6 3.2 %collective-permute-start.12 = (f32[8,384]{1,0:T(8,128)S(1)}, f32[8,384]{1,0:T(8,128)S(1)}, u32[]{:S(2)}, u32[]{:S(2)}) collective-permute-start(f32[8,384]{1,0:T(8,128)S(1)} %add.43.sum_ref), channel_id=1, source_target_pairs={{0,48},{1,49},{2,50},{3,51},{4,52},{5,53},{6,54},{7,55},{8,56},{9,... | collective-permute-start | bytes 36872 | tf_op jit(solution)/shard_map/ppermute | solution.py:260

commit v10 on v9

--- a/solution.py
+++ b/solution.py
@@ -10,7 +10,7 @@
 HALF = ROWS // 2
 CHUNKS = 3
 CHUNK = HALF // CHUNKS
-WRITES = [(i * CHUNK, CHUNK) for i in range(2 * CHUNKS)]
+WRITES = [(start, HALF // 4) for start in range(0, ROWS, HALF // 4)]
 LANES = 128
 MIB = 1 << 20
 

time: 44.8 us -> 44.8 us (level)
  no operation moved by 1% of the time
where the time goes in v10:
time: 44.8 us; the launch traced here: 44.7 us
  starting transfers between devices  19.1 us (43%)
  waiting for transfers between devices  14.7 us (33%)
  Pallas kernels  10.1 us (23%)
  between operations  0.7 us (2%)
    ppermute x15, starting transfers between devices, swap(): return lax.ppermute(x, ('replica', 'tensor'), pairs)  19.1 us
    ppermute x15, waiting for transfers between devices, swap(): return lax.ppermute(x, ('replica', 'tensor'), pairs)  14.7 us
    pallas_call x1, Pallas kernels, merge_other(): pl.pallas_call(load_kernel, in_specs=in_hbm(3), out_specs=[whole()] * 5,...  3.9 us
    pallas_call x1, Pallas kernels, finish(): pl.pallas_call(final_kernel, in_specs=[whole()] * 9, out_specs=in_hbm(3),...  2.89 us
    pallas_call x1, Pallas kernels, make_basis(): pl.pallas_call(body, in_specs=[whole(), whole()], out_specs=[whole(), who...  1.66 us
    pallas_call x2, Pallas kernels, right_term(): pl.pallas_call(right_kernel, in_specs=[whole()] * (2 + len(before)), out_...  0.9 us
  transfers between devices with their start and end apart: 15, of which 12 were waited for; matrix products, arithmetic and copies ran while one was open for 0% of the time, Pallas kernels for 6%

profile of v10, /device:TPU:1, one launch (start us, length us, event | category | flops | bytes accessed | tf_op | source)
XLA Modules:
  0.0 44.7 jit_solution(10798177461091290573)
XLA Ops:
  0.6 3.9 %merge_other.1 = (bf16[3072,384]{1,0:T(8,128)(2,1)S(1)}, f32[8,3072]{1,0:T(8,128)S(1)}, bf16[3072,384]{1,0:T(8,128)(2,1)S(1)}, bf16[3072,384]{1,0:T(8,128)(2,1)S(1)}, f32[8,384]{1,0:T(8,128)S(1)}) custom-call(bf16[1,6144,384]{2,1,0:T(8,128)(2,1)} %g_ref.1, bf16[1,6144,384]{2,1,0:T(8,128)(2,1)} %f_ref.1, f32[8,384]{1,0:T(8,128)} %bitcast.2), custom_call_target="tpu_custom_call" | custom-call | flops 18874368 | bytes 9437184 | tf_op jit(solution)/shard_map/merge_other/pallas_call | solution.py:88
  4.5 1.4 %collective-permute-start = (f32[8,3072]{1,0:T(8,128)S(1)}, f32[8,3072]{1,0:T(8,128)S(1)}, u32[]{:S(2)}, u32[]{:S(2)}) collective-permute-start(f32[8,3072]{1,0:T(8,128)S(1)} %get-tuple-element.21), channel_id=1, source_target_pairs={{0,16},{1,17},{2,18},{3,19},{4,20},{5,21},{6,22},{7,23},{8,24},{9,... | collective-permute-start | bytes 294920 | tf_op jit(solution)/shard_map/ppermute | solution.py:260
  6.0 0.8 %merge_own.1 = (bf16[3072,384]{1,0:T(8,128)(2,1)S(1)}, f32[8,3072]{1,0:T(8,128)S(1)}) custom-call(bf16[3072,384]{1,0:T(8,128)(2,1)S(1)} %get-tuple-element.15.g_ref, bf16[3072,384]{1,0:T(8,128)(2,1)S(1)} %get-tuple-element.16.f_ref, f32[8,384]{1,0:T(8,128)S(1)} %get-tuple-element.17.q_ref), custom_call_target="tpu_custom_call" | custom-call | flops 18874368 | bytes 4718592 | tf_op jit(solution)/shard_map/merge_own/pallas_call | solution.py:113
  6.9 3.2 %collective-permute-start.3 = (f32[8,3072]{1,0:T(8,128)S(1)}, f32[8,3072]{1,0:T(8,128)S(1)}, u32[]{:S(2)}, u32[]{:S(2)}) collective-permute-start(f32[8,3072]{1,0:T(8,128)S(1)} %add.33), channel_id=1, source_target_pairs={{0,80},{1,19},{2,16},{3,83},{4,22},{5,85},{6,86},{7,21},{8,26},{9,... | collective-permute-start | bytes 294920 | tf_op jit(solution)/shard_map/ppermute | solution.py:260
  10.1 0.9 %collective-permute-start.2 = (f32[8,3072]{1,0:T(8,128)S(1)}, f32[8,3072]{1,0:T(8,128)S(1)}, u32[]{:S(2)}, u32[]{:S(2)}) collective-permute-start(f32[8,3072]{1,0:T(8,128)S(1)} %add.33), channel_id=1, source_target_pairs={{0,96},{1,2},{2,1},{3,99},{4,7},{5,101},{6,102},{7,4},{8,11},{9,10... | collective-permute-start | bytes 294920 | tf_op jit(solution)/shard_map/ppermute | solution.py:260
  11.0 1.6 %collective-permute-done.3 = f32[8,3072]{1,0:T(8,128)S(1)} collective-permute-done((f32[8,3072]{1,0:T(8,128)S(1)}, f32[8,3072]{1,0:T(8,128)S(1)}, u32[]{:S(2)}, u32[]{:S(2)}) %collective-permute-start.3) | collective-permute-done | bytes 98336 | tf_op jit(solution)/shard_map/ppermute | solution.py:260
  12.6 2.5 %collective-permute-done.2 = f32[8,3072]{1,0:T(8,128)S(1)} collective-permute-done((f32[8,3072]{1,0:T(8,128)S(1)}, f32[8,3072]{1,0:T(8,128)S(1)}, u32[]{:S(2)}, u32[]{:S(2)}) %collective-permute-start.2) | collective-permute-done | bytes 98336 | tf_op jit(solution)/shard_map/ppermute | solution.py:260
  15.4 4.3 %collective-permute-start.6 = (f32[8,3072]{1,0:T(8,128)S(1)}, f32[8,3072]{1,0:T(8,128)S(1)}, u32[]{:S(2)}, u32[]{:S(2)}) collective-permute-start(f32[8,3072]{1,0:T(8,128)S(1)} %add_add_fusion.2), channel_id=1, source_target_pairs={{0,18},{1,25},{2,26},{3,17},{4,28},{5,23},{6,20},{7,31},{8,16},{9,... | collective-permute-start | bytes 294920 | tf_op jit(solution)/shard_map/ppermute | solution.py:260
  20.1 1.9 %collective-permute-done.6 = f32[8,3072]{1,0:T(8,128)S(1)} collective-permute-done((f32[8,3072]{1,0:T(8,128)S(1)}, f32[8,3072]{1,0:T(8,128)S(1)}, u32[]{:S(2)}, u32[]{:S(2)}) %collective-permute-start.6) | collective-permute-done | bytes 98336 | tf_op jit(solution)/shard_map/ppermute | solution.py:260
  22.0 2.4 %collective-permute-done.5 = f32[8,3072]{1,0:T(8,128)S(1)} collective-permute-done((f32[8,3072]{1,0:T(8,128)S(1)}, f32[8,3072]{1,0:T(8,128)S(1)}, u32[]{:S(2)}, u32[]{:S(2)}) %collective-permute-start.5) | collective-permute-done | bytes 98336 | tf_op jit(solution)/shard_map/ppermute | solution.py:260
  24.4 3.5 %collective-permute-start.9 = (f32[8,3072]{1,0:T(8,128)S(1)}, f32[8,3072]{1,0:T(8,128)S(1)}, u32[]{:S(2)}, u32[]{:S(2)}) collective-permute-start(f32[8,3072]{1,0:T(8,128)S(1)} %add_add_fusion.1), channel_id=1, source_target_pairs={{0,24},{1,81},{2,82},{3,27},{4,84},{5,29},{6,30},{7,87},{8,88},{9,... | collective-permute-start | bytes 294920 | tf_op jit(solution)/shard_map/ppermute | solution.py:260
  27.9 0.8 %collective-permute-start.8 = (f32[8,3072]{1,0:T(8,128)S(1)}, f32[8,3072]{1,0:T(8,128)S(1)}, u32[]{:S(2)}, u32[]{:S(2)}) collective-permute-start(f32[8,3072]{1,0:T(8,128)S(1)} %add_add_fusion.1), channel_id=1, source_target_pairs={{0,12},{1,97},{2,98},{3,15},{4,100},{5,9},{6,10},{7,103},{8,104},{... | collective-permute-start | bytes 294920 | tf_op jit(solution)/shard_map/ppermute | solution.py:260
  28.7 1.5 %collective-permute-done.9 = f32[8,3072]{1,0:T(8,128)S(1)} collective-permute-done((f32[8,3072]{1,0:T(8,128)S(1)}, f32[8,3072]{1,0:T(8,128)S(1)}, u32[]{:S(2)}, u32[]{:S(2)}) %collective-permute-start.9) | collective-permute-done | bytes 98336 | tf_op jit(solution)/shard_map/ppermute | solution.py:260
  30.2 2.7 %collective-permute-done.8 = f32[8,3072]{1,0:T(8,128)S(1)} collective-permute-done((f32[8,3072]{1,0:T(8,128)S(1)}, f32[8,3072]{1,0:T(8,128)S(1)}, u32[]{:S(2)}, u32[]{:S(2)}) %collective-permute-start.8) | collective-permute-done | bytes 98336 | tf_op jit(solution)/shard_map/ppermute | solution.py:260
  33.0 1.0 %collective-permute-start.10 = (f32[8,3072]{1,0:T(8,128)S(1)}, f32[8,3072]{1,0:T(8,128)S(1)}, u32[]{:S(2)}, u32[]{:S(2)}) collective-permute-start(f32[8,3072]{1,0:T(8,128)S(1)} %add_add_fusion.refs_0_.left_ref), channel_id=1, source_target_pairs={{0,16},{1,17},{2,18},{3,19},{4,20},{5,21},{6,22},{7,23},{8,24},{9,... | collective-permute-start | bytes 294920 | tf_op jit(solution)/shard_map/ppermute | solution.py:260
  34.0 0.4 right_own.1.refs_0_
  34.4 0.5 %collective-permute-done.10.refs_1_.left_ref = f32[8,3072]{1,0:T(8,128)S(1)} collective-permute-done((f32[8,3072]{1,0:T(8,128)S(1)}, f32[8,3072]{1,0:T(8,128)S(1)}, u32[]{:S(2)}, u32[]{:S(2)}) %collective-permute-start.10) | collective-permute-done | bytes 98336 | tf_op jit(solution)/shard_map/ppermute | solution.py:260
  34.9 0.5 %right_other.1 = f32[8,384]{1,0:T(8,128)S(1)} custom-call(bf16[3072,384]{1,0:T(8,128)(2,1)S(1)} %get-tuple-element.19.merged_ref.other_ref, f32[8,3072]{1,0:T(8,128)S(1)} %collective-permute-done.10.refs_1_.left_ref, f32[8,384]{1,0:T(8,128)S(1)} %right_own.1.refs_0_), custom_call_target="tpu_custom_call" | custom-call | flops 37748736 | bytes 2359296 | tf_op jit(solution)/shard_map/right_other/pallas_call | solution.py:134
  35.8 0.8 %collective-permute-done.11 = f32[8,384]{1,0:T(8,128)S(1)} collective-permute-done((f32[8,384]{1,0:T(8,128)S(1)}, f32[8,384]{1,0:T(8,128)S(1)}, u32[]{:S(2)}, u32[]{:S(2)}) %collective-permute-start.11) | collective-permute-done | bytes 12320 | tf_op jit(solution)/shard_map/ppermute | solution.py:260
  36.7 0.8 %collective-permute-start.14 = (f32[8,384]{1,0:T(8,128)S(1)}, f32[8,384]{1,0:T(8,128)S(1)}, u32[]{:S(2)}, u32[]{:S(2)}) collective-permute-start(f32[8,384]{1,0:T(8,128)S(1)} %add.43.sum_ref), channel_id=1, source_target_pairs={{0,80},{1,81},{2,82},{3,83},{4,84},{5,85},{6,86},{7,87},{8,88},{9,... | collective-permute-start | bytes 36872 | tf_op jit(solution)/shard_map/ppermute | solution.py:260
  37.5 1.1 %collective-permute-start.13 = (f32[8,384]{1,0:T(8,128)S(1)}, f32[8,384]{1,0:T(8,128)S(1)}, u32[]{:S(2)}, u32[]{:S(2)}) collective-permute-start(f32[8,384]{1,0:T(8,128)S(1)} %add.43.sum_ref), channel_id=1, source_target_pairs={{0,112},{1,113},{2,114},{3,115},{4,116},{5,117},{6,118},{7,119},{8... | collective-permute-start | bytes 36872 | tf_op jit(solution)/shard_map/ppermute | solution.py:260
  38.6 1.2 %collective-permute-start.12 = (f32[8,384]{1,0:T(8,128)S(1)}, f32[8,384]{1,0:T(8,128)S(1)}, u32[]{:S(2)}, u32[]{:S(2)}) collective-permute-start(f32[8,384]{1,0:T(8,128)S(1)} %add.43.sum_ref), channel_id=1, source_target_pairs={{0,48},{1,49},{2,50},{3,51},{4,52},{5,53},{6,54},{7,55},{8,56},{9,... | collective-permute-start | bytes 36872 | tf_op jit(solution)/shard_map/ppermute | solution.py:260
  39.8 1.7 %basis.1 = (f32[64,128]{1,0:T(8,128)S(1)}, bf16[6144,32]{1,0:T(8,128)(2,1)S(1)}) custom-call(f32[8,3072]{1,0:T(8,128)S(1)} %add_add_fusion.refs_0_.left_ref, f32[8,3072]{1,0:T(8,128)S(1)} %collective-permute-done.10.refs_1_.left_ref), custom_call_target="tpu_custom_call" | custom-call | flops 1572864 | bytes 4194304 | tf_op jit(solution)/shard_map/basis/pallas_call | solution.py:178
  41.8 2.9 %finish.1 = (bf16[1,6144,384]{2,1,0:T(8,128)(2,1)}, bf16[768,384]{1,0:T(8,128)(2,1)}, f32[8,384]{1,0:T(8,128)}) custom-call(bf16[3072,384]{1,0:T(8,128)(2,1)S(1)} %get-tuple-element.18.merged_ref.own_ref, bf16[3072,384]{1,0:T(8,128)(2,1)S(1)} %get-tuple-element.19.merged_ref.other_ref, bf16[6144,32]{1,0:T(8,128)(2,1)S(1)} %get-tuple-element.22.basis_ref, ...), custom_call_target="tpu_custom_call" | custom-call | flops 150994944 | bytes 9437184 | tf_op jit(solution)/shard_map/finish/pallas_call | solution.py:232
  (19 shorter events, 1.8 us)
Async XLA Ops:
  4.5 2.4 %collective-permute-start = (f32[8,3072]{1,0:T(8,128)S(1)}, f32[8,3072]{1,0:T(8,128)S(1)}, u32[]{:S(2)}, u32[]{:S(2)}) collective-permute-start(f32[8,3072]{1,0:T(8,128)S(1)} %get-tuple-element.21), channel_id=1, source_target_pairs={{0,16},{1,17},{2,18},{3,19},{4,20},{5,21},{6,22},{7,23},{8,24},{9,... | collective-permute-start | bytes 294920 | tf_op jit(solution)/shard_map/ppermute | solution.py:260
  6.9 5.6 %collective-permute-start.3 = (f32[8,3072]{1,0:T(8,128)S(1)}, f32[8,3072]{1,0:T(8,128)S(1)}, u32[]{:S(2)}, u32[]{:S(2)}) collective-permute-start(f32[8,3072]{1,0:T(8,128)S(1)} %add.33), channel_id=1, source_target_pairs={{0,80},{1,19},{2,16},{3,83},{4,22},{5,85},{6,86},{7,21},{8,26},{9,... | collective-permute-start | bytes 294920 | tf_op jit(solution)/shard_map/ppermute | solution.py:260
  10.1 5.0 %collective-permute-start.2 = (f32[8,3072]{1,0:T(8,128)S(1)}, f32[8,3072]{1,0:T(8,128)S(1)}, u32[]{:S(2)}, u32[]{:S(2)}) collective-permute-start(f32[8,3072]{1,0:T(8,128)S(1)} %add.33), channel_id=1, source_target_pairs={{0,96},{1,2},{2,1},{3,99},{4,7},{5,101},{6,102},{7,4},{8,11},{9,10... | collective-permute-start | bytes 294920 | tf_op jit(solution)/shard_map/ppermute | solution.py:260
  11.0 4.3 %collective-permute-start.1 = (f32[8,3072]{1,0:T(8,128)S(1)}, f32[8,3072]{1,0:T(8,128)S(1)}, u32[]{:S(2)}, u32[]{:S(2)}) collective-permute-start(f32[8,3072]{1,0:T(8,128)S(1)} %add.33), channel_id=1, source_target_pairs={{0,48},{1,16},{2,19},{3,51},{4,21},{5,53},{6,54},{7,22},{8,25},{9,... | collective-permute-start | bytes 294920 | tf_op jit(solution)/shard_map/ppermute | solution.py:260
  15.4 6.6 %collective-permute-start.6 = (f32[8,3072]{1,0:T(8,128)S(1)}, f32[8,3072]{1,0:T(8,128)S(1)}, u32[]{:S(2)}, u32[]{:S(2)}) collective-permute-start(f32[8,3072]{1,0:T(8,128)S(1)} %add_add_fusion.2), channel_id=1, source_target_pairs={{0,18},{1,25},{2,26},{3,17},{4,28},{5,23},{6,20},{7,31},{8,16},{9,... | collective-permute-start | bytes 294920 | tf_op jit(solution)/shard_map/ppermute | solution.py:260
  19.7 4.7 %collective-permute-start.5 = (f32[8,3072]{1,0:T(8,128)S(1)}, f32[8,3072]{1,0:T(8,128)S(1)}, u32[]{:S(2)}, u32[]{:S(2)}) collective-permute-start(f32[8,3072]{1,0:T(8,128)S(1)} %add_add_fusion.2), channel_id=1, source_target_pairs={{0,3},{1,13},{2,14},{3,0},{4,8},{5,6},{6,5},{7,11},{8,4},{9,10},{1... | collective-permute-start | bytes 294920 | tf_op jit(solution)/shard_map/ppermute | solution.py:260
  20.1 4.2 %collective-permute-start.4 = (f32[8,3072]{1,0:T(8,128)S(1)}, f32[8,3072]{1,0:T(8,128)S(1)}, u32[]{:S(2)}, u32[]{:S(2)}) collective-permute-start(f32[8,3072]{1,0:T(8,128)S(1)} %add_add_fusion.2), channel_id=1, source_target_pairs={{0,17},{1,21},{2,22},{3,18},{4,16},{5,20},{6,23},{7,19},{8,28},{9,... | collective-permute-start | bytes 294920 | tf_op jit(solution)/shard_map/ppermute | solution.py:260
  24.4 5.8 %collective-permute-start.9 = (f32[8,3072]{1,0:T(8,128)S(1)}, f32[8,3072]{1,0:T(8,128)S(1)}, u32[]{:S(2)}, u32[]{:S(2)}) collective-permute-start(f32[8,3072]{1,0:T(8,128)S(1)} %add_add_fusion.1), channel_id=1, source_target_pairs={{0,24},{1,81},{2,82},{3,27},{4,84},{5,29},{6,30},{7,87},{8,88},{9,... | collective-permute-start | bytes 294920 | tf_op jit(solution)/shard_map/ppermute | solution.py:260
  27.9 5.0 %collective-permute-start.8 = (f32[8,3072]{1,0:T(8,128)S(1)}, f32[8,3072]{1,0:T(8,128)S(1)}, u32[]{:S(2)}, u32[]{:S(2)}) collective-permute-start(f32[8,3072]{1,0:T(8,128)S(1)} %add_add_fusion.1), channel_id=1, source_target_pairs={{0,12},{1,97},{2,98},{3,15},{4,100},{5,9},{6,10},{7,103},{8,104},{... | collective-permute-start | bytes 294920 | tf_op jit(solution)/shard_map/ppermute | solution.py:260
  28.7 4.3 %collective-permute-start.7 = (f32[8,3072]{1,0:T(8,128)S(1)}, f32[8,3072]{1,0:T(8,128)S(1)}, u32[]{:S(2)}, u32[]{:S(2)}) collective-permute-start(f32[8,3072]{1,0:T(8,128)S(1)} %add_add_fusion.1), channel_id=1, source_target_pairs={{0,20},{1,49},{2,50},{3,23},{4,52},{5,17},{6,18},{7,55},{8,56},{9,... | collective-permute-start | bytes 294920 | tf_op jit(solution)/shard_map/ppermute | solution.py:260
  33.0 1.9 %collective-permute-start.10 = (f32[8,3072]{1,0:T(8,128)S(1)}, f32[8,3072]{1,0:T(8,128)S(1)}, u32[]{:S(2)}, u32[]{:S(2)}) collective-permute-start(f32[8,3072]{1,0:T(8,128)S(1)} %add_add_fusion.refs_0_.left_ref), channel_id=1, source_target_pairs={{0,16},{1,17},{2,18},{3,19},{4,20},{5,21},{6,22},{7,23},{8,24},{9,... | collective-permute-start | bytes 294920 | tf_op jit(solution)/shard_map/ppermute | solution.py:260
  34.0 7.8 %copy-start = (bf16[768,384]{1,0:T(8,128)(2,1)S(1)}, bf16[768,384]{1,0:T(8,128)(2,1)}, u32[]{:S(2)}) copy-start(bf16[768,384]{1,0:T(8,128)(2,1)} %mom_ref.1) | copy-start | bytes 1769476
  35.4 1.3 %collective-permute-start.11 = (f32[8,384]{1,0:T(8,128)S(1)}, f32[8,384]{1,0:T(8,128)S(1)}, u32[]{:S(2)}, u32[]{:S(2)}) collective-permute-start(f32[8,384]{1,0:T(8,128)S(1)} %right_other.1), channel_id=1, source_target_pairs={{0,16},{1,17},{2,18},{3,19},{4,20},{5,21},{6,22},{7,23},{8,24},{9,... | collective-permute-start | bytes 36872 | tf_op jit(solution)/shard_map/ppermute | solution.py:260
  36.7 4.8 %collective-permute-start.14 = (f32[8,384]{1,0:T(8,128)S(1)}, f32[8,384]{1,0:T(8,128)S(1)}, u32[]{:S(2)}, u32[]{:S(2)}) collective-permute-start(f32[8,384]{1,0:T(8,128)S(1)} %add.43.sum_ref), channel_id=1, source_target_pairs={{0,80},{1,81},{2,82},{3,83},{4,84},{5,85},{6,86},{7,87},{8,88},{9,... | collective-permute-start | bytes 36872 | tf_op jit(solution)/shard_map/ppermute | solution.py:260
  37.5 4.3 %collective-permute-start.13 = (f32[8,384]{1,0:T(8,128)S(1)}, f32[8,384]{1,0:T(8,128)S(1)}, u32[]{:S(2)}, u32[]{:S(2)}) collective-permute-start(f32[8,384]{1,0:T(8,128)S(1)} %add.43.sum_ref), channel_id=1, source_target_pairs={{0,112},{1,113},{2,114},{3,115},{4,116},{5,117},{6,118},{7,119},{8... | collective-permute-start | bytes 36872 | tf_op jit(solution)/shard_map/ppermute | solution.py:260
  38.6 3.2 %collective-permute-start.12 = (f32[8,384]{1,0:T(8,128)S(1)}, f32[8,384]{1,0:T(8,128)S(1)}, u32[]{:S(2)}, u32[]{:S(2)}) collective-permute-start(f32[8,384]{1,0:T(8,128)S(1)} %add.43.sum_ref), channel_id=1, source_target_pairs={{0,48},{1,49},{2,50},{3,51},{4,52},{5,53},{6,54},{7,55},{8,56},{9,... | collective-permute-start | bytes 36872 | tf_op jit(solution)/shard_map/ppermute | solution.py:260

commit v11 on v10

--- a/solution.py
+++ b/solution.py
@@ -29,10 +29,6 @@
     return terms
 
 
-def rows_of(half, chunk):
-    return pl.ds(pl.multiple_of(half * HALF + chunk * CHUNK, CHUNK), CHUNK)
-
-
 def merge_chunk(g_ref, f_ref, right, merged_ref, term_ref, i):
     here = pl.ds(i * CHUNK, CHUNK)
     merged = (g_ref[here, :].astype(F32) + f_ref[here, :].astype(F32)).astype(BF16)
@@ -40,11 +36,11 @@
     term_ref[:, here] = lax.dot_general(right, merged, (((1,), (1,)), ((), ())), preferred_element_type=F32)
 
 
-def load_pair(g_ref, f_ref, half, i, g_to, f_to, g_sem, f_sem):
-    here = pl.ds(i * CHUNK, CHUNK)
+def load_pair(g_ref, f_ref, half, start, count, g_to, f_to, g_sem, f_sem):
+    here, rows = pl.ds(start, count), pl.ds(pl.multiple_of(half * HALF + start, CHUNK), count)
     pair = (
-        pltpu.make_async_copy(g_ref.at[0, rows_of(half, i), :], g_to.at[here, :], g_sem),
-        pltpu.make_async_copy(f_ref.at[0, rows_of(half, i), :], f_to.at[here, :], f_sem),
+        pltpu.make_async_copy(g_ref.at[0, rows, :], g_to.at[here, :], g_sem),
+        pltpu.make_async_copy(f_ref.at[0, rows, :], f_to.at[here, :], f_sem),
     )
     for copy in pair:
         copy.start()
@@ -55,11 +51,10 @@
     mine = own_half()
     q_copy = pltpu.make_async_copy(q_ref, q_own, q_sem.at[0])
     q_copy.start()
-    copies = []
-    for half, g_to, f_to in ((1 - mine, g_buf, f_buf), (mine, g_own, f_own)):
-        for i in range(CHUNKS):
-            n = len(copies)
-            copies.append(load_pair(g_ref, f_ref, half, i, g_to, f_to, g_sem.at[n], f_sem.at[n]))
+    copies = [
+        load_pair(g_ref, f_ref, 1 - mine, i * CHUNK, CHUNK, g_buf, f_buf, g_sem.at[i], f_sem.at[i]) for i in range(CHUNKS)
+    ]
+    copies.append(load_pair(g_ref, f_ref, mine, 0, HALF, g_own, f_own, g_sem.at[CHUNKS], f_sem.at[CHUNKS]))
     q_copy.wait()
     right = q_own[...].astype(BF16)
     for i, pair in enumerate(copies):
@@ -99,8 +94,8 @@
         scratch_shapes=[
             half_rows,
             half_rows,
-            pltpu.SemaphoreType.DMA((2 * CHUNKS,)),
-            pltpu.SemaphoreType.DMA((2 * CHUNKS,)),
+            pltpu.SemaphoreType.DMA((CHUNKS + 1,)),
+            pltpu.SemaphoreType.DMA((CHUNKS + 1,)),
             pltpu.SemaphoreType.DMA((1,)),
         ],
         compiler_params=pltpu.CompilerParams(vmem_limit_bytes=16 * MIB),

time: 44.8 us -> 44.8 us (level)
  no operation moved by 1% of the time
where the time goes in v11:
time: 44.8 us; the launch traced here: 44.7 us
  starting transfers between devices  19.1 us (43%)
  waiting for transfers between devices  14.7 us (33%)
  Pallas kernels  10.1 us (23%)
  between operations  0.7 us (2%)
    ppermute x15, starting transfers between devices, swap(): return lax.ppermute(x, ('replica', 'tensor'), pairs)  19.1 us
    ppermute x15, waiting for transfers between devices, swap(): return lax.ppermute(x, ('replica', 'tensor'), pairs)  14.7 us
    pallas_call x1, Pallas kernels, merge_other(): pl.pallas_call(load_kernel, in_specs=in_hbm(3), out_specs=[whole()] * 5,...  3.9 us
    pallas_call x1, Pallas kernels, finish(): pl.pallas_call(final_kernel, in_specs=[whole()] * 9, out_specs=in_hbm(3),...  2.89 us
    pallas_call x1, Pallas kernels, make_basis(): pl.pallas_call(body, in_specs=[whole(), whole()], out_specs=[whole(), who...  1.66 us
    pallas_call x2, Pallas kernels, right_term(): pl.pallas_call(right_kernel, in_specs=[whole()] * (2 + len(before)), out_...  0.9 us
  transfers between devices with their start and end apart: 15, of which 12 were waited for; matrix products, arithmetic and copies ran while one was open for 0% of the time, Pallas kernels for 6%

profile of v11, /device:TPU:1, one launch (start us, length us, event | category | flops | bytes accessed | tf_op | source)
XLA Modules:
  0.0 44.7 jit_solution(10129590462092341104)
XLA Ops:
  0.6 3.9 %merge_other.1 = (bf16[3072,384]{1,0:T(8,128)(2,1)S(1)}, f32[8,3072]{1,0:T(8,128)S(1)}, bf16[3072,384]{1,0:T(8,128)(2,1)S(1)}, bf16[3072,384]{1,0:T(8,128)(2,1)S(1)}, f32[8,384]{1,0:T(8,128)S(1)}) custom-call(bf16[1,6144,384]{2,1,0:T(8,128)(2,1)} %g_ref.1, bf16[1,6144,384]{2,1,0:T(8,128)(2,1)} %f_ref.1, f32[8,384]{1,0:T(8,128)} %bitcast.2), custom_call_target="tpu_custom_call" | custom-call | flops 18874368 | bytes 9437184 | tf_op jit(solution)/shard_map/merge_other/pallas_call | solution.py:83
  4.5 1.5 %collective-permute-start = (f32[8,3072]{1,0:T(8,128)S(1)}, f32[8,3072]{1,0:T(8,128)S(1)}, u32[]{:S(2)}, u32[]{:S(2)}) collective-permute-start(f32[8,3072]{1,0:T(8,128)S(1)} %get-tuple-element.21), channel_id=1, source_target_pairs={{0,16},{1,17},{2,18},{3,19},{4,20},{5,21},{6,22},{7,23},{8,24},{9,... | collective-permute-start | bytes 294920 | tf_op jit(solution)/shard_map/ppermute | solution.py:255
  6.0 0.8 %merge_own.1 = (bf16[3072,384]{1,0:T(8,128)(2,1)S(1)}, f32[8,3072]{1,0:T(8,128)S(1)}) custom-call(bf16[3072,384]{1,0:T(8,128)(2,1)S(1)} %get-tuple-element.15.g_ref, bf16[3072,384]{1,0:T(8,128)(2,1)S(1)} %get-tuple-element.16.f_ref, f32[8,384]{1,0:T(8,128)S(1)} %get-tuple-element.17.q_ref), custom_call_target="tpu_custom_call" | custom-call | flops 18874368 | bytes 4718592 | tf_op jit(solution)/shard_map/merge_own/pallas_call | solution.py:108
  7.0 3.1 %collective-permute-start.3 = (f32[8,3072]{1,0:T(8,128)S(1)}, f32[8,3072]{1,0:T(8,128)S(1)}, u32[]{:S(2)}, u32[]{:S(2)}) collective-permute-start(f32[8,3072]{1,0:T(8,128)S(1)} %add.33), channel_id=1, source_target_pairs={{0,80},{1,19},{2,16},{3,83},{4,22},{5,85},{6,86},{7,21},{8,26},{9,... | collective-permute-start | bytes 294920 | tf_op jit(solution)/shard_map/ppermute | solution.py:255
  10.2 0.9 %collective-permute-start.2 = (f32[8,3072]{1,0:T(8,128)S(1)}, f32[8,3072]{1,0:T(8,128)S(1)}, u32[]{:S(2)}, u32[]{:S(2)}) collective-permute-start(f32[8,3072]{1,0:T(8,128)S(1)} %add.33), channel_id=1, source_target_pairs={{0,96},{1,2},{2,1},{3,99},{4,7},{5,101},{6,102},{7,4},{8,11},{9,10... | collective-permute-start | bytes 294920 | tf_op jit(solution)/shard_map/ppermute | solution.py:255
  11.0 1.6 %collective-permute-done.3 = f32[8,3072]{1,0:T(8,128)S(1)} collective-permute-done((f32[8,3072]{1,0:T(8,128)S(1)}, f32[8,3072]{1,0:T(8,128)S(1)}, u32[]{:S(2)}, u32[]{:S(2)}) %collective-permute-start.3) | collective-permute-done | bytes 98336 | tf_op jit(solution)/shard_map/ppermute | solution.py:255
  12.6 2.5 %collective-permute-done.2 = f32[8,3072]{1,0:T(8,128)S(1)} collective-permute-done((f32[8,3072]{1,0:T(8,128)S(1)}, f32[8,3072]{1,0:T(8,128)S(1)}, u32[]{:S(2)}, u32[]{:S(2)}) %collective-permute-start.2) | collective-permute-done | bytes 98336 | tf_op jit(solution)/shard_map/ppermute | solution.py:255
  15.4 4.3 %collective-permute-start.6 = (f32[8,3072]{1,0:T(8,128)S(1)}, f32[8,3072]{1,0:T(8,128)S(1)}, u32[]{:S(2)}, u32[]{:S(2)}) collective-permute-start(f32[8,3072]{1,0:T(8,128)S(1)} %add_add_fusion.2), channel_id=1, source_target_pairs={{0,18},{1,25},{2,26},{3,17},{4,28},{5,23},{6,20},{7,31},{8,16},{9,... | collective-permute-start | bytes 294920 | tf_op jit(solution)/shard_map/ppermute | solution.py:255
  20.2 1.9 %collective-permute-done.6 = f32[8,3072]{1,0:T(8,128)S(1)} collective-permute-done((f32[8,3072]{1,0:T(8,128)S(1)}, f32[8,3072]{1,0:T(8,128)S(1)}, u32[]{:S(2)}, u32[]{:S(2)}) %collective-permute-start.6) | collective-permute-done | bytes 98336 | tf_op jit(solution)/shard_map/ppermute | solution.py:255
  22.0 2.4 %collective-permute-done.5 = f32[8,3072]{1,0:T(8,128)S(1)} collective-permute-done((f32[8,3072]{1,0:T(8,128)S(1)}, f32[8,3072]{1,0:T(8,128)S(1)}, u32[]{:S(2)}, u32[]{:S(2)}) %collective-permute-start.5) | collective-permute-done | bytes 98336 | tf_op jit(solution)/shard_map/ppermute | solution.py:255
  24.4 3.5 %collective-permute-start.9 = (f32[8,3072]{1,0:T(8,128)S(1)}, f32[8,3072]{1,0:T(8,128)S(1)}, u32[]{:S(2)}, u32[]{:S(2)}) collective-permute-start(f32[8,3072]{1,0:T(8,128)S(1)} %add_add_fusion.1), channel_id=1, source_target_pairs={{0,24},{1,81},{2,82},{3,27},{4,84},{5,29},{6,30},{7,87},{8,88},{9,... | collective-permute-start | bytes 294920 | tf_op jit(solution)/shard_map/ppermute | solution.py:255
  27.9 0.8 %collective-permute-start.8 = (f32[8,3072]{1,0:T(8,128)S(1)}, f32[8,3072]{1,0:T(8,128)S(1)}, u32[]{:S(2)}, u32[]{:S(2)}) collective-permute-start(f32[8,3072]{1,0:T(8,128)S(1)} %add_add_fusion.1), channel_id=1, source_target_pairs={{0,12},{1,97},{2,98},{3,15},{4,100},{5,9},{6,10},{7,103},{8,104},{... | collective-permute-start | bytes 294920 | tf_op jit(solution)/shard_map/ppermute | solution.py:255
  28.7 1.5 %collective-permute-done.9 = f32[8,3072]{1,0:T(8,128)S(1)} collective-permute-done((f32[8,3072]{1,0:T(8,128)S(1)}, f32[8,3072]{1,0:T(8,128)S(1)}, u32[]{:S(2)}, u32[]{:S(2)}) %collective-permute-start.9) | collective-permute-done | bytes 98336 | tf_op jit(solution)/shard_map/ppermute | solution.py:255
  30.2 2.7 %collective-permute-done.8 = f32[8,3072]{1,0:T(8,128)S(1)} collective-permute-done((f32[8,3072]{1,0:T(8,128)S(1)}, f32[8,3072]{1,0:T(8,128)S(1)}, u32[]{:S(2)}, u32[]{:S(2)}) %collective-permute-start.8) | collective-permute-done | bytes 98336 | tf_op jit(solution)/shard_map/ppermute | solution.py:255
  33.0 1.0 %collective-permute-start.10 = (f32[8,3072]{1,0:T(8,128)S(1)}, f32[8,3072]{1,0:T(8,128)S(1)}, u32[]{:S(2)}, u32[]{:S(2)}) collective-permute-start(f32[8,3072]{1,0:T(8,128)S(1)} %add_add_fusion.refs_0_.left_ref), channel_id=1, source_target_pairs={{0,16},{1,17},{2,18},{3,19},{4,20},{5,21},{6,22},{7,23},{8,24},{9,... | collective-permute-start | bytes 294920 | tf_op jit(solution)/shard_map/ppermute | solution.py:255
  34.0 0.4 right_own.1.refs_0_
  34.4 0.5 %collective-permute-done.10.refs_1_.left_ref = f32[8,3072]{1,0:T(8,128)S(1)} collective-permute-done((f32[8,3072]{1,0:T(8,128)S(1)}, f32[8,3072]{1,0:T(8,128)S(1)}, u32[]{:S(2)}, u32[]{:S(2)}) %collective-permute-start.10) | collective-permute-done | bytes 98336 | tf_op jit(solution)/shard_map/ppermute | solution.py:255
  34.9 0.5 %right_other.1 = f32[8,384]{1,0:T(8,128)S(1)} custom-call(bf16[3072,384]{1,0:T(8,128)(2,1)S(1)} %get-tuple-element.19.merged_ref.other_ref, f32[8,3072]{1,0:T(8,128)S(1)} %collective-permute-done.10.refs_1_.left_ref, f32[8,384]{1,0:T(8,128)S(1)} %right_own.1.refs_0_), custom_call_target="tpu_custom_call" | custom-call | flops 37748736 | bytes 2359296 | tf_op jit(solution)/shard_map/right_other/pallas_call | solution.py:129
  35.8 0.8 %collective-permute-done.11 = f32[8,384]{1,0:T(8,128)S(1)} collective-permute-done((f32[8,384]{1,0:T(8,128)S(1)}, f32[8,384]{1,0:T(8,128)S(1)}, u32[]{:S(2)}, u32[]{:S(2)}) %collective-permute-start.11) | collective-permute-done | bytes 12320 | tf_op jit(solution)/shard_map/ppermute | solution.py:255
  36.7 0.8 %collective-permute-start.14 = (f32[8,384]{1,0:T(8,128)S(1)}, f32[8,384]{1,0:T(8,128)S(1)}, u32[]{:S(2)}, u32[]{:S(2)}) collective-permute-start(f32[8,384]{1,0:T(8,128)S(1)} %add.43.sum_ref), channel_id=1, source_target_pairs={{0,80},{1,81},{2,82},{3,83},{4,84},{5,85},{6,86},{7,87},{8,88},{9,... | collective-permute-start | bytes 36872 | tf_op jit(solution)/shard_map/ppermute | solution.py:255
  37.5 1.1 %collective-permute-start.13 = (f32[8,384]{1,0:T(8,128)S(1)}, f32[8,384]{1,0:T(8,128)S(1)}, u32[]{:S(2)}, u32[]{:S(2)}) collective-permute-start(f32[8,384]{1,0:T(8,128)S(1)} %add.43.sum_ref), channel_id=1, source_target_pairs={{0,112},{1,113},{2,114},{3,115},{4,116},{5,117},{6,118},{7,119},{8... | collective-permute-start | bytes 36872 | tf_op jit(solution)/shard_map/ppermute | solution.py:255
  38.6 1.2 %collective-permute-start.12 = (f32[8,384]{1,0:T(8,128)S(1)}, f32[8,384]{1,0:T(8,128)S(1)}, u32[]{:S(2)}, u32[]{:S(2)}) collective-permute-start(f32[8,384]{1,0:T(8,128)S(1)} %add.43.sum_ref), channel_id=1, source_target_pairs={{0,48},{1,49},{2,50},{3,51},{4,52},{5,53},{6,54},{7,55},{8,56},{9,... | collective-permute-start | bytes 36872 | tf_op jit(solution)/shard_map/ppermute | solution.py:255
  39.8 1.7 %basis.1 = (f32[64,128]{1,0:T(8,128)S(1)}, bf16[6144,32]{1,0:T(8,128)(2,1)S(1)}) custom-call(f32[8,3072]{1,0:T(8,128)S(1)} %add_add_fusion.refs_0_.left_ref, f32[8,3072]{1,0:T(8,128)S(1)} %collective-permute-done.10.refs_1_.left_ref), custom_call_target="tpu_custom_call" | custom-call | flops 1572864 | bytes 4194304 | tf_op jit(solution)/shard_map/basis/pallas_call | solution.py:173
  41.8 2.9 %finish.1 = (bf16[1,6144,384]{2,1,0:T(8,128)(2,1)}, bf16[768,384]{1,0:T(8,128)(2,1)}, f32[8,384]{1,0:T(8,128)}) custom-call(bf16[3072,384]{1,0:T(8,128)(2,1)S(1)} %get-tuple-element.18.merged_ref.own_ref, bf16[3072,384]{1,0:T(8,128)(2,1)S(1)} %get-tuple-element.19.merged_ref.other_ref, bf16[6144,32]{1,0:T(8,128)(2,1)S(1)} %get-tuple-element.22.basis_ref, ...), custom_call_target="tpu_custom_call" | custom-call | flops 150994944 | bytes 9437184 | tf_op jit(solution)/shard_map/finish/pallas_call | solution.py:227
  (19 shorter events, 1.8 us)
Async XLA Ops:
  4.5 2.4 %collective-permute-start = (f32[8,3072]{1,0:T(8,128)S(1)}, f32[8,3072]{1,0:T(8,128)S(1)}, u32[]{:S(2)}, u32[]{:S(2)}) collective-permute-start(f32[8,3072]{1,0:T(8,128)S(1)} %get-tuple-element.21), channel_id=1, source_target_pairs={{0,16},{1,17},{2,18},{3,19},{4,20},{5,21},{6,22},{7,23},{8,24},{9,... | collective-permute-start | bytes 294920 | tf_op jit(solution)/shard_map/ppermute | solution.py:255
  7.0 5.6 %collective-permute-start.3 = (f32[8,3072]{1,0:T(8,128)S(1)}, f32[8,3072]{1,0:T(8,128)S(1)}, u32[]{:S(2)}, u32[]{:S(2)}) collective-permute-start(f32[8,3072]{1,0:T(8,128)S(1)} %add.33), channel_id=1, source_target_pairs={{0,80},{1,19},{2,16},{3,83},{4,22},{5,85},{6,86},{7,21},{8,26},{9,... | collective-permute-start | bytes 294920 | tf_op jit(solution)/shard_map/ppermute | solution.py:255
  10.2 5.0 %collective-permute-start.2 = (f32[8,3072]{1,0:T(8,128)S(1)}, f32[8,3072]{1,0:T(8,128)S(1)}, u32[]{:S(2)}, u32[]{:S(2)}) collective-permute-start(f32[8,3072]{1,0:T(8,128)S(1)} %add.33), channel_id=1, source_target_pairs={{0,96},{1,2},{2,1},{3,99},{4,7},{5,101},{6,102},{7,4},{8,11},{9,10... | collective-permute-start | bytes 294920 | tf_op jit(solution)/shard_map/ppermute | solution.py:255
  11.0 4.3 %collective-permute-start.1 = (f32[8,3072]{1,0:T(8,128)S(1)}, f32[8,3072]{1,0:T(8,128)S(1)}, u32[]{:S(2)}, u32[]{:S(2)}) collective-permute-start(f32[8,3072]{1,0:T(8,128)S(1)} %add.33), channel_id=1, source_target_pairs={{0,48},{1,16},{2,19},{3,51},{4,21},{5,53},{6,54},{7,22},{8,25},{9,... | collective-permute-start | bytes 294920 | tf_op jit(solution)/shard_map/ppermute | solution.py:255
  15.4 6.7 %collective-permute-start.6 = (f32[8,3072]{1,0:T(8,128)S(1)}, f32[8,3072]{1,0:T(8,128)S(1)}, u32[]{:S(2)}, u32[]{:S(2)}) collective-permute-start(f32[8,3072]{1,0:T(8,128)S(1)} %add_add_fusion.2), channel_id=1, source_target_pairs={{0,18},{1,25},{2,26},{3,17},{4,28},{5,23},{6,20},{7,31},{8,16},{9,... | collective-permute-start | bytes 294920 | tf_op jit(solution)/shard_map/ppermute | solution.py:255
  19.7 4.7 %collective-permute-start.5 = (f32[8,3072]{1,0:T(8,128)S(1)}, f32[8,3072]{1,0:T(8,128)S(1)}, u32[]{:S(2)}, u32[]{:S(2)}) collective-permute-start(f32[8,3072]{1,0:T(8,128)S(1)} %add_add_fusion.2), channel_id=1, source_target_pairs={{0,3},{1,13},{2,14},{3,0},{4,8},{5,6},{6,5},{7,11},{8,4},{9,10},{1... | collective-permute-start | bytes 294920 | tf_op jit(solution)/shard_map/ppermute | solution.py:255
  20.2 4.2 %collective-permute-start.4 = (f32[8,3072]{1,0:T(8,128)S(1)}, f32[8,3072]{1,0:T(8,128)S(1)}, u32[]{:S(2)}, u32[]{:S(2)}) collective-permute-start(f32[8,3072]{1,0:T(8,128)S(1)} %add_add_fusion.2), channel_id=1, source_target_pairs={{0,17},{1,21},{2,22},{3,18},{4,16},{5,20},{6,23},{7,19},{8,28},{9,... | collective-permute-start | bytes 294920 | tf_op jit(solution)/shard_map/ppermute | solution.py:255
  24.4 5.8 %collective-permute-start.9 = (f32[8,3072]{1,0:T(8,128)S(1)}, f32[8,3072]{1,0:T(8,128)S(1)}, u32[]{:S(2)}, u32[]{:S(2)}) collective-permute-start(f32[8,3072]{1,0:T(8,128)S(1)} %add_add_fusion.1), channel_id=1, source_target_pairs={{0,24},{1,81},{2,82},{3,27},{4,84},{5,29},{6,30},{7,87},{8,88},{9,... | collective-permute-start | bytes 294920 | tf_op jit(solution)/shard_map/ppermute | solution.py:255
  27.9 5.0 %collective-permute-start.8 = (f32[8,3072]{1,0:T(8,128)S(1)}, f32[8,3072]{1,0:T(8,128)S(1)}, u32[]{:S(2)}, u32[]{:S(2)}) collective-permute-start(f32[8,3072]{1,0:T(8,128)S(1)} %add_add_fusion.1), channel_id=1, source_target_pairs={{0,12},{1,97},{2,98},{3,15},{4,100},{5,9},{6,10},{7,103},{8,104},{... | collective-permute-start | bytes 294920 | tf_op jit(solution)/shard_map/ppermute | solution.py:255
  28.7 4.3 %collective-permute-start.7 = (f32[8,3072]{1,0:T(8,128)S(1)}, f32[8,3072]{1,0:T(8,128)S(1)}, u32[]{:S(2)}, u32[]{:S(2)}) collective-permute-start(f32[8,3072]{1,0:T(8,128)S(1)} %add_add_fusion.1), channel_id=1, source_target_pairs={{0,20},{1,49},{2,50},{3,23},{4,52},{5,17},{6,18},{7,55},{8,56},{9,... | collective-permute-start | bytes 294920 | tf_op jit(solution)/shard_map/ppermute | solution.py:255
  33.0 1.9 %collective-permute-start.10 = (f32[8,3072]{1,0:T(8,128)S(1)}, f32[8,3072]{1,0:T(8,128)S(1)}, u32[]{:S(2)}, u32[]{:S(2)}) collective-permute-start(f32[8,3072]{1,0:T(8,128)S(1)} %add_add_fusion.refs_0_.left_ref), channel_id=1, source_target_pairs={{0,16},{1,17},{2,18},{3,19},{4,20},{5,21},{6,22},{7,23},{8,24},{9,... | collective-permute-start | bytes 294920 | tf_op jit(solution)/shard_map/ppermute | solution.py:255
  34.0 7.8 %copy-start = (bf16[768,384]{1,0:T(8,128)(2,1)S(1)}, bf16[768,384]{1,0:T(8,128)(2,1)}, u32[]{:S(2)}) copy-start(bf16[768,384]{1,0:T(8,128)(2,1)} %mom_ref.1) | copy-start | bytes 1769476
  35.4 1.3 %collective-permute-start.11 = (f32[8,384]{1,0:T(8,128)S(1)}, f32[8,384]{1,0:T(8,128)S(1)}, u32[]{:S(2)}, u32[]{:S(2)}) collective-permute-start(f32[8,384]{1,0:T(8,128)S(1)} %right_other.1), channel_id=1, source_target_pairs={{0,16},{1,17},{2,18},{3,19},{4,20},{5,21},{6,22},{7,23},{8,24},{9,... | collective-permute-start | bytes 36872 | tf_op jit(solution)/shard_map/ppermute | solution.py:255
  36.7 4.8 %collective-permute-start.14 = (f32[8,384]{1,0:T(8,128)S(1)}, f32[8,384]{1,0:T(8,128)S(1)}, u32[]{:S(2)}, u32[]{:S(2)}) collective-permute-start(f32[8,384]{1,0:T(8,128)S(1)} %add.43.sum_ref), channel_id=1, source_target_pairs={{0,80},{1,81},{2,82},{3,83},{4,84},{5,85},{6,86},{7,87},{8,88},{9,... | collective-permute-start | bytes 36872 | tf_op jit(solution)/shard_map/ppermute | solution.py:255
  37.5 4.3 %collective-permute-start.13 = (f32[8,384]{1,0:T(8,128)S(1)}, f32[8,384]{1,0:T(8,128)S(1)}, u32[]{:S(2)}, u32[]{:S(2)}) collective-permute-start(f32[8,384]{1,0:T(8,128)S(1)} %add.43.sum_ref), channel_id=1, source_target_pairs={{0,112},{1,113},{2,114},{3,115},{4,116},{5,117},{6,118},{7,119},{8... | collective-permute-start | bytes 36872 | tf_op jit(solution)/shard_map/ppermute | solution.py:255
  38.6 3.2 %collective-permute-start.12 = (f32[8,384]{1,0:T(8,128)S(1)}, f32[8,384]{1,0:T(8,128)S(1)}, u32[]{:S(2)}, u32[]{:S(2)}) collective-permute-start(f32[8,384]{1,0:T(8,128)S(1)} %add.43.sum_ref), channel_id=1, source_target_pairs={{0,48},{1,49},{2,50},{3,51},{4,52},{5,53},{6,54},{7,55},{8,56},{9,... | collective-permute-start | bytes 36872 | tf_op jit(solution)/shard_map/ppermute | solution.py:255

commit v12 on v10

--- a/solution.py
+++ b/solution.py
@@ -187,11 +187,11 @@
 
 
 def final_kernel(
-    own_ref, other_ref, basis_ref, inverse_ref, sum_ref, near_ref, wrap_ref, far_ref, mom_ref,
+    own_ref, other_ref, basis_ref, inverse_ref, sum_ref, sibling_ref, mom_ref,
     fb_ref, mom_out_ref, right_ref,
     fb_buf, mom_buf, right_buf, fb_sem, mom_sem, right_sem,
 ):
-    total = (sum_ref[...] + near_ref[...]) + (wrap_ref[...] + far_ref[...])
+    total = sum_ref[...] + sibling_ref[...]
     pieces = []
     for start in range(0, COLS, LANES):
         piece = jnp.zeros((RANK, LANES), F32)
@@ -231,7 +231,7 @@
     mom_rows = momentum.shape[0]
     return pl.pallas_call(
         final_kernel,
-        in_specs=[whole()] * 9,
+        in_specs=[whole()] * 7,
         out_specs=in_hbm(3),
         out_shape=[
             jax.ShapeDtypeStruct((1, ROWS, COLS), BF16),
@@ -284,8 +284,9 @@
     other = sibling(own)
     term = right_term(merged_other, other, right_term(merged_own, own))
     inverse, basis = make_basis(lax.axis_size("replica"), own, other)
-    term = term + sibling(term)
-    parts = [term, *(swap(term, [steps * LOW["y"] | CORE] * 2) for steps in (1, 3, 2))]
+    near, wrap, far = (swap(term, [steps * LOW["y"] | CORE] * 2) for steps in (1, 3, 2))
+    term = term + near + wrap + far
+    parts = [term, sibling(term)]
     feedback_out, momentum_out, right_t = finish(merged_own, merged_other, basis, inverse, parts, momentum)
     return feedback_out, momentum_out, right_t.T
 

time: 44.8 us -> 45.7 us (1.020)
  waiting for transfers between devices: 14.7 us -> 15.5 us
    ppermute x15, waiting for transfers between devices: 14.7 us -> 15.5 us  [swap(): return lax.ppermute(x, ('replica', 'tensor'), pairs)]
where the time goes in v12:
time: 45.7 us; the launch traced here: 45.6 us
  starting transfers between devices  19.1 us (42%)
  waiting for transfers between devices  15.5 us (34%)
  Pallas kernels  10.2 us (22%)
  between operations  0.71 us (2%)
    ppermute x15, starting transfers between devices, swap(): return lax.ppermute(x, ('replica', 'tensor'), pairs)  19.1 us
    ppermute x15, waiting for transfers between devices, swap(): return lax.ppermute(x, ('replica', 'tensor'), pairs)  15.5 us
    pallas_call x1, Pallas kernels, merge_other(): pl.pallas_call(load_kernel, in_specs=in_hbm(3), out_specs=[whole()] * 5,...  3.9 us
    pallas_call x1, Pallas kernels, finish(): pl.pallas_call(final_kernel, in_specs=[whole()] * 7, out_specs=in_hbm(3),...  2.91 us
    pallas_call x1, Pallas kernels, make_basis(): pl.pallas_call(body, in_specs=[whole(), whole()], out_specs=[whole(), who...  1.66 us
  transfers between devices with their start and end apart: 15, of which 12 were waited for; matrix products, arithmetic and copies ran while one was open for 0% of the time, Pallas kernels for 6%

profile of v12, /device:TPU:1, one launch (start us, length us, event | category | flops | bytes accessed | tf_op | source)
XLA Modules:
  0.0 45.6 jit_solution(14321616861382851503)
XLA Ops:
  0.6 3.9 %merge_other.1 = (bf16[3072,384]{1,0:T(8,128)(2,1)S(1)}, f32[8,3072]{1,0:T(8,128)S(1)}, bf16[3072,384]{1,0:T(8,128)(2,1)S(1)}, bf16[3072,384]{1,0:T(8,128)(2,1)S(1)}, f32[8,384]{1,0:T(8,128)S(1)}) custom-call(bf16[1,6144,384]{2,1,0:T(8,128)(2,1)} %g_ref.1, bf16[1,6144,384]{2,1,0:T(8,128)(2,1)} %f_ref.1, f32[8,384]{1,0:T(8,128)} %bitcast.2), custom_call_target="tpu_custom_call" | custom-call | flops 18874368 | bytes 9437184 | tf_op jit(solution)/shard_map/merge_other/pallas_call | solution.py:88
  4.5 1.4 %collective-permute-start = (f32[8,3072]{1,0:T(8,128)S(1)}, f32[8,3072]{1,0:T(8,128)S(1)}, u32[]{:S(2)}, u32[]{:S(2)}) collective-permute-start(f32[8,3072]{1,0:T(8,128)S(1)} %get-tuple-element.21), channel_id=1, source_target_pairs={{0,16},{1,17},{2,18},{3,19},{4,20},{5,21},{6,22},{7,23},{8,24},{9,... | collective-permute-start | bytes 294920 | tf_op jit(solution)/shard_map/ppermute | solution.py:260
  6.0 0.8 %merge_own.1 = (bf16[3072,384]{1,0:T(8,128)(2,1)S(1)}, f32[8,3072]{1,0:T(8,128)S(1)}) custom-call(bf16[3072,384]{1,0:T(8,128)(2,1)S(1)} %get-tuple-element.15.g_ref, bf16[3072,384]{1,0:T(8,128)(2,1)S(1)} %get-tuple-element.16.f_ref, f32[8,384]{1,0:T(8,128)S(1)} %get-tuple-element.17.q_ref), custom_call_target="tpu_custom_call" | custom-call | flops 18874368 | bytes 4718592 | tf_op jit(solution)/shard_map/merge_own/pallas_call | solution.py:113
  6.9 3.2 %collective-permute-start.3 = (f32[8,3072]{1,0:T(8,128)S(1)}, f32[8,3072]{1,0:T(8,128)S(1)}, u32[]{:S(2)}, u32[]{:S(2)}) collective-permute-start(f32[8,3072]{1,0:T(8,128)S(1)} %add.39), channel_id=1, source_target_pairs={{0,80},{1,19},{2,16},{3,83},{4,22},{5,85},{6,86},{7,21},{8,26},{9,... | collective-permute-start | bytes 294920 | tf_op jit(solution)/shard_map/ppermute | solution.py:260
  10.1 0.9 %collective-permute-start.2 = (f32[8,3072]{1,0:T(8,128)S(1)}, f32[8,3072]{1,0:T(8,128)S(1)}, u32[]{:S(2)}, u32[]{:S(2)}) collective-permute-start(f32[8,3072]{1,0:T(8,128)S(1)} %add.39), channel_id=1, source_target_pairs={{0,96},{1,2},{2,1},{3,99},{4,7},{5,101},{6,102},{7,4},{8,11},{9,10... | collective-permute-start | bytes 294920 | tf_op jit(solution)/shard_map/ppermute | solution.py:260
  11.0 1.6 %collective-permute-done.3 = f32[8,3072]{1,0:T(8,128)S(1)} collective-permute-done((f32[8,3072]{1,0:T(8,128)S(1)}, f32[8,3072]{1,0:T(8,128)S(1)}, u32[]{:S(2)}, u32[]{:S(2)}) %collective-permute-start.3) | collective-permute-done | bytes 98336 | tf_op jit(solution)/shard_map/ppermute | solution.py:260
  12.6 2.5 %collective-permute-done.2 = f32[8,3072]{1,0:T(8,128)S(1)} collective-permute-done((f32[8,3072]{1,0:T(8,128)S(1)}, f32[8,3072]{1,0:T(8,128)S(1)}, u32[]{:S(2)}, u32[]{:S(2)}) %collective-permute-start.2) | collective-permute-done | bytes 98336 | tf_op jit(solution)/shard_map/ppermute | solution.py:260
  15.4 4.3 %collective-permute-start.6 = (f32[8,3072]{1,0:T(8,128)S(1)}, f32[8,3072]{1,0:T(8,128)S(1)}, u32[]{:S(2)}, u32[]{:S(2)}) collective-permute-start(f32[8,3072]{1,0:T(8,128)S(1)} %add_add_fusion.2), channel_id=1, source_target_pairs={{0,18},{1,25},{2,26},{3,17},{4,28},{5,23},{6,20},{7,31},{8,16},{9,... | collective-permute-start | bytes 294920 | tf_op jit(solution)/shard_map/ppermute | solution.py:260
  20.1 1.9 %collective-permute-done.6 = f32[8,3072]{1,0:T(8,128)S(1)} collective-permute-done((f32[8,3072]{1,0:T(8,128)S(1)}, f32[8,3072]{1,0:T(8,128)S(1)}, u32[]{:S(2)}, u32[]{:S(2)}) %collective-permute-start.6) | collective-permute-done | bytes 98336 | tf_op jit(solution)/shard_map/ppermute | solution.py:260
  22.0 2.4 %collective-permute-done.5 = f32[8,3072]{1,0:T(8,128)S(1)} collective-permute-done((f32[8,3072]{1,0:T(8,128)S(1)}, f32[8,3072]{1,0:T(8,128)S(1)}, u32[]{:S(2)}, u32[]{:S(2)}) %collective-permute-start.5) | collective-permute-done | bytes 98336 | tf_op jit(solution)/shard_map/ppermute | solution.py:260
  24.4 3.5 %collective-permute-start.9 = (f32[8,3072]{1,0:T(8,128)S(1)}, f32[8,3072]{1,0:T(8,128)S(1)}, u32[]{:S(2)}, u32[]{:S(2)}) collective-permute-start(f32[8,3072]{1,0:T(8,128)S(1)} %add_add_fusion.1), channel_id=1, source_target_pairs={{0,24},{1,81},{2,82},{3,27},{4,84},{5,29},{6,30},{7,87},{8,88},{9,... | collective-permute-start | bytes 294920 | tf_op jit(solution)/shard_map/ppermute | solution.py:260
  27.9 0.8 %collective-permute-start.8 = (f32[8,3072]{1,0:T(8,128)S(1)}, f32[8,3072]{1,0:T(8,128)S(1)}, u32[]{:S(2)}, u32[]{:S(2)}) collective-permute-start(f32[8,3072]{1,0:T(8,128)S(1)} %add_add_fusion.1), channel_id=1, source_target_pairs={{0,12},{1,97},{2,98},{3,15},{4,100},{5,9},{6,10},{7,103},{8,104},{... | collective-permute-start | bytes 294920 | tf_op jit(solution)/shard_map/ppermute | solution.py:260
  28.7 1.5 %collective-permute-done.9 = f32[8,3072]{1,0:T(8,128)S(1)} collective-permute-done((f32[8,3072]{1,0:T(8,128)S(1)}, f32[8,3072]{1,0:T(8,128)S(1)}, u32[]{:S(2)}, u32[]{:S(2)}) %collective-permute-start.9) | collective-permute-done | bytes 98336 | tf_op jit(solution)/shard_map/ppermute | solution.py:260
  30.2 2.7 %collective-permute-done.8 = f32[8,3072]{1,0:T(8,128)S(1)} collective-permute-done((f32[8,3072]{1,0:T(8,128)S(1)}, f32[8,3072]{1,0:T(8,128)S(1)}, u32[]{:S(2)}, u32[]{:S(2)}) %collective-permute-start.8) | collective-permute-done | bytes 98336 | tf_op jit(solution)/shard_map/ppermute | solution.py:260
  33.0 1.0 %collective-permute-start.10 = (f32[8,3072]{1,0:T(8,128)S(1)}, f32[8,3072]{1,0:T(8,128)S(1)}, u32[]{:S(2)}, u32[]{:S(2)}) collective-permute-start(f32[8,3072]{1,0:T(8,128)S(1)} %add_add_fusion.refs_0_.left_ref), channel_id=1, source_target_pairs={{0,16},{1,17},{2,18},{3,19},{4,20},{5,21},{6,22},{7,23},{8,24},{9,... | collective-permute-start | bytes 294920 | tf_op jit(solution)/shard_map/ppermute | solution.py:260
  34.4 0.5 %collective-permute-done.10.refs_1_.left_ref = f32[8,3072]{1,0:T(8,128)S(1)} collective-permute-done((f32[8,3072]{1,0:T(8,128)S(1)}, f32[8,3072]{1,0:T(8,128)S(1)}, u32[]{:S(2)}, u32[]{:S(2)}) %collective-permute-start.10) | collective-permute-done | bytes 98336 | tf_op jit(solution)/shard_map/ppermute | solution.py:260
  34.9 0.5 %right_other.1 = f32[8,384]{1,0:T(8,128)S(1)} custom-call(bf16[3072,384]{1,0:T(8,128)(2,1)S(1)} %get-tuple-element.19.merged_ref.other_ref, f32[8,3072]{1,0:T(8,128)S(1)} %collective-permute-done.10.refs_1_.left_ref, f32[8,384]{1,0:T(8,128)S(1)} %right_own.1.refs_0_), custom_call_target="tpu_custom_call" | custom-call | flops 37748736 | bytes 2359296 | tf_op jit(solution)/shard_map/right_other/pallas_call | solution.py:134
  35.4 0.9 %collective-permute-start.13 = (f32[8,384]{1,0:T(8,128)S(1)}, f32[8,384]{1,0:T(8,128)S(1)}, u32[]{:S(2)}, u32[]{:S(2)}) collective-permute-start(f32[8,384]{1,0:T(8,128)S(1)} %right_other.1), channel_id=1, source_target_pairs={{0,80},{1,81},{2,82},{3,83},{4,84},{5,85},{6,86},{7,87},{8,88},{9,... | collective-permute-start | bytes 36872 | tf_op jit(solution)/shard_map/ppermute | solution.py:260
  36.3 1.1 %collective-permute-start.12 = (f32[8,384]{1,0:T(8,128)S(1)}, f32[8,384]{1,0:T(8,128)S(1)}, u32[]{:S(2)}, u32[]{:S(2)}) collective-permute-start(f32[8,384]{1,0:T(8,128)S(1)} %right_other.1), channel_id=1, source_target_pairs={{0,112},{1,113},{2,114},{3,115},{4,116},{5,117},{6,118},{7,119},{8... | collective-permute-start | bytes 36872 | tf_op jit(solution)/shard_map/ppermute | solution.py:260
  37.4 1.2 %collective-permute-start.11 = (f32[8,384]{1,0:T(8,128)S(1)}, f32[8,384]{1,0:T(8,128)S(1)}, u32[]{:S(2)}, u32[]{:S(2)}) collective-permute-start(f32[8,384]{1,0:T(8,128)S(1)} %right_other.1), channel_id=1, source_target_pairs={{0,48},{1,49},{2,50},{3,51},{4,52},{5,53},{6,54},{7,55},{8,56},{9,... | collective-permute-start | bytes 36872 | tf_op jit(solution)/shard_map/ppermute | solution.py:260
  38.6 1.5 %collective-permute-done.13 = f32[8,384]{1,0:T(8,128)S(1)} collective-permute-done((f32[8,384]{1,0:T(8,128)S(1)}, f32[8,384]{1,0:T(8,128)S(1)}, u32[]{:S(2)}, u32[]{:S(2)}) %collective-permute-start.13) | collective-permute-done | bytes 12320 | tf_op jit(solution)/shard_map/ppermute | solution.py:260
  40.1 0.5 %collective-permute-done.12 = f32[8,384]{1,0:T(8,128)S(1)} collective-permute-done((f32[8,384]{1,0:T(8,128)S(1)}, f32[8,384]{1,0:T(8,128)S(1)}, u32[]{:S(2)}, u32[]{:S(2)}) %collective-permute-start.12) | collective-permute-done | bytes 12320 | tf_op jit(solution)/shard_map/ppermute | solution.py:260
  41.0 1.7 %basis.1 = (f32[64,128]{1,0:T(8,128)S(1)}, bf16[6144,32]{1,0:T(8,128)(2,1)S(1)}) custom-call(f32[8,3072]{1,0:T(8,128)S(1)} %add_add_fusion.refs_0_.left_ref, f32[8,3072]{1,0:T(8,128)S(1)} %collective-permute-done.10.refs_1_.left_ref), custom_call_target="tpu_custom_call" | custom-call | flops 1572864 | bytes 4194304 | tf_op jit(solution)/shard_map/basis/pallas_call | solution.py:178
  42.7 2.9 %finish.1 = (bf16[1,6144,384]{2,1,0:T(8,128)(2,1)}, bf16[768,384]{1,0:T(8,128)(2,1)}, f32[8,384]{1,0:T(8,128)}) custom-call(bf16[3072,384]{1,0:T(8,128)(2,1)S(1)} %get-tuple-element.18.merged_ref.own_ref, bf16[3072,384]{1,0:T(8,128)(2,1)S(1)} %get-tuple-element.19.merged_ref.other_ref, bf16[6144,32]{1,0:T(8,128)(2,1)S(1)} %get-tuple-element.22.basis_ref, ...), custom_call_target="tpu_custom_call" | custom-call | flops 150994944 | bytes 9437184 | tf_op jit(solution)/shard_map/finish/pallas_call | solution.py:232
  (19 shorter events, 1.9 us)
Async XLA Ops:
  4.5 2.4 %collective-permute-start = (f32[8,3072]{1,0:T(8,128)S(1)}, f32[8,3072]{1,0:T(8,128)S(1)}, u32[]{:S(2)}, u32[]{:S(2)}) collective-permute-start(f32[8,3072]{1,0:T(8,128)S(1)} %get-tuple-element.21), channel_id=1, source_target_pairs={{0,16},{1,17},{2,18},{3,19},{4,20},{5,21},{6,22},{7,23},{8,24},{9,... | collective-permute-start | bytes 294920 | tf_op jit(solution)/shard_map/ppermute | solution.py:260
  6.9 5.6 %collective-permute-start.3 = (f32[8,3072]{1,0:T(8,128)S(1)}, f32[8,3072]{1,0:T(8,128)S(1)}, u32[]{:S(2)}, u32[]{:S(2)}) collective-permute-start(f32[8,3072]{1,0:T(8,128)S(1)} %add.39), channel_id=1, source_target_pairs={{0,80},{1,19},{2,16},{3,83},{4,22},{5,85},{6,86},{7,21},{8,26},{9,... | collective-permute-start | bytes 294920 | tf_op jit(solution)/shard_map/ppermute | solution.py:260
  10.1 5.0 %collective-permute-start.2 = (f32[8,3072]{1,0:T(8,128)S(1)}, f32[8,3072]{1,0:T(8,128)S(1)}, u32[]{:S(2)}, u32[]{:S(2)}) collective-permute-start(f32[8,3072]{1,0:T(8,128)S(1)} %add.39), channel_id=1, source_target_pairs={{0,96},{1,2},{2,1},{3,99},{4,7},{5,101},{6,102},{7,4},{8,11},{9,10... | collective-permute-start | bytes 294920 | tf_op jit(solution)/shard_map/ppermute | solution.py:260
  11.0 4.3 %collective-permute-start.1 = (f32[8,3072]{1,0:T(8,128)S(1)}, f32[8,3072]{1,0:T(8,128)S(1)}, u32[]{:S(2)}, u32[]{:S(2)}) collective-permute-start(f32[8,3072]{1,0:T(8,128)S(1)} %add.39), channel_id=1, source_target_pairs={{0,48},{1,16},{2,19},{3,51},{4,21},{5,53},{6,54},{7,22},{8,25},{9,... | collective-permute-start | bytes 294920 | tf_op jit(solution)/shard_map/ppermute | solution.py:260
  15.4 6.6 %collective-permute-start.6 = (f32[8,3072]{1,0:T(8,128)S(1)}, f32[8,3072]{1,0:T(8,128)S(1)}, u32[]{:S(2)}, u32[]{:S(2)}) collective-permute-start(f32[8,3072]{1,0:T(8,128)S(1)} %add_add_fusion.2), channel_id=1, source_target_pairs={{0,18},{1,25},{2,26},{3,17},{4,28},{5,23},{6,20},{7,31},{8,16},{9,... | collective-permute-start | bytes 294920 | tf_op jit(solution)/shard_map/ppermute | solution.py:260
  19.7 4.7 %collective-permute-start.5 = (f32[8,3072]{1,0:T(8,128)S(1)}, f32[8,3072]{1,0:T(8,128)S(1)}, u32[]{:S(2)}, u32[]{:S(2)}) collective-permute-start(f32[8,3072]{1,0:T(8,128)S(1)} %add_add_fusion.2), channel_id=1, source_target_pairs={{0,3},{1,13},{2,14},{3,0},{4,8},{5,6},{6,5},{7,11},{8,4},{9,10},{1... | collective-permute-start | bytes 294920 | tf_op jit(solution)/shard_map/ppermute | solution.py:260
  20.1 4.2 %collective-permute-start.4 = (f32[8,3072]{1,0:T(8,128)S(1)}, f32[8,3072]{1,0:T(8,128)S(1)}, u32[]{:S(2)}, u32[]{:S(2)}) collective-permute-start(f32[8,3072]{1,0:T(8,128)S(1)} %add_add_fusion.2), channel_id=1, source_target_pairs={{0,17},{1,21},{2,22},{3,18},{4,16},{5,20},{6,23},{7,19},{8,28},{9,... | collective-permute-start | bytes 294920 | tf_op jit(solution)/shard_map/ppermute | solution.py:260
  24.4 5.8 %collective-permute-start.9 = (f32[8,3072]{1,0:T(8,128)S(1)}, f32[8,3072]{1,0:T(8,128)S(1)}, u32[]{:S(2)}, u32[]{:S(2)}) collective-permute-start(f32[8,3072]{1,0:T(8,128)S(1)} %add_add_fusion.1), channel_id=1, source_target_pairs={{0,24},{1,81},{2,82},{3,27},{4,84},{5,29},{6,30},{7,87},{8,88},{9,... | collective-permute-start | bytes 294920 | tf_op jit(solution)/shard_map/ppermute | solution.py:260
  27.9 5.0 %collective-permute-start.8 = (f32[8,3072]{1,0:T(8,128)S(1)}, f32[8,3072]{1,0:T(8,128)S(1)}, u32[]{:S(2)}, u32[]{:S(2)}) collective-permute-start(f32[8,3072]{1,0:T(8,128)S(1)} %add_add_fusion.1), channel_id=1, source_target_pairs={{0,12},{1,97},{2,98},{3,15},{4,100},{5,9},{6,10},{7,103},{8,104},{... | collective-permute-start | bytes 294920 | tf_op jit(solution)/shard_map/ppermute | solution.py:260
  28.7 4.3 %collective-permute-start.7 = (f32[8,3072]{1,0:T(8,128)S(1)}, f32[8,3072]{1,0:T(8,128)S(1)}, u32[]{:S(2)}, u32[]{:S(2)}) collective-permute-start(f32[8,3072]{1,0:T(8,128)S(1)} %add_add_fusion.1), channel_id=1, source_target_pairs={{0,20},{1,49},{2,50},{3,23},{4,52},{5,17},{6,18},{7,55},{8,56},{9,... | collective-permute-start | bytes 294920 | tf_op jit(solution)/shard_map/ppermute | solution.py:260
  33.0 1.9 %collective-permute-start.10 = (f32[8,3072]{1,0:T(8,128)S(1)}, f32[8,3072]{1,0:T(8,128)S(1)}, u32[]{:S(2)}, u32[]{:S(2)}) collective-permute-start(f32[8,3072]{1,0:T(8,128)S(1)} %add_add_fusion.refs_0_.left_ref), channel_id=1, source_target_pairs={{0,16},{1,17},{2,18},{3,19},{4,20},{5,21},{6,22},{7,23},{8,24},{9,... | collective-permute-start | bytes 294920 | tf_op jit(solution)/shard_map/ppermute | solution.py:260
  34.0 8.7 %copy-start = (bf16[768,384]{1,0:T(8,128)(2,1)S(1)}, bf16[768,384]{1,0:T(8,128)(2,1)}, u32[]{:S(2)}) copy-start(bf16[768,384]{1,0:T(8,128)(2,1)} %mom_ref.1) | copy-start | bytes 1769476
  35.4 4.7 %collective-permute-start.13 = (f32[8,384]{1,0:T(8,128)S(1)}, f32[8,384]{1,0:T(8,128)S(1)}, u32[]{:S(2)}, u32[]{:S(2)}) collective-permute-start(f32[8,384]{1,0:T(8,128)S(1)} %right_other.1), channel_id=1, source_target_pairs={{0,80},{1,81},{2,82},{3,83},{4,84},{5,85},{6,86},{7,87},{8,88},{9,... | collective-permute-start | bytes 36872 | tf_op jit(solution)/shard_map/ppermute | solution.py:260
  36.3 4.3 %collective-permute-start.12 = (f32[8,384]{1,0:T(8,128)S(1)}, f32[8,384]{1,0:T(8,128)S(1)}, u32[]{:S(2)}, u32[]{:S(2)}) collective-permute-start(f32[8,384]{1,0:T(8,128)S(1)} %right_other.1), channel_id=1, source_target_pairs={{0,112},{1,113},{2,114},{3,115},{4,116},{5,117},{6,118},{7,119},{8... | collective-permute-start | bytes 36872 | tf_op jit(solution)/shard_map/ppermute | solution.py:260
  37.4 3.2 %collective-permute-start.11 = (f32[8,384]{1,0:T(8,128)S(1)}, f32[8,384]{1,0:T(8,128)S(1)}, u32[]{:S(2)}, u32[]{:S(2)}) collective-permute-start(f32[8,384]{1,0:T(8,128)S(1)} %right_other.1), channel_id=1, source_target_pairs={{0,48},{1,49},{2,50},{3,51},{4,52},{5,53},{6,54},{7,55},{8,56},{9,... | collective-permute-start | bytes 36872 | tf_op jit(solution)/shard_map/ppermute | solution.py:260
  40.6 2.1 %collective-permute-start.14 = (f32[8,384]{1,0:T(8,128)S(1)}, f32[8,384]{1,0:T(8,128)S(1)}, u32[]{:S(2)}, u32[]{:S(2)}) collective-permute-start(f32[8,384]{1,0:T(8,128)S(1)} %add_add_fusion.3.sum_ref), channel_id=1, source_target_pairs={{0,16},{1,17},{2,18},{3,19},{4,20},{5,21},{6,22},{7,23},{8,24},{9,... | collective-permute-start | bytes 36872 | tf_op jit(solution)/shard_map/ppermute | solution.py:260

commit v13 on v10

--- a/solution.py
+++ b/solution.py
@@ -8,7 +8,7 @@
 F32, BF16 = jnp.float32, jnp.bfloat16
 ROWS, COLS, RANK = 6144, 384, 8
 HALF = ROWS // 2
-CHUNKS = 3
+CHUNKS = 4
 CHUNK = HALF // CHUNKS
 WRITES = [(start, HALF // 4) for start in range(0, ROWS, HALF // 4)]
 LANES = 128

time: 44.8 us -> 45.8 us (1.022)
  Pallas kernels: 10.1 us -> 11.1 us
    pallas_call x1, Pallas kernels: 3.9 us -> 4.88 us  [merge_other(): pl.pallas_call(load_kernel, in_specs=in_hbm(3), out_specs=[whole()] * 5,...]
where the time goes in v13:
time: 45.8 us; the launch traced here: 45.7 us
  starting transfers between devices  19.1 us (42%)
  waiting for transfers between devices  14.7 us (32%)
  Pallas kernels  11.1 us (24%)
  between operations  0.7 us (2%)
    ppermute x15, starting transfers between devices, swap(): return lax.ppermute(x, ('replica', 'tensor'), pairs)  19.1 us
    ppermute x15, waiting for transfers between devices, swap(): return lax.ppermute(x, ('replica', 'tensor'), pairs)  14.7 us
    pallas_call x1, Pallas kernels, merge_other(): pl.pallas_call(load_kernel, in_specs=in_hbm(3), out_specs=[whole()] * 5,...  4.88 us
    pallas_call x1, Pallas kernels, finish(): pl.pallas_call(final_kernel, in_specs=[whole()] * 9, out_specs=in_hbm(3),...  2.89 us
    pallas_call x1, Pallas kernels, make_basis(): pl.pallas_call(body, in_specs=[whole(), whole()], out_specs=[whole(), who...  1.66 us
  transfers between devices with their start and end apart: 15, of which 12 were waited for; matrix products, arithmetic and copies ran while one was open for 0% of the time, Pallas kernels for 6%

profile of v13, /device:TPU:1, one launch (start us, length us, event | category | flops | bytes accessed | tf_op | source)
XLA Modules:
  0.0 45.7 jit_solution(17935943514846297679)
XLA Ops:
  0.6 4.9 %merge_other.1 = (bf16[3072,384]{1,0:T(8,128)(2,1)S(1)}, f32[8,3072]{1,0:T(8,128)S(1)}, bf16[3072,384]{1,0:T(8,128)(2,1)S(1)}, bf16[3072,384]{1,0:T(8,128)(2,1)S(1)}, f32[8,384]{1,0:T(8,128)S(1)}) custom-call(bf16[1,6144,384]{2,1,0:T(8,128)(2,1)} %g_ref.1, bf16[1,6144,384]{2,1,0:T(8,128)(2,1)} %f_ref.1, f32[8,384]{1,0:T(8,128)} %bitcast.2), custom_call_target="tpu_custom_call" | custom-call | flops 18874368 | bytes 9437184 | tf_op jit(solution)/shard_map/merge_other/pallas_call | solution.py:88
  5.5 1.5 %collective-permute-start = (f32[8,3072]{1,0:T(8,128)S(1)}, f32[8,3072]{1,0:T(8,128)S(1)}, u32[]{:S(2)}, u32[]{:S(2)}) collective-permute-start(f32[8,3072]{1,0:T(8,128)S(1)} %get-tuple-element.21), channel_id=1, source_target_pairs={{0,16},{1,17},{2,18},{3,19},{4,20},{5,21},{6,22},{7,23},{8,24},{9,... | collective-permute-start | bytes 294920 | tf_op jit(solution)/shard_map/ppermute | solution.py:260
  7.0 0.8 %merge_own.1 = (bf16[3072,384]{1,0:T(8,128)(2,1)S(1)}, f32[8,3072]{1,0:T(8,128)S(1)}) custom-call(bf16[3072,384]{1,0:T(8,128)(2,1)S(1)} %get-tuple-element.15.g_ref, bf16[3072,384]{1,0:T(8,128)(2,1)S(1)} %get-tuple-element.16.f_ref, f32[8,384]{1,0:T(8,128)S(1)} %get-tuple-element.17.q_ref), custom_call_target="tpu_custom_call" | custom-call | flops 18874368 | bytes 4718592 | tf_op jit(solution)/shard_map/merge_own/pallas_call | solution.py:113
  8.0 3.2 %collective-permute-start.3 = (f32[8,3072]{1,0:T(8,128)S(1)}, f32[8,3072]{1,0:T(8,128)S(1)}, u32[]{:S(2)}, u32[]{:S(2)}) collective-permute-start(f32[8,3072]{1,0:T(8,128)S(1)} %add.33), channel_id=1, source_target_pairs={{0,80},{1,19},{2,16},{3,83},{4,22},{5,85},{6,86},{7,21},{8,26},{9,... | collective-permute-start | bytes 294920 | tf_op jit(solution)/shard_map/ppermute | solution.py:260
  11.1 0.9 %collective-permute-start.2 = (f32[8,3072]{1,0:T(8,128)S(1)}, f32[8,3072]{1,0:T(8,128)S(1)}, u32[]{:S(2)}, u32[]{:S(2)}) collective-permute-start(f32[8,3072]{1,0:T(8,128)S(1)} %add.33), channel_id=1, source_target_pairs={{0,96},{1,2},{2,1},{3,99},{4,7},{5,101},{6,102},{7,4},{8,11},{9,10... | collective-permute-start | bytes 294920 | tf_op jit(solution)/shard_map/ppermute | solution.py:260
  12.0 1.6 %collective-permute-done.3 = f32[8,3072]{1,0:T(8,128)S(1)} collective-permute-done((f32[8,3072]{1,0:T(8,128)S(1)}, f32[8,3072]{1,0:T(8,128)S(1)}, u32[]{:S(2)}, u32[]{:S(2)}) %collective-permute-start.3) | collective-permute-done | bytes 98336 | tf_op jit(solution)/shard_map/ppermute | solution.py:260
  13.6 2.5 %collective-permute-done.2 = f32[8,3072]{1,0:T(8,128)S(1)} collective-permute-done((f32[8,3072]{1,0:T(8,128)S(1)}, f32[8,3072]{1,0:T(8,128)S(1)}, u32[]{:S(2)}, u32[]{:S(2)}) %collective-permute-start.2) | collective-permute-done | bytes 98336 | tf_op jit(solution)/shard_map/ppermute | solution.py:260
  16.4 4.3 %collective-permute-start.6 = (f32[8,3072]{1,0:T(8,128)S(1)}, f32[8,3072]{1,0:T(8,128)S(1)}, u32[]{:S(2)}, u32[]{:S(2)}) collective-permute-start(f32[8,3072]{1,0:T(8,128)S(1)} %add_add_fusion.2), channel_id=1, source_target_pairs={{0,18},{1,25},{2,26},{3,17},{4,28},{5,23},{6,20},{7,31},{8,16},{9,... | collective-permute-start | bytes 294920 | tf_op jit(solution)/shard_map/ppermute | solution.py:260
  21.1 1.9 %collective-permute-done.6 = f32[8,3072]{1,0:T(8,128)S(1)} collective-permute-done((f32[8,3072]{1,0:T(8,128)S(1)}, f32[8,3072]{1,0:T(8,128)S(1)}, u32[]{:S(2)}, u32[]{:S(2)}) %collective-permute-start.6) | collective-permute-done | bytes 98336 | tf_op jit(solution)/shard_map/ppermute | solution.py:260
  23.0 2.4 %collective-permute-done.5 = f32[8,3072]{1,0:T(8,128)S(1)} collective-permute-done((f32[8,3072]{1,0:T(8,128)S(1)}, f32[8,3072]{1,0:T(8,128)S(1)}, u32[]{:S(2)}, u32[]{:S(2)}) %collective-permute-start.5) | collective-permute-done | bytes 98336 | tf_op jit(solution)/shard_map/ppermute | solution.py:260
  25.4 3.5 %collective-permute-start.9 = (f32[8,3072]{1,0:T(8,128)S(1)}, f32[8,3072]{1,0:T(8,128)S(1)}, u32[]{:S(2)}, u32[]{:S(2)}) collective-permute-start(f32[8,3072]{1,0:T(8,128)S(1)} %add_add_fusion.1), channel_id=1, source_target_pairs={{0,24},{1,81},{2,82},{3,27},{4,84},{5,29},{6,30},{7,87},{8,88},{9,... | collective-permute-start | bytes 294920 | tf_op jit(solution)/shard_map/ppermute | solution.py:260
  28.9 0.8 %collective-permute-start.8 = (f32[8,3072]{1,0:T(8,128)S(1)}, f32[8,3072]{1,0:T(8,128)S(1)}, u32[]{:S(2)}, u32[]{:S(2)}) collective-permute-start(f32[8,3072]{1,0:T(8,128)S(1)} %add_add_fusion.1), channel_id=1, source_target_pairs={{0,12},{1,97},{2,98},{3,15},{4,100},{5,9},{6,10},{7,103},{8,104},{... | collective-permute-start | bytes 294920 | tf_op jit(solution)/shard_map/ppermute | solution.py:260
  29.6 1.5 %collective-permute-done.9 = f32[8,3072]{1,0:T(8,128)S(1)} collective-permute-done((f32[8,3072]{1,0:T(8,128)S(1)}, f32[8,3072]{1,0:T(8,128)S(1)}, u32[]{:S(2)}, u32[]{:S(2)}) %collective-permute-start.9) | collective-permute-done | bytes 98336 | tf_op jit(solution)/shard_map/ppermute | solution.py:260
  31.2 2.7 %collective-permute-done.8 = f32[8,3072]{1,0:T(8,128)S(1)} collective-permute-done((f32[8,3072]{1,0:T(8,128)S(1)}, f32[8,3072]{1,0:T(8,128)S(1)}, u32[]{:S(2)}, u32[]{:S(2)}) %collective-permute-start.8) | collective-permute-done | bytes 98336 | tf_op jit(solution)/shard_map/ppermute | solution.py:260
  34.0 1.0 %collective-permute-start.10 = (f32[8,3072]{1,0:T(8,128)S(1)}, f32[8,3072]{1,0:T(8,128)S(1)}, u32[]{:S(2)}, u32[]{:S(2)}) collective-permute-start(f32[8,3072]{1,0:T(8,128)S(1)} %add_add_fusion.refs_0_.left_ref), channel_id=1, source_target_pairs={{0,16},{1,17},{2,18},{3,19},{4,20},{5,21},{6,22},{7,23},{8,24},{9,... | collective-permute-start | bytes 294920 | tf_op jit(solution)/shard_map/ppermute | solution.py:260
  35.0 0.4 right_own.1.refs_0_
  35.4 0.5 %collective-permute-done.10.refs_1_.left_ref = f32[8,3072]{1,0:T(8,128)S(1)} collective-permute-done((f32[8,3072]{1,0:T(8,128)S(1)}, f32[8,3072]{1,0:T(8,128)S(1)}, u32[]{:S(2)}, u32[]{:S(2)}) %collective-permute-start.10) | collective-permute-done | bytes 98336 | tf_op jit(solution)/shard_map/ppermute | solution.py:260
  35.9 0.5 right_other.1
  36.8 0.8 %collective-permute-done.11 = f32[8,384]{1,0:T(8,128)S(1)} collective-permute-done((f32[8,384]{1,0:T(8,128)S(1)}, f32[8,384]{1,0:T(8,128)S(1)}, u32[]{:S(2)}, u32[]{:S(2)}) %collective-permute-start.11) | collective-permute-done | bytes 12320 | tf_op jit(solution)/shard_map/ppermute | solution.py:260
  37.6 0.8 %collective-permute-start.14 = (f32[8,384]{1,0:T(8,128)S(1)}, f32[8,384]{1,0:T(8,128)S(1)}, u32[]{:S(2)}, u32[]{:S(2)}) collective-permute-start(f32[8,384]{1,0:T(8,128)S(1)} %add.43.sum_ref), channel_id=1, source_target_pairs={{0,80},{1,81},{2,82},{3,83},{4,84},{5,85},{6,86},{7,87},{8,88},{9,... | collective-permute-start | bytes 36872 | tf_op jit(solution)/shard_map/ppermute | solution.py:260
  38.4 1.1 %collective-permute-start.13 = (f32[8,384]{1,0:T(8,128)S(1)}, f32[8,384]{1,0:T(8,128)S(1)}, u32[]{:S(2)}, u32[]{:S(2)}) collective-permute-start(f32[8,384]{1,0:T(8,128)S(1)} %add.43.sum_ref), channel_id=1, source_target_pairs={{0,112},{1,113},{2,114},{3,115},{4,116},{5,117},{6,118},{7,119},{8... | collective-permute-start | bytes 36872 | tf_op jit(solution)/shard_map/ppermute | solution.py:260
  39.6 1.2 %collective-permute-start.12 = (f32[8,384]{1,0:T(8,128)S(1)}, f32[8,384]{1,0:T(8,128)S(1)}, u32[]{:S(2)}, u32[]{:S(2)}) collective-permute-start(f32[8,384]{1,0:T(8,128)S(1)} %add.43.sum_ref), channel_id=1, source_target_pairs={{0,48},{1,49},{2,50},{3,51},{4,52},{5,53},{6,54},{7,55},{8,56},{9,... | collective-permute-start | bytes 36872 | tf_op jit(solution)/shard_map/ppermute | solution.py:260
  40.8 1.7 %basis.1 = (f32[64,128]{1,0:T(8,128)S(1)}, bf16[6144,32]{1,0:T(8,128)(2,1)S(1)}) custom-call(f32[8,3072]{1,0:T(8,128)S(1)} %add_add_fusion.refs_0_.left_ref, f32[8,3072]{1,0:T(8,128)S(1)} %collective-permute-done.10.refs_1_.left_ref), custom_call_target="tpu_custom_call" | custom-call | flops 1572864 | bytes 4194304 | tf_op jit(solution)/shard_map/basis/pallas_call | solution.py:178
  42.8 2.9 %finish.1 = (bf16[1,6144,384]{2,1,0:T(8,128)(2,1)}, bf16[768,384]{1,0:T(8,128)(2,1)}, f32[8,384]{1,0:T(8,128)}) custom-call(bf16[3072,384]{1,0:T(8,128)(2,1)S(1)} %get-tuple-element.18.merged_ref.own_ref, bf16[3072,384]{1,0:T(8,128)(2,1)S(1)} %get-tuple-element.19.merged_ref.other_ref, bf16[6144,32]{1,0:T(8,128)(2,1)S(1)} %get-tuple-element.22.basis_ref, ...), custom_call_target="tpu_custom_call" | custom-call | flops 150994944 | bytes 9437184 | tf_op jit(solution)/shard_map/finish/pallas_call | solution.py:232
  (19 shorter events, 1.8 us)
Async XLA Ops:
  5.5 2.4 %collective-permute-start = (f32[8,3072]{1,0:T(8,128)S(1)}, f32[8,3072]{1,0:T(8,128)S(1)}, u32[]{:S(2)}, u32[]{:S(2)}) collective-permute-start(f32[8,3072]{1,0:T(8,128)S(1)} %get-tuple-element.21), channel_id=1, source_target_pairs={{0,16},{1,17},{2,18},{3,19},{4,20},{5,21},{6,22},{7,23},{8,24},{9,... | collective-permute-start | bytes 294920 | tf_op jit(solution)/shard_map/ppermute | solution.py:260
  8.0 5.6 %collective-permute-start.3 = (f32[8,3072]{1,0:T(8,128)S(1)}, f32[8,3072]{1,0:T(8,128)S(1)}, u32[]{:S(2)}, u32[]{:S(2)}) collective-permute-start(f32[8,3072]{1,0:T(8,128)S(1)} %add.33), channel_id=1, source_target_pairs={{0,80},{1,19},{2,16},{3,83},{4,22},{5,85},{6,86},{7,21},{8,26},{9,... | collective-permute-start | bytes 294920 | tf_op jit(solution)/shard_map/ppermute | solution.py:260
  11.1 5.0 %collective-permute-start.2 = (f32[8,3072]{1,0:T(8,128)S(1)}, f32[8,3072]{1,0:T(8,128)S(1)}, u32[]{:S(2)}, u32[]{:S(2)}) collective-permute-start(f32[8,3072]{1,0:T(8,128)S(1)} %add.33), channel_id=1, source_target_pairs={{0,96},{1,2},{2,1},{3,99},{4,7},{5,101},{6,102},{7,4},{8,11},{9,10... | collective-permute-start | bytes 294920 | tf_op jit(solution)/shard_map/ppermute | solution.py:260
  12.0 4.3 %collective-permute-start.1 = (f32[8,3072]{1,0:T(8,128)S(1)}, f32[8,3072]{1,0:T(8,128)S(1)}, u32[]{:S(2)}, u32[]{:S(2)}) collective-permute-start(f32[8,3072]{1,0:T(8,128)S(1)} %add.33), channel_id=1, source_target_pairs={{0,48},{1,16},{2,19},{3,51},{4,21},{5,53},{6,54},{7,22},{8,25},{9,... | collective-permute-start | bytes 294920 | tf_op jit(solution)/shard_map/ppermute | solution.py:260
  16.4 6.6 %collective-permute-start.6 = (f32[8,3072]{1,0:T(8,128)S(1)}, f32[8,3072]{1,0:T(8,128)S(1)}, u32[]{:S(2)}, u32[]{:S(2)}) collective-permute-start(f32[8,3072]{1,0:T(8,128)S(1)} %add_add_fusion.2), channel_id=1, source_target_pairs={{0,18},{1,25},{2,26},{3,17},{4,28},{5,23},{6,20},{7,31},{8,16},{9,... | collective-permute-start | bytes 294920 | tf_op jit(solution)/shard_map/ppermute | solution.py:260
  20.7 4.7 %collective-permute-start.5 = (f32[8,3072]{1,0:T(8,128)S(1)}, f32[8,3072]{1,0:T(8,128)S(1)}, u32[]{:S(2)}, u32[]{:S(2)}) collective-permute-start(f32[8,3072]{1,0:T(8,128)S(1)} %add_add_fusion.2), channel_id=1, source_target_pairs={{0,3},{1,13},{2,14},{3,0},{4,8},{5,6},{6,5},{7,11},{8,4},{9,10},{1... | collective-permute-start | bytes 294920 | tf_op jit(solution)/shard_map/ppermute | solution.py:260
  21.1 4.2 %collective-permute-start.4 = (f32[8,3072]{1,0:T(8,128)S(1)}, f32[8,3072]{1,0:T(8,128)S(1)}, u32[]{:S(2)}, u32[]{:S(2)}) collective-permute-start(f32[8,3072]{1,0:T(8,128)S(1)} %add_add_fusion.2), channel_id=1, source_target_pairs={{0,17},{1,21},{2,22},{3,18},{4,16},{5,20},{6,23},{7,19},{8,28},{9,... | collective-permute-start | bytes 294920 | tf_op jit(solution)/shard_map/ppermute | solution.py:260
  25.4 5.8 %collective-permute-start.9 = (f32[8,3072]{1,0:T(8,128)S(1)}, f32[8,3072]{1,0:T(8,128)S(1)}, u32[]{:S(2)}, u32[]{:S(2)}) collective-permute-start(f32[8,3072]{1,0:T(8,128)S(1)} %add_add_fusion.1), channel_id=1, source_target_pairs={{0,24},{1,81},{2,82},{3,27},{4,84},{5,29},{6,30},{7,87},{8,88},{9,... | collective-permute-start | bytes 294920 | tf_op jit(solution)/shard_map/ppermute | solution.py:260
  28.9 5.0 %collective-permute-start.8 = (f32[8,3072]{1,0:T(8,128)S(1)}, f32[8,3072]{1,0:T(8,128)S(1)}, u32[]{:S(2)}, u32[]{:S(2)}) collective-permute-start(f32[8,3072]{1,0:T(8,128)S(1)} %add_add_fusion.1), channel_id=1, source_target_pairs={{0,12},{1,97},{2,98},{3,15},{4,100},{5,9},{6,10},{7,103},{8,104},{... | collective-permute-start | bytes 294920 | tf_op jit(solution)/shard_map/ppermute | solution.py:260
  29.6 4.3 %collective-permute-start.7 = (f32[8,3072]{1,0:T(8,128)S(1)}, f32[8,3072]{1,0:T(8,128)S(1)}, u32[]{:S(2)}, u32[]{:S(2)}) collective-permute-start(f32[8,3072]{1,0:T(8,128)S(1)} %add_add_fusion.1), channel_id=1, source_target_pairs={{0,20},{1,49},{2,50},{3,23},{4,52},{5,17},{6,18},{7,55},{8,56},{9,... | collective-permute-start | bytes 294920 | tf_op jit(solution)/shard_map/ppermute | solution.py:260
  34.0 1.9 %collective-permute-start.10 = (f32[8,3072]{1,0:T(8,128)S(1)}, f32[8,3072]{1,0:T(8,128)S(1)}, u32[]{:S(2)}, u32[]{:S(2)}) collective-permute-start(f32[8,3072]{1,0:T(8,128)S(1)} %add_add_fusion.refs_0_.left_ref), channel_id=1, source_target_pairs={{0,16},{1,17},{2,18},{3,19},{4,20},{5,21},{6,22},{7,23},{8,24},{9,... | collective-permute-start | bytes 294920 | tf_op jit(solution)/shard_map/ppermute | solution.py:260
  35.0 7.8 %copy-start = (bf16[768,384]{1,0:T(8,128)(2,1)S(1)}, bf16[768,384]{1,0:T(8,128)(2,1)}, u32[]{:S(2)}) copy-start(bf16[768,384]{1,0:T(8,128)(2,1)} %mom_ref.1) | copy-start | bytes 1769476
  36.4 1.3 %collective-permute-start.11 = (f32[8,384]{1,0:T(8,128)S(1)}, f32[8,384]{1,0:T(8,128)S(1)}, u32[]{:S(2)}, u32[]{:S(2)}) collective-permute-start(f32[8,384]{1,0:T(8,128)S(1)} %right_other.1), channel_id=1, source_target_pairs={{0,16},{1,17},{2,18},{3,19},{4,20},{5,21},{6,22},{7,23},{8,24},{9,... | collective-permute-start | bytes 36872 | tf_op jit(solution)/shard_map/ppermute | solution.py:260
  37.6 4.8 %collective-permute-start.14 = (f32[8,384]{1,0:T(8,128)S(1)}, f32[8,384]{1,0:T(8,128)S(1)}, u32[]{:S(2)}, u32[]{:S(2)}) collective-permute-start(f32[8,384]{1,0:T(8,128)S(1)} %add.43.sum_ref), channel_id=1, source_target_pairs={{0,80},{1,81},{2,82},{3,83},{4,84},{5,85},{6,86},{7,87},{8,88},{9,... | collective-permute-start | bytes 36872 | tf_op jit(solution)/shard_map/ppermute | solution.py:260
  38.4 4.3 %collective-permute-start.13 = (f32[8,384]{1,0:T(8,128)S(1)}, f32[8,384]{1,0:T(8,128)S(1)}, u32[]{:S(2)}, u32[]{:S(2)}) collective-permute-start(f32[8,384]{1,0:T(8,128)S(1)} %add.43.sum_ref), channel_id=1, source_target_pairs={{0,112},{1,113},{2,114},{3,115},{4,116},{5,117},{6,118},{7,119},{8... | collective-permute-start | bytes 36872 | tf_op jit(solution)/shard_map/ppermute | solution.py:260
  39.6 3.2 %collective-permute-start.12 = (f32[8,384]{1,0:T(8,128)S(1)}, f32[8,384]{1,0:T(8,128)S(1)}, u32[]{:S(2)}, u32[]{:S(2)}) collective-permute-start(f32[8,384]{1,0:T(8,128)S(1)} %add.43.sum_ref), channel_id=1, source_target_pairs={{0,48},{1,49},{2,50},{3,51},{4,52},{5,53},{6,54},{7,55},{8,56},{9,... | collective-permute-start | bytes 36872 | tf_op jit(solution)/shard_map/ppermute | solution.py:260

commit v14 on v13

--- a/solution.py
+++ b/solution.py
@@ -8,7 +8,7 @@
 F32, BF16 = jnp.float32, jnp.bfloat16
 ROWS, COLS, RANK = 6144, 384, 8
 HALF = ROWS // 2
-CHUNKS = 4
+CHUNKS = 2
 CHUNK = HALF // CHUNKS
 WRITES = [(start, HALF // 4) for start in range(0, ROWS, HALF // 4)]
 LANES = 128

time: 45.8 us -> 44.8 us (0.978)
  Pallas kernels: 11.1 us -> 10.1 us
    pallas_call x1, Pallas kernels: 4.88 us -> 3.83 us  [merge_other(): pl.pallas_call(load_kernel, in_specs=in_hbm(3), out_specs=[whole()] * 5,...]
where the time goes in v14:
time: 44.8 us; the launch traced here: 44.6 us
  starting transfers between devices  19.1 us (43%)
  waiting for transfers between devices  14.7 us (33%)
  Pallas kernels  10.1 us (23%)
  between operations  0.7 us (2%)
    ppermute x15, starting transfers between devices, swap(): return lax.ppermute(x, ('replica', 'tensor'), pairs)  19.1 us
    ppermute x15, waiting for transfers between devices, swap(): return lax.ppermute(x, ('replica', 'tensor'), pairs)  14.7 us
    pallas_call x1, Pallas kernels, merge_other(): pl.pallas_call(load_kernel, in_specs=in_hbm(3), out_specs=[whole()] * 5,...  3.83 us
    pallas_call x1, Pallas kernels, finish(): pl.pallas_call(final_kernel, in_specs=[whole()] * 9, out_specs=in_hbm(3),...  2.88 us
    pallas_call x1, Pallas kernels, make_basis(): pl.pallas_call(body, in_specs=[whole(), whole()], out_specs=[whole(), who...  1.66 us
    pallas_call x2, Pallas kernels, right_term(): pl.pallas_call(right_kernel, in_specs=[whole()] * (2 + len(before)), out_...  0.9 us
  transfers between devices with their start and end apart: 15, of which 12 were waited for; matrix products, arithmetic and copies ran while one was open for 0% of the time, Pallas kernels for 6%

profile of v14, /device:TPU:1, one launch (start us, length us, event | category | flops | bytes accessed | tf_op | source)
XLA Modules:
  0.0 44.6 jit_solution(13196991447283956691)
XLA Ops:
  0.6 3.8 %merge_other.1 = (bf16[3072,384]{1,0:T(8,128)(2,1)S(1)}, f32[8,3072]{1,0:T(8,128)S(1)}, bf16[3072,384]{1,0:T(8,128)(2,1)S(1)}, bf16[3072,384]{1,0:T(8,128)(2,1)S(1)}, f32[8,384]{1,0:T(8,128)S(1)}) custom-call(bf16[1,6144,384]{2,1,0:T(8,128)(2,1)} %g_ref.1, bf16[1,6144,384]{2,1,0:T(8,128)(2,1)} %f_ref.1, f32[8,384]{1,0:T(8,128)} %bitcast.2), custom_call_target="tpu_custom_call" | custom-call | flops 18874368 | bytes 9437184 | tf_op jit(solution)/shard_map/merge_other/pallas_call | solution.py:88
  4.5 1.5 %collective-permute-start = (f32[8,3072]{1,0:T(8,128)S(1)}, f32[8,3072]{1,0:T(8,128)S(1)}, u32[]{:S(2)}, u32[]{:S(2)}) collective-permute-start(f32[8,3072]{1,0:T(8,128)S(1)} %get-tuple-element.21), channel_id=1, source_target_pairs={{0,16},{1,17},{2,18},{3,19},{4,20},{5,21},{6,22},{7,23},{8,24},{9,... | collective-permute-start | bytes 294920 | tf_op jit(solution)/shard_map/ppermute | solution.py:260
  6.0 0.8 %merge_own.1 = (bf16[3072,384]{1,0:T(8,128)(2,1)S(1)}, f32[8,3072]{1,0:T(8,128)S(1)}) custom-call(bf16[3072,384]{1,0:T(8,128)(2,1)S(1)} %get-tuple-element.15.g_ref, bf16[3072,384]{1,0:T(8,128)(2,1)S(1)} %get-tuple-element.16.f_ref, f32[8,384]{1,0:T(8,128)S(1)} %get-tuple-element.17.q_ref), custom_call_target="tpu_custom_call" | custom-call | flops 18874368 | bytes 4718592 | tf_op jit(solution)/shard_map/merge_own/pallas_call | solution.py:113
  6.9 3.1 %collective-permute-start.3 = (f32[8,3072]{1,0:T(8,128)S(1)}, f32[8,3072]{1,0:T(8,128)S(1)}, u32[]{:S(2)}, u32[]{:S(2)}) collective-permute-start(f32[8,3072]{1,0:T(8,128)S(1)} %add.33), channel_id=1, source_target_pairs={{0,80},{1,19},{2,16},{3,83},{4,22},{5,85},{6,86},{7,21},{8,26},{9,... | collective-permute-start | bytes 294920 | tf_op jit(solution)/shard_map/ppermute | solution.py:260
  10.1 0.9 %collective-permute-start.2 = (f32[8,3072]{1,0:T(8,128)S(1)}, f32[8,3072]{1,0:T(8,128)S(1)}, u32[]{:S(2)}, u32[]{:S(2)}) collective-permute-start(f32[8,3072]{1,0:T(8,128)S(1)} %add.33), channel_id=1, source_target_pairs={{0,96},{1,2},{2,1},{3,99},{4,7},{5,101},{6,102},{7,4},{8,11},{9,10... | collective-permute-start | bytes 294920 | tf_op jit(solution)/shard_map/ppermute | solution.py:260
  10.9 1.6 %collective-permute-done.3 = f32[8,3072]{1,0:T(8,128)S(1)} collective-permute-done((f32[8,3072]{1,0:T(8,128)S(1)}, f32[8,3072]{1,0:T(8,128)S(1)}, u32[]{:S(2)}, u32[]{:S(2)}) %collective-permute-start.3) | collective-permute-done | bytes 98336 | tf_op jit(solution)/shard_map/ppermute | solution.py:260
  12.6 2.5 %collective-permute-done.2 = f32[8,3072]{1,0:T(8,128)S(1)} collective-permute-done((f32[8,3072]{1,0:T(8,128)S(1)}, f32[8,3072]{1,0:T(8,128)S(1)}, u32[]{:S(2)}, u32[]{:S(2)}) %collective-permute-start.2) | collective-permute-done | bytes 98336 | tf_op jit(solution)/shard_map/ppermute | solution.py:260
  15.3 4.3 %collective-permute-start.6 = (f32[8,3072]{1,0:T(8,128)S(1)}, f32[8,3072]{1,0:T(8,128)S(1)}, u32[]{:S(2)}, u32[]{:S(2)}) collective-permute-start(f32[8,3072]{1,0:T(8,128)S(1)} %add_add_fusion.2), channel_id=1, source_target_pairs={{0,18},{1,25},{2,26},{3,17},{4,28},{5,23},{6,20},{7,31},{8,16},{9,... | collective-permute-start | bytes 294920 | tf_op jit(solution)/shard_map/ppermute | solution.py:260
  20.1 1.9 %collective-permute-done.6 = f32[8,3072]{1,0:T(8,128)S(1)} collective-permute-done((f32[8,3072]{1,0:T(8,128)S(1)}, f32[8,3072]{1,0:T(8,128)S(1)}, u32[]{:S(2)}, u32[]{:S(2)}) %collective-permute-start.6) | collective-permute-done | bytes 98336 | tf_op jit(solution)/shard_map/ppermute | solution.py:260
  22.0 2.4 %collective-permute-done.5 = f32[8,3072]{1,0:T(8,128)S(1)} collective-permute-done((f32[8,3072]{1,0:T(8,128)S(1)}, f32[8,3072]{1,0:T(8,128)S(1)}, u32[]{:S(2)}, u32[]{:S(2)}) %collective-permute-start.5) | collective-permute-done | bytes 98336 | tf_op jit(solution)/shard_map/ppermute | solution.py:260
  24.4 3.5 %collective-permute-start.9 = (f32[8,3072]{1,0:T(8,128)S(1)}, f32[8,3072]{1,0:T(8,128)S(1)}, u32[]{:S(2)}, u32[]{:S(2)}) collective-permute-start(f32[8,3072]{1,0:T(8,128)S(1)} %add_add_fusion.1), channel_id=1, source_target_pairs={{0,24},{1,81},{2,82},{3,27},{4,84},{5,29},{6,30},{7,87},{8,88},{9,... | collective-permute-start | bytes 294920 | tf_op jit(solution)/shard_map/ppermute | solution.py:260
  27.8 0.8 %collective-permute-start.8 = (f32[8,3072]{1,0:T(8,128)S(1)}, f32[8,3072]{1,0:T(8,128)S(1)}, u32[]{:S(2)}, u32[]{:S(2)}) collective-permute-start(f32[8,3072]{1,0:T(8,128)S(1)} %add_add_fusion.1), channel_id=1, source_target_pairs={{0,12},{1,97},{2,98},{3,15},{4,100},{5,9},{6,10},{7,103},{8,104},{... | collective-permute-start | bytes 294920 | tf_op jit(solution)/shard_map/ppermute | solution.py:260
  28.6 1.5 %collective-permute-done.9 = f32[8,3072]{1,0:T(8,128)S(1)} collective-permute-done((f32[8,3072]{1,0:T(8,128)S(1)}, f32[8,3072]{1,0:T(8,128)S(1)}, u32[]{:S(2)}, u32[]{:S(2)}) %collective-permute-start.9) | collective-permute-done | bytes 98336 | tf_op jit(solution)/shard_map/ppermute | solution.py:260
  30.1 2.7 %collective-permute-done.8 = f32[8,3072]{1,0:T(8,128)S(1)} collective-permute-done((f32[8,3072]{1,0:T(8,128)S(1)}, f32[8,3072]{1,0:T(8,128)S(1)}, u32[]{:S(2)}, u32[]{:S(2)}) %collective-permute-start.8) | collective-permute-done | bytes 98336 | tf_op jit(solution)/shard_map/ppermute | solution.py:260
  33.0 1.0 %collective-permute-start.10 = (f32[8,3072]{1,0:T(8,128)S(1)}, f32[8,3072]{1,0:T(8,128)S(1)}, u32[]{:S(2)}, u32[]{:S(2)}) collective-permute-start(f32[8,3072]{1,0:T(8,128)S(1)} %add_add_fusion.refs_0_.left_ref), channel_id=1, source_target_pairs={{0,16},{1,17},{2,18},{3,19},{4,20},{5,21},{6,22},{7,23},{8,24},{9,... | collective-permute-start | bytes 294920 | tf_op jit(solution)/shard_map/ppermute | solution.py:260
  33.9 0.4 %right_own.1.refs_0_ = f32[8,384]{1,0:T(8,128)S(1)} custom-call(bf16[3072,384]{1,0:T(8,128)(2,1)S(1)} %get-tuple-element.18.merged_ref.own_ref, f32[8,3072]{1,0:T(8,128)S(1)} %add_add_fusion.refs_0_.left_ref), custom_call_target="tpu_custom_call" | custom-call | flops 37748736 | bytes 2359296 | tf_op jit(solution)/shard_map/right_own/pallas_call | solution.py:134
  34.4 0.5 %collective-permute-done.10.refs_1_.left_ref = f32[8,3072]{1,0:T(8,128)S(1)} collective-permute-done((f32[8,3072]{1,0:T(8,128)S(1)}, f32[8,3072]{1,0:T(8,128)S(1)}, u32[]{:S(2)}, u32[]{:S(2)}) %collective-permute-start.10) | collective-permute-done | bytes 98336 | tf_op jit(solution)/shard_map/ppermute | solution.py:260
  34.9 0.5 %right_other.1 = f32[8,384]{1,0:T(8,128)S(1)} custom-call(bf16[3072,384]{1,0:T(8,128)(2,1)S(1)} %get-tuple-element.19.merged_ref.other_ref, f32[8,3072]{1,0:T(8,128)S(1)} %collective-permute-done.10.refs_1_.left_ref, f32[8,384]{1,0:T(8,128)S(1)} %right_own.1.refs_0_), custom_call_target="tpu_custom_call" | custom-call | flops 37748736 | bytes 2359296 | tf_op jit(solution)/shard_map/right_other/pallas_call | solution.py:134
  35.8 0.8 %collective-permute-done.11 = f32[8,384]{1,0:T(8,128)S(1)} collective-permute-done((f32[8,384]{1,0:T(8,128)S(1)}, f32[8,384]{1,0:T(8,128)S(1)}, u32[]{:S(2)}, u32[]{:S(2)}) %collective-permute-start.11) | collective-permute-done | bytes 12320 | tf_op jit(solution)/shard_map/ppermute | solution.py:260
  36.6 0.8 %collective-permute-start.14 = (f32[8,384]{1,0:T(8,128)S(1)}, f32[8,384]{1,0:T(8,128)S(1)}, u32[]{:S(2)}, u32[]{:S(2)}) collective-permute-start(f32[8,384]{1,0:T(8,128)S(1)} %add.43.sum_ref), channel_id=1, source_target_pairs={{0,80},{1,81},{2,82},{3,83},{4,84},{5,85},{6,86},{7,87},{8,88},{9,... | collective-permute-start | bytes 36872 | tf_op jit(solution)/shard_map/ppermute | solution.py:260
  37.4 1.1 %collective-permute-start.13 = (f32[8,384]{1,0:T(8,128)S(1)}, f32[8,384]{1,0:T(8,128)S(1)}, u32[]{:S(2)}, u32[]{:S(2)}) collective-permute-start(f32[8,384]{1,0:T(8,128)S(1)} %add.43.sum_ref), channel_id=1, source_target_pairs={{0,112},{1,113},{2,114},{3,115},{4,116},{5,117},{6,118},{7,119},{8... | collective-permute-start | bytes 36872 | tf_op jit(solution)/shard_map/ppermute | solution.py:260
  38.5 1.2 %collective-permute-start.12 = (f32[8,384]{1,0:T(8,128)S(1)}, f32[8,384]{1,0:T(8,128)S(1)}, u32[]{:S(2)}, u32[]{:S(2)}) collective-permute-start(f32[8,384]{1,0:T(8,128)S(1)} %add.43.sum_ref), channel_id=1, source_target_pairs={{0,48},{1,49},{2,50},{3,51},{4,52},{5,53},{6,54},{7,55},{8,56},{9,... | collective-permute-start | bytes 36872 | tf_op jit(solution)/shard_map/ppermute | solution.py:260
  39.8 1.7 %basis.1 = (f32[64,128]{1,0:T(8,128)S(1)}, bf16[6144,32]{1,0:T(8,128)(2,1)S(1)}) custom-call(f32[8,3072]{1,0:T(8,128)S(1)} %add_add_fusion.refs_0_.left_ref, f32[8,3072]{1,0:T(8,128)S(1)} %collective-permute-done.10.refs_1_.left_ref), custom_call_target="tpu_custom_call" | custom-call | flops 1572864 | bytes 4194304 | tf_op jit(solution)/shard_map/basis/pallas_call | solution.py:178
  41.7 2.9 %finish.1 = (bf16[1,6144,384]{2,1,0:T(8,128)(2,1)}, bf16[768,384]{1,0:T(8,128)(2,1)}, f32[8,384]{1,0:T(8,128)}) custom-call(bf16[3072,384]{1,0:T(8,128)(2,1)S(1)} %get-tuple-element.18.merged_ref.own_ref, bf16[3072,384]{1,0:T(8,128)(2,1)S(1)} %get-tuple-element.19.merged_ref.other_ref, bf16[6144,32]{1,0:T(8,128)(2,1)S(1)} %get-tuple-element.22.basis_ref, ...), custom_call_target="tpu_custom_call" | custom-call | flops 150994944 | bytes 9437184 | tf_op jit(solution)/shard_map/finish/pallas_call | solution.py:232
  (19 shorter events, 1.8 us)
Async XLA Ops:
  4.5 2.4 %collective-permute-start = (f32[8,3072]{1,0:T(8,128)S(1)}, f32[8,3072]{1,0:T(8,128)S(1)}, u32[]{:S(2)}, u32[]{:S(2)}) collective-permute-start(f32[8,3072]{1,0:T(8,128)S(1)} %get-tuple-element.21), channel_id=1, source_target_pairs={{0,16},{1,17},{2,18},{3,19},{4,20},{5,21},{6,22},{7,23},{8,24},{9,... | collective-permute-start | bytes 294920 | tf_op jit(solution)/shard_map/ppermute | solution.py:260
  6.9 5.6 %collective-permute-start.3 = (f32[8,3072]{1,0:T(8,128)S(1)}, f32[8,3072]{1,0:T(8,128)S(1)}, u32[]{:S(2)}, u32[]{:S(2)}) collective-permute-start(f32[8,3072]{1,0:T(8,128)S(1)} %add.33), channel_id=1, source_target_pairs={{0,80},{1,19},{2,16},{3,83},{4,22},{5,85},{6,86},{7,21},{8,26},{9,... | collective-permute-start | bytes 294920 | tf_op jit(solution)/shard_map/ppermute | solution.py:260
  10.1 5.0 %collective-permute-start.2 = (f32[8,3072]{1,0:T(8,128)S(1)}, f32[8,3072]{1,0:T(8,128)S(1)}, u32[]{:S(2)}, u32[]{:S(2)}) collective-permute-start(f32[8,3072]{1,0:T(8,128)S(1)} %add.33), channel_id=1, source_target_pairs={{0,96},{1,2},{2,1},{3,99},{4,7},{5,101},{6,102},{7,4},{8,11},{9,10... | collective-permute-start | bytes 294920 | tf_op jit(solution)/shard_map/ppermute | solution.py:260
  10.9 4.3 %collective-permute-start.1 = (f32[8,3072]{1,0:T(8,128)S(1)}, f32[8,3072]{1,0:T(8,128)S(1)}, u32[]{:S(2)}, u32[]{:S(2)}) collective-permute-start(f32[8,3072]{1,0:T(8,128)S(1)} %add.33), channel_id=1, source_target_pairs={{0,48},{1,16},{2,19},{3,51},{4,21},{5,53},{6,54},{7,22},{8,25},{9,... | collective-permute-start | bytes 294920 | tf_op jit(solution)/shard_map/ppermute | solution.py:260
  15.3 6.7 %collective-permute-start.6 = (f32[8,3072]{1,0:T(8,128)S(1)}, f32[8,3072]{1,0:T(8,128)S(1)}, u32[]{:S(2)}, u32[]{:S(2)}) collective-permute-start(f32[8,3072]{1,0:T(8,128)S(1)} %add_add_fusion.2), channel_id=1, source_target_pairs={{0,18},{1,25},{2,26},{3,17},{4,28},{5,23},{6,20},{7,31},{8,16},{9,... | collective-permute-start | bytes 294920 | tf_op jit(solution)/shard_map/ppermute | solution.py:260
  19.7 4.7 %collective-permute-start.5 = (f32[8,3072]{1,0:T(8,128)S(1)}, f32[8,3072]{1,0:T(8,128)S(1)}, u32[]{:S(2)}, u32[]{:S(2)}) collective-permute-start(f32[8,3072]{1,0:T(8,128)S(1)} %add_add_fusion.2), channel_id=1, source_target_pairs={{0,3},{1,13},{2,14},{3,0},{4,8},{5,6},{6,5},{7,11},{8,4},{9,10},{1... | collective-permute-start | bytes 294920 | tf_op jit(solution)/shard_map/ppermute | solution.py:260
  20.1 4.2 %collective-permute-start.4 = (f32[8,3072]{1,0:T(8,128)S(1)}, f32[8,3072]{1,0:T(8,128)S(1)}, u32[]{:S(2)}, u32[]{:S(2)}) collective-permute-start(f32[8,3072]{1,0:T(8,128)S(1)} %add_add_fusion.2), channel_id=1, source_target_pairs={{0,17},{1,21},{2,22},{3,18},{4,16},{5,20},{6,23},{7,19},{8,28},{9,... | collective-permute-start | bytes 294920 | tf_op jit(solution)/shard_map/ppermute | solution.py:260
  24.4 5.8 %collective-permute-start.9 = (f32[8,3072]{1,0:T(8,128)S(1)}, f32[8,3072]{1,0:T(8,128)S(1)}, u32[]{:S(2)}, u32[]{:S(2)}) collective-permute-start(f32[8,3072]{1,0:T(8,128)S(1)} %add_add_fusion.1), channel_id=1, source_target_pairs={{0,24},{1,81},{2,82},{3,27},{4,84},{5,29},{6,30},{7,87},{8,88},{9,... | collective-permute-start | bytes 294920 | tf_op jit(solution)/shard_map/ppermute | solution.py:260
  27.8 5.0 %collective-permute-start.8 = (f32[8,3072]{1,0:T(8,128)S(1)}, f32[8,3072]{1,0:T(8,128)S(1)}, u32[]{:S(2)}, u32[]{:S(2)}) collective-permute-start(f32[8,3072]{1,0:T(8,128)S(1)} %add_add_fusion.1), channel_id=1, source_target_pairs={{0,12},{1,97},{2,98},{3,15},{4,100},{5,9},{6,10},{7,103},{8,104},{... | collective-permute-start | bytes 294920 | tf_op jit(solution)/shard_map/ppermute | solution.py:260
  28.6 4.3 %collective-permute-start.7 = (f32[8,3072]{1,0:T(8,128)S(1)}, f32[8,3072]{1,0:T(8,128)S(1)}, u32[]{:S(2)}, u32[]{:S(2)}) collective-permute-start(f32[8,3072]{1,0:T(8,128)S(1)} %add_add_fusion.1), channel_id=1, source_target_pairs={{0,20},{1,49},{2,50},{3,23},{4,52},{5,17},{6,18},{7,55},{8,56},{9,... | collective-permute-start | bytes 294920 | tf_op jit(solution)/shard_map/ppermute | solution.py:260
  33.0 1.9 %collective-permute-start.10 = (f32[8,3072]{1,0:T(8,128)S(1)}, f32[8,3072]{1,0:T(8,128)S(1)}, u32[]{:S(2)}, u32[]{:S(2)}) collective-permute-start(f32[8,3072]{1,0:T(8,128)S(1)} %add_add_fusion.refs_0_.left_ref), channel_id=1, source_target_pairs={{0,16},{1,17},{2,18},{3,19},{4,20},{5,21},{6,22},{7,23},{8,24},{9,... | collective-permute-start | bytes 294920 | tf_op jit(solution)/shard_map/ppermute | solution.py:260
  33.9 7.8 %copy-start = (bf16[768,384]{1,0:T(8,128)(2,1)S(1)}, bf16[768,384]{1,0:T(8,128)(2,1)}, u32[]{:S(2)}) copy-start(bf16[768,384]{1,0:T(8,128)(2,1)} %mom_ref.1) | copy-start | bytes 1769476
  35.3 1.3 %collective-permute-start.11 = (f32[8,384]{1,0:T(8,128)S(1)}, f32[8,384]{1,0:T(8,128)S(1)}, u32[]{:S(2)}, u32[]{:S(2)}) collective-permute-start(f32[8,384]{1,0:T(8,128)S(1)} %right_other.1), channel_id=1, source_target_pairs={{0,16},{1,17},{2,18},{3,19},{4,20},{5,21},{6,22},{7,23},{8,24},{9,... | collective-permute-start | bytes 36872 | tf_op jit(solution)/shard_map/ppermute | solution.py:260
  36.6 4.8 %collective-permute-start.14 = (f32[8,384]{1,0:T(8,128)S(1)}, f32[8,384]{1,0:T(8,128)S(1)}, u32[]{:S(2)}, u32[]{:S(2)}) collective-permute-start(f32[8,384]{1,0:T(8,128)S(1)} %add.43.sum_ref), channel_id=1, source_target_pairs={{0,80},{1,81},{2,82},{3,83},{4,84},{5,85},{6,86},{7,87},{8,88},{9,... | collective-permute-start | bytes 36872 | tf_op jit(solution)/shard_map/ppermute | solution.py:260
  37.4 4.3 %collective-permute-start.13 = (f32[8,384]{1,0:T(8,128)S(1)}, f32[8,384]{1,0:T(8,128)S(1)}, u32[]{:S(2)}, u32[]{:S(2)}) collective-permute-start(f32[8,384]{1,0:T(8,128)S(1)} %add.43.sum_ref), channel_id=1, source_target_pairs={{0,112},{1,113},{2,114},{3,115},{4,116},{5,117},{6,118},{7,119},{8... | collective-permute-start | bytes 36872 | tf_op jit(solution)/shard_map/ppermute | solution.py:260
  38.5 3.2 %collective-permute-start.12 = (f32[8,384]{1,0:T(8,128)S(1)}, f32[8,384]{1,0:T(8,128)S(1)}, u32[]{:S(2)}, u32[]{:S(2)}) collective-permute-start(f32[8,384]{1,0:T(8,128)S(1)} %add.43.sum_ref), channel_id=1, source_target_pairs={{0,48},{1,49},{2,50},{3,51},{4,52},{5,53},{6,54},{7,55},{8,56},{9,... | collective-permute-start | bytes 36872 | tf_op jit(solution)/shard_map/ppermute | solution.py:260
